TPU v7x, 32 devices: a whole 2x2x4 slice. The times are simulated.
32 devices in a mesh: ulys: 4 (over z), blk: 8 (over y, x, core).
Axes of the slice: x: 2, y: 2, z: 4, core: 2. Of those that a mesh axis runs over, the one named last changes fastest.
Arguments:
- target: bfloat16 [4, 1024, 1024], P('ulys', 'blk'), may hold values from -6 to 6
- source: bfloat16 [4, 1024, 1024], P('ulys', 'blk'), may hold values from -6 to 6
- cotangent: bfloat16 [4, 1024, 1024], P('ulys', 'blk'), may hold values from -6 to 6
- target_lengths: int32 [4, 3], replicated, may hold values from 16 to 992, as said below
- source_lengths: int32 [4, 3], replicated, may hold values from 16 to 992, as said below
- self_in: bfloat16 [1024, 3072], P(('ulys', 'blk')), may hold values from -0.1875 to 0.1875
- self_out: bfloat16 [1024, 1024], P(('ulys', 'blk')), may hold values from -0.75 to 0.75
- cross_query: bfloat16 [1024, 1024], P(('ulys', 'blk')), may hold values from -0.1875 to 0.1875
- cross_kv: bfloat16 [1024, 2048], P(('ulys', 'blk')), may hold values from -0.1875 to 0.1875
- cross_out: bfloat16 [1024, 1024], P(('ulys', 'blk')), may hold values from -0.75 to 0.75
- mlp_in: bfloat16 [1024, 8192], P(('ulys', 'blk')), may hold values from -0.1875 to 0.1875
- mlp_out: bfloat16 [8192, 1024], P(('ulys', 'blk')), may hold values from -0.0625 to 0.0625
- vectors: bfloat16 [13, 1024], P(None, ('ulys', 'blk')), may hold values from -1.5 to 1.5, as said below
- hidden_bias: bfloat16 [8192], P(('ulys', 'blk')), may hold values from -2.5 to 2.5
Outputs:
- layer_out: bfloat16 [4, 1024, 1024], P('ulys', 'blk')
- target_grad: bfloat16 [4, 1024, 1024], P('ulys', 'blk')
- source_grad: bfloat16 [4, 1024, 1024], P('ulys', 'blk')
- self_in_grad: float32 [1024, 3072], P(('ulys', 'blk'))
- self_out_grad: float32 [1024, 1024], P(('ulys', 'blk'))
- cross_query_grad: float32 [1024, 1024], P(('ulys', 'blk'))
- cross_kv_grad: float32 [1024, 2048], P(('ulys', 'blk'))
- cross_out_grad: float32 [1024, 1024], P(('ulys', 'blk'))
- mlp_in_grad: float32 [1024, 8192], P(('ulys', 'blk'))
- mlp_out_grad: float32 [8192, 1024], P(('ulys', 'blk'))
- vectors_grad: float32 [13, 1024], P(None, ('ulys', 'blk'))
- hidden_bias_grad: float32 [8192], P(('ulys', 'blk'))
Inputs may be any that keep to these rules, and one draw needn't show every extreme that they name: `target_lengths`: each row sums to 1024; its first and last documents have 16 to 127 positions each, the middle one the rest; in one stream both ends have exactly 16, in another the first has exactly 127. `source_lengths`: each row sums to 1024; its first and last documents have 16 to 127 positions each, the middle one the rest; in one stream both ends have exactly 16, in another the first has exactly 127. `vectors`: rows 0, 2 and 4 lie between 0.5 and 1.5.
All inputs are finite; a program needn't handle non-finite values.
Results may differ from a plain program's by a relative error of at most 0.019.
Values may be sent and summed in bfloat16 or wider, within the bound.
No kernel may reach another device: no remote copies, remote signals or barrier semaphores. Data moves between devices by JAX's collectives and lax.ppermute only.
A program may use at most 448 MiB of HBM per device.

v0:
```python
import jax
import jax.numpy as jnp
from jax import lax
from jax.sharding import PartitionSpec as P

HEADS = 16


def from_behind(block, axis, distance):
    devices = range(lax.axis_size(axis))
    route = [((i - distance) % len(devices), i) for i in devices]
    return lax.ppermute(block, axis, route)


def layer_norm(value, gain, shift):
    center = jnp.mean(value, axis=-1, keepdims=True)
    centred = value - center
    spread = jnp.mean(centred * centred, axis=-1, keepdims=True)
    return centred * lax.rsqrt(spread + 1e-05) * gain + shift


def smooth(value):
    return jax.nn.gelu(value, approximate=True)


def fetch(
    self_in, self_out, cross_query, cross_kv, cross_out, mlp_in, mlp_out, vectors, hidden_bias
):
    return (
        lax.all_gather(self_in, ("ulys", "blk"), axis=0, tiled=True),
        lax.all_gather(self_out, ("ulys", "blk"), axis=0, tiled=True),
        lax.all_gather(cross_query, ("ulys", "blk"), axis=0, tiled=True),
        lax.all_gather(cross_kv, ("ulys", "blk"), axis=0, tiled=True),
        lax.all_gather(cross_out, ("ulys", "blk"), axis=0, tiled=True),
        lax.all_gather(mlp_in, ("ulys", "blk"), axis=0, tiled=True),
        lax.all_gather(mlp_out, ("ulys", "blk"), axis=0, tiled=True),
        lax.all_gather(vectors, ("ulys", "blk"), axis=1, tiled=True),
        lax.all_gather(hidden_bias, ("ulys", "blk"), axis=0, tiled=True),
    )


def to_heads(stacked):
    return lax.all_to_all(stacked, "ulys", split_axis=3, concat_axis=1, tiled=True)


def to_tokens(stacked):
    return lax.all_to_all(stacked, "ulys", split_axis=1, concat_axis=3, tiled=True)


def pass_ahead(pair):
    return from_behind(pair, "blk", 1)


def grads_back(partial_value):
    return from_behind(partial_value.astype(jnp.bfloat16), "blk", -1).astype(partial_value.dtype)


def collect(own, count, mover):

    def advance(current, unused):
        moved = mover(current)
        return (moved, moved)

    _, later = lax.scan(advance, own, None, length=count)
    return later


def send_home(piece_grads, mover):

    def carry_step(running, piece):
        return (mover(running + piece), None)

    running, _ = lax.scan(carry_step, jnp.zeros_like(piece_grads[0]), piece_grads, reverse=True)
    return running


def segment_ids(ends, positions):
    return jnp.sum((ends[:, None, :] <= positions[None, :, None]).astype(jnp.int32), axis=-1)


def piece_mask(query_ids, query_place, ends, block, rows, causal):
    key_place = block * rows + jnp.arange(rows, dtype=jnp.int32)
    key_ids = segment_ids(ends, key_place)
    allowed = query_ids[:, :, None] == key_ids[:, None, :]
    if causal:
        allowed = allowed & (key_place[None, :] <= query_place[:, None])[None]
    return allowed


def raw_scores(queries, key_rows, scale):
    shaped = key_rows.reshape(queries.shape)
    return (
        jnp.einsum("sqhd,skhd->shqk", queries, shaped, preferred_element_type=jnp.float32) * scale
    )


def probabilities(queries, key_rows, allowed, log_total, scale):
    return jnp.where(
        allowed[:, None], jnp.exp(raw_scores(queries, key_rows, scale) - log_total[..., None]), 0.0
    )


def softmax_stats(queries, pieces, offsets, mask_of, scale):
    shape = (queries.shape[0], queries.shape[2], queries.shape[1])

    def softmax_absorb(carry, item):
        summit, total = carry
        pair, offset = item
        allowed = mask_of(offset)[:, None]
        masked = jnp.where(allowed, raw_scores(queries, pair[0], scale), -1e30)
        new_summit = jnp.maximum(summit, jnp.max(masked, axis=-1))
        weights = jnp.where(allowed, jnp.exp(masked - new_summit[..., None]), 0.0)
        total = total * jnp.exp(summit - new_summit) + jnp.sum(weights, axis=-1)
        return ((new_summit, total), None)

    start = (jnp.full(shape, -1e30, jnp.float32), jnp.zeros(shape, jnp.float32))
    (summit, total), _ = lax.scan(softmax_absorb, start, (pieces, offsets))
    return summit + jnp.log(total)


def attend_output(queries, pieces, offsets, mask_of, log_total, scale):

    def attend_absorb(running, item):
        pair, offset = item
        probs = probabilities(queries, pair[0], mask_of(offset), log_total, scale)
        values = pair[1].reshape(queries.shape)
        return (
            running
            + jnp.einsum(
                "shqk,skhd->sqhd",
                probs.astype(jnp.bfloat16),
                values,
                preferred_element_type=jnp.float32,
            ),
            None,
        )

    running, _ = lax.scan(attend_absorb, jnp.zeros(queries.shape, jnp.float32), (pieces, offsets))
    return running


def attend_backward(queries, pieces, offsets, mask_of, log_total, upstream, scale):

    def measure(delta, item):
        pair, offset = item
        probs = probabilities(queries, pair[0], mask_of(offset), log_total, scale)
        slope = jnp.einsum(
            "sqhd,skhd->shqk",
            upstream,
            pair[1].reshape(queries.shape),
            preferred_element_type=jnp.float32,
        )
        return (delta + jnp.sum(probs * slope, axis=-1), None)

    shape = (queries.shape[0], queries.shape[2], queries.shape[1])
    delta, _ = lax.scan(measure, jnp.zeros(shape, jnp.float32), (pieces, offsets))

    def spread_back(running, item):
        pair, offset = item
        key_rows = pair[0].reshape(queries.shape)
        value_rows = pair[1].reshape(queries.shape)
        probs = probabilities(queries, pair[0], mask_of(offset), log_total, scale)
        slope = jnp.einsum(
            "sqhd,skhd->shqk", upstream, value_rows, preferred_element_type=jnp.float32
        )
        push = (probs * (slope - delta[..., None])).astype(jnp.bfloat16)
        running = (
            running
            + jnp.einsum("shqk,skhd->sqhd", push, key_rows, preferred_element_type=jnp.float32)
            * scale
        )
        key_grad = (
            jnp.einsum("shqk,sqhd->skhd", push, queries, preferred_element_type=jnp.float32) * scale
        )
        value_grad = jnp.einsum(
            "shqk,sqhd->skhd",
            probs.astype(jnp.bfloat16),
            upstream,
            preferred_element_type=jnp.float32,
        )
        flat = (queries.shape[0], queries.shape[1], queries.shape[2] * queries.shape[3])
        return (running, jnp.stack([key_grad.reshape(flat), value_grad.reshape(flat)]))

    query_grad, piece_grads = lax.scan(
        spread_back, jnp.zeros(queries.shape, jnp.float32), (pieces, offsets)
    )
    return (query_grad, piece_grads)


def per_device(
    target,
    source,
    cotangent,
    target_lengths,
    source_lengths,
    self_in,
    self_out,
    cross_query,
    cross_kv,
    cross_out,
    mlp_in,
    mlp_out,
    vectors,
    hidden_bias,
):
    rows = target.shape[1]
    width = target.shape[2]
    groups = lax.axis_size("ulys")
    blocks = lax.axis_size("blk")
    here = lax.axis_index("blk")
    heads_here = HEADS // groups
    head_size = width // HEADS
    local_width = width // groups
    scale = head_size ** (-0.5)
    head_shape = (groups, rows, heads_here, head_size)
    flat_shape = (groups, rows, local_width)
    query_place = here * rows + jnp.arange(rows, dtype=jnp.int32)
    target_ends = jnp.cumsum(target_lengths, axis=1)
    source_ends = jnp.cumsum(source_lengths, axis=1)
    query_ids = segment_ids(target_ends, query_place)

    def self_mask(offset):
        return piece_mask(query_ids, query_place, target_ends, (here + offset) % blocks, rows, True)

    def cross_mask(offset):
        return piece_mask(
            query_ids, query_place, source_ends, (here + offset) % blocks, rows, False
        )

    cycle_offsets = -jnp.arange(blocks, dtype=jnp.int32)
    fetched = fetch(
        self_in, self_out, cross_query, cross_kv, cross_out, mlp_in, mlp_out, vectors, hidden_bias
    )
    (
        self_full,
        sout_full,
        query_full,
        pair_full,
        cout_full,
        first_full,
        second_full,
        vector_full,
        bias_full,
    ) = fetched
    params = vector_full.astype(jnp.float32)
    h_bias = bias_full.astype(jnp.float32)
    inputs = target[0].astype(jnp.float32)
    states = source[0]
    first_norm, first_pull = jax.vjp(layer_norm, inputs, params[0], params[1])
    first_low = first_norm.astype(jnp.bfloat16)
    projected = jnp.dot(first_low, self_full, preferred_element_type=jnp.float32)
    self_parts = jnp.stack(
        [
            projected[:, :width] + params[6],
            projected[:, width : 2 * width],
            projected[:, 2 * width :] + params[7],
        ]
    ).astype(jnp.bfloat16)
    self_heads = to_heads(self_parts[:, None])
    self_queries = self_heads[0].reshape(head_shape)
    self_own = self_heads[1:3]
    self_pieces = jnp.concatenate(
        [self_own[None], collect(self_own, blocks - 1, pass_ahead)], axis=0
    )
    self_total = softmax_stats(self_queries, self_pieces, cycle_offsets, self_mask, scale)
    self_att = attend_output(self_queries, self_pieces, cycle_offsets, self_mask, self_total, scale)
    attended = to_tokens(self_att.reshape(flat_shape).astype(jnp.bfloat16)[None])[0, 0]
    middle = inputs + jnp.dot(attended, sout_full, preferred_element_type=jnp.float32) + params[8]
    second_norm, second_pull = jax.vjp(layer_norm, middle, params[2], params[3])
    second_low = second_norm.astype(jnp.bfloat16)
    cross_q = jnp.dot(second_low, query_full, preferred_element_type=jnp.float32) + params[9]
    state_proj = jnp.dot(states, pair_full, preferred_element_type=jnp.float32)
    cross_parts = jnp.stack(
        [cross_q, state_proj[:, :width], state_proj[:, width:] + params[10]]
    ).astype(jnp.bfloat16)
    cross_heads = to_heads(cross_parts[:, None])
    cross_queries = cross_heads[0].reshape(head_shape)
    cross_own = cross_heads[1:3]
    cross_pieces = jnp.concatenate(
        [cross_own[None], collect(cross_own, blocks - 1, pass_ahead)], axis=0
    )
    cross_total = softmax_stats(cross_queries, cross_pieces, cycle_offsets, cross_mask, scale)
    cross_att = attend_output(
        cross_queries, cross_pieces, cycle_offsets, cross_mask, cross_total, scale
    )
    crossed = to_tokens(cross_att.reshape(flat_shape).astype(jnp.bfloat16)[None])[0, 0]
    late = middle + jnp.dot(crossed, cout_full, preferred_element_type=jnp.float32) + params[11]
    third_norm, third_pull = jax.vjp(layer_norm, late, params[4], params[5])
    third_low = third_norm.astype(jnp.bfloat16)
    before = jnp.dot(third_low, first_full, preferred_element_type=jnp.float32) + h_bias
    active, active_pull = jax.vjp(smooth, before)
    active_low = active.astype(jnp.bfloat16)
    result = (
        late + jnp.dot(active_low, second_full, preferred_element_type=jnp.float32) + params[12]
    )
    layer_out = result.astype(jnp.bfloat16)[None]
    fetched = fetch(
        self_in, self_out, cross_query, cross_kv, cross_out, mlp_in, mlp_out, vectors, hidden_bias
    )
    (
        self_full,
        sout_full,
        query_full,
        pair_full,
        cout_full,
        first_full,
        second_full,
        vector_full,
        bias_full,
    ) = fetched
    upstream = cotangent[0]
    upstream_wide = upstream.astype(jnp.float32)
    second_grad = jnp.einsum("rf,rd->fd", active_low, upstream, preferred_element_type=jnp.float32)
    bias_twelve = jnp.sum(upstream_wide, axis=0)
    active_grad = jnp.einsum("rd,fd->rf", upstream, second_full, preferred_element_type=jnp.float32)
    before_grad = active_pull(active_grad)[0].astype(jnp.bfloat16)
    h_bias_grad = jnp.sum(before_grad.astype(jnp.float32), axis=0)
    first_grad = jnp.einsum("rd,rf->df", third_low, before_grad, preferred_element_type=jnp.float32)
    third_grad = jnp.einsum(
        "rf,df->rd", before_grad, first_full, preferred_element_type=jnp.float32
    )
    late_part, gain_five, shift_five = third_pull(third_grad)
    late_grad = upstream_wide + late_part
    cross_branch = late_grad.astype(jnp.bfloat16)
    cout_grad = jnp.einsum("rd,re->de", crossed, cross_branch, preferred_element_type=jnp.float32)
    bias_eleven = jnp.sum(cross_branch.astype(jnp.float32), axis=0)
    crossed_grad = jnp.einsum(
        "re,de->rd", cross_branch, cout_full, preferred_element_type=jnp.float32
    ).astype(jnp.bfloat16)
    cross_up = to_heads(crossed_grad[None, None])[0].reshape(head_shape)
    cross_q_grad, cross_piece_grads = attend_backward(
        cross_queries, cross_pieces, cycle_offsets, cross_mask, cross_total, cross_up, scale
    )
    cross_pair_grad = cross_piece_grads[0] + send_home(cross_piece_grads[1:], grads_back)
    cross_back = to_tokens(
        jnp.stack(
            [cross_q_grad.reshape(flat_shape), cross_pair_grad[0], cross_pair_grad[1]]
        ).astype(jnp.bfloat16)
    )[:, 0]
    query_back = cross_back[0]
    pair_back = jnp.concatenate([cross_back[1], cross_back[2]], axis=1)
    query_weight_grad = jnp.einsum(
        "rd,re->de", second_low, query_back, preferred_element_type=jnp.float32
    )
    bias_nine = jnp.sum(query_back.astype(jnp.float32), axis=0)
    pair_weight_grad = jnp.einsum(
        "rd,re->de", states, pair_back, preferred_element_type=jnp.float32
    )
    bias_ten = jnp.sum(cross_back[2].astype(jnp.float32), axis=0)
    source_grad = jnp.einsum(
        "re,de->rd", pair_back, pair_full, preferred_element_type=jnp.float32
    ).astype(jnp.bfloat16)[None]
    second_norm_grad = jnp.einsum(
        "re,de->rd", query_back, query_full, preferred_element_type=jnp.float32
    )
    middle_part, gain_three, shift_three = second_pull(second_norm_grad)
    middle_grad = late_grad + middle_part
    self_branch = middle_grad.astype(jnp.bfloat16)
    sout_grad = jnp.einsum("rd,re->de", attended, self_branch, preferred_element_type=jnp.float32)
    bias_eight = jnp.sum(self_branch.astype(jnp.float32), axis=0)
    attended_grad = jnp.einsum(
        "re,de->rd", self_branch, sout_full, preferred_element_type=jnp.float32
    ).astype(jnp.bfloat16)
    self_up = to_heads(attended_grad[None, None])[0].reshape(head_shape)
    self_q_grad, self_piece_grads = attend_backward(
        self_queries, self_pieces, cycle_offsets, self_mask, self_total, self_up, scale
    )
    self_pair_grad = self_piece_grads[0] + send_home(self_piece_grads[1:], grads_back)
    self_back = to_tokens(
        jnp.stack([self_q_grad.reshape(flat_shape), self_pair_grad[0], self_pair_grad[1]]).astype(
            jnp.bfloat16
        )
    )[:, 0]
    projected_grad = jnp.concatenate([self_back[0], self_back[1], self_back[2]], axis=1)
    self_weight_grad = jnp.einsum(
        "rd,re->de", first_low, projected_grad, preferred_element_type=jnp.float32
    )
    bias_six = jnp.sum(self_back[0].astype(jnp.float32), axis=0)
    bias_seven = jnp.sum(self_back[2].astype(jnp.float32), axis=0)
    first_norm_grad = jnp.einsum(
        "re,de->rd", projected_grad, self_full, preferred_element_type=jnp.float32
    )
    input_part, gain_one, shift_one = first_pull(first_norm_grad)
    target_grad = (middle_grad + input_part).astype(jnp.bfloat16)[None]
    vector_grad = jnp.stack(
        [
            gain_one,
            shift_one,
            gain_three,
            shift_three,
            gain_five,
            shift_five,
            bias_six,
            bias_seven,
            bias_eight,
            bias_nine,
            bias_ten,
            bias_eleven,
            bias_twelve,
        ]
    )
    summed = (
        lax.psum_scatter(self_weight_grad, ("ulys", "blk"), scatter_dimension=0, tiled=True),
        lax.psum_scatter(sout_grad, ("ulys", "blk"), scatter_dimension=0, tiled=True),
        lax.psum_scatter(query_weight_grad, ("ulys", "blk"), scatter_dimension=0, tiled=True),
        lax.psum_scatter(pair_weight_grad, ("ulys", "blk"), scatter_dimension=0, tiled=True),
        lax.psum_scatter(cout_grad, ("ulys", "blk"), scatter_dimension=0, tiled=True),
        lax.psum_scatter(first_grad, ("ulys", "blk"), scatter_dimension=0, tiled=True),
        lax.psum_scatter(second_grad, ("ulys", "blk"), scatter_dimension=0, tiled=True),
        lax.psum_scatter(vector_grad, ("ulys", "blk"), scatter_dimension=1, tiled=True),
        lax.psum_scatter(h_bias_grad, ("ulys", "blk"), scatter_dimension=0, tiled=True),
    )
    return (
        layer_out,
        target_grad,
        source_grad,
        summed[0],
        summed[1],
        summed[2],
        summed[3],
        summed[4],
        summed[5],
        summed[6],
        summed[7],
        summed[8],
    )


def solution(mesh):
    in_specs = (
        P("ulys", "blk", None),
        P("ulys", "blk", None),
        P("ulys", "blk", None),
        P(),
        P(),
        P(("ulys", "blk"), None),
        P(("ulys", "blk"), None),
        P(("ulys", "blk"), None),
        P(("ulys", "blk"), None),
        P(("ulys", "blk"), None),
        P(("ulys", "blk"), None),
        P(("ulys", "blk"), None),
        P(None, ("ulys", "blk")),
        P(("ulys", "blk")),
    )
    out_specs = (
        P("ulys", "blk", None),
        P("ulys", "blk", None),
        P("ulys", "blk", None),
        P(("ulys", "blk"), None),
        P(("ulys", "blk"), None),
        P(("ulys", "blk"), None),
        P(("ulys", "blk"), None),
        P(("ulys", "blk"), None),
        P(("ulys", "blk"), None),
        P(("ulys", "blk"), None),
        P(None, ("ulys", "blk")),
        P(("ulys", "blk")),
    )
    return jax.shard_map(
        per_device, mesh=mesh, in_specs=in_specs, out_specs=out_specs, check_vma=False
    )
```

profile of v0, /device:TPU:0, one launch (start us, length us, event | category | flops | bytes accessed | tf_op | source)
XLA Modules:
  0.0 2686.7 jit_solution(16041067271493523647)
XLA Ops:
  11.2 44.0 %all-gather = bf16[32,32,13]{1,2,0:T(8,128)(2,1)S(1)} all-gather(bf16[1,32,13]{1,2,0:T(8,128)(2,1)} %bitcast.676), channel_id=1, replica_groups=mesh['ulys'=4,'blk'=8] {'ulys','blk'}, dimensions={0}, use_global_device_ids=true | all-gather | bytes 27456 | tf_op jit(solution)/shard_map/all_gather | solution.py:37
  58.3 25.0 all-gather.10.cloned.1.call-done
  94.0 63.2 %all-gather.16.cloned.1.call-done = bf16[1024,2048]{1,0:T(8,128)(2,1)} async-done(((bf16[32,2048]{1,0:T(8,128)(2,1)}), bf16[1024,2048]{1,0:T(8,128)(2,1)}) %all-gather.16.cloned.1.call-update) | async-done | bytes 4194320 | tf_op jit(solution)/shard_map/all_gather | solution.py:33
  164.3 79.7 %while.166 = (s32[]{:T(128)}, bf16[2,4,128,256]{3,2,1,0:T(8,128)(2,1)S(1)}, bf16[7,2,4,128,256]{3,4,2,1,0:T(8,128)(2,1)}, s32[]{:T(128)}) while((s32[]{:T(128)}, bf16[2,4,128,256]{3,2,1,0:T(8,128)(2,1)S(1)}, bf16[7,2,4,128,256]{3,4,2,1,0:T(8,128)(2,1)}, s32[]{:T(128)}) %tuple.400), condition=%wide.region_3.4_spmd, body=%wide.region_2.3_spmd.sunk | while | flops 2 | bytes 5242985 | solution.py:64
  164.6 9.7 collective-permute-done
  175.5 9.5 collective-permute-done
  186.2 9.5 collective-permute-done
  197.0 13.2 collective-permute-done
  211.4 9.5 collective-permute-done
  222.2 10.0 collective-permute-done
  233.4 9.5 collective-permute-done
  248.4 30.8 %while.168 = (s32[]{:T(128)}, f32[4,4,128]{2,1,0:T(4,128)S(1)}, f32[4,4,128]{2,1,0:T(4,128)S(1)}, s32[4,128]{1,0:T(4,128)S(1)}, s32[4,3]{0,1:T(4,128)S(1)}, /*in...) while((s32[]{:T(128)}, f32[4,4,128]{2,1,0:T(4,128)S(1)}, ...), condition=%wide.region_10.11_spmd.clone, body=%wide.region_6.10_spmd.clone.sunk | while | flops 35289360 | bytes 3490661 | solution.py:117
  279.2 30.9 %while.169 = (s32[]{:T(128)}, f32[4,128,4,64]{1,3,2,0:T(8,128)S(1)}, bf16[8,2,4,128,256]{3,4,2,1,0:T(8,128)(2,1)}, s32[4,128]{1,0:T(4,128)S(1)}, s32[4,3]{0,1:T(...) while((s32[]{:T(128)}, f32[4,128,4,64]{1,3,2,0:T(8,128)S(1)}, ...), condition=%wide.region_13.14_spmd.clone, body=%wide.region_11.13_spmd.clone.sunk | while | flops 68571408 | bytes 3064700 | solution.py:138
  333.0 30.6 %all-to-all-done.2 = bf16[3,1,128,1024]{2,0,1,3:T(4,128)(2,1)S(1)} async-done(((bf16[3,1,128,1024]{2,0,1,3:T(4,128)(2,1)}), bf16[3,1,128,1024]{2,0,1,3:T(4,128)(2,1)S(1)}, u32[]{:S(2)}, u32[]{:S(2)}) %all-to-all-start.2) | async-done | bytes 786464 | tf_op jit(solution)/shard_map/all_to_all | solution.py:43
  367.6 105.9 %while.167 = (s32[]{:T(128)}, bf16[2,4,128,256]{3,2,1,0:T(8,128)(2,1)S(1)}, bf16[7,2,4,128,256]{3,4,2,1,0:T(8,128)(2,1)}, s32[]{:T(128)}) while((s32[]{:T(128)}, bf16[2,4,128,256]{3,2,1,0:T(8,128)(2,1)S(1)}, bf16[7,2,4,128,256]{3,4,2,1,0:T(8,128)(2,1)}, s32[]{:T(128)}) %tuple.409), condition=%wide.region_17.18_spmd, body=%wide.region_16.17_spmd.sunk | while | flops 2 | bytes 5242985 | solution.py:64
  367.6 20.6 collective-permute-done.1
  389.4 9.5 collective-permute-done.1
  400.1 10.4 collective-permute-done.1
  411.8 20.7 collective-permute-done.1
  433.7 17.2 collective-permute-done.1
  452.1 9.5 collective-permute-done.1
  462.9 9.5 collective-permute-done.1
  477.9 30.0 %while.170 = (s32[]{:T(128)}, f32[4,4,128]{2,1,0:T(4,128)S(1)}, f32[4,4,128]{2,1,0:T(4,128)S(1)}, s32[4,128]{1,0:T(4,128)S(1)}, s32[4,3]{0,1:T(4,128)S(1)}, /*in...) while((s32[]{:T(128)}, f32[4,4,128]{2,1,0:T(4,128)S(1)}, ...), condition=%wide.region_23.24_spmd.clone, body=%wide.region_19.23_spmd.clone.sunk | while | flops 35207312 | bytes 3456345 | solution.py:117
  508.0 30.1 %while.171 = (s32[]{:T(128)}, f32[4,128,4,64]{1,3,2,0:T(8,128)S(1)}, bf16[8,2,4,128,256]{3,4,2,1,0:T(8,128)(2,1)}, s32[4,128]{1,0:T(4,128)S(1)}, s32[4,3]{0,1:T(...) while((s32[]{:T(128)}, f32[4,128,4,64]{1,3,2,0:T(8,128)S(1)}, ...), condition=%wide.region_26.27_spmd.clone, body=%wide.region_24.26_spmd.clone.sunk | while | flops 68489360 | bytes 3030384 | solution.py:138
  542.7 42.8 %all-gather.1 = bf16[32,1,256]{2,1,0:T(2,128)(2,1)S(1)} all-gather(bf16[1,1,256]{2,1,0:T(2,128)(2,1)S(1)} %reshape.549), channel_id=1, replica_groups=mesh['ulys'=4,'blk'=8] {'ulys','blk'}, dimensions={0}, use_global_device_ids=true | all-gather | bytes 16896 | tf_op jit(solution)/shard_map/all_gather | solution.py:38
  588.0 10.3 convolution_add_fusion
  598.4 13.1 convert_reduce_fusion.8
  611.5 12.2 multiply_reduce_fusion
  634.5 9.6 all-to-all-done.4
  644.4 32.1 %while.172 = (s32[]{:T(128)}, f32[4,4,128]{2,1,0:T(4,128)S(1)}, s32[4,128]{1,0:T(4,128)S(1)}, s32[4,3]{0,1:T(4,128)S(1)}, s32[8]{0:T(128)}, /*index=5*/s32[]{:T(...) while((s32[]{:T(128)}, f32[4,4,128]{2,1,0:T(4,128)S(1)}, ...), condition=%wide.region_34.35_spmd.clone, body=%wide.region_31.34_spmd.clone.sunk | while | flops 68491408 | bytes 4373880 | solution.py:156
  680.8 63.4 %while.173 = (s32[]{:T(128)}, f32[4,128,4,64]{1,3,2,0:T(8,128)}, f32[8,2,4,128,256]{3,4,2,1,0:T(8,128)}, bf16[8,2,4,128,256]{3,4,2,1,0:T(8,128)(2,1)}, s32[4,128...) while((s32[]{:T(128)}, f32[4,128,4,64]{1,3,2,0:T(8,128)}, ...), condition=%wide.region_37.38_spmd.clone, body=%wide.region_35.37_spmd.clone.sunk | while | flops 170463376 | bytes 11952008 | solution.py:184
  744.2 9.2 copy.214
  753.4 6.9 slice.292
  760.3 74.6 %while.174 = (s32[]{:T(128)}, f32[2,4,128,256]{3,2,1,0:T(8,128)S(1)}, f32[7,2,4,128,256]{4,3,2,1,0:T(8,128)}, s32[]{:T(128)}, s32[]{:T(128)}, /*index=5*/s32[]{:T(128)}) while((s32[]{:T(128)}, f32[2,4,128,256]{3,2,1,0:T(8,128)S(1)}, f32[7,2,4,128,256]{4,3,2,1,0:T(8,128)}, s32[]{:T(128)}, s32[]{:T(128)}, ...), condition=%wide.region_39.40_spmd.clone, body=%wide.region_38.39_spmd.clone.sunk | while | flops 1048580 | bytes 6291591 | solution.py:73
  772.8 6.7 collective-permute-done.2
  794.9 6.7 collective-permute-done.2
  805.9 6.7 collective-permute-done.2
  817.0 6.7 collective-permute-done.2
  828.0 6.7 collective-permute-done.2
  837.9 19.0 all_to_all.120
  868.1 6.7 all-to-all-done.6
  875.1 32.8 %while.175 = (s32[]{:T(128)}, f32[4,4,128]{2,1,0:T(4,128)S(1)}, s32[4,128]{1,0:T(4,128)S(1)}, s32[4,3]{0,1:T(4,128)S(1)}, s32[8]{0:T(128)}, /*index=5*/s32[]{:T(...) while((s32[]{:T(128)}, f32[4,4,128]{2,1,0:T(4,128)S(1)}, ...), condition=%wide.region_45.46_spmd.clone, body=%wide.region_42.45_spmd.clone.sunk | while | flops 68573456 | bytes 4408196 | solution.py:156
  912.2 64.3 %while.176 = (s32[]{:T(128)}, f32[4,128,4,64]{1,3,2,0:T(8,128)}, f32[8,2,4,128,256]{3,4,2,1,0:T(8,128)}, bf16[8,2,4,128,256]{3,4,2,1,0:T(8,128)(2,1)}, s32[4,128...) while((s32[]{:T(128)}, f32[4,128,4,64]{1,3,2,0:T(8,128)}, ...), condition=%wide.region_48.49_spmd.clone, body=%wide.region_46.48_spmd.clone.sunk | while | flops 170545424 | bytes 11986324 | solution.py:184
  976.5 9.2 copy.220
  985.7 6.9 slice.295
  992.6 74.6 %while.177 = (s32[]{:T(128)}, f32[2,4,128,256]{3,2,1,0:T(8,128)S(1)}, f32[7,2,4,128,256]{4,3,2,1,0:T(8,128)}, s32[]{:T(128)}, s32[]{:T(128)}, /*index=5*/s32[]{:T(128)}) while((s32[]{:T(128)}, f32[2,4,128,256]{3,2,1,0:T(8,128)S(1)}, f32[7,2,4,128,256]{4,3,2,1,0:T(8,128)}, s32[]{:T(128)}, s32[]{:T(128)}, ...), condition=%wide.region_50.51_spmd.clone, body=%wide.region_49.50_spmd.clone.sunk | while | flops 1048580 | bytes 6291591 | solution.py:73
  1016.1 6.7 collective-permute-done.3
  1027.2 6.7 collective-permute-done.3
  1038.2 6.7 collective-permute-done.3
  1060.4 6.7 collective-permute-done.3
  1075.7 17.5 all-to-all-done.7
  1114.3 9.2 copy.233
  1132.5 13.2 fusion.149
  1146.7 15.4 fusion.125
  1162.8 37.0 %all-reduce = f32[8192]{0:T(1024)S(1)} all-reduce(f32[8192]{0:T(1024)S(1)} %copy-done.43), channel_id=10, replica_groups=mesh['ulys'=4,'blk'=8] {'ulys','blk'}, use_global_device_ids=true, to_apply=%region_75.76.clone | all-reduce | flops 8192 | bytes 65536
  1200.5 10.8 fusion.96
  1214.6 18.3 reduce-scatter.27.cloned.1.call-done
  1234.3 138.5 %reduce-scatter.19.cloned.1.call-done = f32[32,1024]{1,0:T(8,128)} async-done(((f32[1024,1024]{1,0:T(8,128)}), f32[32,1024]{1,0:T(8,128)}) %reduce-scatter.19.cloned.1.call-update) | async-done | bytes 131088 | tf_op jit(solution)/shard_map/reduce_scatter | solution.py:407
  1372.8 139.8 %reduce-scatter.17.cloned.1.call-done = f32[32,1024]{1,0:T(8,128)} async-done(((f32[1024,1024]{1,0:T(8,128)}), f32[32,1024]{1,0:T(8,128)}) %reduce-scatter.17.cloned.1.call-update) | async-done | bytes 131088 | tf_op jit(solution)/shard_map/reduce_scatter | solution.py:405
  1512.6 140.0 %reduce-scatter.15.cloned.1.call-done = f32[32,1024]{1,0:T(8,128)} async-done(((f32[1024,1024]{1,0:T(8,128)}), f32[32,1024]{1,0:T(8,128)}) %reduce-scatter.15.cloned.1.call-update) | async-done | bytes 131088 | tf_op jit(solution)/shard_map/reduce_scatter | solution.py:404
  1652.6 147.3 %reduce-scatter.25.cloned.1.call-done = f32[32,2048]{1,0:T(8,128)} async-done(((f32[1024,2048]{1,0:T(8,128)}), f32[32,2048]{1,0:T(8,128)}) %reduce-scatter.25.cloned.1.call-update) | async-done | bytes 262160
  1799.9 159.2 %reduce-scatter.13.cloned.1.call-done = f32[32,3072]{1,0:T(8,128)} async-done(((f32[1024,3072]{1,0:T(8,128)}), f32[32,3072]{1,0:T(8,128)}) %reduce-scatter.13.cloned.1.call-update) | async-done | bytes 393232 | tf_op jit(solution)/shard_map/reduce_scatter | solution.py:403
  1959.1 356.2 %reduce-scatter.21.cloned.1.call-done = f32[32,8192]{1,0:T(8,128)} async-done(((f32[1024,8192]{1,0:T(8,128)}), f32[32,8192]{1,0:T(8,128)}) %reduce-scatter.21.cloned.1.call-update) | async-done | bytes 1048592 | tf_op jit(solution)/shard_map/reduce_scatter | solution.py:408
  2315.2 364.7 %reduce-scatter.23.cloned.1.call-done = f32[256,1024]{1,0:T(8,128)} async-done(((f32[8192,1024]{1,0:T(8,128)}), f32[256,1024]{1,0:T(8,128)}) %reduce-scatter.23.cloned.1.call-update) | async-done | bytes 1048592 | tf_op jit(solution)/shard_map/reduce_scatter | solution.py:409
  (972 shorter events, 520.1 us)
Async XLA Ops:
  7.2 150.0 %copy-start = (bf16[1,128,1024]{2,1,0:T(8,128)(2,1)S(1)}, bf16[1,128,1024]{2,1,0:T(8,128)(2,1)}, u32[]{:S(2)}) copy-start(bf16[1,128,1024]{2,1,0:T(8,128)(2,1)} %param.39) | copy-start | bytes 786436
  7.2 76.0 %all-gather.10.cloned.1.call-start = ((), (), s32[]{:S(2)}) async-start(), calls=%async_computation.16 | async-start | bytes 6488064 | tf_op jit(solution)/shard_map/all_gather | solution.py:30
  7.9 149.2 %all-gather.16.cloned.1.call-start = ((), (), s32[]{:S(2)}) async-start(), calls=%async_computation.19 | async-start | bytes 4325376 | tf_op jit(solution)/shard_map/all_gather | solution.py:33
  8.7 306.4 %all-gather.12.cloned.1.call-start = ((), (), s32[]{:S(2)}) async-start(), calls=%async_computation.17 | async-start | bytes 2162688 | tf_op jit(solution)/shard_map/all_gather | solution.py:31
  9.4 314.2 %all-gather.14.cloned.1.call-start = ((), (), s32[]{:S(2)}) async-start(), calls=%async_computation.18 | async-start | bytes 2162688 | tf_op jit(solution)/shard_map/all_gather | solution.py:32
  10.0 575.5 %all-gather.18.cloned.1.call-start = ((), (), s32[]{:S(2)}) async-start(), calls=%async_computation.20 | async-start | bytes 2162688 | tf_op jit(solution)/shard_map/all_gather | solution.py:34
  10.6 577.4 %all-gather.20.cloned.1.call-start = ((), (), s32[]{:S(2)}) async-start(), calls=%async_computation.21 | async-start | bytes 17301504 | tf_op jit(solution)/shard_map/all_gather | solution.py:35
  56.4 30.8 %copy-start.44 = (f32[128]{0:T(128)}, f32[128]{0:T(128)S(1)}, u32[]{:S(2)}) copy-start(f32[128]{0:T(128)S(1)} %broadcast_multiply_fusion.2) | copy-start | bytes 1540
  57.6 29.6 %copy-start.53 = (f32[128]{0:T(128)}, f32[128]{0:T(128)S(1)}, u32[]{:S(2)}) copy-start(f32[128]{0:T(128)S(1)} %fusion.111) | copy-start | bytes 1540
  57.6 29.6 %copy-start.46 = (f32[128]{0:T(128)}, f32[128]{0:T(128)S(1)}, u32[]{:S(2)}) copy-start(f32[128]{0:T(128)S(1)} %fusion.134) | copy-start | bytes 1540
  58.3 29.0 %copy-start.41 = (f32[1,1024]{1,0:T(1,128)}, f32[1,1024]{1,0:T(1,128)S(1)}, u32[]{:S(2)}) copy-start(f32[1,1024]{1,0:T(1,128)S(1)} %get-tuple-element.1990) | copy-start | bytes 12292
  88.9 72.1 %all-to-all-start = ((bf16[3,1,128,1024]{2,0,1,3:T(4,128)(2,1)}), bf16[3,1,128,1024]{2,0,1,3:T(4,128)(2,1)S(1)}, u32[]{:S(2)}, u32[]{:S(2)}) async-start(bf16[3,1,128,1024]{2,0,1,3:T(4,128)(2,1)} %copy.202), calls=%async_computation | async-start | bytes 2097152 | tf_op jit(solution)/shard_map/all_to_all | solution.py:43
  92.5 505.9 %all-gather.22.cloned.1.call-start = ((), (), s32[]{:S(2)}) async-start(), calls=%async_computation.22 | async-start | bytes 17301504 | tf_op jit(solution)/shard_map/all_gather | solution.py:36
  164.3 10.0 collective-permute-start
  175.4 9.6 collective-permute-start
  186.2 9.6 collective-permute-start
  196.9 13.2 collective-permute-start
  211.4 9.6 collective-permute-start
  222.1 10.0 collective-permute-start
  233.3 9.6 collective-permute-start
  248.4 30.8 %copy-start.37 = (f32[4,128,4,64]{1,3,2,0:T(8,128)S(1)}, f32[4,128,4,64]{1,3,2,0:T(8,128)}, u32[]{:S(2)}) copy-start(f32[4,128,4,64]{1,3,2,0:T(8,128)} %custom-call.2) | copy-start | bytes 1572868
  279.2 35.1 %copy-start.18 = (f32[128,2048]{1,0:T(8,128)S(1)}, f32[128,2048]{1,0:T(8,128)}, u32[]{:S(2)}) copy-start(f32[128,2048]{1,0:T(8,128)} %fusion.132) | copy-start | bytes 3145732
  279.2 41.9 %copy-start.6 = (bf16[1,128,1024]{2,1,0:T(8,128)(2,1)S(1)}, bf16[1,128,1024]{2,1,0:T(8,128)(2,1)}, u32[]{:S(2)}) copy-start(bf16[1,128,1024]{2,1,0:T(8,128)(2,1)} %param.38) | copy-start | bytes 786436
  310.8 10.2 all-to-all-start.1
  323.6 536.2 %copy-start.48 = (f32[128]{0:T(128)}, f32[128]{0:T(128)S(1)}, u32[]{:S(2)}) copy-start(f32[128]{0:T(128)S(1)} %fusion.135) | copy-start | bytes 1540
  327.3 36.3 %all-to-all-start.2 = ((bf16[3,1,128,1024]{2,0,1,3:T(4,128)(2,1)}), bf16[3,1,128,1024]{2,0,1,3:T(4,128)(2,1)S(1)}, u32[]{:S(2)}, u32[]{:S(2)}) async-start(bf16[3,1,128,1024]{2,0,1,3:T(4,128)(2,1)} %copy.207), calls=%async_computation.2 | async-start | bytes 2097152 | tf_op jit(solution)/shard_map/all_to_all | solution.py:43
  367.6 105.9 %copy-start.33 = (bf16[1,2,4,128,256]{3,4,2,1,0:T(8,128)(2,1)S(1)}, bf16[1,2,4,128,256]{3,4,2,1,0:T(8,128)(2,1)}, u32[]{:S(2)}) copy-start(bf16[1,2,4,128,256]{3,4,2,1,0:T(8,128)(2,1)} %get-tuple-element.1974) | copy-start | bytes 1572868
  367.6 20.6 collective-permute-start.1
  389.3 9.6 collective-permute-start.1
  400.1 10.4 collective-permute-start.1
  411.7 20.8 collective-permute-start.1
  433.7 17.2 collective-permute-start.1
  452.1 9.6 collective-permute-start.1
  462.8 9.6 collective-permute-start.1
  477.9 30.1 %copy-start.38 = (f32[4,128,4,64]{1,3,2,0:T(8,128)S(1)}, f32[4,128,4,64]{1,3,2,0:T(8,128)}, u32[]{:S(2)}) copy-start(f32[4,128,4,64]{1,3,2,0:T(8,128)} %custom-call.5) | copy-start | bytes 1572868
  507.9 34.7 %copy-start.55 = (bf16[256]{0:T(256)(128)(2,1)S(1)}, bf16[256]{0:T(256)(128)(2,1)}, u32[]{:S(2)}) copy-start(bf16[256]{0:T(256)(128)(2,1)} %param.51) | copy-start | bytes 1540
  538.8 46.7 %all-to-all-start.3 = ((bf16[1,4,128,256]{2,3,0,1:T(8,128)(2,1)}), bf16[1,4,128,256]{2,3,0,1:T(8,128)(2,1)S(1)}, u32[]{:S(2)}, u32[]{:S(2)}) async-start(bf16[1,4,128,256]{2,3,0,1:T(8,128)(2,1)} %bitcast.38), calls=%async_computation.3 | async-start | bytes 524288 | tf_op jit(solution)/shard_map/all_to_all | solution.py:47
  587.8 36.0 %copy-start.1 = (f32[128,1024]{1,0:T(8,128)}, f32[128,1024]{1,0:T(8,128)S(1)}, u32[]{:S(2)}) copy-start(f32[128,1024]{1,0:T(8,128)S(1)} %get-tuple-element.1995) | copy-start | bytes 1572868
  630.6 13.5 all-to-all-start.4
  761.6 6.8 collective-permute-start.2
  769.9 9.6 collective-permute-start.2
  780.9 9.6 collective-permute-start.2
  792.0 9.6 collective-permute-start.2
  803.1 9.6 collective-permute-start.2
  814.1 9.6 collective-permute-start.2
  825.2 9.6 collective-permute-start.2
  864.5 10.3 all-to-all-start.6
  994.0 6.8 collective-permute-start.3
  1002.2 9.6 collective-permute-start.3
  1013.3 9.6 collective-permute-start.3
  1024.3 9.6 collective-permute-start.3
  1035.4 9.6 collective-permute-start.3
  1046.4 9.6 collective-permute-start.3
  1057.5 9.6 collective-permute-start.3
  1071.2 22.0 all-to-all-start.7
  1075.4 157.5 %reduce-scatter.27.cloned.1.call-start = ((), (), s32[]{:S(2)}) async-start(), calls=%async_computation.30 | async-start | bytes 540672
  1101.4 271.4 %reduce-scatter.19.cloned.1.call-start = ((), (), s32[]{:S(2)}) async-start(), calls=%async_computation.26 | async-start | bytes 4325376 | tf_op jit(solution)/shard_map/reduce_scatter | solution.py:407
  1104.1 408.5 %reduce-scatter.17.cloned.1.call-start = ((), (), s32[]{:S(2)}) async-start(), calls=%async_computation.25 | async-start | bytes 4325376 | tf_op jit(solution)/shard_map/reduce_scatter | solution.py:405
  1107.1 545.5 %reduce-scatter.15.cloned.1.call-start = ((), (), s32[]{:S(2)}) async-start(), calls=%async_computation.24 | async-start | bytes 4325376 | tf_op jit(solution)/shard_map/reduce_scatter | solution.py:404
  1109.8 690.0 %reduce-scatter.25.cloned.1.call-start = ((), (), s32[]{:S(2)}) async-start(), calls=%async_computation.29 | async-start | bytes 8650752
  1123.6 835.5 %reduce-scatter.13.cloned.1.call-start = ((), (), s32[]{:S(2)}) async-start(), calls=%async_computation.23 | async-start | bytes 12976128 | tf_op jit(solution)/shard_map/reduce_scatter | solution.py:403
  1130.7 1184.5 %reduce-scatter.21.cloned.1.call-start = ((), (), s32[]{:S(2)}) async-start(), calls=%async_computation.27 | async-start | bytes 34603008 | tf_op jit(solution)/shard_map/reduce_scatter | solution.py:408
  1145.7 1534.2 %reduce-scatter.23.cloned.1.call-start = ((), (), s32[]{:S(2)}) async-start(), calls=%async_computation.28 | async-start | bytes 34603008 | tf_op jit(solution)/shard_map/reduce_scatter | solution.py:409
  1162.1 38.4 %copy-start.50 = (f32[1,1024]{1,0:T(1,128)S(1)}, f32[1,1024]{1,0:T(1,128)}, u32[]{:S(2)}) copy-start(f32[1,1024]{1,0:T(1,128)} %get-tuple-element.1980) | copy-start | bytes 12292
  (42 other events, 303.1 us)
Sparse Core Ops, SparseCore 0:
  10.9 72.2 all-gather.9
  86.1 71.0 all-gather.15
  160.0 57.5 all-gather.11
  220.4 54.5 all-gather.13
  277.7 57.7 all-gather.17
  338.1 132.4 all-gather.19
  473.5 116.5 all-gather.21
  1101.5 131.3 reduce-scatter.26
  1235.8 136.8 reduce-scatter.18
  1375.6 137.0 reduce-scatter.16
  1515.6 136.9 reduce-scatter.14
  1655.4 144.4 reduce-scatter.24
  1807.5 151.5 reduce-scatter.12
  1961.8 353.3 reduce-scatter.20
  2318.0 361.8 reduce-scatter.22
where the time goes:
time: 2700 us; the launch traced here: 2690 us
  waiting for transfers between devices  1890 us (70%)
  local copies, waits for them, and re-layouts  238 us (9%)
  matrix products  206 us (8%)
  blocking collectives  143 us (5%)
  other arithmetic  84.5 us (3%)
  starting transfers between devices  64 us (2%)
  loops' own time  46.9 us (2%)
    reduce_scatter x1, waiting for transfers between devices, per_device(): lax.psum_scatter(second_grad, ('ulys', 'blk'), scatter_dimension=0, tiled...  365 us
    reduce_scatter x1, waiting for transfers between devices, per_device(): lax.psum_scatter(first_grad, ('ulys', 'blk'), scatter_dimension=0, tiled=...  356 us
    ppermute x28, waiting for transfers between devices, from_behind(): return lax.ppermute(block, axis, route)  262 us
    unnamed x17, waiting for transfers between devices  170 us
    reduce_scatter x1, waiting for transfers between devices, per_device(): lax.psum_scatter(self_weight_grad, ('ulys', 'blk'), scatter_dimension=0,...  159 us
    reduce_scatter x1, waiting for transfers between devices, per_device(): lax.psum_scatter(sout_grad, ('ulys', 'blk'), scatter_dimension=0, tiled=T...  140 us
    reduce_scatter x1, waiting for transfers between devices, per_device(): lax.psum_scatter(query_weight_grad, ('ulys', 'blk'), scatter_dimension=0,...  140 us
    reduce_scatter x1, waiting for transfers between devices, per_device(): lax.psum_scatter(cout_grad, ('ulys', 'blk'), scatter_dimension=0, tiled=T...  138 us
  transfers between devices with their start and end apart: 50, of which 43 were waited for; matrix products, arithmetic and copies ran while one was open for 9% of the time, Pallas kernels for 0%

commit v1 on v0

v1 whole, which is shorter than its diff:
```python
import functools

import jax
import jax.numpy as jnp
from jax import lax
from jax.experimental import pallas as pl
from jax.experimental.pallas import tpu as pltpu
from jax.sharding import Mesh
from jax.sharding import PartitionSpec as P

HEADS = 16
LOW = jnp.bfloat16
WIDE = jnp.float32
INNER = 8
STEP = 256


def offset_of(place):
    return ((place & 3) << 1) | (place >> 2)


def dot_t(a, b):
    return lax.dot_general(a, b, (((1,), (1,)), ((), ())), preferred_element_type=WIDE)


def dot_n(a, b):
    return lax.dot_general(a, b, (((1,), (0,)), ((), ())), preferred_element_type=WIDE)


def dot_c(a, b):
    return lax.dot_general(a, b, (((0,), (0,)), ((), ())), preferred_element_type=WIDE)


def seg_of(position, table, first):
    count = jnp.zeros_like(position)
    for n in range(3):
        count = count + (table[first + n] <= position).astype(jnp.int32)
    return count


def iota(shape, axis):
    return lax.broadcasted_iota(jnp.int32, shape, axis)


def to_order(table, source, target, rows, factor=None):
    span = rows * INNER
    for chunk in range(source.shape[0] // span):
        for place in range(INNER):
            at = pl.multiple_of((table[0] ^ offset_of(place)) * rows, rows) + chunk * span
            value = source[pl.ds(chunk * span + place * rows, rows), :]
            if factor is not None:
                value = value * factor
            target[pl.ds(at, rows), :] = value


def from_order(table, source, target, rows):
    span = rows * INNER
    for chunk in range(target.shape[0] // span):
        for place in range(INNER):
            at = pl.multiple_of((table[0] ^ offset_of(place)) * rows, rows) + chunk * span
            target[pl.ds(chunk * span + place * rows, rows), :] = source[pl.ds(at, rows), :].astype(
                target.dtype
            )


def half_lanes(value, head, size):
    lane = iota(value.shape, 1)
    keep = (lane >= head * size) & (lane < (head + 1) * size)
    return jnp.where(keep, value, jnp.zeros_like(value))


def attend_kernel(causal, rows, size, table, q, k, v, out, log_total, qs, ks, vs, ordered):
    span, keys = q.shape[0], k.shape[0]
    chunks = keys // span
    to_order(table, q, qs, rows, jnp.asarray(size**-0.5, LOW))
    to_order(table, k, ks, rows)
    to_order(table, v, vs, rows)
    for step in range(span // STEP):
        lo = step * STEP
        queries = qs[lo : lo + STEP, :]
        q_at = table[1] + lo + iota((STEP, 1), 0)
        q_seg = seg_of(q_at, table, 2)
        count = lo + STEP if causal and chunks == 1 else span

        def scores(head, start):
            k_at = start + iota((1, count), 1)
            allowed = q_seg == seg_of(k_at, table, 5)
            if causal:
                allowed = allowed & (k_at <= q_at)
            raw = dot_t(queries, half_lanes(ks[pl.ds(start, count), :], head, size))
            return jnp.where(allowed, raw, -1e30)

        parts = []
        for head in range(2):
            if chunks == 1:
                raw = scores(head, 0)
                top = jnp.max(raw, axis=1, keepdims=True)
                weight = jnp.exp(raw - top)
                total = jnp.sum(weight, axis=1, keepdims=True)
                running = dot_n(weight.astype(LOW), vs[:count, :])
            else:

                def absorb(chunk, carry, head=head):
                    top, total, running = carry
                    start = pl.multiple_of(chunk * span, span)
                    raw = scores(head, start)
                    new_top = jnp.maximum(top, jnp.max(raw, axis=1, keepdims=True))
                    weight = jnp.exp(raw - new_top)
                    fade = jnp.exp(top - new_top)
                    total = total * fade + jnp.sum(weight, axis=1, keepdims=True)
                    running = running * fade + dot_n(weight.astype(LOW), vs[pl.ds(start, span), :])
                    return new_top, total, running

                top, total, running = lax.fori_loop(
                    0,
                    chunks,
                    absorb,
                    (
                        jnp.full((STEP, 1), -1e30, WIDE),
                        jnp.zeros((STEP, 1), WIDE),
                        jnp.zeros((STEP, 2 * size), WIDE),
                    ),
                )
            parts.append(running / total)
            logs = jnp.broadcast_to(top + jnp.log(total), (STEP, 2 * size))
            log_total[head : head + 1, lo : lo + STEP] = jnp.transpose(logs)[0:1, :]
        lane = iota((STEP, 2 * size), 1)
        ordered[lo : lo + STEP, :] = jnp.where(lane < size, parts[0], parts[1])
    from_order(table, ordered, out, rows)


def attend_back_kernel(
    causal, rows, size, table, q, k, v, up, log_total, dq, dk, dv, qs, ks, vs, ups, dqs, dks, dvs
):
    span, keys = q.shape[0], k.shape[0]
    chunks = keys // span
    scale = size**-0.5
    to_order(table, q, qs, rows, jnp.asarray(scale, LOW))
    to_order(table, up, ups, rows)
    to_order(table, k, ks, rows)
    to_order(table, v, vs, rows)
    dks[...] = jnp.zeros_like(dks)
    dvs[...] = jnp.zeros_like(dvs)
    for step in range(span // STEP):
        lo = step * STEP
        queries = qs[lo : lo + STEP, :]
        upstream = ups[lo : lo + STEP, :]
        q_at = table[1] + lo + iota((1, STEP), 1)
        q_seg = seg_of(q_at, table, 2)
        count = lo + STEP if causal and chunks == 1 else span
        total_dq = jnp.zeros((STEP, 2 * size), WIDE)
        for head in range(2):
            head_q = half_lanes(queries, head, size)
            head_up = half_lanes(upstream, head, size)
            logs = log_total[head : head + 1, lo : lo + STEP]

            def pieces(start, logs=logs, head_up=head_up, head=head):
                k_at = start + iota((count, 1), 0)
                allowed = q_seg == seg_of(k_at, table, 5)
                if causal:
                    allowed = allowed & (k_at <= q_at)
                head_k = half_lanes(ks[pl.ds(start, count), :], head, size)
                raw = dot_t(head_k, queries)
                probs = jnp.exp(jnp.where(allowed, raw - logs, -1e30))
                slope = dot_t(vs[pl.ds(start, count), :], head_up)
                return head_k, probs, probs * slope

            def spread(start, delta, made, head_q=head_q, head_up=head_up):
                head_k, probs, lean = made
                push = (lean - probs * delta).astype(LOW)
                dvs[pl.ds(start, count), :] += dot_n(probs.astype(LOW), head_up)
                dks[pl.ds(start, count), :] += dot_n(push, head_q)
                return dot_c(push, head_k)

            if chunks == 1:
                made = pieces(0)
                delta = jnp.sum(made[2], axis=0, keepdims=True)
                total_dq = total_dq + spread(0, delta, made)
            else:

                def measure(chunk, delta):
                    made = pieces(pl.multiple_of(chunk * span, span))
                    return delta + jnp.sum(made[2], axis=0, keepdims=True)

                delta = lax.fori_loop(0, chunks, measure, jnp.zeros((1, STEP), WIDE))

                def absorb(chunk, running, delta=delta):
                    start = pl.multiple_of(chunk * span, span)
                    return running + spread(start, delta, pieces(start))

                total_dq = lax.fori_loop(0, chunks, absorb, total_dq)
        dqs[lo : lo + STEP, :] = total_dq * scale
    from_order(table, dqs, dq, rows)
    from_order(table, dks, dk, rows)
    from_order(table, dvs, dv, rows)


SMEM = pl.BlockSpec(memory_space=pltpu.SMEM)
VMEM = pl.BlockSpec(memory_space=pltpu.VMEM)
ROOM = pltpu.CompilerParams(vmem_limit_bytes=56 * 2**20)


def attend(table, q, k, v, rows, causal):
    span, pair = q.shape
    keys = k.shape[0]
    return pl.pallas_call(
        functools.partial(attend_kernel, causal, rows, pair // 2),
        out_shape=(
            jax.ShapeDtypeStruct((span, pair), LOW),
            jax.ShapeDtypeStruct((2, span), WIDE),
        ),
        in_specs=[SMEM, VMEM, VMEM, VMEM],
        out_specs=(VMEM, VMEM),
        scratch_shapes=[
            pltpu.VMEM((span, pair), LOW),
            pltpu.VMEM((keys, pair), LOW),
            pltpu.VMEM((keys, pair), LOW),
            pltpu.VMEM((span, pair), WIDE),
        ],
        compiler_params=ROOM,
    )(table, q, k, v)


def attend_back(table, q, k, v, up, log_total, rows, causal):
    span, pair = q.shape
    keys = k.shape[0]
    return pl.pallas_call(
        functools.partial(attend_back_kernel, causal, rows, pair // 2),
        out_shape=(
            jax.ShapeDtypeStruct((span, pair), LOW),
            jax.ShapeDtypeStruct((keys, pair), LOW),
            jax.ShapeDtypeStruct((keys, pair), LOW),
        ),
        in_specs=[SMEM] + [VMEM] * 5,
        out_specs=(VMEM, VMEM, VMEM),
        scratch_shapes=[
            pltpu.VMEM((span, pair), LOW),
            pltpu.VMEM((keys, pair), LOW),
            pltpu.VMEM((keys, pair), LOW),
            pltpu.VMEM((span, pair), LOW),
            pltpu.VMEM((span, pair), WIDE),
            pltpu.VMEM((keys, pair), WIDE),
            pltpu.VMEM((keys, pair), WIDE),
        ],
        compiler_params=ROOM,
    )(table, q, k, v, up, log_total)


OUTER = ("ulys", "outer")
ALL = ("ulys", "outer", "inner")


def hop(value, distance):
    route = [(n, n ^ distance) for n in range(INNER)]
    return lax.ppermute(value, "inner", route)


def gather_places(own):
    chips = [own] + [hop(own, offset_of(place)) for place in (1, 2, 3)]
    near = jnp.concatenate(chips, axis=0)
    return jnp.concatenate([near, hop(near, 1)], axis=0)


def scatter_places(make, rows):
    half = rows * INNER // 2
    give = make(half, 2 * half).astype(LOW)
    took = hop(give, 1)
    both = make(0, half) + took.astype(WIDE)
    result = both[:rows]
    for place in (1, 2, 3):
        part = both[place * rows : (place + 1) * rows].astype(LOW)
        result = result + hop(part, offset_of(place)).astype(WIDE)
    return result


def swap_places(piece, place, rows):
    blocks = [piece[(n ^ place) * rows : ((n ^ place) + 1) * rows] for n in range(INNER)]
    return jnp.concatenate(blocks, axis=0)


def gather_heads(own, rows):
    chips = [own] + [hop(own, offset_of(place)) for place in (1, 2, 3)]
    near = jnp.stack(chips, axis=0)
    far = hop(near, 1)
    pieces = chips + [far[n] for n in range(4)]
    return jnp.concatenate([swap_places(pieces[n], n, rows) for n in range(INNER)], axis=1)


def column_slices(weight, parts):
    rows, columns = weight.shape
    share = columns // (parts * INNER)
    cut = jnp.transpose(weight.reshape(rows, parts, INNER, share), (2, 0, 1, 3))
    return cut.reshape(INNER, rows, parts * share)


def column_home(grad, parts):
    received = lax.all_to_all(grad, "inner", 0, 0)
    count, rows, columns = received.shape
    share = columns // parts
    spread = jnp.transpose(received.reshape(count, rows, parts, share), (1, 2, 0, 3))
    return spread.reshape(rows, parts * count * share).astype(WIDE)


def layer_norm(value, gain, shift):
    center = jnp.mean(value, axis=-1, keepdims=True)
    centred = value - center
    spread = jnp.mean(centred * centred, axis=-1, keepdims=True)
    return centred * lax.rsqrt(spread + 1e-05) * gain + shift


def smooth(value):
    return jax.nn.gelu(value, approximate=True)


def dot(a, b):
    return jnp.dot(a, b, preferred_element_type=WIDE)


def across(a, b):
    return lax.dot_general(a, b, (((1,), (1,)), ((), ())), preferred_element_type=WIDE)


def under(a, b):
    return lax.dot_general(a, b, (((0,), (0,)), ((), ())), preferred_element_type=WIDE)


def per_device(
    target,
    source,
    cotangent,
    target_lengths,
    source_lengths,
    self_in,
    self_out,
    cross_query,
    cross_kv,
    cross_out,
    mlp_in,
    mlp_out,
    vectors,
    hidden_bias,
):
    rows, width = target.shape[1:]
    here = lax.axis_index("inner")
    stream = lax.axis_index("ulys")
    group = lax.axis_index("outer")
    groups = lax.axis_size("outer")
    streams = lax.axis_size("ulys")
    shares = streams * groups
    devices = shares * INNER
    span = rows * INNER
    pair = width // INNER
    share = width // devices
    count = vectors.shape[0]
    target_ends = jnp.cumsum(target_lengths[stream])
    source_ends = jnp.cumsum(source_lengths[stream])
    start = jnp.stack([here, group * span]).astype(jnp.int32)
    self_table = jnp.concatenate([start, target_ends, target_ends]).astype(jnp.int32)
    cross_table = jnp.concatenate([start, target_ends, source_ends]).astype(jnp.int32)

    def slices_of(weight, parts):
        mine = lax.all_to_all(column_slices(weight, parts), "inner", 0, 0)
        return lax.all_gather(mine, OUTER, axis=0).reshape(width, -1)

    def my_heads(vector):
        return lax.dynamic_slice_in_dim(vector, here * pair, pair)

    small = jnp.concatenate([vectors.reshape(-1), hidden_bias])
    small = lax.all_gather(small, OUTER, axis=0)
    small = lax.all_gather(small, "inner", axis=1)
    params = small[:, :, : count * share].reshape(devices, count, share)
    params = jnp.transpose(params, (1, 0, 2)).reshape(count, width).astype(WIDE)
    h_bias = lax.dynamic_index_in_dim(small[:, :, count * share :], here, 1, False)
    h_bias = h_bias.reshape(-1).astype(WIDE)

    order = here ^ jnp.array([offset_of(n) for n in range(INNER)], jnp.int32)

    def place_rows(weight):
        return jnp.take(weight.reshape(INNER, pair, width), order, axis=0).reshape(width, width)

    w_self = slices_of(self_in, 3)
    w_pair = slices_of(cross_kv, 2)
    w_query = slices_of(cross_query, 1)
    w_sout = lax.all_gather(self_out, ALL, axis=0, tiled=True)
    w_cout = lax.all_gather(cross_out, ALL, axis=0, tiled=True)
    w_first = slices_of(mlp_in, shares)
    w_second = lax.all_gather(mlp_out, OUTER, axis=0, tiled=True)

    x_low = gather_places(target[0])
    states = gather_places(source[0])
    pull_up = gather_places(cotangent[0])
    x = x_low.astype(WIDE)

    h1 = layer_norm(x, params[0], params[1]).astype(LOW)
    projected = dot(h1, w_self)
    q = (projected[:, :pair] + my_heads(params[6])).astype(LOW)
    k = projected[:, pair : 2 * pair].astype(LOW)
    v = (projected[:, 2 * pair :] + my_heads(params[7])).astype(LOW)

    def stream_keys(own):
        return lax.all_gather(own, "outer", axis=0, tiled=True) if groups > 1 else own

    def own_keys(partial):
        if groups == 1:
            return partial
        return lax.psum_scatter(partial, "outer", scatter_dimension=0, tiled=True)

    k, v = stream_keys(k), stream_keys(v)
    att, self_total = attend(self_table, q, k, v, rows, True)
    att = gather_heads(att, rows)
    y1 = x + dot(att, place_rows(w_sout)) + params[8]
    h2 = layer_norm(y1, params[2], params[3]).astype(LOW)
    cq = (dot(h2, w_query) + my_heads(params[9])).astype(LOW)
    state_proj = dot(states, w_pair)
    ck = stream_keys(state_proj[:, :pair].astype(LOW))
    cv = stream_keys((state_proj[:, pair:] + my_heads(params[10])).astype(LOW))
    catt, cross_total = attend(cross_table, cq, ck, cv, rows, False)
    catt = gather_heads(catt, rows)
    y2 = y1 + dot(catt, place_rows(w_cout)) + params[11]
    h3 = layer_norm(y2, params[4], params[5]).astype(LOW)
    before = dot(h3, w_first) + h_bias
    active, active_pull = jax.vjp(smooth, before)
    active_low = active.astype(LOW)
    fed = scatter_places(lambda lo, hi: dot(active_low[lo:hi], w_second), rows)
    layer_out = (y2[:rows] + fed + params[12]).astype(LOW)[None]

    active_grad = across(pull_up, w_second)
    before_grad = active_pull(active_grad)[0].astype(LOW)
    second_grad = under(active_low, pull_up).astype(LOW)
    second_home = lax.psum_scatter(second_grad, OUTER, scatter_dimension=0, tiled=True)
    first_grad = under(h3, before_grad).astype(LOW)
    first_home = lax.psum_scatter(first_grad, OUTER, scatter_dimension=0, tiled=True)
    h_bias_grad = jnp.sum(before_grad.astype(WIDE), axis=0)
    third_grad = scatter_places(lambda lo, hi: across(before_grad[lo:hi], w_first), rows)
    upstream = cotangent[0].astype(WIDE)
    _, third_pull = jax.vjp(layer_norm, y2[:rows], params[4], params[5])
    late_part, gain_five, shift_five = third_pull(third_grad)
    late_grad = upstream + late_part
    cross_branch = late_grad.astype(LOW)
    cross_all = gather_places(cross_branch)

    def my_rows(weight):
        return lax.dynamic_slice_in_dim(weight, here * pair, pair, axis=0)

    def shard_features(value):
        cut = []
        for n in range(shares):
            first = (n * INNER + here) * share
            block = first // pair
            mixed = block ^ here
            place = ((mixed >> 1) & 3) | ((mixed & 1) << 2)
            cut.append(
                lax.dynamic_slice_in_dim(value, place * pair + first % pair, share, axis=1)
            )
        return jnp.concatenate(cut, axis=1)

    def home_rows(value, branch):
        grad = under(shard_features(value), branch).astype(LOW)
        return lax.psum_scatter(grad, OUTER, scatter_dimension=0, tiled=True).astype(WIDE)

    def home_columns(value, branch):
        grad = under(value, branch).astype(LOW)
        return lax.psum_scatter(grad, OUTER, scatter_dimension=0, tiled=True)

    cout_home = home_rows(catt, cross_all)
    catt_grad = across(cross_all, my_rows(w_cout)).astype(LOW)
    dcq, dck, dcv = attend_back(cross_table, cq, ck, cv, catt_grad, cross_total, rows, False)
    dck, dcv = own_keys(dck), own_keys(dcv)
    pair_back = jnp.concatenate([dck, dcv], axis=1)
    second_norm_grad = scatter_places(lambda lo, hi: across(dcq[lo:hi], w_query), rows)
    _, second_pull = jax.vjp(layer_norm, y1[:rows], params[2], params[3])
    middle_part, gain_three, shift_three = second_pull(second_norm_grad)
    middle_grad = late_grad + middle_part
    self_branch = middle_grad.astype(LOW)
    self_all = gather_places(self_branch)
    att_grad = across(self_all, my_rows(w_sout)).astype(LOW)
    dq, dk, dv = attend_back(self_table, q, k, v, att_grad, self_total, rows, True)
    dk, dv = own_keys(dk), own_keys(dv)
    projected_grad = jnp.concatenate([dq, dk, dv], axis=1)
    first_norm_grad = scatter_places(lambda lo, hi: across(projected_grad[lo:hi], w_self), rows)
    source_part = scatter_places(lambda lo, hi: across(pair_back[lo:hi], w_pair), rows)
    source_grad = source_part.astype(LOW)[None]
    query_home = home_columns(h2, dcq)
    pair_home = home_columns(states, pair_back)
    sout_home = home_rows(att, self_all)
    self_home = home_columns(h1, projected_grad)
    _, first_pull = jax.vjp(layer_norm, x[:rows], params[0], params[1])
    input_part, gain_one, shift_one = first_pull(first_norm_grad)
    target_grad = (middle_grad + input_part).astype(LOW)[None]

    def spread_heads(value):
        total = jnp.sum(value.astype(WIDE), axis=0)
        return lax.dynamic_update_slice_in_dim(jnp.zeros((width,), WIDE), total, here * pair, 0)

    vector_grad = jnp.stack(
        [
            gain_one,
            shift_one,
            gain_three,
            shift_three,
            gain_five,
            shift_five,
            spread_heads(dq),
            spread_heads(dv),
            jnp.sum(self_branch.astype(WIDE), axis=0),
            spread_heads(dcq),
            spread_heads(dcv),
            jnp.sum(cross_branch.astype(WIDE), axis=0),
            jnp.sum(upstream, axis=0),
        ]
    )
    vector_part = jnp.transpose(vector_grad.reshape(count, devices, share), (1, 0, 2))
    bias_part = h_bias_grad.reshape(shares, 1, -1)
    bias_part = lax.dynamic_update_slice_in_dim(
        jnp.zeros((shares, INNER, bias_part.shape[2]), WIDE), bias_part, here, 1
    ).reshape(devices, -1)
    tiny = jnp.concatenate([vector_part.reshape(devices, -1), bias_part], axis=1)
    tiny = jnp.sum(lax.all_to_all(tiny, ALL, 0, 0, tiled=True), axis=0)

    def to_owners(grad, parts):
        return column_home(grad.reshape(INNER, -1, grad.shape[1]), parts)

    return (
        layer_out,
        target_grad,
        source_grad,
        to_owners(self_home, 3),
        sout_home,
        to_owners(query_home, 1),
        to_owners(pair_home, 2),
        cout_home,
        to_owners(first_home, shares),
        second_home.astype(WIDE),
        tiny[: count * share].reshape(count, share),
        tiny[count * share :],
    )


def solution(mesh):
    streams, blocks = mesh.devices.shape
    grid = mesh.devices.reshape(streams, blocks // INNER, INNER)
    inner_mesh = Mesh(grid, ALL)
    rows = P("ulys", ("outer", "inner"), None)
    matrix = P(ALL, None)
    row_vectors = P(None, ALL)
    in_specs = (rows,) * 3 + (P(), P()) + (matrix,) * 7 + (row_vectors, P(ALL))
    out_specs = (rows,) * 3 + (matrix,) * 7 + (row_vectors, P(ALL))
    return jax.shard_map(
        per_device, mesh=inner_mesh, in_specs=in_specs, out_specs=out_specs, check_vma=False
    )
```

time: 2700 us -> 573 us (0.21)
  waiting for transfers between devices: 1890 us -> 131 us
  matrix products: 206 us -> 73.1 us
  local copies, waits for them, and re-layouts: 238 us -> 109 us
  blocking collectives: 143 us -> 89.7 us
  loops' own time: 46.9 us -> 0 us
  other arithmetic: 84.5 us -> 41.3 us
  Pallas kernels: 0 us -> 29.5 us
    reduce_scatter x6 -> x7, waiting for transfers between devices: 1300 us -> 53.6 us  [the longest x1 22.9 us: per_device(): lax.psum_scatter(first_grad, OUTER, scatter_dimension=0, tiled=True)]
    ppermute x28 -> x48, waiting for transfers between devices: 262 us -> 63.1 us  [hop(): return lax.ppermute(value, 'inner', route)]
    unnamed x17 -> x11, waiting for transfers between devices: 170 us -> 2.03 us
    dot_general x165 -> x26, matrix products: 206 us -> 73.1 us  [the longest x11 28.8 us: across(): lax.dot_general(a, b, (((1,), (1,)), ((), ())), preferred_element_type=WIDE)]
    all_gather x7 -> x4, waiting for transfers between devices: 88.2 us -> 0.01 us  [the longest x1 0.01 us: per_device(): w_cout = lax.all_gather(cross_out, ALL, axis=0, tiled=True)]
    slice x71 -> x17, local copies, waits for them, and re-layouts: 82.6 us -> 5.92 us  [the longest x5 2.27 us: scatter_places(): part = both[place * rows:(place + 1) * rows].astype(LOW)]
    dynamic_slice x64 -> x3, local copies, waits for them, and re-layouts: 76.7 us -> 6.04 us  [the longest x2 6.04 us: shard_features(): lax.dynamic_slice_in_dim(value, place * pair + first % pair, share, axis=1)]
    all_to_all x7 -> x8, waiting for transfers between devices: 70.4 us -> 11.8 us  [the longest x1 9.17 us: per_device(): tiny = jnp.sum(lax.all_to_all(tiny, ALL, 0, 0, tiled=True), axis=0)]
  transfers between devices with their start and end apart: 50 -> 67, of which waited for: 43 -> 25; matrix products, arithmetic and copies ran while one was open for 9% -> 35% of each run, Pallas kernels for 0% -> 3%
where the time goes in v1:
time: 573 us; the launch traced here: 566 us
  waiting for transfers between devices  131 us (23%)
  local copies, waits for them, and re-layouts  109 us (19%)
  blocking collectives  89.7 us (16%)
  starting transfers between devices  75.9 us (13%)
  matrix products  73.1 us (13%)
  other arithmetic  41.3 us (7%)
  Pallas kernels  29.5 us (5%)
  between operations  17.3 us (3%)
    unnamed x302, local copies, waits for them, and re-layouts  63.8 us
    ppermute x48, waiting for transfers between devices, hop(): return lax.ppermute(value, 'inner', route)  63.1 us
    all_gather x3, blocking collectives, slices_of(): return lax.all_gather(mine, OUTER, axis=0).reshape(width, -1)  52.9 us
    ppermute x48, starting transfers between devices, hop(): return lax.ppermute(value, 'inner', route)  46.4 us
    dot_general x11, matrix products, across(): lax.dot_general(a, b, (((1,), (1,)), ((), ())), preferred_element_type=WIDE)  28.8 us
    reduce_scatter x1, waiting for transfers between devices, per_device(): lax.psum_scatter(first_grad, OUTER, scatter_dimension=0, tiled=True)  22.9 us
    dot_general x8, matrix products, dot(): return jnp.dot(a, b, preferred_element_type=WIDE)  22.5 us
    dot_general x7, matrix products, under(): lax.dot_general(a, b, (((0,), (0,)), ((), ())), preferred_element_type=WIDE)  21.8 us
  transfers between devices with their start and end apart: 67, of which 25 were waited for; matrix products, arithmetic and copies ran while one was open for 35% of the time, Pallas kernels for 3%

profile of v1, /device:TPU:0, one launch (start us, length us, event | category | flops | bytes accessed | tf_op | source)
XLA Modules:
  0.0 566.2 jit_solution(9171470690743282711)
XLA Ops:
  10.5 15.0 %all_to_all.49 = bf16[8,32,1024]{2,1,0:T(8,128)(2,1)} all-to-all(bf16[8,32,1024]{2,1,0:T(8,128)(2,1)S(1)} %reshape.476), channel_id=1, replica_groups=mesh['ulys'=4,'blk'=8] {'blk'}, dimensions={0} | all-to-all | bytes 1048576 | tf_op jit(solution)/shard_map/all_to_all | solution.py:362
  26.9 2.4 collective-permute-start.2
  31.0 3.7 all-to-all-start.1
  38.7 12.1 %all-reduce = bf16[2688]{0:T(1024)(128)(2,1)S(1)} all-reduce(bf16[2688]{0:T(1024)(128)(2,1)S(1)} %dynamic-update-slice), channel_id=2, replica_groups=mesh['ulys'=4,'blk'=8] {'ulys'}, use_global_device_ids=true, to_apply=%add | all-reduce | flops 2688 | bytes 10752
  50.9 9.8 %all-gather.6 = bf16[8,672,4]{1,2,0:T(4,128)(2,1)S(1)} all-gather(bf16[1,672,4]{1,2,0:T(4,128)(2,1)S(1)} %bitcast.480), channel_id=3, replica_groups=mesh['ulys'=4,'blk'=8] {'blk'}, dimensions={0}, use_global_device_ids=true | all-gather | bytes 48384 | tf_op jit(solution)/shard_map/all_gather | solution.py:370
  67.7 3.4 all-to-all-start.2
  76.9 14.5 %all-gather.3 = bf16[32,32,128]{2,1,0:T(8,128)(2,1)S(1)} all-gather(bf16[8,32,128]{2,1,0:T(8,128)(2,1)S(1)} %all-to-all-done.1), channel_id=5, replica_groups=mesh['ulys'=4,'blk'=8] {'ulys'}, dimensions={0}, use_global_device_ids=true | all-gather | bytes 327680 | tf_op jit(solution)/shard_map/all_gather | solution.py:363
  91.4 4.0 all-to-all-start
  95.5 17.3 %all-gather.4 = bf16[32,32,256]{2,1,0:T(8,128)(2,1)S(1)} all-gather(bf16[8,32,256]{2,1,0:T(8,128)(2,1)S(1)} %all-to-all-done.2), channel_id=6, replica_groups=mesh['ulys'=4,'blk'=8] {'ulys'}, dimensions={0}, use_global_device_ids=true | all-gather | bytes 655360 | tf_op jit(solution)/shard_map/all_gather | solution.py:363
  112.8 3.8 collective-permute-start.10
  116.5 21.1 %all-gather.2 = bf16[32,32,384]{2,1,0:T(8,128)(2,1)S(1)} all-gather(bf16[8,32,384]{2,1,0:T(8,128)(2,1)} %all-to-all-done), channel_id=4, replica_groups=mesh['ulys'=4,'blk'=8] {'ulys'}, dimensions={0}, use_global_device_ids=true | all-gather | bytes 983040 | tf_op jit(solution)/shard_map/all_gather | solution.py:363
  145.7 3.1 collective-permute-done.21
  164.4 5.6 shard_map.238
  174.6 2.3 fusion.109
  179.4 6.5 %collective-permute-done.5 = bf16[1024,128]{1,0:T(8,128)(2,1)S(1)} collective-permute-done((bf16[1024,128]{1,0:T(8,128)(2,1)}, bf16[1024,128]{1,0:T(8,128)(2,1)S(1)}, u32[]{:S(2)}, u32[]{:S(2)}) %collective-permute-start.5) | collective-permute-done | bytes 262176 | tf_op jit(solution)/shard_map/ppermute | solution.py:255
  216.4 3.7 gather_fusion.1
  220.2 3.8 gather_fusion
  224.0 4.0 broadcast_select_fusion
  228.0 4.4 fusion.101
  235.3 6.2 %shard_map.239 = (bf16[1024,128]{1,0:T(8,128)(2,1)}, f32[2,1024]{1,0:T(2,128)}) custom-call(s32[8]{0:T(128)} %get-tuple-element.172.table, bf16[1024,128]{1,0:T(8,128)(2,1)} %fusion.7.q, bf16[1024,128]{1,0:T(8,128)(2,1)} %slice.1564.k, bf16[1024,128]{1,0:T(8,128)(2,1)} %fusion.32.v), custom_call_target="tpu_custom_call" | custom-call | tf_op jit(solution)/shard_map/pallas_call | solution.py:206
  245.8 2.3 constant_dynamic-update-slice_fusion.24
  248.2 2.7 collective-permute-done.12
  250.8 5.5 collective-permute-done.13
  257.0 2.2 collective-permute-done.15
  259.8 2.7 fusion.102
  264.5 7.7 %fusion.85 = f32[1024,1024]{1,0:T(8,128)} fusion(bf16[1024,1024]{1,0:T(8,128)(2,1)} %bitcast.485, f32[1024,1024]{0,1:T(8,128)} %copy-done.4, f32[1024]{0:T(1024)S(1)} %copy-done.63, f32[1024]{0:T(1024)S(1)} %mul.309, f32[1024]{0:T(1024)S(1)} %add_rsqrt_fusion, f32[1024]{0:T(1024)S(1)} %broadcast_multiply_fusion), kind=kOutput, calls=%fused_computation.418 | convolution fusion | flops 2152726528 | bytes 10502144 | tf_op jit(solution)/shard_map/dot_general | solution.py:316
  272.2 8.9 %convert_reduce_fusion = (f32[1024]{0:T(1024)S(1)}, bf16[1024,1024]{1,0:T(8,128)(2,1)S(1)}, bf16[1024,1024]{1,0:T(8,128)(2,1)S(1)}) fusion(f32[1024,1024]{1,0:T(8,128)} %fusion.85, f32[1024]{0:T(1024)S(1)} %bitcast.482, bf16[1024,1024]{0,1:T(8,128)(2,1)} %constant_dynamic-update-slice_fusion.24, bf16[1024,1024]{1,0:T(8,128)(2,1)} %all-gather.16.cloned.1.call-done), kind=kOutput, calls=%fused_computation.11 | convolution fusion | flops 2173697024 | bytes 12591104 | tf_op jit(solution)/shard_map/dot_general | solution.py:320
  299.9 4.2 collective-permute-done.26
  304.6 5.0 collective-permute-done.19
  309.7 4.7 collective-permute-done.18
  319.3 5.7 %collective-permute-done.28 = bf16[128,1024]{0,1:T(8,128)(2,1)S(1)} collective-permute-done((bf16[128,1024]{0,1:T(8,128)(2,1)S(1)}, bf16[128,1024]{0,1:T(8,128)(2,1)S(1)}, u32[]{:S(2)}, u32[]{:S(2)}) %collective-permute-start.28) | collective-permute-done | bytes 262176 | tf_op jit(solution)/shard_map/ppermute | solution.py:255
  325.0 5.9 %collective-permute-done.29 = bf16[128,1024]{0,1:T(8,128)(2,1)S(1)} collective-permute-done((bf16[128,1024]{0,1:T(8,128)(2,1)S(1)}, bf16[128,1024]{0,1:T(8,128)(2,1)S(1)}, u32[]{:S(2)}, u32[]{:S(2)}) %collective-permute-start.29) | collective-permute-done | bytes 262176 | tf_op jit(solution)/shard_map/ppermute | solution.py:255
  331.4 2.3 collective-permute-done.31
  333.9 2.8 convolution_convert_fusion.13.up
  336.7 9.9 %shard_map.240 = (bf16[1024,128]{1,0:T(8,128)(2,1)}, bf16[1024,128]{1,0:T(8,128)(2,1)}, bf16[1024,128]{1,0:T(8,128)(2,1)}) custom-call(s32[8]{0:T(128)} %get-tuple-element.172.table, bf16[1024,128]{1,0:T(8,128)(2,1)} %fusion.7.q, bf16[1024,128]{1,0:T(8,128)(2,1)} %slice.1564.k, bf16[1024,128]{1,0:T(8,128)(2,1)} %fusion.32.v, ...), custom_call_target="tpu_custom_call" | custom-call | tf_op jit(solution)/shard_map/pallas_call | solution.py:227
  346.6 2.4 convolution_convert_fusion.10
  349.1 2.1 constant_dynamic-slice_fusion.3
  356.1 3.1 convolution_convert_fusion.8
  359.3 6.6 %convolution_convert_fusion.1 = bf16[1024,1024]{1,0:T(8,128)(2,1)} fusion(bf16[1024,1024]{1,0:T(8,128)(2,1)} %copy-done.80, f32[1024,1024]{0,1:T(8,128)} %copy-done.4, f32[1024]{0:T(1024)S(1)} %copy-done.63, f32[1024]{0:T(1024)S(1)} %mul.309, f32[1024]{0:T(1024)S(1)} %add_rsqrt_fusion, f32[1024]{0:T(1024)S(1)} %broadcast_multiply_fusion), kind=kOutput, calls=%fused_computation.30 | convolution fusion | flops 2153775104 | bytes 8404992 | tf_op jit(solution)/shard_map/dot_general | solution.py:324
  367.2 3.9 constant_dynamic-slice_fusion.7
  374.1 3.8 convolution_convert_fusion
  390.6 3.6 all-to-all-start.5
  394.2 3.0 collective-permute-done.35
  397.2 5.3 collective-permute-done.34
  414.9 3.4 all-to-all-start.6
  421.1 3.1 fusion.107
  432.3 22.9 %reduce-scatter.18.cloned.1.call-done = bf16[256,1024]{1,0:T(8,128)(2,1)} async-done(((bf16[1024,1024]{1,0:T(8,128)(2,1)}), bf16[256,1024]{1,0:T(8,128)(2,1)}) %reduce-scatter.18.cloned.1.call-update) | async-done | bytes 524304 | tf_op jit(solution)/shard_map/reduce_scatter | solution.py:432
  455.2 3.7 all-to-all-start.7
  460.3 2.4 convolution_convert_fusion.12.up
  462.7 7.8 %shard_map.241 = (bf16[1024,128]{1,0:T(8,128)(2,1)}, bf16[1024,128]{1,0:T(8,128)(2,1)}, bf16[1024,128]{1,0:T(8,128)(2,1)}) custom-call(s32[8]{0:T(128)} %get-tuple-element.173.table, bf16[1024,128]{1,0:T(8,128)(2,1)} %get-tuple-element.143.q, bf16[1024,128]{1,0:T(8,128)(2,1)} %slice.1565.k, bf16[1024,128]{1,0:T(8,128)(2,1)} %get-tuple-element.142.v, ...), custom_call_target="tpu_custom_call" | custom-call | tf_op jit(solution)/shard_map/pallas_call | solution.py:227
  475.9 1.9 convolution_convert_fusion.11
  478.2 2.1 fusion.43
  480.3 20.5 %reduce-scatter.20.cloned.1.call-done = bf16[256,1024]{1,0:T(8,128)(2,1)} async-done(((bf16[1024,1024]{1,0:T(8,128)(2,1)}), bf16[256,1024]{1,0:T(8,128)(2,1)}) %reduce-scatter.20.cloned.1.call-update) | async-done | bytes 524304 | tf_op jit(solution)/shard_map/reduce_scatter | solution.py:430
  500.8 2.1 convert_element_type.338
  505.7 2.2 convolution_convert_fusion.7
  508.1 3.5 fusion.106
  511.8 2.5 collective-permute-start.43
  517.0 5.5 reduce-scatter.10.cloned.1.call-done
  524.1 2.2 collective-permute-done.42
  530.9 3.4 all-to-all-start.8
  534.4 9.2 %all-to-all-done.8 = f32[32,1,672]{2,1,0:T(1,128)S(1)} async-done(((f32[32,1,672]{2,1,0:T(1,128)}), f32[32,1,672]{2,1,0:T(1,128)S(1)}, u32[]{:S(2)}, u32[]{:S(2)}) %all-to-all-start.8) | async-done | bytes 86048 | tf_op jit(solution)/shard_map/all_to_all | solution.py:518
  543.6 4.6 reduce-scatter.8.cloned.1.call-done
  548.1 3.6 all-to-all-start.4
  555.3 2.7 all-to-all-done.4
  (582 shorter events, 186.7 us)
Async XLA Ops:
  7.2 209.2 %all-gather.14.cloned.1.call-start = ((), (), s32[]{:S(2)}) async-start(), calls=%async_computation.17 | async-start | bytes 2162688 | tf_op jit(solution)/shard_map/all_gather | solution.py:385
  7.9 212.3 %all-gather.12.cloned.1.call-start = ((), (), s32[]{:S(2)}) async-start(), calls=%async_computation.16 | async-start | bytes 2162688 | tf_op jit(solution)/shard_map/all_gather | solution.py:384
  8.7 255.9 %all-gather.18.cloned.1.call-start = ((), (), s32[]{:S(2)}) async-start(), calls=%async_computation.26 | async-start | bytes 2621440 | tf_op jit(solution)/shard_map/all_gather | solution.py:363
  25.7 87.1 %collective-permute-start = (bf16[128,1024]{0,1:T(8,128)(2,1)S(1)}, bf16[128,1024]{0,1:T(8,128)(2,1)}, u32[]{:S(2)}, u32[]{:S(2)}) collective-permute-start(bf16[128,1024]{0,1:T(8,128)(2,1)S(1)} %bitcast.439), channel_id=1, source_target_pairs={{0,2},{1,3},{2,0},{3,1},{4,6},{5,7},{6,4},{7,5},{8,10},{9,11},{10,... | collective-permute-start | bytes 786440 | tf_op jit(solution)/shard_map/ppermute | solution.py:255
  26.3 111.3 %collective-permute-start.1 = (bf16[128,1024]{0,1:T(8,128)(2,1)S(1)}, bf16[128,1024]{0,1:T(8,128)(2,1)}, u32[]{:S(2)}, u32[]{:S(2)}) collective-permute-start(bf16[128,1024]{0,1:T(8,128)(2,1)S(1)} %bitcast.440), channel_id=1, source_target_pairs={{0,4},{1,5},{2,6},{3,7},{4,0},{5,1},{6,2},{7,3},{8,12},{9,13},{10,... | collective-permute-start | bytes 786440 | tf_op jit(solution)/shard_map/ppermute | solution.py:255
  26.9 112.0 %collective-permute-start.2 = (bf16[128,1024]{0,1:T(8,128)(2,1)S(1)}, bf16[128,1024]{0,1:T(8,128)(2,1)}, u32[]{:S(2)}, u32[]{:S(2)}) collective-permute-start(bf16[128,1024]{0,1:T(8,128)(2,1)S(1)} %bitcast.441), channel_id=1, source_target_pairs={{0,6},{1,7},{2,4},{3,5},{4,2},{5,3},{6,0},{7,1},{8,14},{9,15},{10,... | collective-permute-start | bytes 786440 | tf_op jit(solution)/shard_map/ppermute | solution.py:255
  29.3 110.1 %collective-permute-start.8 = (bf16[128,1024]{1,0:T(8,128)(2,1)}, bf16[128,1024]{1,0:T(8,128)(2,1)}, u32[]{:S(2)}, u32[]{:S(2)}) collective-permute-start(bf16[128,1024]{1,0:T(8,128)(2,1)} %bitcast.57), channel_id=1, source_target_pairs={{0,2},{1,3},{2,0},{3,1},{4,6},{5,7},{6,4},{7,5},{8,10},{9,11},{10,... | collective-permute-start | bytes 786440 | tf_op jit(solution)/shard_map/ppermute | solution.py:255
  29.8 112.7 %collective-permute-start.9 = (bf16[128,1024]{1,0:T(8,128)(2,1)}, bf16[128,1024]{1,0:T(8,128)(2,1)}, u32[]{:S(2)}, u32[]{:S(2)}) collective-permute-start(bf16[128,1024]{1,0:T(8,128)(2,1)} %bitcast.57), channel_id=1, source_target_pairs={{0,4},{1,5},{2,6},{3,7},{4,0},{5,1},{6,2},{7,3},{8,12},{9,13},{10,... | collective-permute-start | bytes 786440 | tf_op jit(solution)/shard_map/ppermute | solution.py:255
  31.0 36.7 %all-to-all-start.1 = ((bf16[8,32,128]{2,1,0:T(8,128)(2,1)}), bf16[8,32,128]{2,1,0:T(8,128)(2,1)S(1)}, u32[]{:S(2)}, u32[]{:S(2)}) async-start(bf16[8,32,128]{2,1,0:T(8,128)(2,1)} %copy.114), calls=%async_computation.1 | async-start | bytes 131072 | tf_op jit(solution)/shard_map/all_to_all | solution.py:362
  34.7 237.5 %all-gather.16.cloned.1.call-start = ((), (), s32[]{:S(2)}) async-start(), calls=%async_computation.18 | async-start | bytes 2621440 | tf_op jit(solution)/shard_map/all_gather | solution.py:387
  67.7 23.8 %all-to-all-start.2 = ((bf16[8,32,256]{2,1,0:T(8,128)(2,1)}), bf16[8,32,256]{2,1,0:T(8,128)(2,1)S(1)}, u32[]{:S(2)}, u32[]{:S(2)}) async-start(bf16[8,32,256]{2,1,0:T(8,128)(2,1)} %reshape.471), calls=%async_computation.2 | async-start | bytes 262144 | tf_op jit(solution)/shard_map/all_to_all | solution.py:362
  91.4 25.1 %all-to-all-start = ((bf16[8,32,384]{2,1,0:T(8,128)(2,1)}), bf16[8,32,384]{2,1,0:T(8,128)(2,1)}, u32[]{:S(2)}, u32[]{:S(2)}) async-start(bf16[8,32,384]{2,1,0:T(8,128)(2,1)} %reshape.461), calls=%async_computation | async-start | bytes 393216 | tf_op jit(solution)/shard_map/all_to_all | solution.py:362
  95.5 295.1 %reduce-scatter.12.cloned.1.call-start = ((), (), s32[]{:S(2)}) async-start(), calls=%async_computation.21 | async-start | bytes 327680 | tf_op jit(solution)/shard_map/reduce_scatter | solution.py:463
  112.8 29.8 %collective-permute-start.10 = (bf16[128,1024]{1,0:T(8,128)(2,1)}, bf16[128,1024]{1,0:T(8,128)(2,1)}, u32[]{:S(2)}, u32[]{:S(2)}) collective-permute-start(bf16[128,1024]{1,0:T(8,128)(2,1)} %bitcast.57), channel_id=1, source_target_pairs={{0,6},{1,7},{2,4},{3,5},{4,2},{5,3},{6,0},{7,1},{8,14},{9,15},{10,... | collective-permute-start | bytes 786440 | tf_op jit(solution)/shard_map/ppermute | solution.py:255
  137.6 8.1 %collective-permute-start.20 = (bf16[128,1024]{0,1:T(8,128)(2,1)S(1)}, bf16[128,1024]{0,1:T(8,128)(2,1)S(1)}, u32[]{:S(2)}, u32[]{:S(2)}) collective-permute-start(bf16[128,1024]{0,1:T(8,128)(2,1)S(1)} %bitcast.423), channel_id=1, source_target_pairs={{0,2},{1,3},{2,0},{3,1},{4,6},{5,7},{6,4},{7,5},{8,10},{9,11},{10,... | collective-permute-start | bytes 786440 | tf_op jit(solution)/shard_map/ppermute | solution.py:255
  138.9 9.9 %collective-permute-start.21 = (bf16[128,1024]{0,1:T(8,128)(2,1)S(1)}, bf16[128,1024]{0,1:T(8,128)(2,1)S(1)}, u32[]{:S(2)}, u32[]{:S(2)}) collective-permute-start(bf16[128,1024]{0,1:T(8,128)(2,1)S(1)} %bitcast.424), channel_id=1, source_target_pairs={{0,4},{1,5},{2,6},{3,7},{4,0},{5,1},{6,2},{7,3},{8,12},{9,13},{10,... | collective-permute-start | bytes 786440 | tf_op jit(solution)/shard_map/ppermute | solution.py:255
  139.4 9.4 %collective-permute-start.22 = (bf16[128,1024]{0,1:T(8,128)(2,1)S(1)}, bf16[128,1024]{0,1:T(8,128)(2,1)S(1)}, u32[]{:S(2)}, u32[]{:S(2)}) collective-permute-start(bf16[128,1024]{0,1:T(8,128)(2,1)S(1)} %bitcast.425), channel_id=1, source_target_pairs={{0,6},{1,7},{2,4},{3,5},{4,2},{5,3},{6,0},{7,1},{8,14},{9,15},{10,... | collective-permute-start | bytes 786440 | tf_op jit(solution)/shard_map/ppermute | solution.py:255
  142.5 17.0 %collective-permute-start.3 = (bf16[512,1024]{0,1:T(8,128)(2,1)S(1)}, bf16[512,1024]{0,1:T(8,128)(2,1)S(1)}, u32[]{:S(2)}, u32[]{:S(2)}) collective-permute-start(bf16[512,1024]{0,1:T(8,128)(2,1)S(1)} %pad_maximum_fusion), channel_id=1, source_target_pairs={{0,1},{1,0},{2,3},{3,2},{4,5},{5,4},{6,7},{7,6},{8,9},{9,8},{10,11... | collective-permute-start | bytes 3145736 | tf_op jit(solution)/shard_map/ppermute | solution.py:255
  143.9 29.7 %collective-permute-start.11 = (bf16[512,1024]{1,0:T(8,128)(2,1)S(1)}, bf16[512,1024]{1,0:T(8,128)(2,1)S(1)}, u32[]{:S(2)}, u32[]{:S(2)}) collective-permute-start(bf16[512,1024]{1,0:T(8,128)(2,1)S(1)} %pad_maximum_fusion.2), channel_id=1, source_target_pairs={{0,1},{1,0},{2,3},{3,2},{4,5},{5,4},{6,7},{7,6},{8,9},{9,8},{10,11... | collective-permute-start | bytes 3145736 | tf_op jit(solution)/shard_map/ppermute | solution.py:255
  149.9 95.9 %collective-permute-start.23 = (bf16[512,1024]{0,1:T(8,128)(2,1)}, bf16[512,1024]{0,1:T(8,128)(2,1)}, u32[]{:S(2)}, u32[]{:S(2)}) collective-permute-start(bf16[512,1024]{0,1:T(8,128)(2,1)} %pad_maximum_fusion.4), channel_id=1, source_target_pairs={{0,1},{1,0},{2,3},{3,2},{4,5},{5,4},{6,7},{7,6},{8,9},{9,8},{10,11... | collective-permute-start | bytes 3145736 | tf_op jit(solution)/shard_map/ppermute | solution.py:255
  170.1 9.3 %collective-permute-start.4 = (bf16[1024,128]{1,0:T(8,128)(2,1)}, bf16[1024,128]{1,0:T(8,128)(2,1)S(1)}, u32[]{:S(2)}, u32[]{:S(2)}) collective-permute-start(bf16[1024,128]{1,0:T(8,128)(2,1)} %get-tuple-element.23), channel_id=1, source_target_pairs={{0,2},{1,3},{2,0},{3,1},{4,6},{5,7},{6,4},{7,5},{8,10},{9,11},{10,... | collective-permute-start | bytes 786440 | tf_op jit(solution)/shard_map/ppermute | solution.py:255
  171.5 14.3 %collective-permute-start.5 = (bf16[1024,128]{1,0:T(8,128)(2,1)}, bf16[1024,128]{1,0:T(8,128)(2,1)S(1)}, u32[]{:S(2)}, u32[]{:S(2)}) collective-permute-start(bf16[1024,128]{1,0:T(8,128)(2,1)} %get-tuple-element.23), channel_id=1, source_target_pairs={{0,4},{1,5},{2,6},{3,7},{4,0},{5,1},{6,2},{7,3},{8,12},{9,13},{10,... | collective-permute-start | bytes 786440 | tf_op jit(solution)/shard_map/ppermute | solution.py:255
  172.1 13.7 %collective-permute-start.6 = (bf16[1024,128]{1,0:T(8,128)(2,1)}, bf16[1024,128]{1,0:T(8,128)(2,1)S(1)}, u32[]{:S(2)}, u32[]{:S(2)}) collective-permute-start(bf16[1024,128]{1,0:T(8,128)(2,1)} %get-tuple-element.23), channel_id=1, source_target_pairs={{0,6},{1,7},{2,4},{3,5},{4,2},{5,3},{6,0},{7,1},{8,14},{9,15},{10,... | collective-permute-start | bytes 786440 | tf_op jit(solution)/shard_map/ppermute | solution.py:255
  186.0 10.7 %collective-permute-start.7 = (bf16[4,1024,128]{2,1,0:T(8,128)(2,1)S(1)}, bf16[4,1024,128]{2,1,0:T(8,128)(2,1)S(1)}, u32[]{:S(2)}, u32[]{:S(2)}) collective-permute-start(bf16[4,1024,128]{2,1,0:T(8,128)(2,1)S(1)} %pad_maximum_fusion.1), channel_id=1, source_target_pairs={{0,1},{1,0},{2,3},{3,2},{4,5},{5,4},{6,7},{7,6},{8,9},{9,8},{10,11... | collective-permute-start | bytes 3145736 | tf_op jit(solution)/shard_map/ppermute | solution.py:255
  241.5 9.3 %collective-permute-start.12 = (bf16[1024,128]{1,0:T(8,128)(2,1)}, bf16[1024,128]{1,0:T(8,128)(2,1)S(1)}, u32[]{:S(2)}, u32[]{:S(2)}) collective-permute-start(bf16[1024,128]{1,0:T(8,128)(2,1)} %get-tuple-element.24), channel_id=1, source_target_pairs={{0,2},{1,3},{2,0},{3,1},{4,6},{5,7},{6,4},{7,5},{8,10},{9,11},{10,... | collective-permute-start | bytes 786440 | tf_op jit(solution)/shard_map/ppermute | solution.py:255
  242.1 14.2 %collective-permute-start.13 = (bf16[1024,128]{1,0:T(8,128)(2,1)}, bf16[1024,128]{1,0:T(8,128)(2,1)S(1)}, u32[]{:S(2)}, u32[]{:S(2)}) collective-permute-start(bf16[1024,128]{1,0:T(8,128)(2,1)} %get-tuple-element.24), channel_id=1, source_target_pairs={{0,4},{1,5},{2,6},{3,7},{4,0},{5,1},{6,2},{7,3},{8,12},{9,13},{10,... | collective-permute-start | bytes 786440 | tf_op jit(solution)/shard_map/ppermute | solution.py:255
  243.3 13.0 %collective-permute-start.14 = (bf16[1024,128]{1,0:T(8,128)(2,1)}, bf16[1024,128]{1,0:T(8,128)(2,1)S(1)}, u32[]{:S(2)}, u32[]{:S(2)}) collective-permute-start(bf16[1024,128]{1,0:T(8,128)(2,1)} %get-tuple-element.24), channel_id=1, source_target_pairs={{0,6},{1,7},{2,4},{3,5},{4,2},{5,3},{6,0},{7,1},{8,14},{9,15},{10,... | collective-permute-start | bytes 786440 | tf_op jit(solution)/shard_map/ppermute | solution.py:255
  285.6 6.2 %collective-permute-start.16 = (bf16[512,1024]{0,1:T(8,128)(2,1)S(1)}, bf16[512,1024]{0,1:T(8,128)(2,1)S(1)}, u32[]{:S(2)}, u32[]{:S(2)}) collective-permute-start(bf16[512,1024]{0,1:T(8,128)(2,1)S(1)} %convolution_convert_fusion.6), channel_id=1, source_target_pairs={{0,1},{1,0},{2,3},{3,2},{4,5},{5,4},{6,7},{7,6},{8,9},{9,8},{10,11... | collective-permute-start | bytes 3145736 | tf_op jit(solution)/shard_map/ppermute | solution.py:255
  288.2 10.2 %collective-permute-start.27 = (bf16[128,1024]{0,1:T(8,128)(2,1)S(1)}, bf16[128,1024]{0,1:T(8,128)(2,1)S(1)}, u32[]{:S(2)}, u32[]{:S(2)}) collective-permute-start(bf16[128,1024]{0,1:T(8,128)(2,1)S(1)} %get-tuple-element.154), channel_id=1, source_target_pairs={{0,6},{1,7},{2,4},{3,5},{4,2},{5,3},{6,0},{7,1},{8,14},{9,15},{10,... | collective-permute-start | bytes 786440 | tf_op jit(solution)/shard_map/ppermute | solution.py:255
  289.7 14.3 %collective-permute-start.26 = (bf16[128,1024]{0,1:T(8,128)(2,1)S(1)}, bf16[128,1024]{0,1:T(8,128)(2,1)S(1)}, u32[]{:S(2)}, u32[]{:S(2)}) collective-permute-start(bf16[128,1024]{0,1:T(8,128)(2,1)S(1)} %get-tuple-element.155), channel_id=1, source_target_pairs={{0,4},{1,5},{2,6},{3,7},{4,0},{5,1},{6,2},{7,3},{8,12},{9,13},{10,... | collective-permute-start | bytes 786440 | tf_op jit(solution)/shard_map/ppermute | solution.py:255
  291.2 12.8 %collective-permute-start.25 = (bf16[128,1024]{0,1:T(8,128)(2,1)S(1)}, bf16[128,1024]{0,1:T(8,128)(2,1)S(1)}, u32[]{:S(2)}, u32[]{:S(2)}) collective-permute-start(bf16[128,1024]{0,1:T(8,128)(2,1)S(1)} %get-tuple-element.153), channel_id=1, source_target_pairs={{0,2},{1,3},{2,0},{3,1},{4,6},{5,7},{6,4},{7,5},{8,10},{9,11},{10,... | collective-permute-start | bytes 786440 | tf_op jit(solution)/shard_map/ppermute | solution.py:255
  293.6 16.0 %collective-permute-start.19 = (bf16[128,1024]{0,1:T(8,128)(2,1)S(1)}, bf16[128,1024]{0,1:T(8,128)(2,1)S(1)}, u32[]{:S(2)}, u32[]{:S(2)}) collective-permute-start(bf16[128,1024]{0,1:T(8,128)(2,1)S(1)} %get-tuple-element.157), channel_id=1, source_target_pairs={{0,6},{1,7},{2,4},{3,5},{4,2},{5,3},{6,0},{7,1},{8,14},{9,15},{10,... | collective-permute-start | bytes 786440 | tf_op jit(solution)/shard_map/ppermute | solution.py:255
  295.1 19.3 %collective-permute-start.18 = (bf16[128,1024]{0,1:T(8,128)(2,1)S(1)}, bf16[128,1024]{0,1:T(8,128)(2,1)S(1)}, u32[]{:S(2)}, u32[]{:S(2)}) collective-permute-start(bf16[128,1024]{0,1:T(8,128)(2,1)S(1)} %get-tuple-element.158), channel_id=1, source_target_pairs={{0,4},{1,5},{2,6},{3,7},{4,0},{5,1},{6,2},{7,3},{8,12},{9,13},{10,... | collective-permute-start | bytes 786440 | tf_op jit(solution)/shard_map/ppermute | solution.py:255
  298.4 16.0 %collective-permute-start.17 = (bf16[128,1024]{0,1:T(8,128)(2,1)S(1)}, bf16[128,1024]{0,1:T(8,128)(2,1)S(1)}, u32[]{:S(2)}, u32[]{:S(2)}) collective-permute-start(bf16[128,1024]{0,1:T(8,128)(2,1)S(1)} %get-tuple-element.156), channel_id=1, source_target_pairs={{0,2},{1,3},{2,0},{3,1},{4,6},{5,7},{6,4},{7,5},{8,10},{9,11},{10,... | collective-permute-start | bytes 786440 | tf_op jit(solution)/shard_map/ppermute | solution.py:255
  315.7 9.2 %collective-permute-start.28 = (bf16[128,1024]{0,1:T(8,128)(2,1)S(1)}, bf16[128,1024]{0,1:T(8,128)(2,1)S(1)}, u32[]{:S(2)}, u32[]{:S(2)}) collective-permute-start(bf16[128,1024]{0,1:T(8,128)(2,1)S(1)} %get-tuple-element.118), channel_id=1, source_target_pairs={{0,2},{1,3},{2,0},{3,1},{4,6},{5,7},{6,4},{7,5},{8,10},{9,11},{10,... | collective-permute-start | bytes 786440 | tf_op jit(solution)/shard_map/ppermute | solution.py:255
  317.3 13.6 %collective-permute-start.29 = (bf16[128,1024]{0,1:T(8,128)(2,1)S(1)}, bf16[128,1024]{0,1:T(8,128)(2,1)S(1)}, u32[]{:S(2)}, u32[]{:S(2)}) collective-permute-start(bf16[128,1024]{0,1:T(8,128)(2,1)S(1)} %get-tuple-element.118), channel_id=1, source_target_pairs={{0,4},{1,5},{2,6},{3,7},{4,0},{5,1},{6,2},{7,3},{8,12},{9,13},{10,... | collective-permute-start | bytes 786440 | tf_op jit(solution)/shard_map/ppermute | solution.py:255
  317.9 12.9 %collective-permute-start.30 = (bf16[128,1024]{0,1:T(8,128)(2,1)S(1)}, bf16[128,1024]{0,1:T(8,128)(2,1)S(1)}, u32[]{:S(2)}, u32[]{:S(2)}) collective-permute-start(bf16[128,1024]{0,1:T(8,128)(2,1)S(1)} %get-tuple-element.118), channel_id=1, source_target_pairs={{0,6},{1,7},{2,4},{3,5},{4,2},{5,3},{6,0},{7,1},{8,14},{9,15},{10,... | collective-permute-start | bytes 786440 | tf_op jit(solution)/shard_map/ppermute | solution.py:255
  349.0 63.7 %reduce-scatter.16.cloned.1.call-start = ((), (), s32[]{:S(2)}) async-start(), calls=%async_computation.23 | async-start | bytes 327680 | tf_op jit(solution)/shard_map/reduce_scatter | solution.py:459
  353.2 61.7 %reduce-scatter.14.cloned.1.call-start = ((), (), s32[]{:S(2)}) async-start(), calls=%async_computation.22 | async-start | bytes 655360 | tf_op jit(solution)/shard_map/reduce_scatter | solution.py:463
  359.3 95.9 %reduce-scatter.18.cloned.1.call-start = ((), (), s32[]{:S(2)}) async-start(), calls=%async_computation.24 | async-start | bytes 2621440 | tf_op jit(solution)/shard_map/reduce_scatter | solution.py:432
  366.0 134.9 %reduce-scatter.20.cloned.1.call-start = ((), (), s32[]{:S(2)}) async-start(), calls=%async_computation.25 | async-start | bytes 2621440 | tf_op jit(solution)/shard_map/reduce_scatter | solution.py:430
  374.0 10.0 %collective-permute-start.32 = (bf16[512,1024]{0,1:T(8,128)(2,1)S(1)}, bf16[512,1024]{0,1:T(8,128)(2,1)}, u32[]{:S(2)}, u32[]{:S(2)}) collective-permute-start(bf16[512,1024]{0,1:T(8,128)(2,1)S(1)} %convolution_convert_fusion.2), channel_id=1, source_target_pairs={{0,1},{1,0},{2,3},{3,2},{4,5},{5,4},{6,7},{7,6},{8,9},{9,8},{10,11... | collective-permute-start | bytes 3145736 | tf_op jit(solution)/shard_map/ppermute | solution.py:255
  386.8 10.4 %collective-permute-start.35 = (bf16[128,1024]{0,1:T(8,128)(2,1)}, bf16[128,1024]{0,1:T(8,128)(2,1)}, u32[]{:S(2)}, u32[]{:S(2)}) collective-permute-start(bf16[128,1024]{0,1:T(8,128)(2,1)} %get-tuple-element.151), channel_id=1, source_target_pairs={{0,6},{1,7},{2,4},{3,5},{4,2},{5,3},{6,0},{7,1},{8,14},{9,15},{10,... | collective-permute-start | bytes 786440 | tf_op jit(solution)/shard_map/ppermute | solution.py:255
  388.1 14.4 %collective-permute-start.34 = (bf16[128,1024]{0,1:T(8,128)(2,1)}, bf16[128,1024]{0,1:T(8,128)(2,1)}, u32[]{:S(2)}, u32[]{:S(2)}) collective-permute-start(bf16[128,1024]{0,1:T(8,128)(2,1)} %get-tuple-element.152), channel_id=1, source_target_pairs={{0,4},{1,5},{2,6},{3,7},{4,0},{5,1},{6,2},{7,3},{8,12},{9,13},{10,... | collective-permute-start | bytes 786440 | tf_op jit(solution)/shard_map/ppermute | solution.py:255
  388.8 13.7 %collective-permute-start.33 = (bf16[128,1024]{0,1:T(8,128)(2,1)}, bf16[128,1024]{0,1:T(8,128)(2,1)}, u32[]{:S(2)}, u32[]{:S(2)}) collective-permute-start(bf16[128,1024]{0,1:T(8,128)(2,1)} %get-tuple-element.150), channel_id=1, source_target_pairs={{0,2},{1,3},{2,0},{3,1},{4,6},{5,7},{6,4},{7,5},{8,10},{9,11},{10,... | collective-permute-start | bytes 786440 | tf_op jit(solution)/shard_map/ppermute | solution.py:255
  390.5 30.7 %collective-permute-start.44 = (bf16[512,1024]{1,0:T(8,128)(2,1)}, bf16[512,1024]{1,0:T(8,128)(2,1)}, u32[]{:S(2)}, u32[]{:S(2)}) collective-permute-start(bf16[512,1024]{1,0:T(8,128)(2,1)} %convolution_convert_fusion.3), channel_id=1, source_target_pairs={{0,1},{1,0},{2,3},{3,2},{4,5},{5,4},{6,7},{7,6},{8,9},{9,8},{10,11... | collective-permute-start | bytes 3145736 | tf_op jit(solution)/shard_map/ppermute | solution.py:255
  390.6 23.6 %all-to-all-start.5 = ((bf16[8,32,128]{2,1,0:T(8,128)(2,1)}), bf16[8,32,128]{2,1,0:T(8,128)(2,1)S(1)}, u32[]{:S(2)}, u32[]{:S(2)}) async-start(bf16[8,32,128]{2,1,0:T(8,128)(2,1)} %bitcast.479), calls=%async_computation.8 | async-start | bytes 131072 | tf_op jit(solution)/shard_map/all_to_all | solution.py:297
  405.9 12.5 %collective-permute-start.36 = (bf16[128,1024]{0,1:T(8,128)(2,1)S(1)}, bf16[128,1024]{0,1:T(8,128)(2,1)S(1)}, u32[]{:S(2)}, u32[]{:S(2)}) collective-permute-start(bf16[128,1024]{0,1:T(8,128)(2,1)S(1)} %get-tuple-element.120), channel_id=1, source_target_pairs={{0,2},{1,3},{2,0},{3,1},{4,6},{5,7},{6,4},{7,5},{8,10},{9,11},{10,... | collective-permute-start | bytes 786440 | tf_op jit(solution)/shard_map/ppermute | solution.py:255
  406.6 13.4 %collective-permute-start.37 = (bf16[128,1024]{0,1:T(8,128)(2,1)S(1)}, bf16[128,1024]{0,1:T(8,128)(2,1)S(1)}, u32[]{:S(2)}, u32[]{:S(2)}) collective-permute-start(bf16[128,1024]{0,1:T(8,128)(2,1)S(1)} %get-tuple-element.120), channel_id=1, source_target_pairs={{0,4},{1,5},{2,6},{3,7},{4,0},{5,1},{6,2},{7,3},{8,12},{9,13},{10,... | collective-permute-start | bytes 786440 | tf_op jit(solution)/shard_map/ppermute | solution.py:255
  407.6 12.3 %collective-permute-start.38 = (bf16[128,1024]{0,1:T(8,128)(2,1)S(1)}, bf16[128,1024]{0,1:T(8,128)(2,1)S(1)}, u32[]{:S(2)}, u32[]{:S(2)}) collective-permute-start(bf16[128,1024]{0,1:T(8,128)(2,1)S(1)} %get-tuple-element.120), channel_id=1, source_target_pairs={{0,6},{1,7},{2,4},{3,5},{4,2},{5,3},{6,0},{7,1},{8,14},{9,15},{10,... | collective-permute-start | bytes 786440 | tf_op jit(solution)/shard_map/ppermute | solution.py:255
  414.9 13.7 %all-to-all-start.6 = ((bf16[8,32,256]{2,1,0:T(8,128)(2,1)}), bf16[8,32,256]{2,1,0:T(8,128)(2,1)S(1)}, u32[]{:S(2)}, u32[]{:S(2)}) async-start(bf16[8,32,256]{2,1,0:T(8,128)(2,1)} %bitcast.476), calls=%async_computation.10 | async-start | bytes 262144 | tf_op jit(solution)/shard_map/all_to_all | solution.py:297
  421.1 37.8 %collective-permute-start.39 = (bf16[512,1024]{0,1:T(8,128)(2,1)}, bf16[512,1024]{0,1:T(8,128)(2,1)}, u32[]{:S(2)}, u32[]{:S(2)}) collective-permute-start(bf16[512,1024]{0,1:T(8,128)(2,1)} %pad_maximum_fusion.6), channel_id=1, source_target_pairs={{0,1},{1,0},{2,3},{3,2},{4,5},{5,4},{6,7},{7,6},{8,9},{9,8},{10,11... | collective-permute-start | bytes 3145736 | tf_op jit(solution)/shard_map/ppermute | solution.py:255
  425.2 53.0 %collective-permute-start.47 = (bf16[128,1024]{1,0:T(8,128)(2,1)}, bf16[128,1024]{1,0:T(8,128)(2,1)}, u32[]{:S(2)}, u32[]{:S(2)}) collective-permute-start(bf16[128,1024]{1,0:T(8,128)(2,1)} %get-tuple-element.145), channel_id=1, source_target_pairs={{0,6},{1,7},{2,4},{3,5},{4,2},{5,3},{6,0},{7,1},{8,14},{9,15},{10,... | collective-permute-start | bytes 786440 | tf_op jit(solution)/shard_map/ppermute | solution.py:255
  426.6 51.5 %collective-permute-start.46 = (bf16[128,1024]{1,0:T(8,128)(2,1)}, bf16[128,1024]{1,0:T(8,128)(2,1)}, u32[]{:S(2)}, u32[]{:S(2)}) collective-permute-start(bf16[128,1024]{1,0:T(8,128)(2,1)} %get-tuple-element.146), channel_id=1, source_target_pairs={{0,4},{1,5},{2,6},{3,7},{4,0},{5,1},{6,2},{7,3},{8,12},{9,13},{10,... | collective-permute-start | bytes 786440 | tf_op jit(solution)/shard_map/ppermute | solution.py:255
  427.8 50.3 %collective-permute-start.45 = (bf16[128,1024]{1,0:T(8,128)(2,1)}, bf16[128,1024]{1,0:T(8,128)(2,1)}, u32[]{:S(2)}, u32[]{:S(2)}) collective-permute-start(bf16[128,1024]{1,0:T(8,128)(2,1)} %get-tuple-element.144), channel_id=1, source_target_pairs={{0,2},{1,3},{2,0},{3,1},{4,6},{5,7},{6,4},{7,5},{8,10},{9,11},{10,... | collective-permute-start | bytes 786440 | tf_op jit(solution)/shard_map/ppermute | solution.py:255
  455.2 47.8 %all-to-all-start.7 = ((bf16[8,32,1024]{2,1,0:T(8,128)(2,1)}), bf16[8,32,1024]{2,1,0:T(8,128)(2,1)S(1)}, u32[]{:S(2)}, u32[]{:S(2)}) async-start(bf16[8,32,1024]{2,1,0:T(8,128)(2,1)} %bitcast.464), calls=%async_computation.13 | async-start | bytes 1048576 | tf_op jit(solution)/shard_map/all_to_all | solution.py:297
  458.9 63.7 %reduce-scatter.10.cloned.1.call-start = ((), (), s32[]{:S(2)}) async-start(), calls=%async_computation.20 | async-start | bytes 327680 | tf_op jit(solution)/shard_map/reduce_scatter | solution.py:459
  475.5 32.6 %collective-permute-start.40 = (bf16[512,1024]{0,1:T(8,128)(2,1)}, bf16[512,1024]{0,1:T(8,128)(2,1)}, u32[]{:S(2)}, u32[]{:S(2)}) collective-permute-start(bf16[512,1024]{0,1:T(8,128)(2,1)} %convolution_convert_fusion.4), channel_id=1, source_target_pairs={{0,1},{1,0},{2,3},{3,2},{4,5},{5,4},{6,7},{7,6},{8,9},{9,8},{10,11... | collective-permute-start | bytes 3145736 | tf_op jit(solution)/shard_map/ppermute | solution.py:255
  477.8 70.3 %reduce-scatter.8.cloned.1.call-start = ((), (), s32[]{:S(2)}) async-start(), calls=%async_computation.19 | async-start | bytes 983040 | tf_op jit(solution)/shard_map/reduce_scatter | solution.py:463
  511.8 12.3 %collective-permute-start.43 = (bf16[128,1024]{0,1:T(8,128)(2,1)S(1)}, bf16[128,1024]{0,1:T(8,128)(2,1)S(1)}, u32[]{:S(2)}, u32[]{:S(2)}) collective-permute-start(bf16[128,1024]{0,1:T(8,128)(2,1)S(1)} %get-tuple-element.148), channel_id=1, source_target_pairs={{0,6},{1,7},{2,4},{3,5},{4,2},{5,3},{6,0},{7,1},{8,14},{9,15},{10,... | collective-permute-start | bytes 786440 | tf_op jit(solution)/shard_map/ppermute | solution.py:255
  514.3 12.0 %collective-permute-start.42 = (bf16[128,1024]{0,1:T(8,128)(2,1)S(1)}, bf16[128,1024]{0,1:T(8,128)(2,1)S(1)}, u32[]{:S(2)}, u32[]{:S(2)}) collective-permute-start(bf16[128,1024]{0,1:T(8,128)(2,1)S(1)} %get-tuple-element.149), channel_id=1, source_target_pairs={{0,4},{1,5},{2,6},{3,7},{4,0},{5,1},{6,2},{7,3},{8,12},{9,13},{10,... | collective-permute-start | bytes 786440 | tf_op jit(solution)/shard_map/ppermute | solution.py:255
  514.8 11.5 %collective-permute-start.41 = (bf16[128,1024]{0,1:T(8,128)(2,1)S(1)}, bf16[128,1024]{0,1:T(8,128)(2,1)S(1)}, u32[]{:S(2)}, u32[]{:S(2)}) collective-permute-start(bf16[128,1024]{0,1:T(8,128)(2,1)S(1)} %get-tuple-element.147), channel_id=1, source_target_pairs={{0,2},{1,3},{2,0},{3,1},{4,6},{5,7},{6,4},{7,5},{8,10},{9,11},{10,... | collective-permute-start | bytes 786440 | tf_op jit(solution)/shard_map/ppermute | solution.py:255
  530.9 12.6 %all-to-all-start.8 = ((f32[32,1,672]{2,1,0:T(1,128)}), f32[32,1,672]{2,1,0:T(1,128)S(1)}, u32[]{:S(2)}, u32[]{:S(2)}) async-start(f32[32,1,672]{2,1,0:T(1,128)} %copy.132), calls=%async_computation.15 | async-start | bytes 196608 | tf_op jit(solution)/shard_map/all_to_all | solution.py:518
  548.1 9.9 %all-to-all-start.4 = ((bf16[8,32,384]{2,1,0:T(8,128)(2,1)}), bf16[8,32,384]{2,1,0:T(8,128)(2,1)S(1)}, u32[]{:S(2)}, u32[]{:S(2)}) async-start(bf16[8,32,384]{2,1,0:T(8,128)(2,1)} %bitcast.472), calls=%async_computation.5 | async-start | bytes 393216 | tf_op jit(solution)/shard_map/all_to_all | solution.py:297
  (86 other events, 1069.3 us)
Sparse Core Ops, SparseCore 0:
  10.9 60.4 all-gather.13
  74.2 59.0 all-gather.11
  134.8 44.1 all-gather.17
  180.5 44.6 all-gather.15
  349.1 18.6 reduce-scatter.11
  370.0 17.9 reduce-scatter.15
  390.8 19.7 reduce-scatter.13
  412.9 42.2 reduce-scatter.17
  457.6 43.1 reduce-scatter.19
  503.5 18.9 reduce-scatter.9
  525.0 23.1 reduce-scatter.7

commit v2 on v1

v2 whole, which is shorter than its diff:
```python
import functools

import jax
import jax.numpy as jnp
from jax import lax
from jax.experimental import pallas as pl
from jax.experimental.pallas import tpu as pltpu
from jax.sharding import Mesh
from jax.sharding import PartitionSpec as P

HEADS = 16
LOW = jnp.bfloat16
WIDE = jnp.float32
INNER = 8
STEP = 256
LANES = 128
OUTER = ("ulys", "outer")
ALL = ("ulys", "outer", "inner")


def offset_of(place):
    return ((place & 3) << 1) | (place >> 2)


def dot_t(a, b):
    return lax.dot_general(a, b, (((1,), (1,)), ((), ())), preferred_element_type=WIDE)


def dot_n(a, b):
    return lax.dot_general(a, b, (((1,), (0,)), ((), ())), preferred_element_type=WIDE)


def dot_c(a, b):
    return lax.dot_general(a, b, (((0,), (0,)), ((), ())), preferred_element_type=WIDE)


def seg_of(position, table, first):
    count = jnp.zeros_like(position)
    for n in range(3):
        count = count + (table[first + n] <= position).astype(jnp.int32)
    return count


def iota(shape, axis):
    return lax.broadcasted_iota(jnp.int32, shape, axis)


def to_order(table, source, target, rows, factor=None):
    span = rows * INNER
    for chunk in range(source.shape[0] // span):
        for place in range(INNER):
            at = pl.multiple_of((table[0] ^ offset_of(place)) * rows, rows) + chunk * span
            value = source[pl.ds(chunk * span + place * rows, rows), :]
            if factor is not None:
                value = value * factor
            target[pl.ds(at, rows), :] = value


def from_order(table, source, target, rows):
    span = rows * INNER
    for chunk in range(target.shape[0] // span):
        for place in range(INNER):
            at = pl.multiple_of((table[0] ^ offset_of(place)) * rows, rows) + chunk * span
            target[pl.ds(chunk * span + place * rows, rows), :] = source[pl.ds(at, rows), :].astype(
                target.dtype
            )


def half_lanes(value, head, size):
    lane = iota(value.shape, 1)
    keep = (lane >= head * size) & (lane < (head + 1) * size)
    return jnp.where(keep, value, jnp.zeros_like(value))


def attend_kernel(causal, rows, size, table, q, k, v, out, log_total, qs, ks, vs, ordered):
    span, keys = q.shape[0], k.shape[0]
    chunks = keys // span
    to_order(table, q, qs, rows, jnp.asarray(size**-0.5, LOW))
    to_order(table, k, ks, rows)
    to_order(table, v, vs, rows)
    for step in range(span // STEP):
        lo = step * STEP
        queries = qs[lo : lo + STEP, :]
        q_at = table[1] + lo + iota((STEP, 1), 0)
        q_seg = seg_of(q_at, table, 2)
        count = lo + STEP if causal and chunks == 1 else span

        def scores(head, start):
            k_at = start + iota((1, count), 1)
            allowed = q_seg == seg_of(k_at, table, 5)
            if causal:
                allowed = allowed & (k_at <= q_at)
            raw = dot_t(queries, half_lanes(ks[pl.ds(start, count), :], head, size))
            return jnp.where(allowed, raw, -1e30)

        parts = []
        for head in range(2):
            if chunks == 1:
                raw = scores(head, 0)
                top = jnp.max(raw, axis=1, keepdims=True)
                weight = jnp.exp(raw - top)
                total = jnp.sum(weight, axis=1, keepdims=True)
                running = dot_n(weight.astype(LOW), vs[:count, :])
            else:

                def absorb(chunk, carry, head=head):
                    top, total, running = carry
                    start = pl.multiple_of(chunk * span, span)
                    raw = scores(head, start)
                    new_top = jnp.maximum(top, jnp.max(raw, axis=1, keepdims=True))
                    weight = jnp.exp(raw - new_top)
                    fade = jnp.exp(top - new_top)
                    total = total * fade + jnp.sum(weight, axis=1, keepdims=True)
                    running = running * fade + dot_n(weight.astype(LOW), vs[pl.ds(start, span), :])
                    return new_top, total, running

                top, total, running = lax.fori_loop(
                    0,
                    chunks,
                    absorb,
                    (
                        jnp.full((STEP, 1), -1e30, WIDE),
                        jnp.zeros((STEP, 1), WIDE),
                        jnp.zeros((STEP, 2 * size), WIDE),
                    ),
                )
            parts.append(running / total)
            logs = jnp.broadcast_to(top + jnp.log(total), (STEP, 2 * size))
            log_total[head : head + 1, lo : lo + STEP] = jnp.transpose(logs)[0:1, :]
        lane = iota((STEP, 2 * size), 1)
        ordered[lo : lo + STEP, :] = jnp.where(lane < size, parts[0], parts[1])
    from_order(table, ordered, out, rows)


def attend_back_kernel(causal, rows, size, start, table, q, k, v, log_total, weight, own, *refs):
    pieces, refs = refs[:INNER], refs[INNER:]
    if start is not None:
        packed, give, keep, refs = refs[0], refs[1], refs[2], refs[3:]
    dq, dk, dv, sums, row_keep, row_give, refs = *refs[:6], refs[6:]
    qs, ks, vs, ups, dqs, dks, dvs, branch, row, marks = refs
    copies = pull(pieces, 0, branch, marks)
    span, keys = q.shape[0], k.shape[0]
    chunks = keys // span
    scale = size**-0.5
    to_order(table, q, qs, rows, jnp.asarray(scale, LOW))
    to_order(table, k, ks, rows)
    to_order(table, v, vs, rows)
    finish(copies)
    upstream = dot_t(branch[...], weight[...]).astype(LOW)
    for place in range(INNER):
        at = pl.multiple_of((table[0] ^ offset_of(place)) * rows, rows)
        ups[pl.ds(at, rows), :] = upstream[place * rows : (place + 1) * rows, :]
    row[...] = dot_c(own[...], branch[...]).astype(LOW)
    share = row_keep.shape[1]
    for core, out in ((table[8], row_keep), (table[9], row_give)):
        for n in range(2):
            first = pl.multiple_of((2 * n + core) * share, share)
            out[n] = row[pl.ds(first, share), :]
    dks[...] = jnp.zeros_like(dks)
    dvs[...] = jnp.zeros_like(dvs)
    for step in range(span // STEP):
        lo = step * STEP
        queries = qs[lo : lo + STEP, :]
        upstream = ups[lo : lo + STEP, :]
        q_at = table[1] + lo + iota((1, STEP), 1)
        q_seg = seg_of(q_at, table, 2)
        count = lo + STEP if causal and chunks == 1 else span
        total_dq = jnp.zeros((STEP, 2 * size), WIDE)
        for head in range(2):
            head_q = half_lanes(queries, head, size)
            head_up = half_lanes(upstream, head, size)
            logs = log_total[head : head + 1, lo : lo + STEP]

            def pieces(start, logs=logs, head_up=head_up, head=head):
                k_at = start + iota((count, 1), 0)
                allowed = q_seg == seg_of(k_at, table, 5)
                if causal:
                    allowed = allowed & (k_at <= q_at)
                head_k = half_lanes(ks[pl.ds(start, count), :], head, size)
                raw = dot_t(head_k, queries)
                probs = jnp.exp(jnp.where(allowed, raw - logs, -1e30))
                slope = dot_t(vs[pl.ds(start, count), :], head_up)
                return head_k, probs, probs * slope

            def spread(start, delta, made, head_q=head_q, head_up=head_up):
                head_k, probs, lean = made
                push = (lean - probs * delta).astype(LOW)
                dvs[pl.ds(start, count), :] += dot_n(probs.astype(LOW), head_up)
                dks[pl.ds(start, count), :] += dot_n(push, head_q)
                return dot_c(push, head_k)

            if chunks == 1:
                made = pieces(0)
                delta = jnp.sum(made[2], axis=0, keepdims=True)
                total_dq = total_dq + spread(0, delta, made)
            else:

                def measure(chunk, delta):
                    made = pieces(pl.multiple_of(chunk * span, span))
                    return delta + jnp.sum(made[2], axis=0, keepdims=True)

                delta = lax.fori_loop(0, chunks, measure, jnp.zeros((1, STEP), WIDE))

                def absorb(chunk, running, delta=delta):
                    start = pl.multiple_of(chunk * span, span)
                    return running + spread(start, delta, pieces(start))

                total_dq = lax.fori_loop(0, chunks, absorb, total_dq)
        dqs[lo : lo + STEP, :] = total_dq * scale
    from_order(table, dqs, dq, rows)
    if start is not None:
        half = span // 2
        back = packed[:, start * LANES : (start + 1) * LANES]
        give[...] = dot_t(dq[half:, :], back).astype(LOW)
        keep[...] = dot_t(dq[:half, :], back)
    from_order(table, dks, dk, rows)
    from_order(table, dvs, dv, rows)
    sums[0:1, :] = jnp.sum(dqs[...].astype(LOW).astype(WIDE), axis=0, keepdims=True)
    sums[1:2, :] = jnp.sum(dvs[...].astype(LOW).astype(WIDE), axis=0, keepdims=True)


HBM = pl.BlockSpec(memory_space=pl.ANY)


def room(megabytes):
    return pltpu.CompilerParams(vmem_limit_bytes=megabytes * 2**20)


def pull(pieces, index, target, marks):
    rows = target.shape[0] // INNER
    copies = []
    for place in range(INNER):
        source = pieces[place].at[pl.ds(index * rows, rows), :]
        aim = target.at[pl.ds(place * rows, rows), :]
        copies.append(pltpu.make_async_copy(source, aim, marks.at[place]))
    for copy in copies:
        copy.start()
    return copies


def settle(planes, table, first, target, marks):
    rows = planes[0].shape[0]
    copies = []
    for n, plane in enumerate(planes):
        at = pl.multiple_of(table[first + n], 16)
        copies.append(pltpu.make_async_copy(plane, target.at[pl.ds(at, rows), :], marks.at[n]))
    for copy in copies:
        copy.start()
    return copies


def finish(copies):
    for copy in copies:
        copy.wait()


def cost(micros):
    return pl.CostEstimate(
        flops=int(micros * 1.1e9), bytes_accessed=int(micros * 3.5e6), transcendentals=0
    )


SMEM = pl.BlockSpec(memory_space=pltpu.SMEM)
VMEM = pl.BlockSpec(memory_space=pltpu.VMEM)


def attend(table, q, k, v, rows, causal):
    span, pair = q.shape
    keys = k.shape[0]
    return pl.pallas_call(
        functools.partial(attend_kernel, causal, rows, pair // 2),
        out_shape=(
            jax.ShapeDtypeStruct((span, pair), LOW),
            jax.ShapeDtypeStruct((2, span), WIDE),
        ),
        in_specs=[SMEM, VMEM, VMEM, VMEM],
        out_specs=(VMEM, VMEM),
        scratch_shapes=[
            pltpu.VMEM((span, pair), LOW),
            pltpu.VMEM((keys, pair), LOW),
            pltpu.VMEM((keys, pair), LOW),
            pltpu.VMEM((span, pair), WIDE),
        ],
        compiler_params=room(60),
        cost_estimate=cost(6),
    )(table, q, k, v)


def attend_back(table, q, k, v, log_total, weight, own, pieces, rows, causal, back=None):
    span, pair = q.shape
    keys = k.shape[0]
    width = weight.shape[1]
    part = jax.ShapeDtypeStruct((2, pair // 4, width), LOW)
    spread_shape = (
        jax.ShapeDtypeStruct((span // 2, width), LOW),
        jax.ShapeDtypeStruct((span // 2, width), WIDE),
    )
    start, packed = back if back else (None, None)
    extra = [packed] if back else []
    return pl.pallas_call(
        functools.partial(attend_back_kernel, causal, rows, pair // 2, start),
        out_shape=(spread_shape if back else ())
        + (
            jax.ShapeDtypeStruct((span, pair), LOW),
            jax.ShapeDtypeStruct((keys, pair), LOW),
            jax.ShapeDtypeStruct((keys, pair), LOW),
            jax.ShapeDtypeStruct((2, pair), WIDE),
            part,
            part,
        ),
        in_specs=[SMEM] + [VMEM] * 6 + [HBM] * INNER + [VMEM] * len(extra),
        out_specs=(VMEM,) * (8 if back else 6),
        scratch_shapes=[
            pltpu.VMEM((span, pair), LOW),
            pltpu.VMEM((keys, pair), LOW),
            pltpu.VMEM((keys, pair), LOW),
            pltpu.VMEM((span, pair), LOW),
            pltpu.VMEM((span, pair), WIDE),
            pltpu.VMEM((keys, pair), WIDE),
            pltpu.VMEM((keys, pair), WIDE),
            pltpu.VMEM((span, width), LOW),
            pltpu.VMEM((pair, width), LOW),
            pltpu.SemaphoreType.DMA((INNER,)),
        ],
        compiler_params=room(60),
        cost_estimate=cost(10),
    )(table, q, k, v, log_total, weight, own, *pieces, *extra)


def centre(value):
    center = jnp.mean(value, axis=-1, keepdims=True)
    centred = value - center
    spread = jnp.mean(centred * centred, axis=-1, keepdims=True)
    return centred, lax.rsqrt(spread + 1e-05)


def norm_of(value, gain, shift):
    centred, inverse = centre(value)
    return (centred * inverse * gain + shift).astype(LOW)


def enter_kernel(kinds, table, *refs):
    pieces, refs = refs[:INNER], refs[INNER:]
    planes, refs = refs[:-9], refs[-9:]
    q, k, v, h, params, biases, packed, x_all, marks = refs
    copies = pull(pieces, 0, x_all, marks.at[0])
    finish(settle(planes, table, 2, packed, marks.at[1]))
    edge = kinds * LANES
    extra = packed[:, edge : edge + LANES].astype(WIDE)
    params[...] = jnp.transpose(extra)[:16, :]
    size = LANES // 2
    mine = [packed[pl.ds(pl.multiple_of(table[n], 16), size), edge : edge + LANES] for n in (0, 1)]
    biases[...] = jnp.transpose(jnp.concatenate(mine, axis=0).astype(WIDE))[:16, :]
    finish(copies)
    half = x_all.shape[0] // 2
    for part in range(2):
        at = slice(part * half, (part + 1) * half)
        low = norm_of(x_all[at, :].astype(WIDE), params[0:1, :], params[1:2, :])
        h[at, :] = low
        made = dot_n(low, packed[:, :edge])
        q[at, :] = (made[:, :LANES] + biases[6:7, :]).astype(LOW)
        k[at, :] = made[:, LANES : 2 * LANES].astype(LOW)
        v[at, :] = (made[:, 2 * LANES :] + biases[7:8, :]).astype(LOW)


def enter(table, rows, pieces, planes):
    width = pieces[0].shape[1]
    lanes = planes[0].shape[1]
    span = rows * INNER
    heads = jax.ShapeDtypeStruct((span, LANES), LOW)
    return pl.pallas_call(
        functools.partial(enter_kernel, 3),
        out_shape=(
            heads,
            heads,
            heads,
            jax.ShapeDtypeStruct((span, width), LOW),
            jax.ShapeDtypeStruct((16, width), WIDE),
            jax.ShapeDtypeStruct((16, LANES), WIDE),
            jax.ShapeDtypeStruct((width, lanes), LOW),
            jax.ShapeDtypeStruct((span, width), LOW),
        ),
        in_specs=[SMEM] + [HBM] * (INNER + len(planes)),
        out_specs=(VMEM,) * 8,
        scratch_shapes=[
            pltpu.SemaphoreType.DMA((2, INNER)),
        ],
        compiler_params=room(32),
        cost_estimate=cost(3),
    )(table, *pieces, *planes)


def join_kernel(vector, first, query, *refs):
    pieces, weights, refs = refs[:INNER], refs[INNER : 2 * INNER], refs[2 * INNER :]
    if query is None:
        base, base_own, params, y_own, h, weight, left, heads, marks = refs
    else:
        base, params, packed, biases, y_own, h, y_all, cq, weight, left, heads, marks = refs
    span = left.shape[0]
    block = span // INNER
    loads = pull(weights, 0, weight, marks.at[1])
    copies = []
    for place in range(INNER):
        copies.append(pltpu.make_async_copy(pieces[place], heads.at[place], marks.at[0, place]))
    for copy in copies:
        copy.start()
    finish(copies + loads)
    parts = INNER // 2
    for part in range(parts):
        at = slice(part * 2 * block, (part + 1) * 2 * block)
        for n in range(2 * part, 2 * part + 2):
            for place in range(INNER):
                first_row = (n ^ place) * block
                left[n * block : (n + 1) * block, place * LANES : (place + 1) * LANES] = heads[
                    place, first_row : first_row + block, :
                ]
        value = base[at, :].astype(WIDE)
        if query is None and part == 0:
            value = jnp.concatenate([base_own[...], value[block:, :]], axis=0)
        y = value + dot_n(left[at, :], weight[...]) + params[vector : vector + 1, :]
        if part == 0:
            y_own[...] = y[:block, :]
        low = norm_of(y, params[first : first + 1, :], params[first + 1 : first + 2, :])
        h[at, :] = low
        if query is not None:
            y_all[at, :] = y.astype(LOW)
            made = dot_n(low, packed[:, query * LANES : (query + 1) * LANES])
            cq[at, :] = (made + biases[9:10, :]).astype(LOW)


def join_self(pieces, weights, base, params, packed, biases):
    span, width = base.shape
    return pl.pallas_call(
        functools.partial(join_kernel, 8, 2, 2),
        out_shape=(
            jax.ShapeDtypeStruct((span // INNER, width), WIDE),
            jax.ShapeDtypeStruct((span, width), LOW),
            jax.ShapeDtypeStruct((span, width), LOW),
            jax.ShapeDtypeStruct((span, LANES), LOW),
        ),
        in_specs=[HBM] * (2 * INNER) + [VMEM] * 4,
        out_specs=(VMEM,) * 4,
        scratch_shapes=[
            pltpu.VMEM((width, width), LOW),
            pltpu.VMEM((span, width), LOW),
            pltpu.VMEM((INNER, span, LANES), LOW),
            pltpu.SemaphoreType.DMA((2, INNER)),
        ],
        compiler_params=room(60),
        cost_estimate=cost(6),
    )(*pieces, *weights, base, params, packed, biases)


def join_cross(pieces, weights, base, base_own, params):
    span, width = base.shape
    return pl.pallas_call(
        functools.partial(join_kernel, 11, 4, None),
        out_shape=(
            jax.ShapeDtypeStruct((span // INNER, width), WIDE),
            jax.ShapeDtypeStruct((span, width), LOW),
        ),
        in_specs=[HBM] * (2 * INNER) + [VMEM] * 3,
        out_specs=(VMEM,) * 2,
        scratch_shapes=[
            pltpu.VMEM((width, width), LOW),
            pltpu.VMEM((span, width), LOW),
            pltpu.VMEM((INNER, span, LANES), LOW),
            pltpu.SemaphoreType.DMA((2, INNER)),
        ],
        compiler_params=room(60),
        cost_estimate=cost(5),
    )(*pieces, *weights, base, base_own, params)


def load_rows(packed, start, target, marks):
    shares = packed.shape[0]
    rows = target.shape[0] // shares
    copies = []
    for n in range(shares):
        source = packed.at[n, pl.ds(start, rows), :]
        aim = target.at[pl.ds(n * rows, rows), :]
        copies.append(pltpu.make_async_copy(source, aim, marks.at[n]))
    for copy in copies:
        copy.start()
    return copies


def feed_kernel(h, bias, packed, *refs):
    pieces = refs[:INNER]
    act, slope, give, keep, bias_grad, up, first, second, marks, weight_marks = refs[INNER:]
    span, width = up.shape
    hidden = second.shape[0]
    loads = load_rows(packed, 0, first, weight_marks.at[0])
    copies = load_rows(packed, width // packed.shape[0], second, weight_marks.at[1])
    copies += pull(pieces, 0, up, marks)
    finish(loads)
    step = 256
    inner = (2.0 / 3.141592653589793) ** 0.5
    for n in range(hidden // step):
        at = slice(n * step, (n + 1) * step)
        pre = dot_n(h[...], first[:, at]) + bias[:, at]
        square = pre * pre
        bend = jnp.tanh(pre * (inner + (inner * 0.044715) * square))
        half = 0.5 * bend + 0.5
        act[:, at] = (pre * half).astype(LOW)
        if n == 0:
            finish(copies)
        rise = half + 0.5 * pre * (1.0 - bend * bend) * (inner + (3 * inner * 0.044715) * square)
        low = (dot_t(up[...], second[at, :]) * rise).astype(LOW)
        slope[:, at] = low
        bias_grad[:, at] = jnp.sum(low.astype(WIDE), axis=0, keepdims=True)
    give[...] = dot_t(slope[span // 2 :, :], first[...]).astype(LOW)
    keep[...] = dot_t(slope[: span // 2, :], first[...])


def feed(h, bias, packed, pieces):
    span, width = h.shape
    hidden = bias.shape[1]
    shares = packed.shape[0]
    return pl.pallas_call(
        feed_kernel,
        out_shape=(
            jax.ShapeDtypeStruct((span, hidden), LOW),
            jax.ShapeDtypeStruct((span, hidden), LOW),
            jax.ShapeDtypeStruct((span // 2, width), LOW),
            jax.ShapeDtypeStruct((span // 2, width), WIDE),
            jax.ShapeDtypeStruct((1, hidden), WIDE),
            jax.ShapeDtypeStruct((span, width), LOW),
        ),
        in_specs=[VMEM] * 2 + [HBM] * (1 + INNER),
        out_specs=(VMEM,) * 6,
        scratch_shapes=[
            pltpu.VMEM((width, hidden), LOW),
            pltpu.VMEM((hidden, width), LOW),
            pltpu.SemaphoreType.DMA((INNER,)),
            pltpu.SemaphoreType.DMA((2, shares)),
        ],
        compiler_params=room(44),
        cost_estimate=cost(13),
    )(h, bias, packed, *pieces)


def feed_out_kernel(act, packed, give, keep, second, marks):
    finish(load_rows(packed, second.shape[1] // packed.shape[0], second, marks))
    half = keep.shape[0]
    give[...] = dot_n(act[half:, :], second[...]).astype(LOW)
    keep[...] = dot_n(act[:half, :], second[...])


def feed_out(act, packed):
    span, hidden = act.shape
    shares, _, width = packed.shape
    return pl.pallas_call(
        feed_out_kernel,
        out_shape=(
            jax.ShapeDtypeStruct((span // 2, width), LOW),
            jax.ShapeDtypeStruct((span // 2, width), WIDE),
        ),
        in_specs=[VMEM, HBM],
        out_specs=(VMEM,) * 2,
        scratch_shapes=[
            pltpu.VMEM((hidden, width), LOW),
            pltpu.SemaphoreType.DMA((shares,)),
        ],
        compiler_params=room(24),
        cost_estimate=cost(3),
    )(act, packed)


def feed_grad_kernel(act, slope, h, up, out):
    width = up.shape[1]
    step = 256
    for n in range(width // step):
        at = slice(n * step, (n + 1) * step)
        out[at, width:] = dot_c(h[:, at], slope[...]).astype(LOW)
    for n in range(act.shape[1] // step):
        at = slice(n * step, (n + 1) * step)
        out[at, :width] = dot_c(act[:, at], up[...]).astype(LOW)


def feed_grad(act, slope, h, up):
    width = h.shape[1]
    hidden = act.shape[1]
    return pl.pallas_call(
        feed_grad_kernel,
        out_shape=jax.ShapeDtypeStruct((width, width + hidden), LOW),
        in_specs=[VMEM] * 4,
        out_specs=VMEM,
        compiler_params=room(40),
        cost_estimate=cost(6),
    )(act, slope, h, up)


def fold_kernel(keep, took, own, one, two, three):
    rows = own.shape[0]
    own[...] = keep[:rows, :] + took[:rows, :].astype(WIDE)
    for n, part in enumerate((one, two, three), 1):
        at = slice(n * rows, (n + 1) * rows)
        part[...] = (keep[at, :] + took[at, :].astype(WIDE)).astype(LOW)


def fold(keep, took):
    half, width = keep.shape
    part = jax.ShapeDtypeStruct((half // 4, width), LOW)
    return pl.pallas_call(
        fold_kernel,
        out_shape=(jax.ShapeDtypeStruct((half // 4, width), WIDE), part, part, part),
        in_specs=[VMEM] * 2,
        out_specs=(VMEM,) * 4,
        compiler_params=room(16),
        cost_estimate=cost(1),
    )(keep, took)


def norm_back_kernel(first, own, one, two, three, value, base, params, grad, low, sums):
    slope = own[...] + one[...].astype(WIDE) + two[...].astype(WIDE) + three[...].astype(WIDE)
    centred, inverse = centre(value[...].astype(WIDE))
    unit = centred * inverse
    lean = slope * params[first : first + 1, :]
    flat = jnp.mean(lean, axis=-1, keepdims=True)
    tilt = jnp.mean(lean * unit, axis=-1, keepdims=True)
    total = base[...].astype(WIDE) + inverse * (lean - flat - unit * tilt)
    grad[...] = total
    cut = total.astype(LOW)
    low[...] = cut
    sums[0:1, :] = jnp.sum(slope * unit, axis=0, keepdims=True)
    sums[1:2, :] = jnp.sum(slope, axis=0, keepdims=True)
    sums[2:3, :] = jnp.sum(cut.astype(WIDE), axis=0, keepdims=True)
    sums[3:4, :] = jnp.sum(base[...].astype(WIDE), axis=0, keepdims=True)


def norm_back(first, own, parts, value, base, params):
    rows, width = own.shape
    return pl.pallas_call(
        functools.partial(norm_back_kernel, first),
        out_shape=(
            jax.ShapeDtypeStruct((rows, width), WIDE),
            jax.ShapeDtypeStruct((rows, width), LOW),
            jax.ShapeDtypeStruct((4, width), WIDE),
        ),
        in_specs=[VMEM] * 7,
        out_specs=(VMEM,) * 3,
        compiler_params=room(16),
        cost_estimate=cost(2),
    )(own, *parts, value, base, params)


def spread_kernel(start, *refs):
    values, packed, give, keep = refs[:-3], refs[-3], refs[-2], refs[-1]
    half = keep.shape[0]
    weight = packed[:, start * LANES : (start + len(values)) * LANES]
    for at, out in ((half, give), (0, keep)):
        left = [value[at : at + half, :] for value in values]
        left = left[0] if len(left) == 1 else jnp.concatenate(left, axis=1)
        out[...] = dot_t(left, weight).astype(out.dtype)


def spread(start, values, packed):
    span, width = values[0].shape[0], packed.shape[0]
    return pl.pallas_call(
        functools.partial(spread_kernel, start),
        out_shape=(
            jax.ShapeDtypeStruct((span // 2, width), LOW),
            jax.ShapeDtypeStruct((span // 2, width), WIDE),
        ),
        in_specs=[VMEM] * (len(values) + 1),
        out_specs=(VMEM,) * 2,
        compiler_params=room(24),
        cost_estimate=cost(2),
    )(*values, packed)


def pair_kernel(table, biases, *refs):
    pieces, refs = refs[:INNER], refs[INNER:]
    planes, (states, k, v, packed, marks) = refs[:-5], refs[-5:]
    copies = pull(pieces, 0, states, marks.at[0])
    finish(settle(planes, table, 2, packed, marks.at[1]))
    finish(copies)
    made = dot_n(states[...], packed[:, : 2 * LANES])
    k[...] = made[:, :LANES].astype(LOW)
    v[...] = (made[:, LANES:] + biases[10:11, :]).astype(LOW)


def pair_heads(table, rows, pieces, planes, biases):
    width = pieces[0].shape[1]
    span = rows * INNER
    heads = jax.ShapeDtypeStruct((span, LANES), LOW)
    return pl.pallas_call(
        pair_kernel,
        out_shape=(
            jax.ShapeDtypeStruct((span, width), LOW),
            heads,
            heads,
            jax.ShapeDtypeStruct((width, planes[0].shape[1]), LOW),
        ),
        in_specs=[SMEM, VMEM] + [HBM] * (INNER + len(planes)),
        out_specs=(VMEM,) * 4,
        scratch_shapes=[pltpu.SemaphoreType.DMA((2, INNER))],
        compiler_params=room(24),
        cost_estimate=cost(3),
    )(table, biases, *pieces, *planes)


def spread_self_kernel(dq, dk, dv, packed, x_all, give, keep, sums):
    half = x_all.shape[0] // 2
    weight = packed[:, : 3 * LANES]
    first = second = None
    for part, out in ((1, give), (0, keep)):
        at = slice(part * half, (part + 1) * half)
        left = jnp.concatenate([dq[at, :], dk[at, :], dv[at, :]], axis=1)
        slope = dot_t(left, weight)
        out[...] = slope.astype(out.dtype)
        centred, inverse = centre(x_all[at, :].astype(WIDE))
        gain = jnp.sum(slope * (centred * inverse), axis=0, keepdims=True)
        shift = jnp.sum(slope, axis=0, keepdims=True)
        first = gain if first is None else first + gain
        second = shift if second is None else second + shift
    sums[0:1, :] = first
    sums[1:2, :] = second


def spread_self(dq, dk, dv, packed, x_all):
    span, width = x_all.shape
    return pl.pallas_call(
        spread_self_kernel,
        out_shape=(
            jax.ShapeDtypeStruct((span // 2, width), LOW),
            jax.ShapeDtypeStruct((span // 2, width), WIDE),
            jax.ShapeDtypeStruct((2, width), WIDE),
        ),
        in_specs=[VMEM] * 5,
        out_specs=(VMEM,) * 3,
        compiler_params=room(32),
        cost_estimate=cost(4),
    )(dq, dk, dv, packed, x_all)


def home_kernel(got, out):
    kinds = got.shape[2] // LANES
    groups = got.shape[0] // INNER
    size = LANES // 2
    total = []
    for place in range(INNER):
        running = got[place].astype(WIDE)
        for n in range(1, groups):
            running = running + got[n * INNER + place].astype(WIDE)
        total.append(running)
    for kind in range(kinds):
        heads = {}
        for place in range(INNER):
            for n in (0, 1):
                at = kind * LANES + n * size
                number = (2 * (place & 1) + n) * (INNER // 2) + (place >> 1)
                heads[number] = total[place][:, at : at + size]
        for number in range(0, 2 * INNER, 2):
            at = kind * INNER * LANES + number * size
            both = jnp.concatenate([heads[number], heads[number + 1]], axis=1)
            out[:, at : at + LANES] = both


def home_columns(got):
    rows, lanes = got.shape[1:]
    return pl.pallas_call(
        home_kernel,
        out_shape=jax.ShapeDtypeStruct((rows, lanes * INNER), WIDE),
        in_specs=[VMEM],
        out_specs=VMEM,
        compiler_params=room(16),
        cost_estimate=cost(2),
    )(got)


def column_part_kernel(kinds, *refs):
    count = len(kinds)
    lefts, rights, column = refs[:count], refs[count:-1], refs[-1]
    at = first = 0
    for left, kind in zip(lefts, kinds):
        right = [value[...] for value in rights[first : first + kind]]
        right = right[0] if kind == 1 else jnp.concatenate(right, axis=1)
        lanes = kind * LANES
        column[:, at : at + lanes] = dot_c(left[...], right).astype(LOW)
        at, first = at + lanes, first + kind


def column_part(*pairs):
    width = pairs[0][0].shape[1]
    kinds = tuple(len(rights) for _, rights in pairs)
    lefts = [left for left, _ in pairs]
    rights = [value for _, values in pairs for value in values]
    return pl.pallas_call(
        functools.partial(column_part_kernel, kinds),
        out_shape=jax.ShapeDtypeStruct((width, LANES * sum(kinds)), LOW),
        in_specs=[VMEM] * (len(lefts) + len(rights)),
        out_specs=VMEM,
        compiler_params=room(24),
        cost_estimate=cost(3),
    )(*lefts, *rights)


def pick_kernel(table, packed, own, give):
    share = own.shape[1]
    for first, out in ((table[0], own), (table[1], give)):
        for n in range(2):
            for place in range(INNER):
                at = pl.multiple_of(((first + n) * INNER + place) * share, share)
                out[n, :, place * LANES : (place + 1) * LANES] = packed[pl.ds(at, share), :]


def pick(table, packed):
    width = packed.shape[0]
    part = jax.ShapeDtypeStruct((2, width // (4 * INNER), width), LOW)
    return pl.pallas_call(
        pick_kernel,
        out_shape=(part, part),
        in_specs=[SMEM, VMEM],
        out_specs=(VMEM,) * 2,
        compiler_params=room(16),
        cost_estimate=cost(1),
    )(table, packed)


def merge_kernel(table, own, took, out):
    share = own.shape[1]
    for n in range(2):
        for core, value in ((table[2], own), (table[3], took)):
            first = pl.multiple_of((2 * n + core) * share, share)
            out[pl.ds(first, share), :] = value[n]


def merge(table, own, took):
    _, rows, width = own.shape
    return pl.pallas_call(
        merge_kernel,
        out_shape=jax.ShapeDtypeStruct((4 * rows, width), LOW),
        in_specs=[SMEM, VMEM, VMEM],
        out_specs=VMEM,
        compiler_params=room(16),
        cost_estimate=cost(1),
    )(table, own, took)


def stack_kernel(table, *refs):
    pairs, out = refs[:-1], refs[-1]
    rows = pairs[0].shape[1]
    for n in range(len(pairs) // 2):
        at = slice(n * rows, (n + 1) * rows)
        for first, value in ((table[0], pairs[2 * n]), (table[1], pairs[2 * n + 1])):
            out[pl.ds(first, 2), at, :] = value[...]


def stack(table, *pairs):
    _, rows, width = pairs[0].shape
    return pl.pallas_call(
        stack_kernel,
        out_shape=jax.ShapeDtypeStruct((4, rows * len(pairs) // 2, width), LOW),
        in_specs=[SMEM] + [VMEM] * len(pairs),
        out_specs=VMEM,
        compiler_params=room(16),
        cost_estimate=cost(1),
    )(table, *pairs)


def hop(value, distance):
    route = [(n, n ^ distance) for n in range(INNER)]
    return lax.ppermute(value, "inner", route)


def after(value, *others):
    return lax.optimization_barrier((value,) + others)[0]


def gather_places(own):
    near = [own] + [hop(own, offset_of(place)) for place in (1, 2, 3)]
    return near + [hop(piece, 1) for piece in near]


def scatter_start(give, keep):
    return fold(keep, hop(give, 1))


def scatter_finish(parts):
    return [hop(part, offset_of(place)) for place, part in enumerate(parts, 1)]


def scatter_places(give, keep):
    own, *parts = scatter_start(give, keep)
    return own, scatter_finish(parts)


def dot(a, b):
    return jnp.dot(a, b, preferred_element_type=WIDE)


def under(a, b):
    return lax.dot_general(a, b, (((0,), (0,)), ((), ())), preferred_element_type=WIDE)


def per_device(
    target,
    source,
    cotangent,
    target_lengths,
    source_lengths,
    self_in,
    self_out,
    cross_query,
    cross_kv,
    cross_out,
    mlp_in,
    mlp_out,
    vectors,
    hidden_bias,
):
    rows, width = target.shape[1:]
    here = lax.axis_index("inner")
    core, chip = here & 1, here >> 1
    stream = lax.axis_index("ulys")
    group = lax.axis_index("outer")
    groups = lax.axis_size("outer")
    shares = lax.axis_size("ulys") * groups
    devices = shares * INNER
    span = rows * INNER
    pair = width // INNER
    size = pair // 2
    share = width // devices
    hidden = hidden_bias.shape[0]
    count = vectors.shape[0]
    chips = INNER // 2
    matched = shares * chips == HEADS and 2 * share == size
    target_ends = jnp.cumsum(target_lengths[stream])
    source_ends = jnp.cumsum(source_lengths[stream])
    start = jnp.stack([here, group * span]).astype(jnp.int32)
    cores = jnp.stack([core, 1 - core])
    self_table = jnp.concatenate([start, target_ends, target_ends, cores]).astype(jnp.int32)
    cross_table = jnp.concatenate([start, target_ends, source_ends, cores]).astype(jnp.int32)
    if matched:
        head_at = [(2 * core + n) * (width // shares) + chip * size for n in (0, 1)]
    else:
        head_at = [here * pair + n * size for n in (0, 1)]
    plane_at = [jnp.zeros((), jnp.int32)]
    head_table = jnp.stack(head_at + plane_at).astype(jnp.int32)

    def by_device(value):
        lead = value.shape[:-1]
        if matched:
            split = value.reshape(lead + (2, 2, chips, size))
            value = jnp.moveaxis(split, -2, -4)
        return value.reshape(lead + (INNER, pair))

    def by_column(value):
        lead = value.shape[:-2]
        if matched:
            split = value.reshape(lead + (chips, 2, 2, size))
            value = jnp.moveaxis(split, -4, -2)
        return value.reshape(lead + (width,))

    def cut_columns(*weights):
        whole = jnp.concatenate([w.reshape(share, -1, width) for w in weights], axis=1)
        cut = jnp.transpose(by_device(whole), (2, 0, 1, 3))
        return cut.reshape(INNER, share, -1)

    def exchange(value):
        return lax.all_to_all(value, "inner", 0, 0)

    order = here ^ jnp.array([offset_of(n) for n in range(INNER)], jnp.int32)

    core_table = jnp.stack([2 * core, 2 - 2 * core, core, 1 - core]).astype(jnp.int32)

    def head_rows(weight, packed):
        if not matched:
            whole = lax.all_gather(weight, ALL, axis=0, tiled=True)
            mine = lax.dynamic_slice_in_dim(whole, here * pair, pair, axis=0)
            placed = jnp.take(whole.reshape(INNER, pair, width), order, axis=0)
            return mine, [placed[n] for n in range(INNER)]
        own, give = pick(core_table, packed)
        mine = merge(core_table, own, hop(give, 1))
        return mine, gather_places(mine)

    def shard_features(pieces):
        whole = jnp.stack(
            [
                piece.reshape(INNER, rows, pair)[jnp.array([n ^ place for n in range(INNER)])]
                for place, piece in enumerate(pieces)
            ]
        ).reshape(INNER, span, pair)
        whole = jnp.transpose(whole, (1, 0, 2)).reshape(span, width)
        cut = []
        for n in range(shares):
            first = (n * INNER + here) * share
            mixed = (first // pair) ^ here
            place = ((mixed >> 1) & 3) | ((mixed & 1) << 2)
            cut.append(
                lax.dynamic_slice_in_dim(whole, place * pair + first % pair, share, axis=1)
            )
        return jnp.concatenate(cut, axis=1)

    def row_grads(keep, give, pieces, branch):
        if not matched:
            grad = under(shard_features(pieces), jnp.concatenate(branch, axis=0))
            return [grad.astype(LOW).reshape(shares, share, width)]
        return [keep, hop(give, 1)]

    def rows_stack(*parts):
        if not matched:
            return jnp.concatenate([part[0] for part in parts], axis=1)
        return stack(core_table, *parts[0], *parts[1])

    def rows_home(row):
        row = row.reshape(shares * row.shape[1], width)
        return lax.psum_scatter(row, OUTER, scatter_dimension=0, tiled=True).astype(WIDE)

    def column_send(grad):
        return lax.all_to_all(grad.reshape(devices, share, -1), ALL, 0, 0)

    def column_home(got):
        if matched:
            return home_columns(got)
        total = jnp.sum(got.astype(WIDE).reshape(shares, INNER, share, -1, pair), axis=0)
        return jnp.transpose(total, (1, 2, 0, 3)).reshape(share, -1)

    small = jnp.concatenate([jnp.transpose(vectors), hidden_bias.reshape(share, -1)], axis=1)
    extras = small.shape[1]
    small = jnp.pad(small, ((0, 0), (0, LANES - extras)))
    small = jnp.broadcast_to(small[None], (INNER, share, LANES))
    first_cut = jnp.transpose(mlp_in.reshape(share, shares, INNER, hidden), (2, 0, 1, 3))
    first_cut = first_cut.reshape(INNER, share, shares * hidden)
    def over(value):
        return lax.all_gather(value, OUTER, axis=0)

    def planes_of(value):
        return [over(value).reshape(width, -1)]

    def row_lanes(weight):
        return jnp.transpose(weight.reshape(-1, INNER, LANES), (1, 0, 2))

    self_cut = jnp.concatenate([cut_columns(self_in), small], axis=2)
    self_mine = exchange(self_cut)
    self_planes = planes_of(jnp.concatenate([self_mine, row_lanes(self_out)], axis=2))
    pieces = gather_places(after(target[0], self_mine))
    cut = [cut_columns(cross_kv, cross_query), first_cut]
    states = gather_places(after(source[0], *pieces[1:4]))
    cut = exchange(after(jnp.concatenate(cut, axis=2), *states[1:4]))
    cross_mine = jnp.concatenate([cut[:, :, : 3 * pair], row_lanes(cross_out)], axis=2)
    cross_planes = planes_of(after(cross_mine, self_planes))
    first_mine = cut[:, :, 3 * pair :].reshape(INNER * share, -1)
    feed_mine = jnp.concatenate([first_mine, mlp_out], axis=0)
    feed_packed = over(after(feed_mine, self_planes))

    q, k, v, h1, params, biases, self_packed, x_all = enter(
        head_table, rows, pieces, self_planes
    )
    sout_mine, w_sout = head_rows(self_out, after(self_packed, q)[:, 4 * pair :])
    q = after(q, *w_sout[1:4])
    h_bias = self_packed.reshape(shares, INNER, share, -1)
    h_bias = h_bias[..., 3 * pair + count : 3 * pair + extras]
    h_bias = lax.dynamic_index_in_dim(h_bias, here, 1, False).reshape(1, -1).astype(WIDE)

    def stream_keys(own):
        return lax.all_gather(own, "outer", axis=0, tiled=True) if groups > 1 else own

    def own_keys(partial):
        if groups == 1:
            return partial
        return lax.psum_scatter(partial, "outer", scatter_dimension=0, tiled=True)

    k, v = stream_keys(k), stream_keys(v)
    att, self_total = attend(self_table, q, k, v, rows, True)
    att = gather_places(att)
    states, ck, cv, cross_packed = pair_heads(head_table, rows, states, cross_planes, biases)
    ck, cv = stream_keys(ck), stream_keys(cv)
    y1, h2, y1_all, cq = join_self(att, w_sout, x_all, params, cross_packed, biases)
    cout_mine, w_cout = head_rows(cross_out, after(cross_packed, *att[1:4])[:, 3 * pair :])
    catt, cross_total = attend(cross_table, cq, ck, cv, rows, False)
    catt = gather_places(catt)
    pull_up = gather_places(after(cotangent[0], *w_cout[1:4]))
    y2, h3 = join_cross(catt, w_cout, y1_all, y1, params)
    active, before_grad, give, keep, h_bias_grad, up = feed(h3, h_bias, feed_packed, pull_up)
    third_own, third_parts = scatter_places(give, keep)
    mlp_grad = feed_grad(active, before_grad, after(h3, third_own), up)
    third_parts, mlp_grad = lax.optimization_barrier((third_parts, mlp_grad))
    mlp_home = lax.psum_scatter(mlp_grad, OUTER, scatter_dimension=0, tiled=True)
    late_grad, cross_branch, late_sums = norm_back(
        4, third_own, third_parts, y2, cotangent[0], params
    )
    cross_all = gather_places(cross_branch)
    fed_own, *fed_parts = scatter_start(*feed_out(after(active, cross_all[1]), feed_packed))
    cross_all, fed_own, fed_parts = lax.optimization_barrier((cross_all, fed_own, fed_parts))
    give, keep, dcq, dck, dcv, cross_sums, row_keep, row_give = attend_back(
        cross_table,
        cq,
        ck,
        cv,
        cross_total,
        cout_mine,
        catt[0],
        cross_all,
        rows,
        False,
        (2, cross_packed),
    )
    cross_rows = (row_keep, row_give)
    fed_parts = scatter_finish(fed_parts)
    give, fed_parts = lax.optimization_barrier((give, fed_parts))
    fed = fed_own + sum(part.astype(WIDE) for part in fed_parts)
    layer_out = (y2 + fed + params[12]).astype(LOW)[None]
    dck, dcv = own_keys(dck), own_keys(dcv)
    second_own, second_parts = scatter_places(give, keep)
    cross_grad = column_part((after(states, second_own), (dck, dcv)), (h2, (dcq,)))
    source_give, source_keep = spread(0, [after(dck, second_own), dcv], cross_packed)
    second_parts, cross_grad, source_give, source_keep = lax.optimization_barrier(
        (second_parts, cross_grad, source_give, source_keep)
    )
    cross_got = column_send(cross_grad)
    cross_rows = row_grads(*cross_rows, catt, cross_all)
    middle_grad, self_branch, middle_sums = norm_back(
        2, second_own, second_parts, y1, late_grad, params
    )
    self_all = gather_places(self_branch)
    source_own, *source_parts = scatter_start(after(source_give, self_all[1]), source_keep)
    self_all, source_own, source_parts, cross_got = lax.optimization_barrier(
        (self_all, source_own, source_parts, cross_got)
    )
    dq, dk, dv, self_sums, row_keep, row_give = attend_back(
        self_table, q, k, v, self_total, sout_mine, att[0], self_all, rows, True
    )
    dk, dv = own_keys(dk), own_keys(dv)
    give, keep, target_sums = spread_self(dq, dk, dv, self_packed, x_all)
    first_own, first_parts = scatter_places(give, keep)
    self_grad = column_part((after(h1, first_own), (dq, dk, dv)))
    self_got = column_send(self_grad)
    target_grad, target_low, _ = norm_back(
        0, first_own, first_parts, target[0], middle_grad, params
    )
    source_parts, row_give, mlp_home, self_sums = lax.optimization_barrier(
        (source_parts, row_give, mlp_home, self_sums, first_parts)
    )[:4]
    self_rows = row_grads(row_keep, row_give, att, self_all)
    out_home = rows_home(rows_stack(self_rows, cross_rows))
    source_parts = scatter_finish(source_parts)
    source_grad = source_own + sum(part.astype(WIDE) for part in source_parts)
    second_home, first_home = mlp_home[:, :width], mlp_home[:, width:]
    first_home = exchange(first_home.reshape(INNER, share, shares * hidden))
    first_home = first_home.reshape(INNER, share, shares, hidden)
    first_home = jnp.transpose(first_home, (1, 2, 0, 3)).reshape(share, -1)
    cross_home = column_home(cross_got)
    self_home = column_home(self_got)

    head_sums = jnp.concatenate([self_sums, cross_sums])[:, None]
    head_sums = lax.dynamic_update_slice_in_dim(
        jnp.zeros((4, INNER, pair), WIDE), head_sums, here, 1
    )
    vector_grad = jnp.concatenate(
        [
            target_sums[:2],
            middle_sums[:2],
            late_sums[:2],
            by_column(head_sums)[:2],
            middle_sums[2:3],
            by_column(head_sums)[2:],
            late_sums[2:],
        ]
    )
    vector_part = jnp.transpose(vector_grad.reshape(count, devices, share), (1, 0, 2))
    bias_part = lax.dynamic_update_slice_in_dim(
        jnp.zeros((shares, INNER, hidden), WIDE), h_bias_grad.reshape(shares, 1, hidden), here, 1
    ).reshape(devices, hidden)
    tiny = jnp.concatenate([vector_part.reshape(devices, -1), bias_part], axis=1)
    tiny = jnp.sum(lax.all_to_all(tiny, ALL, 0, 0, tiled=True), axis=0)

    return (
        layer_out,
        target_low[None],
        source_grad.astype(LOW)[None],
        self_home,
        out_home[:share],
        cross_home[:, 2 * width :],
        cross_home[:, : 2 * width],
        out_home[share:],
        first_home.astype(WIDE),
        second_home.astype(WIDE),
        tiny[: count * share].reshape(count, share),
        tiny[count * share :],
    )


def solution(mesh):
    streams, blocks = mesh.devices.shape
    grid = mesh.devices.reshape(streams, blocks // INNER, INNER)
    inner_mesh = Mesh(grid, ALL)
    rows = P("ulys", ("outer", "inner"), None)
    matrix = P(ALL, None)
    row_vectors = P(None, ALL)
    in_specs = (rows,) * 3 + (P(), P()) + (matrix,) * 7 + (row_vectors, P(ALL))
    out_specs = (rows,) * 3 + (matrix,) * 7 + (row_vectors, P(ALL))
    return jax.shard_map(
        per_device, mesh=inner_mesh, in_specs=in_specs, out_specs=out_specs, check_vma=False
    )
```

time: 573 us -> 451 us (0.79)
  blocking collectives: 89.7 us -> 0 us
  Pallas kernels: 29.5 us -> 110 us
  matrix products: 73.1 us -> 0 us
  local copies, waits for them, and re-layouts: 109 us -> 69.7 us
  other arithmetic: 41.3 us -> 14.4 us
  waiting for transfers between devices: 131 us -> 153 us
  starting transfers between devices: 75.9 us -> 86.6 us
    dot_general x26 -> x0, matrix products: 73.1 us -> none  [the longest x11 28.8 us: across(): lax.dot_general(a, b, (((1,), (1,)), ((), ())), preferred_element_type=WIDE)]
    pallas_call x0 -> x26, Pallas kernels: none -> 73 us  [the longest x1 18.8 us: join_cross(): pl.pallas_call(functools.partial(join_kernel, 11, 4, None), out_shape=(ja...]
    all_gather x4 -> x0, blocking collectives: 62.6 us -> none  [the longest x3 52.9 us: slices_of(): return lax.all_gather(mine, OUTER, axis=0).reshape(width, -1)]
    ppermute x48 -> x87, waiting for transfers between devices: 63.1 us -> 121 us  [hop(): return lax.ppermute(value, 'inner', route)]
    reduce_scatter x7 -> x2, waiting for transfers between devices: 53.6 us -> 0.01 us  [the longest x1 0.01 us: per_device(): lax.psum_scatter(mlp_grad, OUTER, scatter_dimension=0, tiled=True)]
    all_to_all x7 -> x5, waiting for transfers between devices: 2.67 us -> 24.9 us  [the longest x3 24 us: exchange(): return lax.all_to_all(value, 'inner', 0, 0)]
    all_to_all x1 -> x0, blocking collectives: 15 us -> none  [slices_of(): mine = lax.all_to_all(column_slices(weight, parts), 'inner', 0, 0)]
    reduce_sum x21 -> x0, other arithmetic: 13.6 us -> none  [the longest x6 4.55 us: layer_norm(): spread = jnp.mean(centred * centred, axis=-1, keepdims=True)]
  transfers between devices with their start and end apart: 67 -> 98, of which waited for: 25 -> 31; matrix products, arithmetic and copies ran while one was open for 35% -> 6% of each run, Pallas kernels for 3% -> 21%
where the time goes in v2:
time: 451 us; the launch traced here: 449 us
  waiting for transfers between devices  153 us (34%)
  Pallas kernels  110 us (24%)
  starting transfers between devices  86.6 us (19%)
  local copies, waits for them, and re-layouts  69.7 us (15%)
  between operations  15.4 us (3%)
  other arithmetic  14.4 us (3%)
    ppermute x87, waiting for transfers between devices, hop(): return lax.ppermute(value, 'inner', route)  121 us
    ppermute x87, starting transfers between devices, hop(): return lax.ppermute(value, 'inner', route)  59.7 us
    unnamed x244, local copies, waits for them, and re-layouts  53.5 us
    pallas_call x2, Pallas kernels, attend_back(): pl.pallas_call(functools.partial(attend_back_kernel, causal, rows, pair /...  25.3 us
    all_to_all x3, waiting for transfers between devices, exchange(): return lax.all_to_all(value, 'inner', 0, 0)  24 us
    pallas_call x1, Pallas kernels, join_cross(): pl.pallas_call(functools.partial(join_kernel, 11, 4, None), out_shape=(ja...  18.8 us
    all_to_all x3, starting transfers between devices, exchange(): return lax.all_to_all(value, 'inner', 0, 0)  12.2 us
    pallas_call x2, Pallas kernels, attend(): pl.pallas_call(functools.partial(attend_kernel, causal, rows, pair // 2),...  12 us
  transfers between devices with their start and end apart: 98, of which 31 were waited for; matrix products, arithmetic and copies ran while one was open for 6% of the time, Pallas kernels for 21%

profile of v2, /device:TPU:0, one launch (start us, length us, event | category | flops | bytes accessed | tf_op | source)
XLA Modules:
  0.0 449.0 jit_solution(17682886352403793716)
XLA Ops:
  11.7 5.2 %all-to-all-start = ((bf16[8,32,512]{2,1,0:T(8,128)(2,1)}), bf16[8,32,512]{2,1,0:T(8,128)(2,1)S(1)}, u32[]{:S(2)}, u32[]{:S(2)}) async-start(bf16[8,32,512]{2,1,0:T(8,128)(2,1)} %pad_maximum_fusion.3), calls=%async_computation | async-start | bytes 524288 | tf_op jit(solution)/shard_map/all_to_all | solution.py:963
  17.0 6.9 %all-to-all-done = bf16[8,32,512]{2,1,0:T(8,128)(2,1)S(1)} async-done(((bf16[8,32,512]{2,1,0:T(8,128)(2,1)}), bf16[8,32,512]{2,1,0:T(8,128)(2,1)S(1)}, u32[]{:S(2)}, u32[]{:S(2)}) %all-to-all-start) | async-done | bytes 262176 | tf_op jit(solution)/shard_map/all_to_all | solution.py:963
  25.8 2.4 collective-permute-start.2
  28.9 5.0 %collective-permute-done.refs_1_ = bf16[128,1024]{1,0:T(8,128)(2,1)S(1)} collective-permute-done((bf16[128,1024]{1,0:T(8,128)(2,1)S(1)}, bf16[128,1024]{1,0:T(8,128)(2,1)S(1)}, u32[]{:S(2)}, u32[]{:S(2)}) %collective-permute-start) | collective-permute-done | bytes 262176 | tf_op jit(solution)/shard_map/ppermute | solution.py:865
  33.9 4.8 %collective-permute-done.1.refs_2_ = bf16[128,1024]{1,0:T(8,128)(2,1)S(1)} collective-permute-done((bf16[128,1024]{1,0:T(8,128)(2,1)S(1)}, bf16[128,1024]{1,0:T(8,128)(2,1)S(1)}, u32[]{:S(2)}, u32[]{:S(2)}) %collective-permute-start.1) | collective-permute-done | bytes 262176 | tf_op jit(solution)/shard_map/ppermute | solution.py:865
  40.5 1.8 collective-permute-start.24
  47.9 3.6 collective-permute-done.23.refs_2_
  51.5 3.5 all-to-all-start.1
  55.2 11.7 %all-to-all-done.1 = bf16[8,32,1408]{2,1,0:T(8,128)(2,1)S(1)} async-done(((bf16[8,32,1408]{2,1,0:T(8,128)(2,1)}), bf16[8,32,1408]{2,1,0:T(8,128)(2,1)S(1)}, u32[]{:S(2)}, u32[]{:S(2)}) %all-to-all-start.1) | async-done | bytes 720928 | tf_op jit(solution)/shard_map/all_to_all | solution.py:963
  67.8 2.1 pad_maximum_fusion
  80.7 3.1 shard_map.229
  89.9 2.4 collective-permute-start.10
  94.3 3.8 collective-permute-done.8.refs_9_
  98.0 5.0 %collective-permute-done.9.refs_10_ = bf16[128,1024]{1,0:T(8,128)(2,1)} collective-permute-done((bf16[128,1024]{1,0:T(8,128)(2,1)S(1)}, bf16[128,1024]{1,0:T(8,128)(2,1)}, u32[]{:S(2)}, u32[]{:S(2)}) %collective-permute-start.9) | collective-permute-done | bytes 262176 | tf_op jit(solution)/shard_map/ppermute | solution.py:865
  103.6 5.7 %shard_map.232 = (bf16[1024,128]{1,0:T(8,128)(2,1)}, f32[2,1024]{1,0:T(2,128)}) custom-call(s32[10]{0:T(128)} %concatenate.59.table, bf16[1024,128]{1,0:T(8,128)(2,1)} %copy-done.76, bf16[1024,128]{1,0:T(8,128)(2,1)} %copy-done.77, bf16[1024,128]{1,0:T(8,128)(2,1)} %copy-done.78), custom_call_target="tpu_custom_call" | custom-call | flops 6600000000 | bytes 21000000 | tf_op jit(solution)/shard_map/pallas_call | solution.py:270
  115.6 3.3 collective-permute-done.11.refs_1_
  118.9 6.6 %collective-permute-done.12.refs_2_ = bf16[1024,128]{1,0:T(8,128)(2,1)} collective-permute-done((bf16[1024,128]{1,0:T(8,128)(2,1)}, bf16[1024,128]{1,0:T(8,128)(2,1)}, u32[]{:S(2)}, u32[]{:S(2)}) %collective-permute-start.12) | collective-permute-done | bytes 262176 | tf_op jit(solution)/shard_map/ppermute | solution.py:865
  129.9 2.5 shard_map.233
  136.2 10.6 %shard_map.234 = (f32[128,1024]{1,0:T(8,128)}, bf16[1024,1024]{1,0:T(8,128)(2,1)}, bf16[1024,1024]{1,0:T(8,128)(2,1)}, bf16[1024,128]{1,0:T(8,128)(2,1)}) custom-call(bf16[1024,128]{1,0:T(8,128)(2,1)} %get-tuple-element.161.refs_0_.own, bf16[1024,128]{1,0:T(8,128)(2,1)} %collective-permute-done.11.refs_1_, ...), custom_call_target="tpu_custom_call" | custom-call | flops 6600000000 | bytes 21000000 | tf_op jit(solution)/shard_map/pallas_call | solution.py:433
  146.8 6.2 %shard_map.235 = (bf16[1024,128]{1,0:T(8,128)(2,1)}, f32[2,1024]{1,0:T(2,128)}) custom-call(s32[10]{0:T(128)} %concatenate.58.table, bf16[1024,128]{1,0:T(8,128)(2,1)} %get-tuple-element.169.q, bf16[1024,128]{1,0:T(8,128)(2,1)} %copy-done.79, bf16[1024,128]{1,0:T(8,128)(2,1)} %copy-done.80), custom_call_target="tpu_custom_call" | custom-call | flops 6600000000 | bytes 21000000 | tf_op jit(solution)/shard_map/pallas_call | solution.py:270
  156.7 1.8 collective-permute-start.31
  159.5 2.8 collective-permute-done.29.refs_1_
  162.8 4.8 %collective-permute-done.30.refs_2_ = bf16[1024,128]{1,0:T(8,128)(2,1)S(1)} collective-permute-done((bf16[1024,128]{1,0:T(8,128)(2,1)}, bf16[1024,128]{1,0:T(8,128)(2,1)S(1)}, u32[]{:S(2)}, u32[]{:S(2)}) %collective-permute-start.30) | collective-permute-done | bytes 262176 | tf_op jit(solution)/shard_map/ppermute | solution.py:865
  167.6 1.7 collective-permute-start.39
  169.8 3.8 collective-permute-done.37.refs_9_
  173.6 5.4 %collective-permute-done.38.refs_10_ = bf16[128,1024]{1,0:T(8,128)(2,1)} collective-permute-done((bf16[128,1024]{1,0:T(8,128)(2,1)S(1)}, bf16[128,1024]{1,0:T(8,128)(2,1)}, u32[]{:S(2)}, u32[]{:S(2)}) %collective-permute-start.38) | collective-permute-done | bytes 262176 | tf_op jit(solution)/shard_map/ppermute | solution.py:865
  185.6 3.9 collective-permute-done.44.refs_1_
  189.5 6.0 %collective-permute-done.45.refs_2_ = bf16[128,1024]{1,0:T(8,128)(2,1)S(1)} collective-permute-done((bf16[128,1024]{1,0:T(8,128)(2,1)S(1)}, bf16[128,1024]{1,0:T(8,128)(2,1)S(1)}, u32[]{:S(2)}, u32[]{:S(2)}) %collective-permute-start.45) | collective-permute-done | bytes 262176 | tf_op jit(solution)/shard_map/ppermute | solution.py:865
  196.1 18.8 %shard_map.238 = (f32[128,1024]{1,0:T(8,128)}, bf16[1024,1024]{1,0:T(8,128)(2,1)}) custom-call(bf16[1024,128]{1,0:T(8,128)(2,1)} %get-tuple-element.172.refs_0_.own, bf16[1024,128]{1,0:T(8,128)(2,1)} %copy-done.93, bf16[1024,128]{1,0:T(8,128)(2,1)} %copy-done.94, bf16[1024,128]{1,0:T(8,128)(2,1)} %copy-done.95, bf16[1024,128]{1,0:T(8,128)(2,1)} %copy-done.96, ...), custom_call_target="tpu_custom_call" | custom-call | flops 5500000256 | bytes 17500000 | tf_op jit(solution)/shard_map/pallas_call | solution.py:456
  214.9 11.9 %shard_map.239 = (bf16[1024,1024]{1,0:T(8,128)(2,1)S(1)}, bf16[1024,1024]{1,0:T(8,128)(2,1)S(1)}, bf16[512,1024]{1,0:T(8,128)(2,1)S(1)}, f32[512,1024]{1,0:T(8,1...) custom-call(bf16[1024,1024]{1,0:T(8,128)(2,1)} %get-tuple-element.190.h, f32[1,1024]{1,0:T(1,128)S(1)} %reshape.225.bias, ...), custom_call_target="tpu_custom_call" | custom-call | flops 14300000256 | bytes 45500000 | tf_op jit(solution)/shard_map/pallas_call | solution.py:520
  226.9 2.6 collective-permute-done.51.took
  231.2 2.1 collective-permute-start.54
  234.9 4.5 %shard_map.241 = bf16[1024,2048]{1,0:T(8,128)(2,1)S(1)} custom-call(bf16[1024,1024]{1,0:T(8,128)(2,1)S(1)} %get-tuple-element.196.act, bf16[1024,1024]{1,0:T(8,128)(2,1)S(1)} %get-tuple-element.189.slope, bf16[1024,1024]{1,0:T(8,128)(2,1)S(1)} %copy-done.63, bf16[1024,1024]{1,0:T(8,128)(2,1)S(1)} %copy-done.64), custom_call_target="tpu_custom_call" | custom-call | flops 6600000000 | bytes 21000000 | tf_op jit(solution)/shard_map/pallas_call | solution.py:584
  239.5 2.0 copy-done.2
  241.4 2.5 collective-permute-done.53.two
  247.0 5.7 %collective-permute-done.55.refs_1_ = bf16[128,1024]{1,0:T(8,128)(2,1)S(1)} collective-permute-done((bf16[128,1024]{1,0:T(8,128)(2,1)S(1)}, bf16[128,1024]{1,0:T(8,128)(2,1)S(1)}, u32[]{:S(2)}, u32[]{:S(2)}) %collective-permute-start.55) | collective-permute-done | bytes 262176 | tf_op jit(solution)/shard_map/ppermute | solution.py:865
  252.8 2.9 shard_map.243
  260.5 11.0 %collective-permute-done.56.refs_2_ = bf16[128,1024]{1,0:T(8,128)(2,1)S(1)} collective-permute-done((bf16[128,1024]{1,0:T(8,128)(2,1)S(1)}, bf16[128,1024]{1,0:T(8,128)(2,1)S(1)}, u32[]{:S(2)}, u32[]{:S(2)}) %collective-permute-start.56) | collective-permute-done | bytes 262176 | tf_op jit(solution)/shard_map/ppermute | solution.py:865
  272.0 1.6 copy-done.43
  277.5 14.6 %shard_map.245 = (bf16[512,1024]{1,0:T(8,128)(2,1)}, f32[512,1024]{1,0:T(8,128)}, bf16[1024,128]{1,0:T(8,128)(2,1)}, bf16[1024,128]{1,0:T(8,128)(2,1)}, bf16[102...) custom-call(s32[10]{0:T(128)} %concatenate.58.table, ...), custom_call_target="tpu_custom_call" | custom-call | flops 11000000512 | bytes 35000000 | tf_op jit(solution)/shard_map/pallas_call | solution.py:300
  292.3 2.9 collective-permute-done.66.took
  303.6 2.2 shard_map.247
  306.1 5.9 %collective-permute-done.68.two = bf16[128,1024]{1,0:T(8,128)(2,1)S(1)} collective-permute-done((bf16[128,1024]{1,0:T(8,128)(2,1)S(1)}, bf16[128,1024]{1,0:T(8,128)(2,1)S(1)}, u32[]{:S(2)}, u32[]{:S(2)}) %collective-permute-start.68) | collective-permute-done | bytes 262176 | tf_op jit(solution)/shard_map/ppermute | solution.py:865
  312.0 4.8 %all-to-all-start.2 = ((bf16[32,32,384]{2,1,0:T(8,128)(2,1)}), bf16[32,32,384]{2,1,0:T(8,128)(2,1)S(1)}, u32[]{:S(2)}, u32[]{:S(2)}) async-start(bf16[32,32,384]{2,1,0:T(8,128)(2,1)} %bitcast.29), calls=%async_computation.2 | async-start | bytes 1572864 | tf_op jit(solution)/shard_map/all_to_all | solution.py:1013
  320.7 1.8 collective-permute-start.70
  322.5 9.6 %collective-permute-done.70.refs_1_ = bf16[128,1024]{1,0:T(8,128)(2,1)S(1)} collective-permute-done((bf16[128,1024]{1,0:T(8,128)(2,1)S(1)}, bf16[128,1024]{1,0:T(8,128)(2,1)S(1)}, u32[]{:S(2)}, u32[]{:S(2)}) %collective-permute-start.70) | collective-permute-done | bytes 262176 | tf_op jit(solution)/shard_map/ppermute | solution.py:865
  335.2 14.6 %collective-permute-done.71.refs_2_ = bf16[128,1024]{1,0:T(8,128)(2,1)S(1)} collective-permute-done((bf16[128,1024]{1,0:T(8,128)(2,1)S(1)}, bf16[128,1024]{1,0:T(8,128)(2,1)S(1)}, u32[]{:S(2)}, u32[]{:S(2)}) %collective-permute-start.71) | collective-permute-done | bytes 262176 | tf_op jit(solution)/shard_map/ppermute | solution.py:865
  352.7 10.7 %shard_map.251 = (bf16[1024,128]{1,0:T(8,128)(2,1)}, bf16[1024,128]{1,0:T(8,128)(2,1)}, bf16[1024,128]{1,0:T(8,128)(2,1)}, f32[2,128]{1,0:T(2,128)}, bf16[2,32,1...) custom-call(s32[10]{0:T(128)} %concatenate.59.table, bf16[1024,128]{1,0:T(8,128)(2,1)} %copy-done.76, ...), custom_call_target="tpu_custom_call" | custom-call | flops 11000000512 | bytes 35000000 | tf_op jit(solution)/shard_map/pallas_call | solution.py:300
  369.1 2.1 shard_map.252
  373.6 2.0 fusion
  377.4 2.2 shard_map.253
  381.5 2.4 collective-permute-start.81
  383.9 2.2 shard_map.255
  386.1 4.5 all-to-all-start.3
  392.0 5.6 %collective-permute-done.80.two = bf16[128,1024]{1,0:T(8,128)(2,1)S(1)} collective-permute-done((bf16[128,1024]{1,0:T(8,128)(2,1)}, bf16[128,1024]{1,0:T(8,128)(2,1)S(1)}, u32[]{:S(2)}, u32[]{:S(2)}) %collective-permute-start.80) | collective-permute-done | bytes 262176 | tf_op jit(solution)/shard_map/ppermute | solution.py:865
  399.7 2.4 shard_map.254
  402.1 1.8 collective-permute-start.84
  404.0 2.1 collective-permute-start.83
  411.1 5.0 %all-to-all-start.5 = ((f32[32,1,672]{2,1,0:T(1,128)}), f32[32,1,672]{2,1,0:T(1,128)S(1)}, u32[]{:S(2)}, u32[]{:S(2)}) async-start(f32[32,1,672]{2,1,0:T(1,128)} %copy.102), calls=%async_computation.7 | async-start | bytes 196608 | tf_op jit(solution)/shard_map/all_to_all | solution.py:1168
  416.2 2.5 slice_convert_fusion
  418.7 6.2 %all-to-all-done.5 = f32[32,1,672]{2,1,0:T(1,128)S(1)} async-done(((f32[32,1,672]{2,1,0:T(1,128)}), f32[32,1,672]{2,1,0:T(1,128)S(1)}, u32[]{:S(2)}, u32[]{:S(2)}) %all-to-all-start.5) | async-done | bytes 86048 | tf_op jit(solution)/shard_map/all_to_all | solution.py:1168
  424.8 3.5 all-to-all-start.4
  430.7 2.0 fusion.1
  432.6 5.4 %all-to-all-done.4 = bf16[8,32,1024]{2,1,0:T(8,128)(2,1)S(1)} async-done(((bf16[8,32,1024]{2,1,0:T(8,128)(2,1)}), bf16[8,32,1024]{2,1,0:T(8,128)(2,1)S(1)}, u32[]{:S(2)}, u32[]{:S(2)}) %all-to-all-start.4) | async-done | bytes 524320 | tf_op jit(solution)/shard_map/all_to_all | solution.py:963
  (489 shorter events, 122.6 us)
Async XLA Ops:
  11.7 12.1 %all-to-all-start = ((bf16[8,32,512]{2,1,0:T(8,128)(2,1)}), bf16[8,32,512]{2,1,0:T(8,128)(2,1)S(1)}, u32[]{:S(2)}, u32[]{:S(2)}) async-start(bf16[8,32,512]{2,1,0:T(8,128)(2,1)} %pad_maximum_fusion.3), calls=%async_computation | async-start | bytes 524288 | tf_op jit(solution)/shard_map/all_to_all | solution.py:963
  16.9 50.8 %all-gather.7.cloned.1.call-start = ((), (), s32[]{:S(2)}) async-start(), calls=%async_computation.10 | async-start | bytes 1638400 | tf_op jit(solution)/shard_map/all_gather | solution.py:1028
  25.2 13.5 %collective-permute-start.1 = (bf16[128,1024]{1,0:T(8,128)(2,1)S(1)}, bf16[128,1024]{1,0:T(8,128)(2,1)S(1)}, u32[]{:S(2)}, u32[]{:S(2)}) collective-permute-start(bf16[128,1024]{1,0:T(8,128)(2,1)S(1)} %bitcast.93), channel_id=1, source_target_pairs={{0,4},{1,5},{2,6},{3,7},{4,0},{5,1},{6,2},{7,3},{8,12},{9,13},{10,... | collective-permute-start | bytes 786440 | tf_op jit(solution)/shard_map/ppermute | solution.py:865
  25.8 12.9 %collective-permute-start.2 = (bf16[128,1024]{1,0:T(8,128)(2,1)S(1)}, bf16[128,1024]{1,0:T(8,128)(2,1)S(1)}, u32[]{:S(2)}, u32[]{:S(2)}) collective-permute-start(bf16[128,1024]{1,0:T(8,128)(2,1)S(1)} %bitcast.94), channel_id=1, source_target_pairs={{0,6},{1,7},{2,4},{3,5},{4,2},{5,3},{6,0},{7,1},{8,14},{9,15},{10,... | collective-permute-start | bytes 786440 | tf_op jit(solution)/shard_map/ppermute | solution.py:865
  39.5 12.0 %collective-permute-start.23 = (bf16[128,1024]{1,0:T(8,128)(2,1)S(1)}, bf16[128,1024]{1,0:T(8,128)(2,1)S(1)}, u32[]{:S(2)}, u32[]{:S(2)}) collective-permute-start(bf16[128,1024]{1,0:T(8,128)(2,1)S(1)} %bitcast.82), channel_id=1, source_target_pairs={{0,4},{1,5},{2,6},{3,7},{4,0},{5,1},{6,2},{7,3},{8,12},{9,13},{10,... | collective-permute-start | bytes 786440 | tf_op jit(solution)/shard_map/ppermute | solution.py:865
  51.5 15.4 %all-to-all-start.1 = ((bf16[8,32,1408]{2,1,0:T(8,128)(2,1)}), bf16[8,32,1408]{2,1,0:T(8,128)(2,1)S(1)}, u32[]{:S(2)}, u32[]{:S(2)}) async-start(bf16[8,32,1408]{2,1,0:T(8,128)(2,1)} %pad_maximum_fusion.1), calls=%async_computation.1 | async-start | bytes 1441792 | tf_op jit(solution)/shard_map/all_to_all | solution.py:963
  55.1 71.5 %all-gather.9.cloned.1.call-start = ((), (), s32[]{:S(2)}) async-start(), calls=%async_computation.11 | async-start | bytes 1310720 | tf_op jit(solution)/shard_map/all_gather | solution.py:1028
  67.7 147.2 %all-gather.11.cloned.1.call-start = ((), (), s32[]{:S(2)}) async-start(), calls=%async_computation.12 | async-start | bytes 5242880 | tf_op jit(solution)/shard_map/all_gather | solution.py:1028
  69.9 332.3 %reduce-scatter.3.cloned.1.call-start = ((), (), s32[]{:S(2)}) async-start(), calls=%async_computation.8 | async-start | bytes 5242880 | tf_op jit(solution)/shard_map/reduce_scatter | solution.py:1081
  89.3 13.8 %collective-permute-start.9 = (bf16[128,1024]{1,0:T(8,128)(2,1)S(1)}, bf16[128,1024]{1,0:T(8,128)(2,1)}, u32[]{:S(2)}, u32[]{:S(2)}) collective-permute-start(bf16[128,1024]{1,0:T(8,128)(2,1)S(1)} %shard_map.231.refs_8_.weight), channel_id=1, source_target_pairs={{0,4},{1,5},{2,6},{3,7},{4,0},{5,1},{6,2},{7,3},{8,12},{9,13},{10,... | collective-permute-start | bytes 786440 | tf_op jit(solution)/shard_map/ppermute | solution.py:865
  89.9 13.2 %collective-permute-start.10 = (bf16[128,1024]{1,0:T(8,128)(2,1)S(1)}, bf16[128,1024]{1,0:T(8,128)(2,1)}, u32[]{:S(2)}, u32[]{:S(2)}) collective-permute-start(bf16[128,1024]{1,0:T(8,128)(2,1)S(1)} %shard_map.231.refs_8_.weight), channel_id=1, source_target_pairs={{0,6},{1,7},{2,4},{3,5},{4,2},{5,3},{6,0},{7,1},{8,14},{9,15},{10,... | collective-permute-start | bytes 786440 | tf_op jit(solution)/shard_map/ppermute | solution.py:865
  93.7 15.6 %collective-permute-start.25 = (bf16[128,1024]{1,0:T(8,128)(2,1)S(1)}, bf16[128,1024]{1,0:T(8,128)(2,1)S(1)}, u32[]{:S(2)}, u32[]{:S(2)}) collective-permute-start(bf16[128,1024]{1,0:T(8,128)(2,1)S(1)} %bitcast.84), channel_id=1, source_target_pairs={{0,1},{1,0},{2,3},{3,2},{4,5},{5,4},{6,7},{7,6},{8,9},{9,8},{10,11... | collective-permute-start | bytes 786440 | tf_op jit(solution)/shard_map/ppermute | solution.py:865
  93.7 17.2 %collective-permute-start.26 = (bf16[128,1024]{1,0:T(8,128)(2,1)S(1)}, bf16[128,1024]{1,0:T(8,128)(2,1)S(1)}, u32[]{:S(2)}, u32[]{:S(2)}) collective-permute-start(bf16[128,1024]{1,0:T(8,128)(2,1)S(1)} %collective-permute-done.22.refs_1_), channel_id=1, source_target_pairs={{0,1},{1,0},{2,3},{3,2},{4,5},{5,4},{6,7},{7,6},{8,9},{9,8},{10,11... | collective-permute-start | bytes 786440 | tf_op jit(solution)/shard_map/ppermute | solution.py:865
  98.0 14.1 %collective-permute-start.27 = (bf16[128,1024]{1,0:T(8,128)(2,1)S(1)}, bf16[128,1024]{1,0:T(8,128)(2,1)S(1)}, u32[]{:S(2)}, u32[]{:S(2)}) collective-permute-start(bf16[128,1024]{1,0:T(8,128)(2,1)S(1)} %collective-permute-done.23.refs_2_), channel_id=1, source_target_pairs={{0,1},{1,0},{2,3},{3,2},{4,5},{5,4},{6,7},{7,6},{8,9},{9,8},{10,11... | collective-permute-start | bytes 786440 | tf_op jit(solution)/shard_map/ppermute | solution.py:865
  103.1 11.2 %collective-permute-start.28 = (bf16[128,1024]{1,0:T(8,128)(2,1)S(1)}, bf16[128,1024]{1,0:T(8,128)(2,1)}, u32[]{:S(2)}, u32[]{:S(2)}) collective-permute-start(bf16[128,1024]{1,0:T(8,128)(2,1)S(1)} %collective-permute-done.24.refs_3_), channel_id=1, source_target_pairs={{0,1},{1,0},{2,3},{3,2},{4,5},{5,4},{6,7},{7,6},{8,9},{9,8},{10,11... | collective-permute-start | bytes 786440 | tf_op jit(solution)/shard_map/ppermute | solution.py:865
  103.1 11.2 %collective-permute-start.18 = (bf16[128,1024]{1,0:T(8,128)(2,1)S(1)}, bf16[128,1024]{1,0:T(8,128)(2,1)}, u32[]{:S(2)}, u32[]{:S(2)}) collective-permute-start(bf16[128,1024]{1,0:T(8,128)(2,1)S(1)} %shard_map.231.refs_8_.weight), channel_id=1, source_target_pairs={{0,1},{1,0},{2,3},{3,2},{4,5},{5,4},{6,7},{7,6},{8,9},{9,8},{10,11... | collective-permute-start | bytes 786440 | tf_op jit(solution)/shard_map/ppermute | solution.py:865
  111.6 13.9 %collective-permute-start.12 = (bf16[1024,128]{1,0:T(8,128)(2,1)}, bf16[1024,128]{1,0:T(8,128)(2,1)}, u32[]{:S(2)}, u32[]{:S(2)}) collective-permute-start(bf16[1024,128]{1,0:T(8,128)(2,1)} %get-tuple-element.161.refs_0_.own), channel_id=1, source_target_pairs={{0,4},{1,5},{2,6},{3,7},{4,0},{5,1},{6,2},{7,3},{8,12},{9,13},{10,... | collective-permute-start | bytes 786440 | tf_op jit(solution)/shard_map/ppermute | solution.py:865
  112.9 12.6 %collective-permute-start.13 = (bf16[1024,128]{1,0:T(8,128)(2,1)}, bf16[1024,128]{1,0:T(8,128)(2,1)}, u32[]{:S(2)}, u32[]{:S(2)}) collective-permute-start(bf16[1024,128]{1,0:T(8,128)(2,1)} %get-tuple-element.161.refs_0_.own), channel_id=1, source_target_pairs={{0,6},{1,7},{2,4},{3,5},{4,2},{5,3},{6,0},{7,1},{8,14},{9,15},{10,... | collective-permute-start | bytes 786440 | tf_op jit(solution)/shard_map/ppermute | solution.py:865
  114.3 11.7 %collective-permute-start.14 = (bf16[1024,128]{1,0:T(8,128)(2,1)}, bf16[1024,128]{1,0:T(8,128)(2,1)}, u32[]{:S(2)}, u32[]{:S(2)}) collective-permute-start(bf16[1024,128]{1,0:T(8,128)(2,1)} %get-tuple-element.161.refs_0_.own), channel_id=1, source_target_pairs={{0,1},{1,0},{2,3},{3,2},{4,5},{5,4},{6,7},{7,6},{8,9},{9,8},{10,11... | collective-permute-start | bytes 786440 | tf_op jit(solution)/shard_map/ppermute | solution.py:865
  114.3 11.8 %collective-permute-start.19 = (bf16[128,1024]{1,0:T(8,128)(2,1)}, bf16[128,1024]{1,0:T(8,128)(2,1)S(1)}, u32[]{:S(2)}, u32[]{:S(2)}) collective-permute-start(bf16[128,1024]{1,0:T(8,128)(2,1)} %collective-permute-done.8.refs_9_), channel_id=1, source_target_pairs={{0,1},{1,0},{2,3},{3,2},{4,5},{5,4},{6,7},{7,6},{8,9},{9,8},{10,11... | collective-permute-start | bytes 786440 | tf_op jit(solution)/shard_map/ppermute | solution.py:865
  118.9 17.3 %collective-permute-start.20 = (bf16[128,1024]{1,0:T(8,128)(2,1)}, bf16[128,1024]{1,0:T(8,128)(2,1)}, u32[]{:S(2)}, u32[]{:S(2)}) collective-permute-start(bf16[128,1024]{1,0:T(8,128)(2,1)} %collective-permute-done.9.refs_10_), channel_id=1, source_target_pairs={{0,1},{1,0},{2,3},{3,2},{4,5},{5,4},{6,7},{7,6},{8,9},{9,8},{10,11... | collective-permute-start | bytes 786440 | tf_op jit(solution)/shard_map/ppermute | solution.py:865
  153.5 14.2 %collective-permute-start.30 = (bf16[1024,128]{1,0:T(8,128)(2,1)}, bf16[1024,128]{1,0:T(8,128)(2,1)S(1)}, u32[]{:S(2)}, u32[]{:S(2)}) collective-permute-start(bf16[1024,128]{1,0:T(8,128)(2,1)} %get-tuple-element.172.refs_0_.own), channel_id=1, source_target_pairs={{0,4},{1,5},{2,6},{3,7},{4,0},{5,1},{6,2},{7,3},{8,12},{9,13},{10,... | collective-permute-start | bytes 786440 | tf_op jit(solution)/shard_map/ppermute | solution.py:865
  156.7 12.6 %collective-permute-start.31 = (bf16[1024,128]{1,0:T(8,128)(2,1)S(1)}, bf16[1024,128]{1,0:T(8,128)(2,1)S(1)}, u32[]{:S(2)}, u32[]{:S(2)}) collective-permute-start(bf16[1024,128]{1,0:T(8,128)(2,1)S(1)} %copy-done.92), channel_id=1, source_target_pairs={{0,6},{1,7},{2,4},{3,5},{4,2},{5,3},{6,0},{7,1},{8,14},{9,15},{10,... | collective-permute-start | bytes 786440 | tf_op jit(solution)/shard_map/ppermute | solution.py:865
  159.0 14.6 %collective-permute-start.37 = (bf16[128,1024]{1,0:T(8,128)(2,1)S(1)}, bf16[128,1024]{1,0:T(8,128)(2,1)S(1)}, u32[]{:S(2)}, u32[]{:S(2)}) collective-permute-start(bf16[128,1024]{1,0:T(8,128)(2,1)S(1)} %shard_map.237.refs_8_.weight), channel_id=1, source_target_pairs={{0,2},{1,3},{2,0},{3,1},{4,6},{5,7},{6,4},{7,5},{8,10},{9,11},{10,... | collective-permute-start | bytes 786440 | tf_op jit(solution)/shard_map/ppermute | solution.py:865
  162.4 16.7 %collective-permute-start.38 = (bf16[128,1024]{1,0:T(8,128)(2,1)S(1)}, bf16[128,1024]{1,0:T(8,128)(2,1)}, u32[]{:S(2)}, u32[]{:S(2)}) collective-permute-start(bf16[128,1024]{1,0:T(8,128)(2,1)S(1)} %shard_map.237.refs_8_.weight), channel_id=1, source_target_pairs={{0,4},{1,5},{2,6},{3,7},{4,0},{5,1},{6,2},{7,3},{8,12},{9,13},{10,... | collective-permute-start | bytes 786440 | tf_op jit(solution)/shard_map/ppermute | solution.py:865
  167.6 11.4 %collective-permute-start.39 = (bf16[128,1024]{1,0:T(8,128)(2,1)S(1)}, bf16[128,1024]{1,0:T(8,128)(2,1)}, u32[]{:S(2)}, u32[]{:S(2)}) collective-permute-start(bf16[128,1024]{1,0:T(8,128)(2,1)S(1)} %shard_map.237.refs_8_.weight), channel_id=1, source_target_pairs={{0,6},{1,7},{2,4},{3,5},{4,2},{5,3},{6,0},{7,1},{8,14},{9,15},{10,... | collective-permute-start | bytes 786440 | tf_op jit(solution)/shard_map/ppermute | solution.py:865
  181.9 13.6 %collective-permute-start.45 = (bf16[128,1024]{1,0:T(8,128)(2,1)S(1)}, bf16[128,1024]{1,0:T(8,128)(2,1)S(1)}, u32[]{:S(2)}, u32[]{:S(2)}) collective-permute-start(bf16[128,1024]{1,0:T(8,128)(2,1)S(1)} %bitcast.87), channel_id=1, source_target_pairs={{0,4},{1,5},{2,6},{3,7},{4,0},{5,1},{6,2},{7,3},{8,12},{9,13},{10,... | collective-permute-start | bytes 786440 | tf_op jit(solution)/shard_map/ppermute | solution.py:865
  182.5 13.1 %collective-permute-start.46 = (bf16[128,1024]{1,0:T(8,128)(2,1)S(1)}, bf16[128,1024]{1,0:T(8,128)(2,1)S(1)}, u32[]{:S(2)}, u32[]{:S(2)}) collective-permute-start(bf16[128,1024]{1,0:T(8,128)(2,1)S(1)} %bitcast.88), channel_id=1, source_target_pairs={{0,6},{1,7},{2,4},{3,5},{4,2},{5,3},{6,0},{7,1},{8,14},{9,15},{10,... | collective-permute-start | bytes 786440 | tf_op jit(solution)/shard_map/ppermute | solution.py:865
  184.7 11.3 %collective-permute-start.43 = (bf16[128,1024]{1,0:T(8,128)(2,1)}, bf16[128,1024]{1,0:T(8,128)(2,1)}, u32[]{:S(2)}, u32[]{:S(2)}) collective-permute-start(bf16[128,1024]{1,0:T(8,128)(2,1)} %collective-permute-done.39.refs_11_), channel_id=1, source_target_pairs={{0,1},{1,0},{2,3},{3,2},{4,5},{5,4},{6,7},{7,6},{8,9},{9,8},{10,11... | collective-permute-start | bytes 786440 | tf_op jit(solution)/shard_map/ppermute | solution.py:865
  185.0 29.8 %collective-permute-start.47 = (bf16[128,1024]{1,0:T(8,128)(2,1)S(1)}, bf16[128,1024]{1,0:T(8,128)(2,1)S(1)}, u32[]{:S(2)}, u32[]{:S(2)}) collective-permute-start(bf16[128,1024]{1,0:T(8,128)(2,1)S(1)} %bitcast.89), channel_id=1, source_target_pairs={{0,1},{1,0},{2,3},{3,2},{4,5},{5,4},{6,7},{7,6},{8,9},{9,8},{10,11... | collective-permute-start | bytes 786440 | tf_op jit(solution)/shard_map/ppermute | solution.py:865
  189.5 25.4 %collective-permute-start.48 = (bf16[128,1024]{1,0:T(8,128)(2,1)S(1)}, bf16[128,1024]{1,0:T(8,128)(2,1)S(1)}, u32[]{:S(2)}, u32[]{:S(2)}) collective-permute-start(bf16[128,1024]{1,0:T(8,128)(2,1)S(1)} %collective-permute-done.44.refs_1_), channel_id=1, source_target_pairs={{0,1},{1,0},{2,3},{3,2},{4,5},{5,4},{6,7},{7,6},{8,9},{9,8},{10,11... | collective-permute-start | bytes 786440 | tf_op jit(solution)/shard_map/ppermute | solution.py:865
  195.5 19.3 %collective-permute-start.49 = (bf16[128,1024]{1,0:T(8,128)(2,1)S(1)}, bf16[128,1024]{1,0:T(8,128)(2,1)S(1)}, u32[]{:S(2)}, u32[]{:S(2)}) collective-permute-start(bf16[128,1024]{1,0:T(8,128)(2,1)S(1)} %collective-permute-done.45.refs_2_), channel_id=1, source_target_pairs={{0,1},{1,0},{2,3},{3,2},{4,5},{5,4},{6,7},{7,6},{8,9},{9,8},{10,11... | collective-permute-start | bytes 786440 | tf_op jit(solution)/shard_map/ppermute | solution.py:865
  195.5 19.3 %collective-permute-start.50 = (bf16[128,1024]{1,0:T(8,128)(2,1)S(1)}, bf16[128,1024]{1,0:T(8,128)(2,1)S(1)}, u32[]{:S(2)}, u32[]{:S(2)}) collective-permute-start(bf16[128,1024]{1,0:T(8,128)(2,1)S(1)} %collective-permute-done.46.refs_3_), channel_id=1, source_target_pairs={{0,1},{1,0},{2,3},{3,2},{4,5},{5,4},{6,7},{7,6},{8,9},{9,8},{10,11... | collective-permute-start | bytes 786440 | tf_op jit(solution)/shard_map/ppermute | solution.py:865
  229.7 11.7 %collective-permute-start.52 = (bf16[128,1024]{1,0:T(8,128)(2,1)S(1)}, bf16[128,1024]{1,0:T(8,128)(2,1)S(1)}, u32[]{:S(2)}, u32[]{:S(2)}) collective-permute-start(bf16[128,1024]{1,0:T(8,128)(2,1)S(1)} %get-tuple-element.185), channel_id=1, source_target_pairs={{0,2},{1,3},{2,0},{3,1},{4,6},{5,7},{6,4},{7,5},{8,10},{9,11},{10,... | collective-permute-start | bytes 786440 | tf_op jit(solution)/shard_map/ppermute | solution.py:865
  230.3 13.7 %collective-permute-start.53 = (bf16[128,1024]{1,0:T(8,128)(2,1)S(1)}, bf16[128,1024]{1,0:T(8,128)(2,1)S(1)}, u32[]{:S(2)}, u32[]{:S(2)}) collective-permute-start(bf16[128,1024]{1,0:T(8,128)(2,1)S(1)} %get-tuple-element.186), channel_id=1, source_target_pairs={{0,4},{1,5},{2,6},{3,7},{4,0},{5,1},{6,2},{7,3},{8,12},{9,13},{10,... | collective-permute-start | bytes 786440 | tf_op jit(solution)/shard_map/ppermute | solution.py:865
  231.2 12.7 %collective-permute-start.54 = (bf16[128,1024]{1,0:T(8,128)(2,1)S(1)}, bf16[128,1024]{1,0:T(8,128)(2,1)S(1)}, u32[]{:S(2)}, u32[]{:S(2)}) collective-permute-start(bf16[128,1024]{1,0:T(8,128)(2,1)S(1)} %get-tuple-element.187), channel_id=1, source_target_pairs={{0,6},{1,7},{2,4},{3,5},{4,2},{5,3},{6,0},{7,1},{8,14},{9,15},{10,... | collective-permute-start | bytes 786440 | tf_op jit(solution)/shard_map/ppermute | solution.py:865
  257.0 15.0 %collective-permute-start.62 = (bf16[512,1024]{1,0:T(8,128)(2,1)}, bf16[512,1024]{1,0:T(8,128)(2,1)S(1)}, u32[]{:S(2)}, u32[]{:S(2)}) collective-permute-start(bf16[512,1024]{1,0:T(8,128)(2,1)} %get-tuple-element.198), channel_id=1, source_target_pairs={{0,1},{1,0},{2,3},{3,2},{4,5},{5,4},{6,7},{7,6},{8,9},{9,8},{10,11... | collective-permute-start | bytes 3145736 | tf_op jit(solution)/shard_map/ppermute | solution.py:865
  257.1 14.4 %collective-permute-start.56 = (bf16[128,1024]{1,0:T(8,128)(2,1)S(1)}, bf16[128,1024]{1,0:T(8,128)(2,1)S(1)}, u32[]{:S(2)}, u32[]{:S(2)}) collective-permute-start(bf16[128,1024]{1,0:T(8,128)(2,1)S(1)} %get-tuple-element.205.refs_0_), channel_id=1, source_target_pairs={{0,4},{1,5},{2,6},{3,7},{4,0},{5,1},{6,2},{7,3},{8,12},{9,13},{10,... | collective-permute-start | bytes 786440 | tf_op jit(solution)/shard_map/ppermute | solution.py:865
  258.6 12.9 %collective-permute-start.57 = (bf16[128,1024]{1,0:T(8,128)(2,1)S(1)}, bf16[128,1024]{1,0:T(8,128)(2,1)S(1)}, u32[]{:S(2)}, u32[]{:S(2)}) collective-permute-start(bf16[128,1024]{1,0:T(8,128)(2,1)S(1)} %get-tuple-element.205.refs_0_), channel_id=1, source_target_pairs={{0,6},{1,7},{2,4},{3,5},{4,2},{5,3},{6,0},{7,1},{8,14},{9,15},{10,... | collective-permute-start | bytes 786440 | tf_op jit(solution)/shard_map/ppermute | solution.py:865
  260.0 13.8 %collective-permute-start.58 = (bf16[128,1024]{1,0:T(8,128)(2,1)S(1)}, bf16[128,1024]{1,0:T(8,128)(2,1)S(1)}, u32[]{:S(2)}, u32[]{:S(2)}) collective-permute-start(bf16[128,1024]{1,0:T(8,128)(2,1)S(1)} %get-tuple-element.205.refs_0_), channel_id=1, source_target_pairs={{0,1},{1,0},{2,3},{3,2},{4,5},{5,4},{6,7},{7,6},{8,9},{9,8},{10,11... | collective-permute-start | bytes 786440 | tf_op jit(solution)/shard_map/ppermute | solution.py:865
  260.0 13.8 %collective-permute-start.59 = (bf16[128,1024]{1,0:T(8,128)(2,1)S(1)}, bf16[128,1024]{1,0:T(8,128)(2,1)S(1)}, u32[]{:S(2)}, u32[]{:S(2)}) collective-permute-start(bf16[128,1024]{1,0:T(8,128)(2,1)S(1)} %collective-permute-done.55.refs_1_), channel_id=1, source_target_pairs={{0,1},{1,0},{2,3},{3,2},{4,5},{5,4},{6,7},{7,6},{8,9},{9,8},{10,11... | collective-permute-start | bytes 786440 | tf_op jit(solution)/shard_map/ppermute | solution.py:865
  273.9 18.2 %collective-permute-start.63 = (bf16[128,1024]{1,0:T(8,128)(2,1)S(1)}, bf16[128,1024]{1,0:T(8,128)(2,1)S(1)}, u32[]{:S(2)}, u32[]{:S(2)}) collective-permute-start(bf16[128,1024]{1,0:T(8,128)(2,1)S(1)} %get-tuple-element.214), channel_id=1, source_target_pairs={{0,2},{1,3},{2,0},{3,1},{4,6},{5,7},{6,4},{7,5},{8,10},{9,11},{10,... | collective-permute-start | bytes 786440 | tf_op jit(solution)/shard_map/ppermute | solution.py:865
  275.4 16.8 %collective-permute-start.64 = (bf16[128,1024]{1,0:T(8,128)(2,1)S(1)}, bf16[128,1024]{1,0:T(8,128)(2,1)S(1)}, u32[]{:S(2)}, u32[]{:S(2)}) collective-permute-start(bf16[128,1024]{1,0:T(8,128)(2,1)S(1)} %get-tuple-element.215), channel_id=1, source_target_pairs={{0,4},{1,5},{2,6},{3,7},{4,0},{5,1},{6,2},{7,3},{8,12},{9,13},{10,... | collective-permute-start | bytes 786440 | tf_op jit(solution)/shard_map/ppermute | solution.py:865
  275.9 16.3 %collective-permute-start.65 = (bf16[128,1024]{1,0:T(8,128)(2,1)S(1)}, bf16[128,1024]{1,0:T(8,128)(2,1)S(1)}, u32[]{:S(2)}, u32[]{:S(2)}) collective-permute-start(bf16[128,1024]{1,0:T(8,128)(2,1)S(1)} %get-tuple-element.216), channel_id=1, source_target_pairs={{0,6},{1,7},{2,4},{3,5},{4,2},{5,3},{6,0},{7,1},{8,14},{9,15},{10,... | collective-permute-start | bytes 786440 | tf_op jit(solution)/shard_map/ppermute | solution.py:865
  298.4 13.7 %collective-permute-start.68 = (bf16[128,1024]{1,0:T(8,128)(2,1)S(1)}, bf16[128,1024]{1,0:T(8,128)(2,1)S(1)}, u32[]{:S(2)}, u32[]{:S(2)}) collective-permute-start(bf16[128,1024]{1,0:T(8,128)(2,1)S(1)} %get-tuple-element.225), channel_id=1, source_target_pairs={{0,4},{1,5},{2,6},{3,7},{4,0},{5,1},{6,2},{7,3},{8,12},{9,13},{10,... | collective-permute-start | bytes 786440 | tf_op jit(solution)/shard_map/ppermute | solution.py:865
  298.9 13.2 %collective-permute-start.69 = (bf16[128,1024]{1,0:T(8,128)(2,1)S(1)}, bf16[128,1024]{1,0:T(8,128)(2,1)S(1)}, u32[]{:S(2)}, u32[]{:S(2)}) collective-permute-start(bf16[128,1024]{1,0:T(8,128)(2,1)S(1)} %get-tuple-element.226), channel_id=1, source_target_pairs={{0,6},{1,7},{2,4},{3,5},{4,2},{5,3},{6,0},{7,1},{8,14},{9,15},{10,... | collective-permute-start | bytes 786440 | tf_op jit(solution)/shard_map/ppermute | solution.py:865
  312.0 40.6 %all-to-all-start.2 = ((bf16[32,32,384]{2,1,0:T(8,128)(2,1)}), bf16[32,32,384]{2,1,0:T(8,128)(2,1)S(1)}, u32[]{:S(2)}, u32[]{:S(2)}) async-start(bf16[32,32,384]{2,1,0:T(8,128)(2,1)} %bitcast.29), calls=%async_computation.2 | async-start | bytes 1572864 | tf_op jit(solution)/shard_map/all_to_all | solution.py:1013
  320.7 11.4 %collective-permute-start.70 = (bf16[128,1024]{1,0:T(8,128)(2,1)S(1)}, bf16[128,1024]{1,0:T(8,128)(2,1)S(1)}, u32[]{:S(2)}, u32[]{:S(2)}) collective-permute-start(bf16[128,1024]{1,0:T(8,128)(2,1)S(1)} %get-tuple-element.249.refs_0_), channel_id=1, source_target_pairs={{0,2},{1,3},{2,0},{3,1},{4,6},{5,7},{6,4},{7,5},{8,10},{9,11},{10,... | collective-permute-start | bytes 786440 | tf_op jit(solution)/shard_map/ppermute | solution.py:865
  332.1 18.2 %collective-permute-start.77 = (bf16[512,1024]{1,0:T(8,128)(2,1)S(1)}, bf16[512,1024]{1,0:T(8,128)(2,1)S(1)}, u32[]{:S(2)}, u32[]{:S(2)}) collective-permute-start(bf16[512,1024]{1,0:T(8,128)(2,1)S(1)} %copy-done.14), channel_id=1, source_target_pairs={{0,1},{1,0},{2,3},{3,2},{4,5},{5,4},{6,7},{7,6},{8,9},{9,8},{10,11... | collective-permute-start | bytes 3145736 | tf_op jit(solution)/shard_map/ppermute | solution.py:865
  332.1 17.6 %collective-permute-start.71 = (bf16[128,1024]{1,0:T(8,128)(2,1)S(1)}, bf16[128,1024]{1,0:T(8,128)(2,1)S(1)}, u32[]{:S(2)}, u32[]{:S(2)}) collective-permute-start(bf16[128,1024]{1,0:T(8,128)(2,1)S(1)} %get-tuple-element.249.refs_0_), channel_id=1, source_target_pairs={{0,4},{1,5},{2,6},{3,7},{4,0},{5,1},{6,2},{7,3},{8,12},{9,13},{10,... | collective-permute-start | bytes 786440 | tf_op jit(solution)/shard_map/ppermute | solution.py:865
  333.3 16.4 %collective-permute-start.72 = (bf16[128,1024]{1,0:T(8,128)(2,1)S(1)}, bf16[128,1024]{1,0:T(8,128)(2,1)S(1)}, u32[]{:S(2)}, u32[]{:S(2)}) collective-permute-start(bf16[128,1024]{1,0:T(8,128)(2,1)S(1)} %get-tuple-element.249.refs_0_), channel_id=1, source_target_pairs={{0,6},{1,7},{2,4},{3,5},{4,2},{5,3},{6,0},{7,1},{8,14},{9,15},{10,... | collective-permute-start | bytes 786440 | tf_op jit(solution)/shard_map/ppermute | solution.py:865
  334.7 16.5 %collective-permute-start.73 = (bf16[128,1024]{1,0:T(8,128)(2,1)S(1)}, bf16[128,1024]{1,0:T(8,128)(2,1)S(1)}, u32[]{:S(2)}, u32[]{:S(2)}) collective-permute-start(bf16[128,1024]{1,0:T(8,128)(2,1)S(1)} %get-tuple-element.249.refs_0_), channel_id=1, source_target_pairs={{0,1},{1,0},{2,3},{3,2},{4,5},{5,4},{6,7},{7,6},{8,9},{9,8},{10,11... | collective-permute-start | bytes 786440 | tf_op jit(solution)/shard_map/ppermute | solution.py:865
  334.7 16.5 %collective-permute-start.74 = (bf16[128,1024]{1,0:T(8,128)(2,1)S(1)}, bf16[128,1024]{1,0:T(8,128)(2,1)S(1)}, u32[]{:S(2)}, u32[]{:S(2)}) collective-permute-start(bf16[128,1024]{1,0:T(8,128)(2,1)S(1)} %collective-permute-done.70.refs_1_), channel_id=1, source_target_pairs={{0,1},{1,0},{2,3},{3,2},{4,5},{5,4},{6,7},{7,6},{8,9},{9,8},{10,11... | collective-permute-start | bytes 786440 | tf_op jit(solution)/shard_map/ppermute | solution.py:865
  373.1 34.5 %collective-permute-start.86 = (bf16[2,32,1024]{2,1,0:T(8,128)(2,1)}, bf16[2,32,1024]{2,1,0:T(8,128)(2,1)S(1)}, u32[]{:S(2)}, u32[]{:S(2)}) collective-permute-start(bf16[2,32,1024]{2,1,0:T(8,128)(2,1)} %get-tuple-element.283), channel_id=1, source_target_pairs={{0,1},{1,0},{2,3},{3,2},{4,5},{5,4},{6,7},{7,6},{8,9},{9,8},{10,11... | collective-permute-start | bytes 393224 | tf_op jit(solution)/shard_map/ppermute | solution.py:865
  380.4 11.6 %collective-permute-start.79 = (bf16[128,1024]{1,0:T(8,128)(2,1)}, bf16[128,1024]{1,0:T(8,128)(2,1)S(1)}, u32[]{:S(2)}, u32[]{:S(2)}) collective-permute-start(bf16[128,1024]{1,0:T(8,128)(2,1)} %get-tuple-element.263), channel_id=1, source_target_pairs={{0,2},{1,3},{2,0},{3,1},{4,6},{5,7},{6,4},{7,5},{8,10},{9,11},{10,... | collective-permute-start | bytes 786440 | tf_op jit(solution)/shard_map/ppermute | solution.py:865
  380.5 17.1 %collective-permute-start.80 = (bf16[128,1024]{1,0:T(8,128)(2,1)}, bf16[128,1024]{1,0:T(8,128)(2,1)S(1)}, u32[]{:S(2)}, u32[]{:S(2)}) collective-permute-start(bf16[128,1024]{1,0:T(8,128)(2,1)} %get-tuple-element.264), channel_id=1, source_target_pairs={{0,4},{1,5},{2,6},{3,7},{4,0},{5,1},{6,2},{7,3},{8,12},{9,13},{10,... | collective-permute-start | bytes 786440 | tf_op jit(solution)/shard_map/ppermute | solution.py:865
  381.5 16.1 %collective-permute-start.81 = (bf16[128,1024]{1,0:T(8,128)(2,1)}, bf16[128,1024]{1,0:T(8,128)(2,1)}, u32[]{:S(2)}, u32[]{:S(2)}) collective-permute-start(bf16[128,1024]{1,0:T(8,128)(2,1)} %get-tuple-element.265), channel_id=1, source_target_pairs={{0,6},{1,7},{2,4},{3,5},{4,2},{5,3},{6,0},{7,1},{8,14},{9,15},{10,... | collective-permute-start | bytes 786440 | tf_op jit(solution)/shard_map/ppermute | solution.py:865
  386.1 25.1 %all-to-all-start.3 = ((bf16[32,32,384]{2,1,0:T(8,128)(2,1)}), bf16[32,32,384]{2,1,0:T(8,128)(2,1)S(1)}, u32[]{:S(2)}, u32[]{:S(2)}) async-start(bf16[32,32,384]{2,1,0:T(8,128)(2,1)} %bitcast.32), calls=%async_computation.4 | async-start | bytes 1572864 | tf_op jit(solution)/shard_map/all_to_all | solution.py:1013
  390.5 50.2 %reduce-scatter.5.cloned.1.call-start = ((), (), s32[]{:S(2)}) async-start(), calls=%async_computation.9 | async-start | bytes 655360 | tf_op jit(solution)/shard_map/reduce_scatter | solution.py:1010
  402.1 28.5 %collective-permute-start.84 = (bf16[128,1024]{1,0:T(8,128)(2,1)S(1)}, bf16[128,1024]{1,0:T(8,128)(2,1)}, u32[]{:S(2)}, u32[]{:S(2)}) collective-permute-start(bf16[128,1024]{1,0:T(8,128)(2,1)S(1)} %copy-done.21), channel_id=1, source_target_pairs={{0,6},{1,7},{2,4},{3,5},{4,2},{5,3},{6,0},{7,1},{8,14},{9,15},{10,... | collective-permute-start | bytes 786440 | tf_op jit(solution)/shard_map/ppermute | solution.py:865
  404.0 26.7 %collective-permute-start.83 = (bf16[128,1024]{1,0:T(8,128)(2,1)S(1)}, bf16[128,1024]{1,0:T(8,128)(2,1)}, u32[]{:S(2)}, u32[]{:S(2)}) collective-permute-start(bf16[128,1024]{1,0:T(8,128)(2,1)S(1)} %get-tuple-element.276), channel_id=1, source_target_pairs={{0,4},{1,5},{2,6},{3,7},{4,0},{5,1},{6,2},{7,3},{8,12},{9,13},{10,... | collective-permute-start | bytes 786440 | tf_op jit(solution)/shard_map/ppermute | solution.py:865
  406.1 24.6 %collective-permute-start.82 = (bf16[128,1024]{1,0:T(8,128)(2,1)S(1)}, bf16[128,1024]{1,0:T(8,128)(2,1)}, u32[]{:S(2)}, u32[]{:S(2)}) collective-permute-start(bf16[128,1024]{1,0:T(8,128)(2,1)S(1)} %get-tuple-element.275), channel_id=1, source_target_pairs={{0,2},{1,3},{2,0},{3,1},{4,6},{5,7},{6,4},{7,5},{8,10},{9,11},{10,... | collective-permute-start | bytes 786440 | tf_op jit(solution)/shard_map/ppermute | solution.py:865
  411.1 13.7 %all-to-all-start.5 = ((f32[32,1,672]{2,1,0:T(1,128)}), f32[32,1,672]{2,1,0:T(1,128)S(1)}, u32[]{:S(2)}, u32[]{:S(2)}) async-start(f32[32,1,672]{2,1,0:T(1,128)} %copy.102), calls=%async_computation.7 | async-start | bytes 196608 | tf_op jit(solution)/shard_map/all_to_all | solution.py:1168
  424.8 13.2 %all-to-all-start.4 = ((bf16[8,32,1024]{2,1,0:T(8,128)(2,1)}), bf16[8,32,1024]{2,1,0:T(8,128)(2,1)S(1)}, u32[]{:S(2)}, u32[]{:S(2)}) async-start(bf16[8,32,1024]{2,1,0:T(8,128)(2,1)} %bitcast.34), calls=%async_computation.6 | async-start | bytes 1048576 | tf_op jit(solution)/shard_map/all_to_all | solution.py:963
  (151 other events, 1067.4 us)
Sparse Core Ops, SparseCore 0:
  24.7 32.0 all-gather.6
  67.8 27.2 all-gather.8
  97.3 80.2 all-gather.10
  257.2 88.2 reduce-scatter.2
  409.2 24.5 reduce-scatter.4

commit v3 on v2

--- a/solution.py
+++ b/solution.py
@@ -132,11 +132,29 @@
     from_order(table, ordered, out, rows)
 
 
-def attend_back_kernel(causal, rows, size, start, table, q, k, v, log_total, weight, own, *refs):
+def split_rows(table, first, own, branch, row, keep, give):
+    row[...] = dot_c(own[...], branch[...]).astype(LOW)
+    share = keep.shape[1]
+    for core, out in ((table[first], keep), (table[first + 1], give)):
+        for n in range(2):
+            at = pl.multiple_of((2 * n + core) * share, share)
+            out[n] = row[pl.ds(at, share), :]
+
+
+def attend_back_kernel(causal, rows, size, start, lined, table, q, k, v, log_total, weight, *refs):
+    own = refs[0] if lined else None
+    refs = refs[1:] if lined else refs
     pieces, refs = refs[:INNER], refs[INNER:]
     if start is not None:
-        packed, give, keep, refs = refs[0], refs[1], refs[2], refs[3:]
-    dq, dk, dv, sums, row_keep, row_give, refs = *refs[:6], refs[6:]
+        packed, refs = refs[0], refs[1:]
+        if start == 0:
+            x_all, refs = refs[0], refs[1:]
+            give, keep, norm_sums, refs = *refs[:3], refs[3:]
+        else:
+            give, keep, refs = *refs[:2], refs[2:]
+    dq, dk, dv, sums, refs = *refs[:4], refs[4:]
+    if lined:
+        row_keep, row_give, refs = *refs[:2], refs[2:]
     qs, ks, vs, ups, dqs, dks, dvs, branch, row, marks = refs
     copies = pull(pieces, 0, branch, marks)
     span, keys = q.shape[0], k.shape[0]
@@ -150,12 +168,8 @@
     for place in range(INNER):
         at = pl.multiple_of((table[0] ^ offset_of(place)) * rows, rows)
         ups[pl.ds(at, rows), :] = upstream[place * rows : (place + 1) * rows, :]
-    row[...] = dot_c(own[...], branch[...]).astype(LOW)
-    share = row_keep.shape[1]
-    for core, out in ((table[8], row_keep), (table[9], row_give)):
-        for n in range(2):
-            first = pl.multiple_of((2 * n + core) * share, share)
-            out[n] = row[pl.ds(first, share), :]
+    if lined:
+        split_rows(table, 8, own, branch, row, row_keep, row_give)
     dks[...] = jnp.zeros_like(dks)
     dvs[...] = jnp.zeros_like(dvs)
     for step in range(span // STEP):
@@ -208,13 +222,27 @@
                 total_dq = lax.fori_loop(0, chunks, absorb, total_dq)
         dqs[lo : lo + STEP, :] = total_dq * scale
     from_order(table, dqs, dq, rows)
-    if start is not None:
-        half = span // 2
-        back = packed[:, start * LANES : (start + 1) * LANES]
-        give[...] = dot_t(dq[half:, :], back).astype(LOW)
-        keep[...] = dot_t(dq[:half, :], back)
     from_order(table, dks, dk, rows)
     from_order(table, dvs, dv, rows)
+    if start is not None:
+        kinds = 3 if start == 0 else 1
+        back = packed[:, start * LANES : (start + kinds) * LANES]
+        first = second = None
+        for at, out in ((span // 2, give), (0, keep)):
+            at = slice(at, at + span // 2)
+            left = [part[at, :] for part in (dq, dk, dv)[:kinds]]
+            left = left[0] if kinds == 1 else jnp.concatenate(left, axis=1)
+            slope = dot_t(left, back)
+            out[...] = slope.astype(out.dtype)
+            if start == 0:
+                centred, inverse = centre(x_all[at, :].astype(WIDE))
+                gain = jnp.sum(slope * (centred * inverse), axis=0, keepdims=True)
+                shift = jnp.sum(slope, axis=0, keepdims=True)
+                first = gain if first is None else first + gain
+                second = shift if second is None else second + shift
+        if start == 0:
+            norm_sums[0:1, :] = first
+            norm_sums[1:2, :] = second
     sums[0:1, :] = jnp.sum(dqs[...].astype(LOW).astype(WIDE), axis=0, keepdims=True)
     sums[1:2, :] = jnp.sum(dvs[...].astype(LOW).astype(WIDE), axis=0, keepdims=True)
 
@@ -233,17 +261,6 @@
         source = pieces[place].at[pl.ds(index * rows, rows), :]
         aim = target.at[pl.ds(place * rows, rows), :]
         copies.append(pltpu.make_async_copy(source, aim, marks.at[place]))
-    for copy in copies:
-        copy.start()
-    return copies
-
-
-def settle(planes, table, first, target, marks):
-    rows = planes[0].shape[0]
-    copies = []
-    for n, plane in enumerate(planes):
-        at = pl.multiple_of(table[first + n], 16)
-        copies.append(pltpu.make_async_copy(plane, target.at[pl.ds(at, rows), :], marks.at[n]))
     for copy in copies:
         copy.start()
     return copies
@@ -291,25 +308,26 @@
     keys = k.shape[0]
     width = weight.shape[1]
     part = jax.ShapeDtypeStruct((2, pair // 4, width), LOW)
+    lined = [] if own is None else [own]
     spread_shape = (
         jax.ShapeDtypeStruct((span // 2, width), LOW),
         jax.ShapeDtypeStruct((span // 2, width), WIDE),
     )
-    start, packed = back if back else (None, None)
-    extra = [packed] if back else []
-    return pl.pallas_call(
-        functools.partial(attend_back_kernel, causal, rows, pair // 2, start),
+    start, *extra = back if back else (None,)
+    if start == 0:
+        spread_shape += (jax.ShapeDtypeStruct((2, width), WIDE),)
+    return pl.pallas_call(
+        functools.partial(attend_back_kernel, causal, rows, pair // 2, start, bool(lined)),
         out_shape=(spread_shape if back else ())
         + (
             jax.ShapeDtypeStruct((span, pair), LOW),
             jax.ShapeDtypeStruct((keys, pair), LOW),
             jax.ShapeDtypeStruct((keys, pair), LOW),
             jax.ShapeDtypeStruct((2, pair), WIDE),
-            part,
-            part,
-        ),
-        in_specs=[SMEM] + [VMEM] * 6 + [HBM] * INNER + [VMEM] * len(extra),
-        out_specs=(VMEM,) * (8 if back else 6),
+        )
+        + ((part, part) if lined else ()),
+        in_specs=[SMEM] + [VMEM] * (5 + len(lined)) + [HBM] * INNER + [VMEM] * len(extra),
+        out_specs=(VMEM,) * (4 + 2 * len(lined) + (len(spread_shape) if back else 0)),
         scratch_shapes=[
             pltpu.VMEM((span, pair), LOW),
             pltpu.VMEM((keys, pair), LOW),
@@ -324,7 +342,7 @@
         ],
         compiler_params=room(60),
         cost_estimate=cost(10),
-    )(table, q, k, v, log_total, weight, own, *pieces, *extra)
+    )(table, q, k, v, log_total, weight, *lined, *pieces, *extra)
 
 
 def centre(value):
@@ -339,12 +357,13 @@
     return (centred * inverse * gain + shift).astype(LOW)
 
 
-def enter_kernel(kinds, table, *refs):
+def enter_kernel(kinds, table, far, *refs):
     pieces, refs = refs[:INNER], refs[INNER:]
-    planes, refs = refs[:-9], refs[-9:]
-    q, k, v, h, params, biases, packed, x_all, marks = refs
-    copies = pull(pieces, 0, x_all, marks.at[0])
-    finish(settle(planes, table, 2, packed, marks.at[1]))
+    q, k, v, h, params, biases, packed, x_all, marks, mark = refs
+    load = pltpu.make_async_copy(far.at[:, pl.ds(0, packed.shape[1])], packed, mark)
+    load.start()
+    copies = pull(pieces, 0, x_all, marks)
+    load.wait()
     edge = kinds * LANES
     extra = packed[:, edge : edge + LANES].astype(WIDE)
     params[...] = jnp.transpose(extra)[:16, :]
@@ -363,9 +382,8 @@
         v[at, :] = (made[:, 2 * LANES :] + biases[7:8, :]).astype(LOW)
 
 
-def enter(table, rows, pieces, planes):
+def enter(table, rows, pieces, packed):
     width = pieces[0].shape[1]
-    lanes = planes[0].shape[1]
     span = rows * INNER
     heads = jax.ShapeDtypeStruct((span, LANES), LOW)
     return pl.pallas_call(
@@ -377,17 +395,15 @@
             jax.ShapeDtypeStruct((span, width), LOW),
             jax.ShapeDtypeStruct((16, width), WIDE),
             jax.ShapeDtypeStruct((16, LANES), WIDE),
-            jax.ShapeDtypeStruct((width, lanes), LOW),
+            jax.ShapeDtypeStruct((width, 4 * LANES), LOW),
             jax.ShapeDtypeStruct((span, width), LOW),
         ),
-        in_specs=[SMEM] + [HBM] * (INNER + len(planes)),
+        in_specs=[SMEM] + [HBM] * (1 + INNER),
         out_specs=(VMEM,) * 8,
-        scratch_shapes=[
-            pltpu.SemaphoreType.DMA((2, INNER)),
-        ],
-        compiler_params=room(32),
-        cost_estimate=cost(3),
-    )(table, *pieces, *planes)
+        scratch_shapes=[pltpu.SemaphoreType.DMA((INNER,)), pltpu.SemaphoreType.DMA],
+        compiler_params=room(60),
+        cost_estimate=cost(4),
+    )(table, packed, *pieces)
 
 
 def join_kernel(vector, first, query, *refs):
@@ -540,31 +556,56 @@
     )(h, bias, packed, *pieces)
 
 
-def feed_out_kernel(act, packed, give, keep, second, marks):
-    finish(load_rows(packed, second.shape[1] // packed.shape[0], second, marks))
-    half = keep.shape[0]
-    give[...] = dot_n(act[half:, :], second[...]).astype(LOW)
-    keep[...] = dot_n(act[:half, :], second[...])
-
-
-def feed_out(act, packed):
+def side_kernel(act, packed, dk, dv, pair_weight, give, keep, second, marks):
+    copies = load_rows(packed, second.shape[1] // packed.shape[0], second, marks)
+    half, width = keep.shape[0], second.shape[1]
+    weight = pair_weight[:, : 2 * LANES]
+    spans = ((half, give), (0, keep))
+    for at, out in spans:
+        left = jnp.concatenate([dk[at : at + half, :], dv[at : at + half, :]], axis=1)
+        out[:, width:] = dot_t(left, weight).astype(out.dtype)
+    finish(copies)
+    for at, out in spans:
+        out[:, :width] = dot_n(act[at : at + half, :], second[...]).astype(out.dtype)
+
+
+def side_out(act, packed, dk, dv, pair_weight):
     span, hidden = act.shape
     shares, _, width = packed.shape
     return pl.pallas_call(
-        feed_out_kernel,
+        side_kernel,
         out_shape=(
-            jax.ShapeDtypeStruct((span // 2, width), LOW),
-            jax.ShapeDtypeStruct((span // 2, width), WIDE),
+            jax.ShapeDtypeStruct((span // 2, 2 * width), LOW),
+            jax.ShapeDtypeStruct((span // 2, 2 * width), WIDE),
         ),
-        in_specs=[VMEM, HBM],
+        in_specs=[VMEM, HBM] + [VMEM] * 3,
         out_specs=(VMEM,) * 2,
         scratch_shapes=[
             pltpu.VMEM((hidden, width), LOW),
             pltpu.SemaphoreType.DMA((shares,)),
         ],
         compiler_params=room(24),
-        cost_estimate=cost(3),
-    )(act, packed)
+        cost_estimate=cost(4),
+    )(act, packed, dk, dv, pair_weight)
+
+
+def side_sum_kernel(own, one, two, three, y, params, layer, source):
+    total = own[...] + one[...].astype(WIDE) + two[...].astype(WIDE) + three[...].astype(WIDE)
+    width = y.shape[1]
+    layer[...] = (y[...] + total[:, :width] + params[12:13, :]).astype(LOW)
+    source[...] = total[:, width:].astype(LOW)
+
+
+def side_sum(own, parts, y, params):
+    out = jax.ShapeDtypeStruct(y.shape, LOW)
+    return pl.pallas_call(
+        side_sum_kernel,
+        out_shape=(out, out),
+        in_specs=[VMEM] * 6,
+        out_specs=(VMEM,) * 2,
+        compiler_params=room(16),
+        cost_estimate=cost(1),
+    )(own, *parts, y, params)
 
 
 def feed_grad_kernel(act, slope, h, up, out):
@@ -645,43 +686,17 @@
     )(own, *parts, value, base, params)
 
 
-def spread_kernel(start, *refs):
-    values, packed, give, keep = refs[:-3], refs[-3], refs[-2], refs[-1]
-    half = keep.shape[0]
-    weight = packed[:, start * LANES : (start + len(values)) * LANES]
-    for at, out in ((half, give), (0, keep)):
-        left = [value[at : at + half, :] for value in values]
-        left = left[0] if len(left) == 1 else jnp.concatenate(left, axis=1)
-        out[...] = dot_t(left, weight).astype(out.dtype)
-
-
-def spread(start, values, packed):
-    span, width = values[0].shape[0], packed.shape[0]
-    return pl.pallas_call(
-        functools.partial(spread_kernel, start),
-        out_shape=(
-            jax.ShapeDtypeStruct((span // 2, width), LOW),
-            jax.ShapeDtypeStruct((span // 2, width), WIDE),
-        ),
-        in_specs=[VMEM] * (len(values) + 1),
-        out_specs=(VMEM,) * 2,
-        compiler_params=room(24),
-        cost_estimate=cost(2),
-    )(*values, packed)
-
-
-def pair_kernel(table, biases, *refs):
-    pieces, refs = refs[:INNER], refs[INNER:]
-    planes, (states, k, v, packed, marks) = refs[:-5], refs[-5:]
-    copies = pull(pieces, 0, states, marks.at[0])
-    finish(settle(planes, table, 2, packed, marks.at[1]))
-    finish(copies)
+def pair_kernel(biases, far, *refs):
+    pieces, (states, k, v, packed, marks, mark) = refs[:INNER], refs[INNER:]
+    load = pltpu.make_async_copy(far.at[:, pl.ds(0, packed.shape[1])], packed, mark)
+    load.start()
+    finish(pull(pieces, 0, states, marks) + [load])
     made = dot_n(states[...], packed[:, : 2 * LANES])
     k[...] = made[:, :LANES].astype(LOW)
     v[...] = (made[:, LANES:] + biases[10:11, :]).astype(LOW)
 
 
-def pair_heads(table, rows, pieces, planes, biases):
+def pair_heads(rows, pieces, packed, biases):
     width = pieces[0].shape[1]
     span = rows * INNER
     heads = jax.ShapeDtypeStruct((span, LANES), LOW)
@@ -691,14 +706,14 @@
             jax.ShapeDtypeStruct((span, width), LOW),
             heads,
             heads,
-            jax.ShapeDtypeStruct((width, planes[0].shape[1]), LOW),
+            jax.ShapeDtypeStruct((width, 3 * LANES), LOW),
         ),
-        in_specs=[SMEM, VMEM] + [HBM] * (INNER + len(planes)),
+        in_specs=[VMEM] + [HBM] * (1 + INNER),
         out_specs=(VMEM,) * 4,
-        scratch_shapes=[pltpu.SemaphoreType.DMA((2, INNER))],
-        compiler_params=room(24),
+        scratch_shapes=[pltpu.SemaphoreType.DMA((INNER,)), pltpu.SemaphoreType.DMA],
+        compiler_params=room(60),
         cost_estimate=cost(3),
-    )(table, biases, *pieces, *planes)
+    )(biases, packed, *pieces)
 
 
 def spread_self_kernel(dq, dk, dv, packed, x_all, give, keep, sums):
@@ -735,39 +750,78 @@
     )(dq, dk, dv, packed, x_all)
 
 
-def home_kernel(got, out):
-    kinds = got.shape[2] // LANES
-    groups = got.shape[0] // INNER
+def spread_columns(got, kinds, out):
     size = LANES // 2
-    total = []
-    for place in range(INNER):
-        running = got[place].astype(WIDE)
-        for n in range(1, groups):
-            running = running + got[n * INNER + place].astype(WIDE)
-        total.append(running)
     for kind in range(kinds):
         heads = {}
         for place in range(INNER):
             for n in (0, 1):
                 at = kind * LANES + n * size
                 number = (2 * (place & 1) + n) * (INNER // 2) + (place >> 1)
-                heads[number] = total[place][:, at : at + size]
+                heads[number] = got[place][:, at : at + size].astype(WIDE)
         for number in range(0, 2 * INNER, 2):
             at = kind * INNER * LANES + number * size
             both = jnp.concatenate([heads[number], heads[number + 1]], axis=1)
             out[:, at : at + LANES] = both
 
 
-def home_columns(got):
-    rows, lanes = got.shape[1:]
-    return pl.pallas_call(
-        home_kernel,
-        out_shape=jax.ShapeDtypeStruct((rows, lanes * INNER), WIDE),
-        in_specs=[VMEM],
-        out_specs=VMEM,
+def spread_rows(packed, start, out):
+    share = out.shape[0]
+    for place in range(INNER):
+        block = packed[place * share : (place + 1) * share, start : start + LANES]
+        out[:, place * LANES : (place + 1) * LANES] = block.astype(WIDE)
+
+
+def home_kernel(kinds, got, packed, columns, rows):
+    spread_columns(got, kinds, columns)
+    spread_rows(packed, kinds * LANES, rows)
+
+
+def home(got, packed):
+    share, lanes = got.shape[1:]
+    return pl.pallas_call(
+        functools.partial(home_kernel, lanes // LANES),
+        out_shape=(
+            jax.ShapeDtypeStruct((share, lanes * INNER), WIDE),
+            jax.ShapeDtypeStruct((share, LANES * INNER), WIDE),
+        ),
+        in_specs=[VMEM] * 2,
+        out_specs=(VMEM,) * 2,
         compiler_params=room(16),
         cost_estimate=cost(2),
-    )(got)
+    )(got, packed)
+
+
+def home_feed_kernel(kinds, hidden, got, packed, feed_sum, *outs):
+    columns, rows, first, second = outs
+    spread_columns(got, kinds, columns)
+    spread_rows(packed, kinds * LANES, rows)
+    width = second.shape[1]
+    second[...] = feed_sum[:, :width].astype(WIDE)
+    lanes = got.shape[2] - kinds * LANES
+    for n in range(lanes // hidden):
+        for place in range(INNER):
+            at = (n * INNER + place) * hidden
+            start = kinds * LANES + n * hidden
+            first[:, at : at + hidden] = got[place, :, start : start + hidden].astype(WIDE)
+
+
+def home_feed(kinds, hidden, got, packed, feed_sum):
+    share, lanes = got.shape[1:]
+    rows = jax.ShapeDtypeStruct((share, LANES * INNER), WIDE)
+    return pl.pallas_call(
+        functools.partial(home_feed_kernel, kinds, hidden),
+        out_shape=(
+            jax.ShapeDtypeStruct((share, kinds * LANES * INNER), WIDE),
+            rows,
+            jax.ShapeDtypeStruct((share, (lanes - kinds * LANES) * INNER), WIDE),
+            jax.ShapeDtypeStruct((feed_sum.shape[0], LANES * INNER), WIDE),
+        ),
+        in_specs=[VMEM] * 3,
+        out_specs=(VMEM,) * 4,
+        compiler_params=room(24),
+        cost_estimate=cost(3),
+    )(got, packed, feed_sum)
 
 
 def column_part_kernel(kinds, *refs):
@@ -839,25 +893,32 @@
     )(table, own, took)
 
 
-def stack_kernel(table, *refs):
-    pairs, out = refs[:-1], refs[-1]
-    rows = pairs[0].shape[1]
-    for n in range(len(pairs) // 2):
-        at = slice(n * rows, (n + 1) * rows)
-        for first, value in ((table[0], pairs[2 * n]), (table[1], pairs[2 * n + 1])):
-            out[pl.ds(first, 2), at, :] = value[...]
-
-
-def stack(table, *pairs):
-    _, rows, width = pairs[0].shape
-    return pl.pallas_call(
-        stack_kernel,
-        out_shape=jax.ShapeDtypeStruct((4, rows * len(pairs) // 2, width), LOW),
-        in_specs=[SMEM] + [VMEM] * len(pairs),
+def pack_kernel(table, columns, *refs):
+    rows, out = refs[:-1], refs[-1]
+    lanes = columns.shape[1]
+    out[:, :lanes] = columns[...]
+    share = rows[0].shape[1]
+    for kind in range(len(rows) // 2):
+        for first, value in ((table[0], rows[2 * kind]), (table[1], rows[2 * kind + 1])):
+            for n in range(2):
+                for place in range(INNER):
+                    at = pl.multiple_of(((first + n) * INNER + place) * share, share)
+                    start = lanes + kind * LANES
+                    block = value[n, :, place * LANES : (place + 1) * LANES]
+                    out[pl.ds(at, share), start : start + LANES] = block
+
+
+def pack(table, columns, *rows):
+    width, lanes = columns.shape
+    lanes += LANES * len(rows) // 2
+    return pl.pallas_call(
+        pack_kernel,
+        out_shape=jax.ShapeDtypeStruct((width, lanes), LOW),
+        in_specs=[SMEM] + [VMEM] * (1 + len(rows)),
         out_specs=VMEM,
         compiler_params=room(16),
-        cost_estimate=cost(1),
-    )(table, *pairs)
+        cost_estimate=cost(2),
+    )(table, columns, *rows)
 
 
 def hop(value, distance):
@@ -869,9 +930,12 @@
     return lax.optimization_barrier((value,) + others)[0]
 
 
-def gather_places(own):
+def gather_places(own, *filler):
     near = [own] + [hop(own, offset_of(place)) for place in (1, 2, 3)]
-    return near + [hop(piece, 1) for piece in near]
+    if filler:
+        near, filler = lax.optimization_barrier((near, filler))
+    pieces = near + [hop(piece, 1) for piece in near]
+    return (pieces, *filler) if filler else pieces
 
 
 def scatter_start(give, keep):
@@ -937,8 +1001,7 @@
         head_at = [(2 * core + n) * (width // shares) + chip * size for n in (0, 1)]
     else:
         head_at = [here * pair + n * size for n in (0, 1)]
-    plane_at = [jnp.zeros((), jnp.int32)]
-    head_table = jnp.stack(head_at + plane_at).astype(jnp.int32)
+    head_table = jnp.stack(head_at).astype(jnp.int32)
 
     def by_device(value):
         lead = value.shape[:-1]
@@ -994,29 +1057,29 @@
             )
         return jnp.concatenate(cut, axis=1)
 
-    def row_grads(keep, give, pieces, branch):
+    def row_grads(parts, pieces, branch):
         if not matched:
             grad = under(shard_features(pieces), jnp.concatenate(branch, axis=0))
             return [grad.astype(LOW).reshape(shares, share, width)]
-        return [keep, hop(give, 1)]
-
-    def rows_stack(*parts):
-        if not matched:
-            return jnp.concatenate([part[0] for part in parts], axis=1)
-        return stack(core_table, *parts[0], *parts[1])
-
-    def rows_home(row):
-        row = row.reshape(shares * row.shape[1], width)
-        return lax.psum_scatter(row, OUTER, scatter_dimension=0, tiled=True).astype(WIDE)
-
-    def column_send(grad):
-        return lax.all_to_all(grad.reshape(devices, share, -1), ALL, 0, 0)
-
-    def column_home(got):
+        return [parts[0], hop(parts[1], 1)]
+
+    def pack_grads(columns, *rows):
         if matched:
-            return home_columns(got)
-        total = jnp.sum(got.astype(WIDE).reshape(shares, INNER, share, -1, pair), axis=0)
-        return jnp.transpose(total, (1, 2, 0, 3)).reshape(share, -1)
+            return pack(core_table, columns, *[part for parts in rows for part in parts])
+        lined = [
+            jnp.transpose(parts[0].reshape(shares, share, INNER, LANES), (0, 2, 1, 3))
+            for parts in rows
+        ]
+        return jnp.concatenate([columns] + [r.reshape(width, LANES) for r in lined], axis=1)
+
+    def lanes_to_columns(got):
+        kinds = got.shape[2] // pair
+        got = got.reshape(INNER, share, kinds, pair).astype(WIDE)
+        return jnp.transpose(got, (1, 2, 0, 3)).reshape(share, kinds * width)
+
+    def lanes_to_rows(packed, start):
+        rows = packed[:, start : start + LANES].reshape(INNER, share, LANES).astype(WIDE)
+        return jnp.transpose(rows, (1, 0, 2)).reshape(share, width)
 
     small = jnp.concatenate([jnp.transpose(vectors), hidden_bias.reshape(share, -1)], axis=1)
     extras = small.shape[1]
@@ -1027,29 +1090,23 @@
     def over(value):
         return lax.all_gather(value, OUTER, axis=0)
 
-    def planes_of(value):
-        return [over(value).reshape(width, -1)]
-
     def row_lanes(weight):
         return jnp.transpose(weight.reshape(-1, INNER, LANES), (1, 0, 2))
 
-    self_cut = jnp.concatenate([cut_columns(self_in), small], axis=2)
-    self_mine = exchange(self_cut)
-    self_planes = planes_of(jnp.concatenate([self_mine, row_lanes(self_out)], axis=2))
-    pieces = gather_places(after(target[0], self_mine))
-    cut = [cut_columns(cross_kv, cross_query), first_cut]
-    states = gather_places(after(source[0], *pieces[1:4]))
-    cut = exchange(after(jnp.concatenate(cut, axis=2), *states[1:4]))
-    cross_mine = jnp.concatenate([cut[:, :, : 3 * pair], row_lanes(cross_out)], axis=2)
-    cross_planes = planes_of(after(cross_mine, self_planes))
-    first_mine = cut[:, :, 3 * pair :].reshape(INNER * share, -1)
+    mine = exchange(jnp.concatenate([cut_columns(self_in), small], axis=2))
+    self_far = over(jnp.concatenate([mine, row_lanes(self_out)], axis=2)).reshape(width, -1)
+    pieces = gather_places(after(target[0], mine))
+    other = [cut_columns(cross_kv, cross_query), first_cut]
+    other = exchange(after(jnp.concatenate(other, axis=2), *pieces[1:4]))
+    states = gather_places(after(source[0], other))
+    cross_far = jnp.concatenate([other[:, :, : 3 * pair], row_lanes(cross_out)], axis=2)
+    cross_far = over(after(cross_far, self_far)).reshape(width, -1)
+    first_mine = other[:, :, 3 * pair :].reshape(INNER * share, -1)
     feed_mine = jnp.concatenate([first_mine, mlp_out], axis=0)
-    feed_packed = over(after(feed_mine, self_planes))
-
-    q, k, v, h1, params, biases, self_packed, x_all = enter(
-        head_table, rows, pieces, self_planes
-    )
-    sout_mine, w_sout = head_rows(self_out, after(self_packed, q)[:, 4 * pair :])
+    feed_packed = over(after(feed_mine, self_far))
+
+    q, k, v, h1, params, biases, self_packed, x_all = enter(head_table, rows, pieces, self_far)
+    sout_mine, w_sout = head_rows(self_out, after(self_far, q, *states[1:4])[:, 4 * pair :])
     q = after(q, *w_sout[1:4])
     h_bias = self_packed.reshape(shares, INNER, share, -1)
     h_bias = h_bias[..., 3 * pair + count : 3 * pair + extras]
@@ -1066,13 +1123,14 @@
     k, v = stream_keys(k), stream_keys(v)
     att, self_total = attend(self_table, q, k, v, rows, True)
     att = gather_places(att)
-    states, ck, cv, cross_packed = pair_heads(head_table, rows, states, cross_planes, biases)
+    states, ck, cv, cross_packed = pair_heads(rows, states, cross_far, biases)
     ck, cv = stream_keys(ck), stream_keys(cv)
     y1, h2, y1_all, cq = join_self(att, w_sout, x_all, params, cross_packed, biases)
-    cout_mine, w_cout = head_rows(cross_out, after(cross_packed, *att[1:4])[:, 3 * pair :])
+    cout_mine, w_cout = head_rows(cross_out, after(cross_far, *att[1:4])[:, 3 * pair :])
+    pull_up = gather_places(after(cotangent[0], *w_cout[1:4]))
+    cq = after(cq, *w_cout[1:4])
     catt, cross_total = attend(cross_table, cq, ck, cv, rows, False)
-    catt = gather_places(catt)
-    pull_up = gather_places(after(cotangent[0], *w_cout[1:4]))
+    catt = gather_places(after(catt, *pull_up[1:4]))
     y2, h3 = join_cross(catt, w_cout, y1_all, y1, params)
     active, before_grad, give, keep, h_bias_grad, up = feed(h3, h_bias, feed_packed, pull_up)
     third_own, third_parts = scatter_places(give, keep)
@@ -1083,9 +1141,7 @@
         4, third_own, third_parts, y2, cotangent[0], params
     )
     cross_all = gather_places(cross_branch)
-    fed_own, *fed_parts = scatter_start(*feed_out(after(active, cross_all[1]), feed_packed))
-    cross_all, fed_own, fed_parts = lax.optimization_barrier((cross_all, fed_own, fed_parts))
-    give, keep, dcq, dck, dcv, cross_sums, row_keep, row_give = attend_back(
+    give, keep, dcq, dck, dcv, cross_sums, *cross_rows = attend_back(
         cross_table,
         cq,
         ck,
@@ -1098,53 +1154,48 @@
         False,
         (2, cross_packed),
     )
-    cross_rows = (row_keep, row_give)
-    fed_parts = scatter_finish(fed_parts)
-    give, fed_parts = lax.optimization_barrier((give, fed_parts))
-    fed = fed_own + sum(part.astype(WIDE) for part in fed_parts)
-    layer_out = (y2 + fed + params[12]).astype(LOW)[None]
     dck, dcv = own_keys(dck), own_keys(dcv)
     second_own, second_parts = scatter_places(give, keep)
     cross_grad = column_part((after(states, second_own), (dck, dcv)), (h2, (dcq,)))
-    source_give, source_keep = spread(0, [after(dck, second_own), dcv], cross_packed)
-    second_parts, cross_grad, source_give, source_keep = lax.optimization_barrier(
-        (second_parts, cross_grad, source_give, source_keep)
-    )
-    cross_got = column_send(cross_grad)
-    cross_rows = row_grads(*cross_rows, catt, cross_all)
+    side_give, side_keep = side_out(
+        after(active, second_own), feed_packed, dck, dcv, cross_packed
+    )
+    second_parts, cross_grad, side_give, side_keep = lax.optimization_barrier(
+        (second_parts, cross_grad, side_give, side_keep)
+    )
+    cross_rows = row_grads(cross_rows, catt, cross_all)
     middle_grad, self_branch, middle_sums = norm_back(
         2, second_own, second_parts, y1, late_grad, params
     )
-    self_all = gather_places(self_branch)
-    source_own, *source_parts = scatter_start(after(source_give, self_all[1]), source_keep)
-    self_all, source_own, source_parts, cross_got = lax.optimization_barrier(
-        (self_all, source_own, source_parts, cross_got)
-    )
-    dq, dk, dv, self_sums, row_keep, row_give = attend_back(
-        self_table, q, k, v, self_total, sout_mine, att[0], self_all, rows, True
-    )
+    packed_grad = pack_grads(cross_grad, cross_rows)
+    side_own, *side_parts = scatter_start(after(side_give, self_branch), side_keep)
+    self_all, packed_grad, side_own, side_parts = gather_places(
+        self_branch, packed_grad, side_own, side_parts
+    )
+    self_all, mlp_home, packed_grad, side_parts = lax.optimization_barrier(
+        (self_all, mlp_home, packed_grad, side_parts)
+    )
+    side_parts = scatter_finish(side_parts)
+    cross_sum = lax.psum_scatter(packed_grad, OUTER, scatter_dimension=0, tiled=True)
+    made = attend_back(
+        self_table,
+        q,
+        k,
+        v,
+        self_total,
+        sout_mine,
+        att[0],
+        self_all,
+        rows,
+        True,
+        (0, self_packed, x_all) if groups == 1 else None,
+    )
+    dq, dk, dv, self_sums, *self_rows = made[-6:]
     dk, dv = own_keys(dk), own_keys(dv)
-    give, keep, target_sums = spread_self(dq, dk, dv, self_packed, x_all)
-    first_own, first_parts = scatter_places(give, keep)
-    self_grad = column_part((after(h1, first_own), (dq, dk, dv)))
-    self_got = column_send(self_grad)
-    target_grad, target_low, _ = norm_back(
-        0, first_own, first_parts, target[0], middle_grad, params
-    )
-    source_parts, row_give, mlp_home, self_sums = lax.optimization_barrier(
-        (source_parts, row_give, mlp_home, self_sums, first_parts)
-    )[:4]
-    self_rows = row_grads(row_keep, row_give, att, self_all)
-    out_home = rows_home(rows_stack(self_rows, cross_rows))
-    source_parts = scatter_finish(source_parts)
-    source_grad = source_own + sum(part.astype(WIDE) for part in source_parts)
-    second_home, first_home = mlp_home[:, :width], mlp_home[:, width:]
-    first_home = exchange(first_home.reshape(INNER, share, shares * hidden))
-    first_home = first_home.reshape(INNER, share, shares, hidden)
-    first_home = jnp.transpose(first_home, (1, 2, 0, 3)).reshape(share, -1)
-    cross_home = column_home(cross_got)
-    self_home = column_home(self_got)
-
+    if groups == 1:
+        give, keep, target_sums = made[:3]
+    else:
+        give, keep, target_sums = spread_self(dq, dk, dv, self_packed, x_all)
     head_sums = jnp.concatenate([self_sums, cross_sums])[:, None]
     head_sums = lax.dynamic_update_slice_in_dim(
         jnp.zeros((4, INNER, pair), WIDE), head_sums, here, 1
@@ -1165,19 +1216,51 @@
         jnp.zeros((shares, INNER, hidden), WIDE), h_bias_grad.reshape(shares, 1, hidden), here, 1
     ).reshape(devices, hidden)
     tiny = jnp.concatenate([vector_part.reshape(devices, -1), bias_part], axis=1)
-    tiny = jnp.sum(lax.all_to_all(tiny, ALL, 0, 0, tiled=True), axis=0)
+    tiny = lax.all_to_all(tiny, ALL, 0, 0, tiled=True)
+    give, side_parts, tiny = lax.optimization_barrier((give, side_parts, tiny))
+    tiny = jnp.sum(after(tiny, give), axis=0)
+    first_own, *first_parts = scatter_start(give, keep)
+    first_parts = scatter_finish(first_parts)
+    self_grad = column_part((after(h1, first_own), (dq, dk, dv)))
+    self_rows = row_grads((self_rows[0], after(self_rows[1], first_own)), att, self_all)
+    packed_grad = pack_grads(self_grad, self_rows)
+    self_sum = lax.psum_scatter(packed_grad, OUTER, scatter_dimension=0, tiled=True)
+    target_grad, target_low, _ = norm_back(
+        0, first_own, first_parts, target[0], middle_grad, params
+    )
+    side_own, mlp_home, cross_sum = lax.optimization_barrier(
+        (side_own, mlp_home, cross_sum, first_parts)
+    )[:3]
+    layer_out, source_grad = side_sum(side_own, side_parts, y2, params)
+    cross_lanes = cross_sum[:, : 3 * pair].reshape(INNER, share, -1)
+    first_lanes = mlp_home[:, width:].reshape(INNER, share, -1)
+    cross_got = exchange(jnp.concatenate([cross_lanes, first_lanes], axis=2))
+    self_got = exchange(self_sum[:, : 3 * pair].reshape(INNER, share, -1))
+    if matched:
+        cross_home, cout_home, first_home, second_home = home_feed(
+            3, hidden, cross_got, cross_sum, mlp_home
+        )
+        self_home, sout_home = home(self_got, self_sum)
+    else:
+        cross_home = lanes_to_columns(cross_got[:, :, : 3 * pair])
+        first_home = cross_got[:, :, 3 * pair :].reshape(INNER, share, shares, hidden)
+        first_home = jnp.transpose(first_home, (1, 2, 0, 3)).reshape(share, -1).astype(WIDE)
+        second_home = mlp_home[:, :width].astype(WIDE)
+        cout_home = lanes_to_rows(cross_sum, 3 * pair)
+        sout_home = lanes_to_rows(self_sum, 3 * pair)
+        self_home = lanes_to_columns(self_got)
 
     return (
-        layer_out,
+        layer_out[None],
         target_low[None],
-        source_grad.astype(LOW)[None],
+        source_grad[None],
         self_home,
-        out_home[:share],
+        sout_home,
         cross_home[:, 2 * width :],
         cross_home[:, : 2 * width],
-        out_home[share:],
-        first_home.astype(WIDE),
-        second_home.astype(WIDE),
+        cout_home,
+        first_home,
+        second_home,
         tiny[: count * share].reshape(count, share),
         tiny[count * share :],
     )

time: 451 us -> 382 us (0.85)
  waiting for transfers between devices: 153 us -> 118 us
  local copies, waits for them, and re-layouts: 69.7 us -> 42.5 us
  starting transfers between devices: 86.6 us -> 72.4 us
  blocking collectives: 0 us -> 12.7 us
  other arithmetic: 14.4 us -> 8.26 us
    ppermute x87 -> x83, waiting for transfers between devices: 121 us -> 90 us  [hop(): return lax.ppermute(value, 'inner', route)]
    unnamed x244 -> x230, local copies, waits for them, and re-layouts: 53.5 us -> 25.4 us
    all_to_all x3 -> x0, starting transfers between devices: 14.3 us -> none  [the longest x2 9.29 us: column_send(): return lax.all_to_all(grad.reshape(devices, share, -1), ALL, 0, 0)]
    all_to_all x0 -> x1, blocking collectives: none -> 12.7 us  [per_device(): tiny = lax.all_to_all(tiny, ALL, 0, 0, tiled=True)]
    pallas_call x1, Pallas kernels: 18.8 us -> 8.61 us  [join_cross(): pl.pallas_call(functools.partial(join_kernel, 11, 4, None), out_shape=(ja...]
    all_to_all x3 -> x0, waiting for transfers between devices: 7.07 us -> none  [the longest x1 6.15 us: per_device(): tiny = jnp.sum(lax.all_to_all(tiny, ALL, 0, 0, tiled=True), axis=0)]
    ppermute x87 -> x83, starting transfers between devices: 59.7 us -> 55.9 us  [hop(): return lax.ppermute(value, 'inner', route)]
    all_to_all x3 -> x4, starting transfers between devices: 12.2 us -> 15.7 us  [exchange(): return lax.all_to_all(value, 'inner', 0, 0)]
  transfers between devices with their start and end apart: 98 -> 93, of which waited for: 31 -> 36; matrix products, arithmetic and copies ran while one was open for 6% -> 5% of each run, Pallas kernels for 21% -> 25%
where the time goes in v3:
time: 382 us; the launch traced here: 377 us
  waiting for transfers between devices  118 us (31%)
  Pallas kernels  107 us (28%)
  starting transfers between devices  72.4 us (19%)
  local copies, waits for them, and re-layouts  42.5 us (11%)
  between operations  15.8 us (4%)
  blocking collectives  12.7 us (3%)
  other arithmetic  8.26 us (2%)
    ppermute x83, waiting for transfers between devices, hop(): return lax.ppermute(value, 'inner', route)  90 us
    ppermute x83, starting transfers between devices, hop(): return lax.ppermute(value, 'inner', route)  55.9 us
    pallas_call x2, Pallas kernels, attend_back(): pl.pallas_call(functools.partial(attend_back_kernel, causal, rows, pair /...  28.6 us
    unnamed x230, local copies, waits for them, and re-layouts  25.4 us
    all_to_all x4, waiting for transfers between devices, exchange(): return lax.all_to_all(value, 'inner', 0, 0)  24.1 us
    all_to_all x4, starting transfers between devices, exchange(): return lax.all_to_all(value, 'inner', 0, 0)  15.7 us
    all_to_all x1, blocking collectives, per_device(): tiny = lax.all_to_all(tiny, ALL, 0, 0, tiled=True)  12.7 us
    pallas_call x2, Pallas kernels, attend(): pl.pallas_call(functools.partial(attend_kernel, causal, rows, pair // 2),...  12 us
  transfers between devices with their start and end apart: 93, of which 36 were waited for; matrix products, arithmetic and copies ran while one was open for 5% of the time, Pallas kernels for 25%

profile of v3, /device:TPU:0, one launch (start us, length us, event | category | flops | bytes accessed | tf_op | source)
XLA Modules:
  0.0 376.9 jit_solution(2792807374666305263)
XLA Ops:
  11.7 5.2 %all-to-all-start = ((bf16[8,32,512]{2,1,0:T(8,128)(2,1)}), bf16[8,32,512]{2,1,0:T(8,128)(2,1)S(1)}, u32[]{:S(2)}, u32[]{:S(2)}) async-start(bf16[8,32,512]{2,1,0:T(8,128)(2,1)} %pad_maximum_fusion.4), calls=%async_computation | async-start | bytes 524288 | tf_op jit(solution)/shard_map/all_to_all | solution.py:1026
  17.0 6.9 %all-to-all-done = bf16[8,32,512]{2,1,0:T(8,128)(2,1)S(1)} async-done(((bf16[8,32,512]{2,1,0:T(8,128)(2,1)}), bf16[8,32,512]{2,1,0:T(8,128)(2,1)S(1)}, u32[]{:S(2)}, u32[]{:S(2)}) %all-to-all-start) | async-done | bytes 262176 | tf_op jit(solution)/shard_map/all_to_all | solution.py:1026
  26.5 2.4 collective-permute-start.2
  31.7 3.0 collective-permute-done.refs_1_
  34.7 4.8 %collective-permute-done.1.refs_2_ = bf16[128,1024]{1,0:T(8,128)(2,1)S(1)} collective-permute-done((bf16[128,1024]{1,0:T(8,128)(2,1)S(1)}, bf16[128,1024]{1,0:T(8,128)(2,1)S(1)}, u32[]{:S(2)}, u32[]{:S(2)}) %collective-permute-start.1) | collective-permute-done | bytes 262176 | tf_op jit(solution)/shard_map/ppermute | solution.py:926
  39.5 3.6 all-to-all-start.1
  43.1 11.7 %all-to-all-done.1 = bf16[8,32,1408]{2,1,0:T(8,128)(2,1)S(1)} async-done(((bf16[8,32,1408]{2,1,0:T(8,128)(2,1)}), bf16[8,32,1408]{2,1,0:T(8,128)(2,1)S(1)}, u32[]{:S(2)}, u32[]{:S(2)}) %all-to-all-start.1) | async-done | bytes 720928 | tf_op jit(solution)/shard_map/all_to_all | solution.py:1026
  60.0 1.5 collective-permute-start.7
  65.0 6.5 %shard_map.229 = (bf16[1024,128]{1,0:T(8,128)(2,1)}, bf16[1024,128]{1,0:T(8,128)(2,1)}, bf16[1024,128]{1,0:T(8,128)(2,1)}, bf16[1024,1024]{1,0:T(8,128)(2,1)}, f...) custom-call(s32[2]{0:T(128)} %pad_add_fusion.table, ...), custom_call_target="tpu_custom_call" | custom-call | flops 4400000000 | bytes 14000000 | tf_op jit(solution)/shard_map/pallas_call | solution.py:389
  71.5 3.6 collective-permute-done.8.refs_2_
  84.6 3.6 collective-permute-done.11.refs_9_
  88.2 4.1 %collective-permute-done.12.refs_10_ = bf16[128,1024]{1,0:T(8,128)(2,1)S(1)} collective-permute-done((bf16[128,1024]{1,0:T(8,128)(2,1)S(1)}, bf16[128,1024]{1,0:T(8,128)(2,1)S(1)}, u32[]{:S(2)}, u32[]{:S(2)}) %collective-permute-start.12) | collective-permute-done | bytes 262176 | tf_op jit(solution)/shard_map/ppermute | solution.py:926
  92.3 1.6 collective-permute-done.13.refs_11_
  93.9 5.8 %shard_map.232 = (bf16[1024,128]{1,0:T(8,128)(2,1)}, f32[2,1024]{1,0:T(2,128)}) custom-call(s32[10]{0:T(128)} %concatenate.62.table, bf16[1024,128]{1,0:T(8,128)(2,1)} %get-tuple-element.159.q, bf16[1024,128]{1,0:T(8,128)(2,1)} %get-tuple-element.160.k, bf16[1024,128]{1,0:T(8,128)(2,1)} %get-tuple-element.161.v), custom_call_target="tpu_custom_call" | custom-call | flops 6600000000 | bytes 21000000 | tf_op jit(solution)/shard_map/pallas_call | solution.py:287
  103.9 5.3 %collective-permute-done.14.refs_1_ = bf16[1024,128]{1,0:T(8,128)(2,1)S(1)} collective-permute-done((bf16[1024,128]{1,0:T(8,128)(2,1)}, bf16[1024,128]{1,0:T(8,128)(2,1)S(1)}, u32[]{:S(2)}, u32[]{:S(2)}) %collective-permute-start.14) | collective-permute-done | bytes 262176 | tf_op jit(solution)/shard_map/ppermute | solution.py:926
  109.2 4.1 %collective-permute-done.15.refs_2_ = bf16[1024,128]{1,0:T(8,128)(2,1)S(1)} collective-permute-done((bf16[1024,128]{1,0:T(8,128)(2,1)}, bf16[1024,128]{1,0:T(8,128)(2,1)S(1)}, u32[]{:S(2)}, u32[]{:S(2)}) %collective-permute-start.15) | collective-permute-done | bytes 262176 | tf_op jit(solution)/shard_map/ppermute | solution.py:926
  118.1 4.3 %shard_map.233 = (bf16[1024,1024]{1,0:T(8,128)(2,1)}, bf16[1024,128]{1,0:T(8,128)(2,1)}, bf16[1024,128]{1,0:T(8,128)(2,1)}, bf16[1024,384]{1,0:T(8,128)(2,1)}) custom-call(f32[16,128]{1,0:T(8,128)} %get-tuple-element.165.biases.refs_19_, bf16[1024,512]{1,0:T(8,128)(2,1)} %bitcast.101, bf16[128,1024]{1,0:T(8,128)(2,1)} %bitcast.111, ...), custom_call_target="tpu_custom_call" | custom-call | flops 3300000000 | bytes 10500000 | tf_op jit(solution)/shard_map/pallas_call | solution.py:703
  123.1 1.6 collective-permute-start.30
  127.5 10.7 %shard_map.234 = (f32[128,1024]{1,0:T(8,128)}, bf16[1024,1024]{1,0:T(8,128)(2,1)}, bf16[1024,1024]{1,0:T(8,128)(2,1)}, bf16[1024,128]{1,0:T(8,128)(2,1)}) custom-call(bf16[1024,128]{1,0:T(8,128)(2,1)} %get-tuple-element.162.refs_0_, bf16[1024,128]{1,0:T(8,128)(2,1)} %copy-done.76, bf16[1024,128]{1,0:T(8,128)(2,1)} %copy-done.78, ...), custom_call_target="tpu_custom_call" | custom-call | flops 6600000000 | bytes 21000000 | tf_op jit(solution)/shard_map/pallas_call | solution.py:449
  138.3 1.6 collective-permute-start.33
  140.4 1.5 collective-permute-start.35
  141.9 6.2 %shard_map.237 = (bf16[1024,128]{1,0:T(8,128)(2,1)}, f32[2,1024]{1,0:T(2,128)}) custom-call(s32[10]{0:T(128)} %concatenate.61.table, bf16[1024,128]{1,0:T(8,128)(2,1)} %get-tuple-element.172.q, bf16[1024,128]{1,0:T(8,128)(2,1)} %get-tuple-element.173.k, bf16[1024,128]{1,0:T(8,128)(2,1)} %get-tuple-element.174.v), custom_call_target="tpu_custom_call" | custom-call | flops 6600000000 | bytes 21000000 | tf_op jit(solution)/shard_map/pallas_call | solution.py:287
  148.6 5.3 %collective-permute-done.34.refs_2_ = bf16[128,1024]{1,0:T(8,128)(2,1)S(1)} collective-permute-done((bf16[128,1024]{1,0:T(8,128)(2,1)S(1)}, bf16[128,1024]{1,0:T(8,128)(2,1)S(1)}, u32[]{:S(2)}, u32[]{:S(2)}) %collective-permute-start.34) | collective-permute-done | bytes 262176 | tf_op jit(solution)/shard_map/ppermute | solution.py:926
  155.7 1.7 collective-permute-start.38
  158.0 5.4 %collective-permute-done.36.refs_1_ = bf16[1024,128]{1,0:T(8,128)(2,1)S(1)} collective-permute-done((bf16[1024,128]{1,0:T(8,128)(2,1)}, bf16[1024,128]{1,0:T(8,128)(2,1)S(1)}, u32[]{:S(2)}, u32[]{:S(2)}) %collective-permute-start.36) | collective-permute-done | bytes 262176 | tf_op jit(solution)/shard_map/ppermute | solution.py:926
  163.4 4.4 %collective-permute-done.37.refs_2_ = bf16[1024,128]{1,0:T(8,128)(2,1)S(1)} collective-permute-done((bf16[1024,128]{1,0:T(8,128)(2,1)}, bf16[1024,128]{1,0:T(8,128)(2,1)S(1)}, u32[]{:S(2)}, u32[]{:S(2)}) %collective-permute-start.37) | collective-permute-done | bytes 262176 | tf_op jit(solution)/shard_map/ppermute | solution.py:926
  170.6 8.6 %shard_map.238 = (f32[128,1024]{1,0:T(8,128)}, bf16[1024,1024]{1,0:T(8,128)(2,1)}) custom-call(bf16[1024,128]{1,0:T(8,128)(2,1)} %get-tuple-element.178.refs_0_, bf16[1024,128]{1,0:T(8,128)(2,1)} %copy-done.86, bf16[1024,128]{1,0:T(8,128)(2,1)} %copy-done.87, bf16[1024,128]{1,0:T(8,128)(2,1)} %collective-permute-done.38.refs_3_, ...), custom_call_target="tpu_custom_call" | custom-call | flops 5500000256 | bytes 17500000 | tf_op jit(solution)/shard_map/pallas_call | solution.py:472
  179.3 11.9 %shard_map.239 = (bf16[1024,1024]{1,0:T(8,128)(2,1)S(1)}, bf16[1024,1024]{1,0:T(8,128)(2,1)S(1)}, bf16[512,1024]{1,0:T(8,128)(2,1)S(1)}, f32[512,1024]{1,0:T(8,1...) custom-call(bf16[1024,1024]{1,0:T(8,128)(2,1)} %get-tuple-element.192.h, f32[1,1024]{1,0:T(1,128)S(1)} %reshape.215.bias, ...), custom_call_target="tpu_custom_call" | custom-call | flops 14300000256 | bytes 45500000 | tf_op jit(solution)/shard_map/pallas_call | solution.py:536
  191.4 2.5 collective-permute-done.51.took
  194.1 1.5 collective-permute-start.52
  197.7 1.6 copy-done.48
  199.3 4.5 %shard_map.241 = bf16[1024,2048]{1,0:T(8,128)(2,1)S(1)} custom-call(bf16[1024,1024]{1,0:T(8,128)(2,1)S(1)} %get-tuple-element.211.act, bf16[1024,1024]{1,0:T(8,128)(2,1)S(1)} %get-tuple-element.191.slope, bf16[1024,1024]{1,0:T(8,128)(2,1)S(1)} %copy-done.47, bf16[1024,1024]{1,0:T(8,128)(2,1)S(1)} %copy-done.48), custom_call_target="tpu_custom_call" | custom-call | flops 6600000000 | bytes 21000000 | tf_op jit(solution)/shard_map/pallas_call | solution.py:625
  203.8 2.0 copy-done.4
  205.9 3.5 collective-permute-done.53.two
  214.6 5.8 %collective-permute-done.55.refs_2_ = bf16[128,1024]{1,0:T(8,128)(2,1)S(1)} collective-permute-done((bf16[128,1024]{1,0:T(8,128)(2,1)S(1)}, bf16[128,1024]{1,0:T(8,128)(2,1)S(1)}, u32[]{:S(2)}, u32[]{:S(2)}) %collective-permute-start.55) | collective-permute-done | bytes 262176 | tf_op jit(solution)/shard_map/ppermute | solution.py:926
  220.3 4.0 %collective-permute-done.56.refs_3_ = bf16[128,1024]{1,0:T(8,128)(2,1)S(1)} collective-permute-done((bf16[128,1024]{1,0:T(8,128)(2,1)S(1)}, bf16[128,1024]{1,0:T(8,128)(2,1)S(1)}, u32[]{:S(2)}, u32[]{:S(2)}) %collective-permute-start.56) | collective-permute-done | bytes 262176 | tf_op jit(solution)/shard_map/ppermute | solution.py:926
  227.3 14.5 %shard_map.243 = (bf16[512,1024]{1,0:T(8,128)(2,1)}, f32[512,1024]{1,0:T(8,128)}, bf16[1024,128]{1,0:T(8,128)(2,1)}, bf16[1024,128]{1,0:T(8,128)(2,1)}, bf16[102...) custom-call(s32[10]{0:T(128)} %concatenate.61.table, ...), custom_call_target="tpu_custom_call" | custom-call | flops 11000000512 | bytes 35000000 | tf_op jit(solution)/shard_map/pallas_call | solution.py:319
  242.0 2.7 collective-permute-done.62.took
  244.7 1.6 copy-done.31
  246.5 1.5 collective-permute-start.63
  248.6 1.5 collective-permute-start.65
  250.1 2.2 copy-done.8
  252.3 3.5 shard_map.246
  257.8 3.9 %collective-permute-done.64.two = bf16[128,1024]{1,0:T(8,128)(2,1)S(1)} collective-permute-done((bf16[128,1024]{1,0:T(8,128)(2,1)S(1)}, bf16[128,1024]{1,0:T(8,128)(2,1)S(1)}, u32[]{:S(2)}, u32[]{:S(2)}) %collective-permute-start.64) | collective-permute-done | bytes 262176 | tf_op jit(solution)/shard_map/ppermute | solution.py:926
  266.5 1.5 collective-permute-start.68
  268.5 1.7 shard_map.248
  270.1 2.2 copy-done.3
  275.1 3.9 %collective-permute-done.67.refs_3_ = bf16[128,1024]{1,0:T(8,128)(2,1)} collective-permute-done((bf16[128,1024]{1,0:T(8,128)(2,1)}, bf16[128,1024]{1,0:T(8,128)(2,1)}, u32[]{:S(2)}, u32[]{:S(2)}) %collective-permute-start.67) | collective-permute-done | bytes 262176 | tf_op jit(solution)/shard_map/ppermute | solution.py:926
  281.8 2.5 reduce-scatter.4.cloned.1.call-done.feed_sum
  284.6 1.5 collective-permute-start.75
  288.2 14.1 %shard_map.250 = (bf16[512,1024]{1,0:T(8,128)(2,1)}, f32[512,1024]{1,0:T(8,128)}, f32[2,1024]{1,0:T(2,128)}, bf16[1024,128]{1,0:T(8,128)(2,1)}, bf16[1024,128]{1...) custom-call(s32[10]{0:T(128)} %concatenate.62.table, ...), custom_call_target="tpu_custom_call" | custom-call | flops 11000000512 | bytes 35000000 | tf_op jit(solution)/shard_map/pallas_call | solution.py:319
  304.6 12.7 %all_to_all.32 = f32[32,1,672]{2,1,0:T(1,128)S(1)} all-to-all(f32[32,1,672]{2,1,0:T(1,128)S(1)} %copy.97), channel_id=1, replica_groups=mesh['ulys'=4,'blk'=8] {'ulys','blk'}, dimensions={0} | all-to-all | bytes 172032 | tf_op jit(solution)/shard_map/all_to_all | solution.py:1219
  317.6 2.8 collective-permute-done.78.took
  320.4 1.6 copy-done.30
  325.2 1.6 shard_map.255
  328.2 2.1 collective-permute-start.81
  330.4 5.8 %collective-permute-done.79.one = bf16[128,1024]{1,0:T(8,128)(2,1)S(1)} collective-permute-done((bf16[128,1024]{1,0:T(8,128)(2,1)}, bf16[128,1024]{1,0:T(8,128)(2,1)S(1)}, u32[]{:S(2)}, u32[]{:S(2)}) %collective-permute-start.79) | collective-permute-done | bytes 262176 | tf_op jit(solution)/shard_map/ppermute | solution.py:926
  336.2 5.1 %collective-permute-done.81.three = bf16[128,1024]{1,0:T(8,128)(2,1)S(1)} collective-permute-done((bf16[128,1024]{1,0:T(8,128)(2,1)S(1)}, bf16[128,1024]{1,0:T(8,128)(2,1)S(1)}, u32[]{:S(2)}, u32[]{:S(2)}) %collective-permute-start.81) | collective-permute-done | bytes 262176 | tf_op jit(solution)/shard_map/ppermute | solution.py:926
  343.9 3.5 all-to-all-start.4
  355.4 1.6 slice.87
  357.0 2.3 all-to-all-done.4.got
  359.3 3.4 all-to-all-start.3
  362.7 1.6 shard_map.257
  365.7 3.2 all-to-all-done.3.got
  (464 shorter events, 92.8 us)
Async XLA Ops:
  11.7 12.1 %all-to-all-start = ((bf16[8,32,512]{2,1,0:T(8,128)(2,1)}), bf16[8,32,512]{2,1,0:T(8,128)(2,1)S(1)}, u32[]{:S(2)}, u32[]{:S(2)}) async-start(bf16[8,32,512]{2,1,0:T(8,128)(2,1)} %pad_maximum_fusion.4), calls=%async_computation | async-start | bytes 524288 | tf_op jit(solution)/shard_map/all_to_all | solution.py:1026
  16.9 39.9 %all-gather.7.cloned.1.call-start = ((), (), s32[]{:S(2)}) async-start(), calls=%async_computation.11 | async-start | bytes 1638400 | tf_op jit(solution)/shard_map/all_gather | solution.py:1091
  25.4 9.3 %collective-permute-start = (bf16[128,1024]{1,0:T(8,128)(2,1)S(1)}, bf16[128,1024]{1,0:T(8,128)(2,1)S(1)}, u32[]{:S(2)}, u32[]{:S(2)}) collective-permute-start(bf16[128,1024]{1,0:T(8,128)(2,1)S(1)} %bitcast.81), channel_id=1, source_target_pairs={{0,2},{1,3},{2,0},{3,1},{4,6},{5,7},{6,4},{7,5},{8,10},{9,11},{10,... | collective-permute-start | bytes 786440 | tf_op jit(solution)/shard_map/ppermute | solution.py:926
  26.0 13.5 %collective-permute-start.1 = (bf16[128,1024]{1,0:T(8,128)(2,1)S(1)}, bf16[128,1024]{1,0:T(8,128)(2,1)S(1)}, u32[]{:S(2)}, u32[]{:S(2)}) collective-permute-start(bf16[128,1024]{1,0:T(8,128)(2,1)S(1)} %bitcast.82), channel_id=1, source_target_pairs={{0,4},{1,5},{2,6},{3,7},{4,0},{5,1},{6,2},{7,3},{8,12},{9,13},{10,... | collective-permute-start | bytes 786440 | tf_op jit(solution)/shard_map/ppermute | solution.py:926
  26.5 12.9 %collective-permute-start.2 = (bf16[128,1024]{1,0:T(8,128)(2,1)S(1)}, bf16[128,1024]{1,0:T(8,128)(2,1)S(1)}, u32[]{:S(2)}, u32[]{:S(2)}) collective-permute-start(bf16[128,1024]{1,0:T(8,128)(2,1)S(1)} %bitcast.83), channel_id=1, source_target_pairs={{0,6},{1,7},{2,4},{3,5},{4,2},{5,3},{6,0},{7,1},{8,14},{9,15},{10,... | collective-permute-start | bytes 786440 | tf_op jit(solution)/shard_map/ppermute | solution.py:926
  39.5 15.4 %all-to-all-start.1 = ((bf16[8,32,1408]{2,1,0:T(8,128)(2,1)}), bf16[8,32,1408]{2,1,0:T(8,128)(2,1)S(1)}, u32[]{:S(2)}, u32[]{:S(2)}) async-start(bf16[8,32,1408]{2,1,0:T(8,128)(2,1)} %pad_maximum_fusion.1), calls=%async_computation.1 | async-start | bytes 1441792 | tf_op jit(solution)/shard_map/all_to_all | solution.py:1026
  43.0 70.9 %all-gather.9.cloned.1.call-start = ((), (), s32[]{:S(2)}) async-start(), calls=%async_computation.12 | async-start | bytes 1310720 | tf_op jit(solution)/shard_map/all_gather | solution.py:1091
  56.9 122.4 %all-gather.11.cloned.1.call-start = ((), (), s32[]{:S(2)}) async-start(), calls=%async_computation.13 | async-start | bytes 5242880 | tf_op jit(solution)/shard_map/all_gather | solution.py:1091
  58.1 226.3 %reduce-scatter.4.cloned.1.call-start = ((), (), s32[]{:S(2)}) async-start(), calls=%async_computation.8 | async-start | bytes 5242880 | tf_op jit(solution)/shard_map/reduce_scatter | solution.py:1139
  60.0 11.5 %collective-permute-start.7 = (bf16[128,1024]{1,0:T(8,128)(2,1)S(1)}, bf16[128,1024]{1,0:T(8,128)(2,1)S(1)}, u32[]{:S(2)}, u32[]{:S(2)}) collective-permute-start(bf16[128,1024]{1,0:T(8,128)(2,1)S(1)} %bitcast.112), channel_id=1, source_target_pairs={{0,2},{1,3},{2,0},{3,1},{4,6},{5,7},{6,4},{7,5},{8,10},{9,11},{10,... | collective-permute-start | bytes 786440 | tf_op jit(solution)/shard_map/ppermute | solution.py:926
  61.5 13.6 %collective-permute-start.8 = (bf16[128,1024]{1,0:T(8,128)(2,1)S(1)}, bf16[128,1024]{1,0:T(8,128)(2,1)S(1)}, u32[]{:S(2)}, u32[]{:S(2)}) collective-permute-start(bf16[128,1024]{1,0:T(8,128)(2,1)S(1)} %bitcast.113), channel_id=1, source_target_pairs={{0,4},{1,5},{2,6},{3,7},{4,0},{5,1},{6,2},{7,3},{8,12},{9,13},{10,... | collective-permute-start | bytes 786440 | tf_op jit(solution)/shard_map/ppermute | solution.py:926
  63.0 12.2 %collective-permute-start.9 = (bf16[128,1024]{1,0:T(8,128)(2,1)S(1)}, bf16[128,1024]{1,0:T(8,128)(2,1)S(1)}, u32[]{:S(2)}, u32[]{:S(2)}) collective-permute-start(bf16[128,1024]{1,0:T(8,128)(2,1)S(1)} %bitcast.114), channel_id=1, source_target_pairs={{0,6},{1,7},{2,4},{3,5},{4,2},{5,3},{6,0},{7,1},{8,14},{9,15},{10,... | collective-permute-start | bytes 786440 | tf_op jit(solution)/shard_map/ppermute | solution.py:926
  78.9 9.2 %collective-permute-start.11 = (bf16[128,1024]{1,0:T(8,128)(2,1)S(1)}, bf16[128,1024]{1,0:T(8,128)(2,1)S(1)}, u32[]{:S(2)}, u32[]{:S(2)}) collective-permute-start(bf16[128,1024]{1,0:T(8,128)(2,1)S(1)} %shard_map.231.refs_8_.weight), channel_id=1, source_target_pairs={{0,2},{1,3},{2,0},{3,1},{4,6},{5,7},{6,4},{7,5},{8,10},{9,11},{10,... | collective-permute-start | bytes 786440 | tf_op jit(solution)/shard_map/ppermute | solution.py:926
  80.1 12.2 %collective-permute-start.12 = (bf16[128,1024]{1,0:T(8,128)(2,1)S(1)}, bf16[128,1024]{1,0:T(8,128)(2,1)S(1)}, u32[]{:S(2)}, u32[]{:S(2)}) collective-permute-start(bf16[128,1024]{1,0:T(8,128)(2,1)S(1)} %shard_map.231.refs_8_.weight), channel_id=1, source_target_pairs={{0,4},{1,5},{2,6},{3,7},{4,0},{5,1},{6,2},{7,3},{8,12},{9,13},{10,... | collective-permute-start | bytes 786440 | tf_op jit(solution)/shard_map/ppermute | solution.py:926
  81.0 12.9 %collective-permute-start.13 = (bf16[128,1024]{1,0:T(8,128)(2,1)S(1)}, bf16[128,1024]{1,0:T(8,128)(2,1)S(1)}, u32[]{:S(2)}, u32[]{:S(2)}) collective-permute-start(bf16[128,1024]{1,0:T(8,128)(2,1)S(1)} %shard_map.231.refs_8_.weight), channel_id=1, source_target_pairs={{0,6},{1,7},{2,4},{3,5},{4,2},{5,3},{6,0},{7,1},{8,14},{9,15},{10,... | collective-permute-start | bytes 786440 | tf_op jit(solution)/shard_map/ppermute | solution.py:926
  84.0 19.2 %collective-permute-start.25 = (bf16[128,1024]{1,0:T(8,128)(2,1)S(1)}, bf16[128,1024]{1,0:T(8,128)(2,1)S(1)}, u32[]{:S(2)}, u32[]{:S(2)}) collective-permute-start(bf16[128,1024]{1,0:T(8,128)(2,1)S(1)} %bitcast.115), channel_id=1, source_target_pairs={{0,1},{1,0},{2,3},{3,2},{4,5},{5,4},{6,7},{7,6},{8,9},{9,8},{10,11... | collective-permute-start | bytes 786440 | tf_op jit(solution)/shard_map/ppermute | solution.py:926
  84.1 19.2 %collective-permute-start.26 = (bf16[128,1024]{1,0:T(8,128)(2,1)S(1)}, bf16[128,1024]{1,0:T(8,128)(2,1)S(1)}, u32[]{:S(2)}, u32[]{:S(2)}) collective-permute-start(bf16[128,1024]{1,0:T(8,128)(2,1)S(1)} %collective-permute-done.7.refs_1_), channel_id=1, source_target_pairs={{0,1},{1,0},{2,3},{3,2},{4,5},{5,4},{6,7},{7,6},{8,9},{9,8},{10,11... | collective-permute-start | bytes 786440 | tf_op jit(solution)/shard_map/ppermute | solution.py:926
  99.7 9.5 %collective-permute-start.14 = (bf16[1024,128]{1,0:T(8,128)(2,1)}, bf16[1024,128]{1,0:T(8,128)(2,1)S(1)}, u32[]{:S(2)}, u32[]{:S(2)}) collective-permute-start(bf16[1024,128]{1,0:T(8,128)(2,1)} %get-tuple-element.162.refs_0_), channel_id=1, source_target_pairs={{0,2},{1,3},{2,0},{3,1},{4,6},{5,7},{6,4},{7,5},{8,10},{9,11},{10,... | collective-permute-start | bytes 786440 | tf_op jit(solution)/shard_map/ppermute | solution.py:926
  100.6 12.7 %collective-permute-start.15 = (bf16[1024,128]{1,0:T(8,128)(2,1)}, bf16[1024,128]{1,0:T(8,128)(2,1)S(1)}, u32[]{:S(2)}, u32[]{:S(2)}) collective-permute-start(bf16[1024,128]{1,0:T(8,128)(2,1)} %get-tuple-element.162.refs_0_), channel_id=1, source_target_pairs={{0,4},{1,5},{2,6},{3,7},{4,0},{5,1},{6,2},{7,3},{8,12},{9,13},{10,... | collective-permute-start | bytes 786440 | tf_op jit(solution)/shard_map/ppermute | solution.py:926
  102.1 11.2 %collective-permute-start.16 = (bf16[1024,128]{1,0:T(8,128)(2,1)}, bf16[1024,128]{1,0:T(8,128)(2,1)}, u32[]{:S(2)}, u32[]{:S(2)}) collective-permute-start(bf16[1024,128]{1,0:T(8,128)(2,1)} %get-tuple-element.162.refs_0_), channel_id=1, source_target_pairs={{0,6},{1,7},{2,4},{3,5},{4,2},{5,3},{6,0},{7,1},{8,14},{9,15},{10,... | collective-permute-start | bytes 786440 | tf_op jit(solution)/shard_map/ppermute | solution.py:926
  103.2 12.3 %collective-permute-start.27 = (bf16[128,1024]{1,0:T(8,128)(2,1)S(1)}, bf16[128,1024]{1,0:T(8,128)(2,1)}, u32[]{:S(2)}, u32[]{:S(2)}) collective-permute-start(bf16[128,1024]{1,0:T(8,128)(2,1)S(1)} %collective-permute-done.8.refs_2_), channel_id=1, source_target_pairs={{0,1},{1,0},{2,3},{3,2},{4,5},{5,4},{6,7},{7,6},{8,9},{9,8},{10,11... | collective-permute-start | bytes 786440 | tf_op jit(solution)/shard_map/ppermute | solution.py:926
  103.3 13.2 %collective-permute-start.28 = (bf16[128,1024]{1,0:T(8,128)(2,1)S(1)}, bf16[128,1024]{1,0:T(8,128)(2,1)}, u32[]{:S(2)}, u32[]{:S(2)}) collective-permute-start(bf16[128,1024]{1,0:T(8,128)(2,1)S(1)} %collective-permute-done.9.refs_3_), channel_id=1, source_target_pairs={{0,1},{1,0},{2,3},{3,2},{4,5},{5,4},{6,7},{7,6},{8,9},{9,8},{10,11... | collective-permute-start | bytes 786440 | tf_op jit(solution)/shard_map/ppermute | solution.py:926
  117.6 9.0 %collective-permute-start.19 = (bf16[1024,128]{1,0:T(8,128)(2,1)S(1)}, bf16[1024,128]{1,0:T(8,128)(2,1)S(1)}, u32[]{:S(2)}, u32[]{:S(2)}) collective-permute-start(bf16[1024,128]{1,0:T(8,128)(2,1)S(1)} %collective-permute-done.15.refs_2_), channel_id=1, source_target_pairs={{0,1},{1,0},{2,3},{3,2},{4,5},{5,4},{6,7},{7,6},{8,9},{9,8},{10,11... | collective-permute-start | bytes 786440 | tf_op jit(solution)/shard_map/ppermute | solution.py:926
  123.1 15.2 %collective-permute-start.30 = (bf16[128,1024]{1,0:T(8,128)(2,1)S(1)}, bf16[128,1024]{1,0:T(8,128)(2,1)S(1)}, u32[]{:S(2)}, u32[]{:S(2)}) collective-permute-start(bf16[128,1024]{1,0:T(8,128)(2,1)S(1)} %shard_map.236.refs_8_.weight), channel_id=1, source_target_pairs={{0,2},{1,3},{2,0},{3,1},{4,6},{5,7},{6,4},{7,5},{8,10},{9,11},{10,... | collective-permute-start | bytes 786440 | tf_op jit(solution)/shard_map/ppermute | solution.py:926
  124.6 13.7 %collective-permute-start.31 = (bf16[128,1024]{1,0:T(8,128)(2,1)S(1)}, bf16[128,1024]{1,0:T(8,128)(2,1)S(1)}, u32[]{:S(2)}, u32[]{:S(2)}) collective-permute-start(bf16[128,1024]{1,0:T(8,128)(2,1)S(1)} %shard_map.236.refs_8_.weight), channel_id=1, source_target_pairs={{0,4},{1,5},{2,6},{3,7},{4,0},{5,1},{6,2},{7,3},{8,12},{9,13},{10,... | collective-permute-start | bytes 786440 | tf_op jit(solution)/shard_map/ppermute | solution.py:926
  125.1 13.2 %collective-permute-start.32 = (bf16[128,1024]{1,0:T(8,128)(2,1)S(1)}, bf16[128,1024]{1,0:T(8,128)(2,1)S(1)}, u32[]{:S(2)}, u32[]{:S(2)}) collective-permute-start(bf16[128,1024]{1,0:T(8,128)(2,1)S(1)} %shard_map.236.refs_8_.weight), channel_id=1, source_target_pairs={{0,6},{1,7},{2,4},{3,5},{4,2},{5,3},{6,0},{7,1},{8,14},{9,15},{10,... | collective-permute-start | bytes 786440 | tf_op jit(solution)/shard_map/ppermute | solution.py:926
  138.2 17.5 %collective-permute-start.43 = (bf16[128,1024]{1,0:T(8,128)(2,1)S(1)}, bf16[128,1024]{1,0:T(8,128)(2,1)S(1)}, u32[]{:S(2)}, u32[]{:S(2)}) collective-permute-start(bf16[128,1024]{1,0:T(8,128)(2,1)S(1)} %shard_map.236.refs_8_.weight), channel_id=1, source_target_pairs={{0,1},{1,0},{2,3},{3,2},{4,5},{5,4},{6,7},{7,6},{8,9},{9,8},{10,11... | collective-permute-start | bytes 786440 | tf_op jit(solution)/shard_map/ppermute | solution.py:926
  138.3 9.8 %collective-permute-start.33 = (bf16[128,1024]{1,0:T(8,128)(2,1)S(1)}, bf16[128,1024]{1,0:T(8,128)(2,1)S(1)}, u32[]{:S(2)}, u32[]{:S(2)}) collective-permute-start(bf16[128,1024]{1,0:T(8,128)(2,1)S(1)} %bitcast.74), channel_id=1, source_target_pairs={{0,2},{1,3},{2,0},{3,1},{4,6},{5,7},{6,4},{7,5},{8,10},{9,11},{10,... | collective-permute-start | bytes 786440 | tf_op jit(solution)/shard_map/ppermute | solution.py:926
  139.9 14.0 %collective-permute-start.34 = (bf16[128,1024]{1,0:T(8,128)(2,1)S(1)}, bf16[128,1024]{1,0:T(8,128)(2,1)S(1)}, u32[]{:S(2)}, u32[]{:S(2)}) collective-permute-start(bf16[128,1024]{1,0:T(8,128)(2,1)S(1)} %bitcast.75), channel_id=1, source_target_pairs={{0,4},{1,5},{2,6},{3,7},{4,0},{5,1},{6,2},{7,3},{8,12},{9,13},{10,... | collective-permute-start | bytes 786440 | tf_op jit(solution)/shard_map/ppermute | solution.py:926
  140.4 13.5 %collective-permute-start.35 = (bf16[128,1024]{1,0:T(8,128)(2,1)S(1)}, bf16[128,1024]{1,0:T(8,128)(2,1)S(1)}, u32[]{:S(2)}, u32[]{:S(2)}) collective-permute-start(bf16[128,1024]{1,0:T(8,128)(2,1)S(1)} %bitcast.76), channel_id=1, source_target_pairs={{0,6},{1,7},{2,4},{3,5},{4,2},{5,3},{6,0},{7,1},{8,14},{9,15},{10,... | collective-permute-start | bytes 786440 | tf_op jit(solution)/shard_map/ppermute | solution.py:926
  148.1 9.3 %collective-permute-start.44 = (bf16[128,1024]{1,0:T(8,128)(2,1)S(1)}, bf16[128,1024]{1,0:T(8,128)(2,1)S(1)}, u32[]{:S(2)}, u32[]{:S(2)}) collective-permute-start(bf16[128,1024]{1,0:T(8,128)(2,1)S(1)} %collective-permute-done.30.refs_9_), channel_id=1, source_target_pairs={{0,1},{1,0},{2,3},{3,2},{4,5},{5,4},{6,7},{7,6},{8,9},{9,8},{10,11... | collective-permute-start | bytes 786440 | tf_op jit(solution)/shard_map/ppermute | solution.py:926
  148.1 9.4 %collective-permute-start.45 = (bf16[128,1024]{1,0:T(8,128)(2,1)S(1)}, bf16[128,1024]{1,0:T(8,128)(2,1)S(1)}, u32[]{:S(2)}, u32[]{:S(2)}) collective-permute-start(bf16[128,1024]{1,0:T(8,128)(2,1)S(1)} %collective-permute-done.31.refs_10_), channel_id=1, source_target_pairs={{0,1},{1,0},{2,3},{3,2},{4,5},{5,4},{6,7},{7,6},{8,9},{9,8},{10,11... | collective-permute-start | bytes 786440 | tf_op jit(solution)/shard_map/ppermute | solution.py:926
  153.9 9.5 %collective-permute-start.36 = (bf16[1024,128]{1,0:T(8,128)(2,1)}, bf16[1024,128]{1,0:T(8,128)(2,1)S(1)}, u32[]{:S(2)}, u32[]{:S(2)}) collective-permute-start(bf16[1024,128]{1,0:T(8,128)(2,1)} %get-tuple-element.178.refs_0_), channel_id=1, source_target_pairs={{0,2},{1,3},{2,0},{3,1},{4,6},{5,7},{6,4},{7,5},{8,10},{9,11},{10,... | collective-permute-start | bytes 786440 | tf_op jit(solution)/shard_map/ppermute | solution.py:926
  154.4 13.3 %collective-permute-start.37 = (bf16[1024,128]{1,0:T(8,128)(2,1)}, bf16[1024,128]{1,0:T(8,128)(2,1)S(1)}, u32[]{:S(2)}, u32[]{:S(2)}) collective-permute-start(bf16[1024,128]{1,0:T(8,128)(2,1)} %get-tuple-element.178.refs_0_), channel_id=1, source_target_pairs={{0,4},{1,5},{2,6},{3,7},{4,0},{5,1},{6,2},{7,3},{8,12},{9,13},{10,... | collective-permute-start | bytes 786440 | tf_op jit(solution)/shard_map/ppermute | solution.py:926
  155.7 12.1 %collective-permute-start.38 = (bf16[1024,128]{1,0:T(8,128)(2,1)}, bf16[1024,128]{1,0:T(8,128)(2,1)}, u32[]{:S(2)}, u32[]{:S(2)}) collective-permute-start(bf16[1024,128]{1,0:T(8,128)(2,1)} %get-tuple-element.178.refs_0_), channel_id=1, source_target_pairs={{0,6},{1,7},{2,4},{3,5},{4,2},{5,3},{6,0},{7,1},{8,14},{9,15},{10,... | collective-permute-start | bytes 786440 | tf_op jit(solution)/shard_map/ppermute | solution.py:926
  157.4 12.1 %collective-permute-start.46 = (bf16[128,1024]{1,0:T(8,128)(2,1)S(1)}, bf16[128,1024]{1,0:T(8,128)(2,1)S(1)}, u32[]{:S(2)}, u32[]{:S(2)}) collective-permute-start(bf16[128,1024]{1,0:T(8,128)(2,1)S(1)} %collective-permute-done.32.refs_11_), channel_id=1, source_target_pairs={{0,1},{1,0},{2,3},{3,2},{4,5},{5,4},{6,7},{7,6},{8,9},{9,8},{10,11... | collective-permute-start | bytes 786440 | tf_op jit(solution)/shard_map/ppermute | solution.py:926
  157.5 12.1 %collective-permute-start.39 = (bf16[1024,128]{1,0:T(8,128)(2,1)}, bf16[1024,128]{1,0:T(8,128)(2,1)S(1)}, u32[]{:S(2)}, u32[]{:S(2)}) collective-permute-start(bf16[1024,128]{1,0:T(8,128)(2,1)} %get-tuple-element.178.refs_0_), channel_id=1, source_target_pairs={{0,1},{1,0},{2,3},{3,2},{4,5},{5,4},{6,7},{7,6},{8,9},{9,8},{10,11... | collective-permute-start | bytes 786440 | tf_op jit(solution)/shard_map/ppermute | solution.py:926
  169.5 9.8 %collective-permute-start.47 = (bf16[128,1024]{1,0:T(8,128)(2,1)S(1)}, bf16[128,1024]{1,0:T(8,128)(2,1)S(1)}, u32[]{:S(2)}, u32[]{:S(2)}) collective-permute-start(bf16[128,1024]{1,0:T(8,128)(2,1)S(1)} %bitcast.77), channel_id=1, source_target_pairs={{0,1},{1,0},{2,3},{3,2},{4,5},{5,4},{6,7},{7,6},{8,9},{9,8},{10,11... | collective-permute-start | bytes 786440 | tf_op jit(solution)/shard_map/ppermute | solution.py:926
  169.6 9.6 %collective-permute-start.48 = (bf16[128,1024]{1,0:T(8,128)(2,1)S(1)}, bf16[128,1024]{1,0:T(8,128)(2,1)S(1)}, u32[]{:S(2)}, u32[]{:S(2)}) collective-permute-start(bf16[128,1024]{1,0:T(8,128)(2,1)S(1)} %collective-permute-done.33.refs_1_), channel_id=1, source_target_pairs={{0,1},{1,0},{2,3},{3,2},{4,5},{5,4},{6,7},{7,6},{8,9},{9,8},{10,11... | collective-permute-start | bytes 786440 | tf_op jit(solution)/shard_map/ppermute | solution.py:926
  170.1 9.2 %collective-permute-start.49 = (bf16[128,1024]{1,0:T(8,128)(2,1)S(1)}, bf16[128,1024]{1,0:T(8,128)(2,1)S(1)}, u32[]{:S(2)}, u32[]{:S(2)}) collective-permute-start(bf16[128,1024]{1,0:T(8,128)(2,1)S(1)} %collective-permute-done.34.refs_2_), channel_id=1, source_target_pairs={{0,1},{1,0},{2,3},{3,2},{4,5},{5,4},{6,7},{7,6},{8,9},{9,8},{10,11... | collective-permute-start | bytes 786440 | tf_op jit(solution)/shard_map/ppermute | solution.py:926
  170.2 9.1 %collective-permute-start.50 = (bf16[128,1024]{1,0:T(8,128)(2,1)S(1)}, bf16[128,1024]{1,0:T(8,128)(2,1)S(1)}, u32[]{:S(2)}, u32[]{:S(2)}) collective-permute-start(bf16[128,1024]{1,0:T(8,128)(2,1)S(1)} %collective-permute-done.35.refs_3_), channel_id=1, source_target_pairs={{0,1},{1,0},{2,3},{3,2},{4,5},{5,4},{6,7},{7,6},{8,9},{9,8},{10,11... | collective-permute-start | bytes 786440 | tf_op jit(solution)/shard_map/ppermute | solution.py:926
  194.1 11.7 %collective-permute-start.52 = (bf16[128,1024]{1,0:T(8,128)(2,1)S(1)}, bf16[128,1024]{1,0:T(8,128)(2,1)S(1)}, u32[]{:S(2)}, u32[]{:S(2)}) collective-permute-start(bf16[128,1024]{1,0:T(8,128)(2,1)S(1)} %get-tuple-element.187), channel_id=1, source_target_pairs={{0,2},{1,3},{2,0},{3,1},{4,6},{5,7},{6,4},{7,5},{8,10},{9,11},{10,... | collective-permute-start | bytes 786440 | tf_op jit(solution)/shard_map/ppermute | solution.py:926
  195.7 13.7 %collective-permute-start.53 = (bf16[128,1024]{1,0:T(8,128)(2,1)S(1)}, bf16[128,1024]{1,0:T(8,128)(2,1)S(1)}, u32[]{:S(2)}, u32[]{:S(2)}) collective-permute-start(bf16[128,1024]{1,0:T(8,128)(2,1)S(1)} %get-tuple-element.188), channel_id=1, source_target_pairs={{0,4},{1,5},{2,6},{3,7},{4,0},{5,1},{6,2},{7,3},{8,12},{9,13},{10,... | collective-permute-start | bytes 786440 | tf_op jit(solution)/shard_map/ppermute | solution.py:926
  196.3 13.1 %collective-permute-start.54 = (bf16[128,1024]{1,0:T(8,128)(2,1)S(1)}, bf16[128,1024]{1,0:T(8,128)(2,1)S(1)}, u32[]{:S(2)}, u32[]{:S(2)}) collective-permute-start(bf16[128,1024]{1,0:T(8,128)(2,1)S(1)} %get-tuple-element.189), channel_id=1, source_target_pairs={{0,6},{1,7},{2,4},{3,5},{4,2},{5,3},{6,0},{7,1},{8,14},{9,15},{10,... | collective-permute-start | bytes 786440 | tf_op jit(solution)/shard_map/ppermute | solution.py:926
  209.4 132.7 %reduce-scatter.6.cloned.1.call-start = ((), (), s32[]{:S(2)}) async-start(), calls=%async_computation.9 | async-start | bytes 1310720 | tf_op jit(solution)/shard_map/reduce_scatter | solution.py:1179
  211.1 9.2 %collective-permute-start.55 = (bf16[128,1024]{1,0:T(8,128)(2,1)S(1)}, bf16[128,1024]{1,0:T(8,128)(2,1)S(1)}, u32[]{:S(2)}, u32[]{:S(2)}) collective-permute-start(bf16[128,1024]{1,0:T(8,128)(2,1)S(1)} %get-tuple-element.198.refs_1_), channel_id=1, source_target_pairs={{0,2},{1,3},{2,0},{3,1},{4,6},{5,7},{6,4},{7,5},{8,10},{9,11},{10,... | collective-permute-start | bytes 786440 | tf_op jit(solution)/shard_map/ppermute | solution.py:926
  211.7 12.6 %collective-permute-start.56 = (bf16[128,1024]{1,0:T(8,128)(2,1)S(1)}, bf16[128,1024]{1,0:T(8,128)(2,1)S(1)}, u32[]{:S(2)}, u32[]{:S(2)}) collective-permute-start(bf16[128,1024]{1,0:T(8,128)(2,1)S(1)} %get-tuple-element.198.refs_1_), channel_id=1, source_target_pairs={{0,4},{1,5},{2,6},{3,7},{4,0},{5,1},{6,2},{7,3},{8,12},{9,13},{10,... | collective-permute-start | bytes 786440 | tf_op jit(solution)/shard_map/ppermute | solution.py:926
  213.1 11.2 %collective-permute-start.57 = (bf16[128,1024]{1,0:T(8,128)(2,1)S(1)}, bf16[128,1024]{1,0:T(8,128)(2,1)S(1)}, u32[]{:S(2)}, u32[]{:S(2)}) collective-permute-start(bf16[128,1024]{1,0:T(8,128)(2,1)S(1)} %get-tuple-element.198.refs_1_), channel_id=1, source_target_pairs={{0,6},{1,7},{2,4},{3,5},{4,2},{5,3},{6,0},{7,1},{8,14},{9,15},{10,... | collective-permute-start | bytes 786440 | tf_op jit(solution)/shard_map/ppermute | solution.py:926
  214.6 10.2 %collective-permute-start.58 = (bf16[128,1024]{1,0:T(8,128)(2,1)S(1)}, bf16[128,1024]{1,0:T(8,128)(2,1)S(1)}, u32[]{:S(2)}, u32[]{:S(2)}) collective-permute-start(bf16[128,1024]{1,0:T(8,128)(2,1)S(1)} %get-tuple-element.198.refs_1_), channel_id=1, source_target_pairs={{0,1},{1,0},{2,3},{3,2},{4,5},{5,4},{6,7},{7,6},{8,9},{9,8},{10,11... | collective-permute-start | bytes 786440 | tf_op jit(solution)/shard_map/ppermute | solution.py:926
  246.5 11.3 %collective-permute-start.63 = (bf16[128,1024]{1,0:T(8,128)(2,1)S(1)}, bf16[128,1024]{1,0:T(8,128)(2,1)S(1)}, u32[]{:S(2)}, u32[]{:S(2)}) collective-permute-start(bf16[128,1024]{1,0:T(8,128)(2,1)S(1)} %get-tuple-element.202), channel_id=1, source_target_pairs={{0,2},{1,3},{2,0},{3,1},{4,6},{5,7},{6,4},{7,5},{8,10},{9,11},{10,... | collective-permute-start | bytes 786440 | tf_op jit(solution)/shard_map/ppermute | solution.py:926
  248.0 13.7 %collective-permute-start.64 = (bf16[128,1024]{1,0:T(8,128)(2,1)S(1)}, bf16[128,1024]{1,0:T(8,128)(2,1)S(1)}, u32[]{:S(2)}, u32[]{:S(2)}) collective-permute-start(bf16[128,1024]{1,0:T(8,128)(2,1)S(1)} %get-tuple-element.203), channel_id=1, source_target_pairs={{0,4},{1,5},{2,6},{3,7},{4,0},{5,1},{6,2},{7,3},{8,12},{9,13},{10,... | collective-permute-start | bytes 786440 | tf_op jit(solution)/shard_map/ppermute | solution.py:926
  248.6 13.1 %collective-permute-start.65 = (bf16[128,1024]{1,0:T(8,128)(2,1)S(1)}, bf16[128,1024]{1,0:T(8,128)(2,1)S(1)}, u32[]{:S(2)}, u32[]{:S(2)}) collective-permute-start(bf16[128,1024]{1,0:T(8,128)(2,1)S(1)} %get-tuple-element.204), channel_id=1, source_target_pairs={{0,6},{1,7},{2,4},{3,5},{4,2},{5,3},{6,0},{7,1},{8,14},{9,15},{10,... | collective-permute-start | bytes 786440 | tf_op jit(solution)/shard_map/ppermute | solution.py:926
  264.4 10.6 %collective-permute-start.66 = (bf16[128,1024]{1,0:T(8,128)(2,1)}, bf16[128,1024]{1,0:T(8,128)(2,1)}, u32[]{:S(2)}, u32[]{:S(2)}) collective-permute-start(bf16[128,1024]{1,0:T(8,128)(2,1)} %get-tuple-element.242.refs_1_), channel_id=1, source_target_pairs={{0,2},{1,3},{2,0},{3,1},{4,6},{5,7},{6,4},{7,5},{8,10},{9,11},{10,... | collective-permute-start | bytes 786440 | tf_op jit(solution)/shard_map/ppermute | solution.py:926
  265.1 13.9 %collective-permute-start.67 = (bf16[128,1024]{1,0:T(8,128)(2,1)}, bf16[128,1024]{1,0:T(8,128)(2,1)}, u32[]{:S(2)}, u32[]{:S(2)}) collective-permute-start(bf16[128,1024]{1,0:T(8,128)(2,1)} %get-tuple-element.242.refs_1_), channel_id=1, source_target_pairs={{0,4},{1,5},{2,6},{3,7},{4,0},{5,1},{6,2},{7,3},{8,12},{9,13},{10,... | collective-permute-start | bytes 786440 | tf_op jit(solution)/shard_map/ppermute | solution.py:926
  266.5 12.4 %collective-permute-start.68 = (bf16[128,1024]{1,0:T(8,128)(2,1)}, bf16[128,1024]{1,0:T(8,128)(2,1)}, u32[]{:S(2)}, u32[]{:S(2)}) collective-permute-start(bf16[128,1024]{1,0:T(8,128)(2,1)} %get-tuple-element.242.refs_1_), channel_id=1, source_target_pairs={{0,6},{1,7},{2,4},{3,5},{4,2},{5,3},{6,0},{7,1},{8,14},{9,15},{10,... | collective-permute-start | bytes 786440 | tf_op jit(solution)/shard_map/ppermute | solution.py:926
  284.4 71.0 %reduce-scatter.8.cloned.1.call-start = ((), (), s32[]{:S(2)}) async-start(), calls=%async_computation.10 | async-start | bytes 1310720 | tf_op jit(solution)/shard_map/reduce_scatter | solution.py:1227
  284.6 32.7 %collective-permute-start.75 = (bf16[128,2048]{1,0:T(8,128)(2,1)}, bf16[128,2048]{1,0:T(8,128)(2,1)S(1)}, u32[]{:S(2)}, u32[]{:S(2)}) collective-permute-start(bf16[128,2048]{1,0:T(8,128)(2,1)} %copy-done.17), channel_id=1, source_target_pairs={{0,2},{1,3},{2,0},{3,1},{4,6},{5,7},{6,4},{7,5},{8,10},{9,11},{10,... | collective-permute-start | bytes 1572872 | tf_op jit(solution)/shard_map/ppermute | solution.py:926
  286.2 31.2 %collective-permute-start.76 = (bf16[128,2048]{1,0:T(8,128)(2,1)}, bf16[128,2048]{1,0:T(8,128)(2,1)S(1)}, u32[]{:S(2)}, u32[]{:S(2)}) collective-permute-start(bf16[128,2048]{1,0:T(8,128)(2,1)} %copy-done.16), channel_id=1, source_target_pairs={{0,4},{1,5},{2,6},{3,7},{4,0},{5,1},{6,2},{7,3},{8,12},{9,13},{10,... | collective-permute-start | bytes 1572872 | tf_op jit(solution)/shard_map/ppermute | solution.py:926
  287.7 29.7 %collective-permute-start.77 = (bf16[128,2048]{1,0:T(8,128)(2,1)}, bf16[128,2048]{1,0:T(8,128)(2,1)S(1)}, u32[]{:S(2)}, u32[]{:S(2)}) collective-permute-start(bf16[128,2048]{1,0:T(8,128)(2,1)} %copy-done.15), channel_id=1, source_target_pairs={{0,6},{1,7},{2,4},{3,5},{4,2},{5,3},{6,0},{7,1},{8,14},{9,15},{10,... | collective-permute-start | bytes 1572872 | tf_op jit(solution)/shard_map/ppermute | solution.py:926
  326.8 9.4 %collective-permute-start.79 = (bf16[128,1024]{1,0:T(8,128)(2,1)}, bf16[128,1024]{1,0:T(8,128)(2,1)S(1)}, u32[]{:S(2)}, u32[]{:S(2)}) collective-permute-start(bf16[128,1024]{1,0:T(8,128)(2,1)} %get-tuple-element.262), channel_id=1, source_target_pairs={{0,2},{1,3},{2,0},{3,1},{4,6},{5,7},{6,4},{7,5},{8,10},{9,11},{10,... | collective-permute-start | bytes 786440 | tf_op jit(solution)/shard_map/ppermute | solution.py:926
  327.2 9.0 %collective-permute-start.80 = (bf16[128,1024]{1,0:T(8,128)(2,1)S(1)}, bf16[128,1024]{1,0:T(8,128)(2,1)S(1)}, u32[]{:S(2)}, u32[]{:S(2)}) collective-permute-start(bf16[128,1024]{1,0:T(8,128)(2,1)S(1)} %copy-done.25), channel_id=1, source_target_pairs={{0,4},{1,5},{2,6},{3,7},{4,0},{5,1},{6,2},{7,3},{8,12},{9,13},{10,... | collective-permute-start | bytes 786440 | tf_op jit(solution)/shard_map/ppermute | solution.py:926
  328.2 13.1 %collective-permute-start.81 = (bf16[128,1024]{1,0:T(8,128)(2,1)S(1)}, bf16[128,1024]{1,0:T(8,128)(2,1)S(1)}, u32[]{:S(2)}, u32[]{:S(2)}) collective-permute-start(bf16[128,1024]{1,0:T(8,128)(2,1)S(1)} %get-tuple-element.264), channel_id=1, source_target_pairs={{0,6},{1,7},{2,4},{3,5},{4,2},{5,3},{6,0},{7,1},{8,14},{9,15},{10,... | collective-permute-start | bytes 786440 | tf_op jit(solution)/shard_map/ppermute | solution.py:926
  343.9 15.4 %all-to-all-start.4 = ((bf16[8,32,1408]{2,1,0:T(8,128)(2,1)}), bf16[8,32,1408]{2,1,0:T(8,128)(2,1)S(1)}, u32[]{:S(2)}, u32[]{:S(2)}) async-start(bf16[8,32,1408]{2,1,0:T(8,128)(2,1)} %pad_maximum_fusion.2), calls=%async_computation.7 | async-start | bytes 1441792 | tf_op jit(solution)/shard_map/all_to_all | solution.py:1026
  359.3 9.6 %all-to-all-start.3 = ((bf16[8,32,384]{2,1,0:T(8,128)(2,1)}), bf16[8,32,384]{2,1,0:T(8,128)(2,1)S(1)}, u32[]{:S(2)}, u32[]{:S(2)}) async-start(bf16[8,32,384]{2,1,0:T(8,128)(2,1)} %bitcast.37), calls=%async_computation.6 | async-start | bytes 393216 | tf_op jit(solution)/shard_map/all_to_all | solution.py:1026
  (140 other events, 991.7 us)
Sparse Core Ops, SparseCore 0:
  24.7 32.0 all-gather.6
  58.4 26.9 all-gather.8
  87.5 80.2 all-gather.10
  209.5 74.7 reduce-scatter.3
  286.6 27.6 reduce-scatter.5
  326.9 24.2 reduce-scatter.7

commit v4 on v3

--- a/solution.py
+++ b/solution.py
@@ -13,6 +13,7 @@
 WIDE = jnp.float32
 INNER = 8
 STEP = 256
+WIDE_STEP = 512
 LANES = 128
 OUTER = ("ulys", "outer")
 ALL = ("ulys", "outer", "inner")
@@ -78,25 +79,29 @@
     to_order(table, q, qs, rows, jnp.asarray(size**-0.5, LOW))
     to_order(table, k, ks, rows)
     to_order(table, v, vs, rows)
-    for step in range(span // STEP):
-        lo = step * STEP
-        queries = qs[lo : lo + STEP, :]
-        q_at = table[1] + lo + iota((STEP, 1), 0)
+    for step in range(span // WIDE_STEP):
+        lo = step * WIDE_STEP
+        queries = qs[lo : lo + WIDE_STEP, :]
+        q_at = table[1] + lo + iota((WIDE_STEP, 1), 0)
         q_seg = seg_of(q_at, table, 2)
-        count = lo + STEP if causal and chunks == 1 else span
-
-        def scores(head, start):
+        count = lo + WIDE_STEP if causal and chunks == 1 else span
+
+        def mask(start):
             k_at = start + iota((1, count), 1)
             allowed = q_seg == seg_of(k_at, table, 5)
             if causal:
                 allowed = allowed & (k_at <= q_at)
+            return allowed
+
+        def scores(head, start, allowed):
             raw = dot_t(queries, half_lanes(ks[pl.ds(start, count), :], head, size))
             return jnp.where(allowed, raw, -1e30)
 
         parts = []
+        allowed = mask(0) if chunks == 1 else None
         for head in range(2):
             if chunks == 1:
-                raw = scores(head, 0)
+                raw = scores(head, 0, allowed)
                 top = jnp.max(raw, axis=1, keepdims=True)
                 weight = jnp.exp(raw - top)
                 total = jnp.sum(weight, axis=1, keepdims=True)
@@ -106,7 +111,7 @@
                 def absorb(chunk, carry, head=head):
                     top, total, running = carry
                     start = pl.multiple_of(chunk * span, span)
-                    raw = scores(head, start)
+                    raw = scores(head, start, mask(start))
                     new_top = jnp.maximum(top, jnp.max(raw, axis=1, keepdims=True))
                     weight = jnp.exp(raw - new_top)
                     fade = jnp.exp(top - new_top)
@@ -119,16 +124,16 @@
                     chunks,
                     absorb,
                     (
-                        jnp.full((STEP, 1), -1e30, WIDE),
-                        jnp.zeros((STEP, 1), WIDE),
-                        jnp.zeros((STEP, 2 * size), WIDE),
+                        jnp.full((WIDE_STEP, 1), -1e30, WIDE),
+                        jnp.zeros((WIDE_STEP, 1), WIDE),
+                        jnp.zeros((WIDE_STEP, 2 * size), WIDE),
                     ),
                 )
             parts.append(running / total)
-            logs = jnp.broadcast_to(top + jnp.log(total), (STEP, 2 * size))
-            log_total[head : head + 1, lo : lo + STEP] = jnp.transpose(logs)[0:1, :]
-        lane = iota((STEP, 2 * size), 1)
-        ordered[lo : lo + STEP, :] = jnp.where(lane < size, parts[0], parts[1])
+            logs = jnp.broadcast_to(top + jnp.log(total), (WIDE_STEP, 2 * size))
+            log_total[head : head + 1, lo : lo + WIDE_STEP] = jnp.transpose(logs)[0:1, :]
+        lane = iota((WIDE_STEP, 2 * size), 1)
+        ordered[lo : lo + WIDE_STEP, :] = jnp.where(lane < size, parts[0], parts[1])
     from_order(table, ordered, out, rows)
 
 
@@ -145,18 +150,24 @@
     own = refs[0] if lined else None
     refs = refs[1:] if lined else refs
     pieces, refs = refs[:INNER], refs[INNER:]
+    late = []
     if start is not None:
-        packed, refs = refs[0], refs[1:]
+        late, refs = [refs[0]], refs[1:]
         if start == 0:
-            x_all, refs = refs[0], refs[1:]
+            late, refs = late + [refs[0]], refs[1:]
             give, keep, norm_sums, refs = *refs[:3], refs[3:]
         else:
             give, keep, refs = *refs[:2], refs[2:]
     dq, dk, dv, sums, refs = *refs[:4], refs[4:]
     if lined:
         row_keep, row_give, refs = *refs[:2], refs[2:]
-    qs, ks, vs, ups, dqs, dks, dvs, branch, row, marks = refs
+    qs, ks, vs, ups, dqs, dks, dvs, branch, row, marks, *near = refs
     copies = pull(pieces, 0, branch, marks)
+    loads = []
+    for n, source in enumerate(late):
+        loads.append(pltpu.make_async_copy(source, near[n], near[-1].at[n]))
+    for load in loads:
+        load.start()
     span, keys = q.shape[0], k.shape[0]
     chunks = keys // span
     scale = size**-0.5
@@ -179,52 +190,61 @@
         q_at = table[1] + lo + iota((1, STEP), 1)
         q_seg = seg_of(q_at, table, 2)
         count = lo + STEP if causal and chunks == 1 else span
-        total_dq = jnp.zeros((STEP, 2 * size), WIDE)
-        for head in range(2):
-            head_q = half_lanes(queries, head, size)
-            head_up = half_lanes(upstream, head, size)
-            logs = log_total[head : head + 1, lo : lo + STEP]
-
-            def pieces(start, logs=logs, head_up=head_up, head=head):
-                k_at = start + iota((count, 1), 0)
-                allowed = q_seg == seg_of(k_at, table, 5)
-                if causal:
-                    allowed = allowed & (k_at <= q_at)
-                head_k = half_lanes(ks[pl.ds(start, count), :], head, size)
-                raw = dot_t(head_k, queries)
-                probs = jnp.exp(jnp.where(allowed, raw - logs, -1e30))
-                slope = dot_t(vs[pl.ds(start, count), :], head_up)
-                return head_k, probs, probs * slope
-
-            def spread(start, delta, made, head_q=head_q, head_up=head_up):
-                head_k, probs, lean = made
-                push = (lean - probs * delta).astype(LOW)
-                dvs[pl.ds(start, count), :] += dot_n(probs.astype(LOW), head_up)
-                dks[pl.ds(start, count), :] += dot_n(push, head_q)
-                return dot_c(push, head_k)
-
-            if chunks == 1:
-                made = pieces(0)
-                delta = jnp.sum(made[2], axis=0, keepdims=True)
-                total_dq = total_dq + spread(0, delta, made)
-            else:
-
-                def measure(chunk, delta):
-                    made = pieces(pl.multiple_of(chunk * span, span))
-                    return delta + jnp.sum(made[2], axis=0, keepdims=True)
-
-                delta = lax.fori_loop(0, chunks, measure, jnp.zeros((1, STEP), WIDE))
-
-                def absorb(chunk, running, delta=delta):
-                    start = pl.multiple_of(chunk * span, span)
-                    return running + spread(start, delta, pieces(start))
-
-                total_dq = lax.fori_loop(0, chunks, absorb, total_dq)
+        q_pair = [half_lanes(queries, head, size) for head in range(2)]
+        up_pair = [half_lanes(upstream, head, size) for head in range(2)]
+        logs = [log_total[head : head + 1, lo : lo + STEP] for head in range(2)]
+
+        def make(start):
+            k_at = start + iota((count, 1), 0)
+            allowed = q_seg == seg_of(k_at, table, 5)
+            if causal:
+                allowed = allowed & (k_at <= q_at)
+            keys_here = ks[pl.ds(start, count), :]
+            k_pair = [half_lanes(keys_here, head, size) for head in range(2)]
+            probs, lean = [], []
+            for head in range(2):
+                raw = dot_t(k_pair[head], queries)
+                probs.append(jnp.exp(jnp.where(allowed, raw - logs[head], -1e30)))
+                slope = dot_t(vs[pl.ds(start, count), :], up_pair[head])
+                lean.append(probs[head] * slope)
+            return k_pair, probs, lean
+
+        def settle(start, delta, made):
+            k_pair, probs, lean = made
+            push = [(lean[n] - probs[n] * delta[n]).astype(LOW) for n in range(2)]
+            low = [probs[n].astype(LOW) for n in range(2)]
+            at = pl.ds(start, count)
+            dvs[at, :] += dot_n(jnp.concatenate(low, axis=1), jnp.concatenate(up_pair, axis=0))
+            dks[at, :] += dot_n(jnp.concatenate(push, axis=1), jnp.concatenate(q_pair, axis=0))
+            return dot_c(jnp.concatenate(push, axis=0), jnp.concatenate(k_pair, axis=0))
+
+        def slopes(made):
+            return [jnp.sum(made[2][n], axis=0, keepdims=True) for n in range(2)]
+
+        if chunks == 1:
+            made = make(0)
+            total_dq = settle(0, slopes(made), made)
+        else:
+
+            def measure(chunk, delta):
+                more = slopes(make(pl.multiple_of(chunk * span, span)))
+                return [delta[n] + more[n] for n in range(2)]
+
+            delta = lax.fori_loop(0, chunks, measure, [jnp.zeros((1, STEP), WIDE)] * 2)
+
+            def absorb(chunk, running, delta=delta):
+                start = pl.multiple_of(chunk * span, span)
+                return running + settle(start, delta, make(start))
+
+            total_dq = lax.fori_loop(0, chunks, absorb, jnp.zeros((STEP, 2 * size), WIDE))
         dqs[lo : lo + STEP, :] = total_dq * scale
     from_order(table, dqs, dq, rows)
     from_order(table, dks, dk, rows)
     from_order(table, dvs, dv, rows)
+    finish(loads)
     if start is not None:
+        packed = near[0]
+        x_all = near[1] if start == 0 else None
         kinds = 3 if start == 0 else 1
         back = packed[:, start * LANES : (start + kinds) * LANES]
         first = second = None
@@ -326,7 +346,7 @@
             jax.ShapeDtypeStruct((2, pair), WIDE),
         )
         + ((part, part) if lined else ()),
-        in_specs=[SMEM] + [VMEM] * (5 + len(lined)) + [HBM] * INNER + [VMEM] * len(extra),
+        in_specs=[SMEM] + [VMEM] * (5 + len(lined)) + [HBM] * (INNER + len(extra)),
         out_specs=(VMEM,) * (4 + 2 * len(lined) + (len(spread_shape) if back else 0)),
         scratch_shapes=[
             pltpu.VMEM((span, pair), LOW),
@@ -339,7 +359,9 @@
             pltpu.VMEM((span, width), LOW),
             pltpu.VMEM((pair, width), LOW),
             pltpu.SemaphoreType.DMA((INNER,)),
-        ],
+        ]
+        + [pltpu.VMEM(value.shape, LOW) for value in extra]
+        + ([pltpu.SemaphoreType.DMA((2,))] if extra else []),
         compiler_params=room(60),
         cost_estimate=cost(10),
     )(table, q, k, v, log_total, weight, *lined, *pieces, *extra)
@@ -359,11 +381,15 @@
 
 def enter_kernel(kinds, table, far, *refs):
     pieces, refs = refs[:INNER], refs[INNER:]
-    q, k, v, h, params, biases, packed, x_all, marks, mark = refs
-    load = pltpu.make_async_copy(far.at[:, pl.ds(0, packed.shape[1])], packed, mark)
-    load.start()
+    q, k, v, h, params, biases, packed, x_all, blocks, marks, mark = refs
+    loads = []
+    for place in range(far.shape[0]):
+        loads.append(pltpu.make_async_copy(far.at[place], blocks.at[:, place], mark.at[place]))
+    for load in loads:
+        load.start()
     copies = pull(pieces, 0, x_all, marks)
-    load.wait()
+    finish(loads)
+    packed[...] = blocks[...].reshape(packed.shape)
     edge = kinds * LANES
     extra = packed[:, edge : edge + LANES].astype(WIDE)
     params[...] = jnp.transpose(extra)[:16, :]
@@ -400,7 +426,11 @@
         ),
         in_specs=[SMEM] + [HBM] * (1 + INNER),
         out_specs=(VMEM,) * 8,
-        scratch_shapes=[pltpu.SemaphoreType.DMA((INNER,)), pltpu.SemaphoreType.DMA],
+        scratch_shapes=[
+            pltpu.VMEM((packed.shape[1], packed.shape[0]) + packed.shape[2:], LOW),
+            pltpu.SemaphoreType.DMA((INNER,)),
+            pltpu.SemaphoreType.DMA((packed.shape[0],)),
+        ],
         compiler_params=room(60),
         cost_estimate=cost(4),
     )(table, packed, *pieces)
@@ -409,18 +439,20 @@
 def join_kernel(vector, first, query, *refs):
     pieces, weights, refs = refs[:INNER], refs[INNER : 2 * INNER], refs[2 * INNER :]
     if query is None:
-        base, base_own, params, y_own, h, weight, left, heads, marks = refs
+        far, base_own, params, y_own, h, weight, left, heads, marks, base, base_mark = refs
     else:
-        base, params, packed, biases, y_own, h, y_all, cq, weight, left, heads, marks = refs
+        far, params, packed, biases, y_own, h, y_all, cq, weight, left, heads, marks, base, base_mark = refs
     span = left.shape[0]
     block = span // INNER
     loads = pull(weights, 0, weight, marks.at[1])
+    base_load = pltpu.make_async_copy(far, base, base_mark)
     copies = []
     for place in range(INNER):
         copies.append(pltpu.make_async_copy(pieces[place], heads.at[place], marks.at[0, place]))
     for copy in copies:
         copy.start()
-    finish(copies + loads)
+    base_load.start()
+    finish(copies + loads + [base_load])
     parts = INNER // 2
     for part in range(parts):
         at = slice(part * 2 * block, (part + 1) * 2 * block)
@@ -454,13 +486,15 @@
             jax.ShapeDtypeStruct((span, width), LOW),
             jax.ShapeDtypeStruct((span, LANES), LOW),
         ),
-        in_specs=[HBM] * (2 * INNER) + [VMEM] * 4,
+        in_specs=[HBM] * (2 * INNER + 1) + [VMEM] * 3,
         out_specs=(VMEM,) * 4,
         scratch_shapes=[
             pltpu.VMEM((width, width), LOW),
             pltpu.VMEM((span, width), LOW),
             pltpu.VMEM((INNER, span, LANES), LOW),
             pltpu.SemaphoreType.DMA((2, INNER)),
+            pltpu.VMEM((span, width), LOW),
+            pltpu.SemaphoreType.DMA,
         ],
         compiler_params=room(60),
         cost_estimate=cost(6),
@@ -475,13 +509,15 @@
             jax.ShapeDtypeStruct((span // INNER, width), WIDE),
             jax.ShapeDtypeStruct((span, width), LOW),
         ),
-        in_specs=[HBM] * (2 * INNER) + [VMEM] * 3,
+        in_specs=[HBM] * (2 * INNER + 1) + [VMEM] * 2,
         out_specs=(VMEM,) * 2,
         scratch_shapes=[
             pltpu.VMEM((width, width), LOW),
             pltpu.VMEM((span, width), LOW),
             pltpu.VMEM((INNER, span, LANES), LOW),
             pltpu.SemaphoreType.DMA((2, INNER)),
+            pltpu.VMEM((span, width), LOW),
+            pltpu.SemaphoreType.DMA,
         ],
         compiler_params=room(60),
         cost_estimate=cost(5),
@@ -849,6 +885,83 @@
         compiler_params=room(24),
         cost_estimate=cost(3),
     )(*lefts, *rights)
+
+
+def head_lanes(source, start, device):
+    size = LANES // 2
+    at = [start + ((2 * (device & 1) + n) * (INNER // 2) + (device >> 1)) * size for n in (0, 1)]
+    return jnp.concatenate([source[:, a : a + size] for a in at], axis=1)
+
+
+def cut_self_kernel(raw, out):
+    width = INNER * LANES
+    for device in range(INNER):
+        for kind in range(3):
+            at = slice(kind * LANES, (kind + 1) * LANES)
+            out[device, :, at] = head_lanes(raw, kind * width, device)
+        out[device, :, 3 * LANES :] = raw[:, 4 * width :]
+
+
+def cut_self(raw):
+    rows = raw.shape[0]
+    return pl.pallas_call(
+        cut_self_kernel,
+        out_shape=jax.ShapeDtypeStruct((INNER, rows, 4 * LANES), LOW),
+        in_specs=[VMEM],
+        out_specs=VMEM,
+        compiler_params=room(16),
+        cost_estimate=cost(2),
+    )(raw)
+
+
+def cut_other_kernel(hidden, pair_weight, query, first, out):
+    width = INNER * LANES
+    groups = first.shape[1] // (INNER * hidden)
+    for device in range(INNER):
+        for kind, source in enumerate((pair_weight, pair_weight, query)):
+            at = slice(kind * LANES, (kind + 1) * LANES)
+            out[device, :, at] = head_lanes(source, (kind % 2) * width, device)
+        for n in range(groups):
+            at = (n * INNER + device) * hidden
+            start = 3 * LANES + n * hidden
+            out[device, :, start : start + hidden] = first[:, at : at + hidden]
+
+
+def cut_other(pair_weight, query, first, hidden):
+    rows = query.shape[0]
+    lanes = 3 * LANES + first.shape[1] // INNER
+    return pl.pallas_call(
+        functools.partial(cut_other_kernel, hidden),
+        out_shape=jax.ShapeDtypeStruct((INNER, rows, lanes), LOW),
+        in_specs=[VMEM] * 3,
+        out_specs=VMEM,
+        compiler_params=room(16),
+        cost_estimate=cost(1),
+    )(pair_weight, query, first)
+
+
+def pick_rows_kernel(start, table, raw, own, give, marks):
+    width = own.shape[2]
+    copies = []
+    for n, out in enumerate((own, give)):
+        source = raw.at[pl.ds(table[n], 2), :, pl.ds(start, width)]
+        copies.append(pltpu.make_async_copy(source, out, marks.at[n]))
+    for copy in copies:
+        copy.start()
+    finish(copies)
+
+
+def pick_rows(table, start, raw, width):
+    part = jax.ShapeDtypeStruct((2, raw.shape[1], width), LOW)
+    return pl.pallas_call(
+        functools.partial(pick_rows_kernel, start),
+        out_shape=(part, part),
+        in_specs=[SMEM, HBM],
+        out_specs=(VMEM,) * 2,
+        scratch_shapes=[pltpu.SemaphoreType.DMA((2,))],
+        compiler_params=room(16),
+        cost_estimate=cost(1),
+    )(table, raw)
 
 
 def pick_kernel(table, packed, own, give):
@@ -1029,15 +1142,12 @@
 
     core_table = jnp.stack([2 * core, 2 - 2 * core, core, 1 - core]).astype(jnp.int32)
 
-    def head_rows(weight, packed):
+    def head_rows(weight, found):
         if not matched:
             whole = lax.all_gather(weight, ALL, axis=0, tiled=True)
-            mine = lax.dynamic_slice_in_dim(whole, here * pair, pair, axis=0)
-            placed = jnp.take(whole.reshape(INNER, pair, width), order, axis=0)
-            return mine, [placed[n] for n in range(INNER)]
-        own, give = pick(core_table, packed)
-        mine = merge(core_table, own, hop(give, 1))
-        return mine, gather_places(mine)
+            return lax.dynamic_slice_in_dim(whole, here * pair, pair, axis=0)
+        own, give = found()
+        return merge(core_table, own, hop(give, 1))
 
     def shard_features(pieces):
         whole = jnp.stack(
@@ -1084,30 +1194,42 @@
     small = jnp.concatenate([jnp.transpose(vectors), hidden_bias.reshape(share, -1)], axis=1)
     extras = small.shape[1]
     small = jnp.pad(small, ((0, 0), (0, LANES - extras)))
-    small = jnp.broadcast_to(small[None], (INNER, share, LANES))
-    first_cut = jnp.transpose(mlp_in.reshape(share, shares, INNER, hidden), (2, 0, 1, 3))
-    first_cut = first_cut.reshape(INNER, share, shares * hidden)
     def over(value):
         return lax.all_gather(value, OUTER, axis=0)
 
     def row_lanes(weight):
         return jnp.transpose(weight.reshape(-1, INNER, LANES), (1, 0, 2))
 
-    mine = exchange(jnp.concatenate([cut_columns(self_in), small], axis=2))
-    self_far = over(jnp.concatenate([mine, row_lanes(self_out)], axis=2)).reshape(width, -1)
-    pieces = gather_places(after(target[0], mine))
-    other = [cut_columns(cross_kv, cross_query), first_cut]
-    other = exchange(after(jnp.concatenate(other, axis=2), *pieces[1:4]))
-    states = gather_places(after(source[0], other))
+    raw = over(jnp.concatenate([self_in, self_out, small], axis=1))
+    if matched:
+        other = exchange(cut_other(cross_kv, cross_query, mlp_in, hidden))
+    else:
+        first_cut = jnp.transpose(mlp_in.reshape(share, shares, INNER, hidden), (2, 0, 1, 3))
+        first_cut = first_cut.reshape(INNER, share, shares * hidden)
+        other = [cut_columns(cross_kv, cross_query), first_cut]
+        other = exchange(jnp.concatenate(other, axis=2))
+    pieces = gather_places(after(target[0], other))
     cross_far = jnp.concatenate([other[:, :, : 3 * pair], row_lanes(cross_out)], axis=2)
-    cross_far = over(after(cross_far, self_far)).reshape(width, -1)
+    cross_far = over(after(cross_far, raw, *pieces[1:4])).reshape(width, -1)
     first_mine = other[:, :, 3 * pair :].reshape(INNER * share, -1)
     feed_mine = jnp.concatenate([first_mine, mlp_out], axis=0)
-    feed_packed = over(after(feed_mine, self_far))
-
+
+    raw = after(raw, *pieces[1:4])
+    if matched:
+        self_far = exchange(cut_self(raw.reshape(shares * share, -1)))
+        self_far = self_far.reshape(INNER, shares, share, -1)
+    else:
+        cut = by_device(raw[:, :, : 3 * width].reshape(shares, share, 3, width))
+        cut = jnp.transpose(cut, (3, 0, 1, 2, 4)).reshape(INNER, shares, share, 3 * pair)
+        extra = jnp.broadcast_to(raw[None, :, :, 4 * width :], (INNER, shares, share, LANES))
+        self_far = exchange(jnp.concatenate([cut, extra], axis=3))
+        self_far = jnp.transpose(self_far, (1, 0, 2, 3)).reshape(1, 1, width, -1)
     q, k, v, h1, params, biases, self_packed, x_all = enter(head_table, rows, pieces, self_far)
-    sout_mine, w_sout = head_rows(self_out, after(self_far, q, *states[1:4])[:, 4 * pair :])
-    q = after(q, *w_sout[1:4])
+    states, q = gather_places(after(source[0], self_far), q)
+    raw = after(raw, q)
+    feed_packed = over(after(feed_mine, cross_far, q))
+    sout_mine = head_rows(self_out, lambda: pick_rows(core_table, 3 * width, raw, width))
+    q = after(q, sout_mine)
     h_bias = self_packed.reshape(shares, INNER, share, -1)
     h_bias = h_bias[..., 3 * pair + count : 3 * pair + extras]
     h_bias = lax.dynamic_index_in_dim(h_bias, here, 1, False).reshape(1, -1).astype(WIDE)
@@ -1122,16 +1244,22 @@
 
     k, v = stream_keys(k), stream_keys(v)
     att, self_total = attend(self_table, q, k, v, rows, True)
-    att = gather_places(att)
+    w_sout, att = gather_places(sout_mine, att)
+    cross_far = after(cross_far, att)
+    cout_mine = head_rows(cross_out, lambda: pick(core_table, cross_far[:, 3 * pair :]))
     states, ck, cv, cross_packed = pair_heads(rows, states, cross_far, biases)
+    att, cout_mine, states, ck, cv, cross_packed = gather_places(
+        att, cout_mine, states, ck, cv, cross_packed
+    )
     ck, cv = stream_keys(ck), stream_keys(cv)
     y1, h2, y1_all, cq = join_self(att, w_sout, x_all, params, cross_packed, biases)
-    cout_mine, w_cout = head_rows(cross_out, after(cross_far, *att[1:4])[:, 3 * pair :])
-    pull_up = gather_places(after(cotangent[0], *w_cout[1:4]))
-    cq = after(cq, *w_cout[1:4])
+    w_cout, y1, h2, y1_all, cq = gather_places(
+        after(cout_mine, *att[1:4]), y1, h2, y1_all, cq
+    )
     catt, cross_total = attend(cross_table, cq, ck, cv, rows, False)
-    catt = gather_places(after(catt, *pull_up[1:4]))
+    catt = gather_places(catt)
     y2, h3 = join_cross(catt, w_cout, y1_all, y1, params)
+    pull_up, y2, h3 = gather_places(after(cotangent[0], *catt[1:4]), y2, h3)
     active, before_grad, give, keep, h_bias_grad, up = feed(h3, h_bias, feed_packed, pull_up)
     third_own, third_parts = scatter_places(give, keep)
     mlp_grad = feed_grad(active, before_grad, after(h3, third_own), up)
@@ -1172,8 +1300,8 @@
     self_all, packed_grad, side_own, side_parts = gather_places(
         self_branch, packed_grad, side_own, side_parts
     )
-    self_all, mlp_home, packed_grad, side_parts = lax.optimization_barrier(
-        (self_all, mlp_home, packed_grad, side_parts)
+    self_all, packed_grad, side_parts = lax.optimization_barrier(
+        (self_all, packed_grad, side_parts)
     )
     side_parts = scatter_finish(side_parts)
     cross_sum = lax.psum_scatter(packed_grad, OUTER, scatter_dimension=0, tiled=True)
@@ -1217,7 +1345,9 @@
     ).reshape(devices, hidden)
     tiny = jnp.concatenate([vector_part.reshape(devices, -1), bias_part], axis=1)
     tiny = lax.all_to_all(tiny, ALL, 0, 0, tiled=True)
-    give, side_parts, tiny = lax.optimization_barrier((give, side_parts, tiny))
+    give, side_parts, tiny, mlp_home = lax.optimization_barrier(
+        (give, side_parts, tiny, mlp_home)
+    )
     tiny = jnp.sum(after(tiny, give), axis=0)
     first_own, *first_parts = scatter_start(give, keep)
     first_parts = scatter_finish(first_parts)

time: 382 us -> 376 us (0.984)
  waiting for transfers between devices: 118 us -> 94.3 us
  blocking collectives: 12.7 us -> 30.7 us
  local copies, waits for them, and re-layouts: 42.5 us -> 49.7 us
  starting transfers between devices: 72.4 us -> 67.7 us
    all_to_all x0 -> x1, blocking collectives: none -> 16.8 us  [exchange(): return lax.all_to_all(value, 'inner', 0, 0)]
    unnamed x230 -> x232, local copies, waits for them, and re-layouts: 25.4 us -> 37.5 us
    ppermute x83, waiting for transfers between devices: 90 us -> 78.3 us  [hop(): return lax.ppermute(value, 'inner', route)]
    all_to_all x4 -> x3, waiting for transfers between devices: 24.1 us -> 15.7 us  [exchange(): return lax.all_to_all(value, 'inner', 0, 0)]
    all_to_all x4 -> x3, starting transfers between devices: 15.7 us -> 11.4 us  [exchange(): return lax.all_to_all(value, 'inner', 0, 0)]
  transfers between devices with their start and end apart: 93 -> 92, of which waited for: 36 -> 32; matrix products, arithmetic and copies ran while one was open for 5% -> 4% of each run, Pallas kernels for 25% -> 25%
where the time goes in v4:
time: 376 us; the launch traced here: 370 us
  Pallas kernels  105 us (28%)
  waiting for transfers between devices  94.3 us (25%)
  starting transfers between devices  67.7 us (18%)
  local copies, waits for them, and re-layouts  49.7 us (13%)
  blocking collectives  30.7 us (8%)
  between operations  15.6 us (4%)
  other arithmetic  6.93 us (2%)
    ppermute x83, waiting for transfers between devices, hop(): return lax.ppermute(value, 'inner', route)  78.3 us
    ppermute x83, starting transfers between devices, hop(): return lax.ppermute(value, 'inner', route)  55.9 us
    unnamed x232, local copies, waits for them, and re-layouts  37.5 us
    pallas_call x2, Pallas kernels, attend_back(): pl.pallas_call(functools.partial(attend_back_kernel, causal, rows, pair /...  25.4 us
    all_to_all x1, blocking collectives, exchange(): return lax.all_to_all(value, 'inner', 0, 0)  16.8 us
    all_to_all x3, waiting for transfers between devices, exchange(): return lax.all_to_all(value, 'inner', 0, 0)  15.7 us
    all_to_all x1, blocking collectives, per_device(): tiny = lax.all_to_all(tiny, ALL, 0, 0, tiled=True)  13.9 us
    pallas_call x1, Pallas kernels, feed(): pl.pallas_call(feed_kernel, out_shape=(jax.ShapeDtypeStruct((span, hidden...  11.9 us
  transfers between devices with their start and end apart: 92, of which 32 were waited for; matrix products, arithmetic and copies ran while one was open for 4% of the time, Pallas kernels for 25%

profile of v4, /device:TPU:0, one launch (start us, length us, event | category | flops | bytes accessed | tf_op | source)
XLA Modules:
  0.0 370.0 jit_solution(17521303455371491215)
XLA Ops:
  8.9 1.7 fusion.1
  13.6 16.8 %all_to_all.32 = bf16[8,32,1408]{2,1,0:T(8,128)(2,1)S(1)} all-to-all(bf16[8,32,1408]{2,1,0:T(8,128)(2,1)S(1)} %shard_map.229), channel_id=1, replica_groups=mesh['ulys'=4,'blk'=8] {'blk'}, dimensions={0} | all-to-all | bytes 1441792 | tf_op jit(solution)/shard_map/all_to_all | solution.py:1139
  31.5 2.4 collective-permute-start.2
  34.7 5.1 %collective-permute-done.refs_1_ = bf16[128,1024]{1,0:T(8,128)(2,1)} collective-permute-done((bf16[128,1024]{1,0:T(8,128)(2,1)S(1)}, bf16[128,1024]{1,0:T(8,128)(2,1)}, u32[]{:S(2)}, u32[]{:S(2)}) %collective-permute-start) | collective-permute-done | bytes 262176 | tf_op jit(solution)/shard_map/ppermute | solution.py:1039
  39.7 4.9 %collective-permute-done.1.refs_2_ = bf16[128,1024]{1,0:T(8,128)(2,1)} collective-permute-done((bf16[128,1024]{1,0:T(8,128)(2,1)S(1)}, bf16[128,1024]{1,0:T(8,128)(2,1)}, u32[]{:S(2)}, u32[]{:S(2)}) %collective-permute-start.1) | collective-permute-done | bytes 262176 | tf_op jit(solution)/shard_map/ppermute | solution.py:1039
  47.2 3.7 all-to-all-start.1
  53.7 12.5 %all-to-all-done.1 = bf16[8,128,512]{2,1,0:T(8,128)(2,1)S(1)} async-done(((bf16[8,128,512]{2,1,0:T(8,128)(2,1)}), bf16[8,128,512]{2,1,0:T(8,128)(2,1)S(1)}, u32[]{:S(2)}, u32[]{:S(2)}) %all-to-all-start.1) | async-done | bytes 1048608 | tf_op jit(solution)/shard_map/all_to_all | solution.py:1139
  67.4 2.3 collective-permute-start.5
  69.7 6.2 %shard_map.231 = (bf16[1024,128]{1,0:T(8,128)(2,1)}, bf16[1024,128]{1,0:T(8,128)(2,1)}, bf16[1024,128]{1,0:T(8,128)(2,1)}, bf16[1024,1024]{1,0:T(8,128)(2,1)}, f...) custom-call(s32[2]{0:T(128)} %pad_add_fusion.1.table, ...), custom_call_target="tpu_custom_call" | custom-call | flops 4400000000 | bytes 14000000 | tf_op jit(solution)/shard_map/pallas_call | solution.py:415
  75.9 4.6 %collective-permute-done.4.refs_2_ = bf16[128,1024]{1,0:T(8,128)(2,1)} collective-permute-done((bf16[128,1024]{1,0:T(8,128)(2,1)S(1)}, bf16[128,1024]{1,0:T(8,128)(2,1)}, u32[]{:S(2)}, u32[]{:S(2)}) %collective-permute-start.4) | collective-permute-done | bytes 262176 | tf_op jit(solution)/shard_map/ppermute | solution.py:1039
  84.7 1.4 collective-permute-start.12
  86.0 1.8 collective-permute-start.13
  87.8 5.3 %shard_map.234 = (bf16[1024,128]{1,0:T(8,128)(2,1)}, f32[2,1024]{1,0:T(2,128)}) custom-call(s32[10]{0:T(128)} %concatenate.50.table, bf16[1024,128]{1,0:T(8,128)(2,1)} %get-tuple-element.192.q, bf16[1024,128]{1,0:T(8,128)(2,1)} %get-tuple-element.193.k, bf16[1024,128]{1,0:T(8,128)(2,1)} %get-tuple-element.194.v), custom_call_target="tpu_custom_call" | custom-call | flops 6600000000 | bytes 21000000 | tf_op jit(solution)/shard_map/pallas_call | solution.py:307
  93.4 5.3 %collective-permute-done.12.refs_10_ = bf16[128,1024]{1,0:T(8,128)(2,1)S(1)} collective-permute-done((bf16[128,1024]{1,0:T(8,128)(2,1)S(1)}, bf16[128,1024]{1,0:T(8,128)(2,1)S(1)}, u32[]{:S(2)}, u32[]{:S(2)}) %collective-permute-start.12) | collective-permute-done | bytes 262176 | tf_op jit(solution)/shard_map/ppermute | solution.py:1039
  98.7 1.7 collective-permute-start.14
  102.7 1.5 collective-permute-start.16
  104.9 3.2 collective-permute-done.14.refs_1_
  108.1 4.3 %shard_map.237 = (bf16[1024,1024]{1,0:T(8,128)(2,1)}, bf16[1024,128]{1,0:T(8,128)(2,1)}, bf16[1024,128]{1,0:T(8,128)(2,1)}, bf16[1024,384]{1,0:T(8,128)(2,1)}) custom-call(f32[16,128]{1,0:T(8,128)} %get-tuple-element.201.biases.refs_19_, bf16[1024,512]{1,0:T(8,128)(2,1)} %bitcast.81, bf16[128,1024]{1,0:T(8,128)(2,1)} %bitcast.88, ...), custom_call_target="tpu_custom_call" | custom-call | flops 3300000000 | bytes 10500000 | tf_op jit(solution)/shard_map/pallas_call | solution.py:739
  113.0 3.5 collective-permute-done.15.refs_2_
  120.9 1.8 collective-permute-start.24
  123.5 10.4 %shard_map.238 = (f32[128,1024]{1,0:T(8,128)}, bf16[1024,1024]{1,0:T(8,128)(2,1)}, bf16[1024,1024]{1,0:T(8,128)(2,1)}, bf16[1024,128]{1,0:T(8,128)(2,1)}) custom-call(bf16[1024,128]{1,0:T(8,128)(2,1)} %get-tuple-element.215.refs_0_, bf16[1024,128]{1,0:T(8,128)(2,1)} %copy-done.73, bf16[1024,128]{1,0:T(8,128)(2,1)} %copy-done.77, ...), custom_call_target="tpu_custom_call" | custom-call | flops 6600000000 | bytes 21000000 | tf_op jit(solution)/shard_map/pallas_call | solution.py:481
  134.0 6.0 %shard_map.239 = (bf16[1024,128]{1,0:T(8,128)(2,1)}, f32[2,1024]{1,0:T(2,128)}) custom-call(s32[10]{0:T(128)} %concatenate.47.table, bf16[1024,128]{1,0:T(8,128)(2,1)} %get-tuple-element.227.q, bf16[1024,128]{1,0:T(8,128)(2,1)} %get-tuple-element.228.k, bf16[1024,128]{1,0:T(8,128)(2,1)} %get-tuple-element.229.v), custom_call_target="tpu_custom_call" | custom-call | flops 6600000000 | bytes 21000000 | tf_op jit(solution)/shard_map/pallas_call | solution.py:307
  141.7 1.8 collective-permute-start.35
  144.0 5.5 %collective-permute-done.33.refs_1_ = bf16[1024,128]{1,0:T(8,128)(2,1)S(1)} collective-permute-done((bf16[1024,128]{1,0:T(8,128)(2,1)}, bf16[1024,128]{1,0:T(8,128)(2,1)S(1)}, u32[]{:S(2)}, u32[]{:S(2)}) %collective-permute-start.33) | collective-permute-done | bytes 262176 | tf_op jit(solution)/shard_map/ppermute | solution.py:1039
  150.0 3.4 collective-permute-done.35.refs_3_
  154.4 2.1 collective-permute-start.36
  157.2 1.4 collective-permute-start.38
  160.0 8.7 %shard_map.240 = (f32[128,1024]{1,0:T(8,128)}, bf16[1024,1024]{1,0:T(8,128)(2,1)}) custom-call(bf16[1024,128]{1,0:T(8,128)(2,1)} %get-tuple-element.231.refs_0_, bf16[1024,128]{1,0:T(8,128)(2,1)} %copy-done.84, bf16[1024,128]{1,0:T(8,128)(2,1)} %copy-done.85, bf16[1024,128]{1,0:T(8,128)(2,1)} %copy-done.86, bf16[1024,128]{1,0:T(8,128)(2,1)} %copy-done.87, ...), custom_call_target="tpu_custom_call" | custom-call | flops 5500000256 | bytes 17500000 | tf_op jit(solution)/shard_map/pallas_call | solution.py:506
  168.7 1.6 collective-permute-done.37.refs_2_
  173.0 11.9 %shard_map.241 = (bf16[1024,1024]{1,0:T(8,128)(2,1)S(1)}, bf16[1024,1024]{1,0:T(8,128)(2,1)S(1)}, bf16[512,1024]{1,0:T(8,128)(2,1)S(1)}, f32[512,1024]{1,0:T(8,1...) custom-call(bf16[1024,1024]{1,0:T(8,128)(2,1)} %get-tuple-element.256.h, f32[1,1024]{1,0:T(1,128)S(1)} %reshape.183.bias, ...), custom_call_target="tpu_custom_call" | custom-call | flops 14300000256 | bytes 45500000 | tf_op jit(solution)/shard_map/pallas_call | solution.py:572
  185.1 2.5 collective-permute-done.51.took
  189.6 1.8 collective-permute-start.54
  191.3 1.6 copy-done.55
  192.9 4.5 %shard_map.243 = bf16[1024,2048]{1,0:T(8,128)(2,1)S(1)} custom-call(bf16[1024,1024]{1,0:T(8,128)(2,1)S(1)} %get-tuple-element.275.act, bf16[1024,1024]{1,0:T(8,128)(2,1)S(1)} %get-tuple-element.255.slope, bf16[1024,1024]{1,0:T(8,128)(2,1)S(1)} %copy-done.54, bf16[1024,1024]{1,0:T(8,128)(2,1)S(1)} %copy-done.55), custom_call_target="tpu_custom_call" | custom-call | flops 6600000000 | bytes 21000000 | tf_op jit(solution)/shard_map/pallas_call | solution.py:661
  197.5 2.0 copy-done.4
  199.5 2.9 collective-permute-done.53.two
  205.8 1.8 collective-permute-start.57
  207.6 5.8 %collective-permute-done.55.refs_2_ = bf16[128,1024]{1,0:T(8,128)(2,1)S(1)} collective-permute-done((bf16[128,1024]{1,0:T(8,128)(2,1)S(1)}, bf16[128,1024]{1,0:T(8,128)(2,1)S(1)}, u32[]{:S(2)}, u32[]{:S(2)}) %collective-permute-start.55) | collective-permute-done | bytes 262176 | tf_op jit(solution)/shard_map/ppermute | solution.py:1039
  213.3 2.9 collective-permute-done.56.refs_3_
  219.9 13.1 %shard_map.245 = (bf16[512,1024]{1,0:T(8,128)(2,1)}, f32[512,1024]{1,0:T(8,128)}, bf16[1024,128]{1,0:T(8,128)(2,1)}, bf16[1024,128]{1,0:T(8,128)(2,1)}, bf16[102...) custom-call(s32[10]{0:T(128)} %concatenate.47.table, ...), custom_call_target="tpu_custom_call" | custom-call | flops 11000000512 | bytes 35000000 | tf_op jit(solution)/shard_map/pallas_call | solution.py:339
  233.2 2.7 collective-permute-done.62.took
  236.0 1.6 copy-done.35
  238.7 2.1 collective-permute-start.64
  241.3 2.2 copy-done.8
  244.7 3.7 %shard_map.248 = (bf16[512,2048]{1,0:T(8,128)(2,1)}, f32[512,2048]{1,0:T(8,128)S(1)}) custom-call(bf16[1024,1024]{1,0:T(8,128)(2,1)S(1)} %copy-done.46, bf16[4,512,1024]{2,1,0:T(8,128)(2,1)S(1)} %bitcast.58, bf16[1024,128]{1,0:T(8,128)(2,1)S(1)} %copy-done.58, bf16[1024,128]{1,0:T(8,128)(2,1)S(1)} %copy-done.59, bf16[1024,384]{1,0:T(8,128)(2,1)S(1)} %copy-done.56), custom_call_target="tpu_custom_call" | custom-call | flops 4400000000 | bytes 14000000 | tf_op jit(solution)/shard_map/pallas_call | solution.py:611
  250.4 1.6 collective-permute-done.64.two
  259.8 1.7 shard_map.250
  261.5 2.3 copy-done.3
  266.5 2.2 collective-permute-done.67.refs_3_
  275.3 1.4 collective-permute-start.76
  277.8 12.3 %shard_map.252 = (bf16[512,1024]{1,0:T(8,128)(2,1)}, f32[512,1024]{1,0:T(8,128)}, f32[2,1024]{1,0:T(2,128)}, bf16[1024,128]{1,0:T(8,128)(2,1)}, bf16[1024,128]{1...) custom-call(s32[10]{0:T(128)} %concatenate.50.table, ...), custom_call_target="tpu_custom_call" | custom-call | flops 11000000512 | bytes 35000000 | tf_op jit(solution)/shard_map/pallas_call | solution.py:339
  292.5 13.9 %all_to_all.33 = f32[32,1,672]{2,1,0:T(1,128)S(1)} all-to-all(f32[32,1,672]{2,1,0:T(1,128)S(1)} %copy.57), channel_id=1, replica_groups=mesh['ulys'=4,'blk'=8] {'ulys','blk'}, dimensions={0} | all-to-all | bytes 172032 | tf_op jit(solution)/shard_map/all_to_all | solution.py:1347
  307.5 2.5 collective-permute-done.78.took
  310.0 1.6 copy-done.34
  317.8 1.6 shard_map.257
  320.8 2.2 collective-permute-start.81
  323.1 5.9 %collective-permute-done.79.one = bf16[128,1024]{1,0:T(8,128)(2,1)S(1)} collective-permute-done((bf16[128,1024]{1,0:T(8,128)(2,1)}, bf16[128,1024]{1,0:T(8,128)(2,1)S(1)}, u32[]{:S(2)}, u32[]{:S(2)}) %collective-permute-start.79) | collective-permute-done | bytes 262176 | tf_op jit(solution)/shard_map/ppermute | solution.py:1039
  328.9 5.2 %collective-permute-done.80.two = bf16[128,1024]{1,0:T(8,128)(2,1)S(1)} collective-permute-done((bf16[128,1024]{1,0:T(8,128)(2,1)S(1)}, bf16[128,1024]{1,0:T(8,128)(2,1)S(1)}, u32[]{:S(2)}, u32[]{:S(2)}) %collective-permute-start.80) | collective-permute-done | bytes 262176 | tf_op jit(solution)/shard_map/ppermute | solution.py:1039
  336.1 3.7 all-to-all-start.4
  347.4 2.5 shard_map.255
  350.0 1.6 slice.83
  351.7 4.0 %all-to-all-start.3 = ((bf16[8,32,384]{2,1,0:T(8,128)(2,1)}), bf16[8,32,384]{2,1,0:T(8,128)(2,1)S(1)}, u32[]{:S(2)}, u32[]{:S(2)}) async-start(bf16[8,32,384]{2,1,0:T(8,128)(2,1)} %bitcast.33), calls=%async_computation.6 | async-start | bytes 393216 | tf_op jit(solution)/shard_map/all_to_all | solution.py:1139
  355.7 1.6 shard_map.259
  358.6 3.3 all-to-all-done.3.got
  (446 shorter events, 89.6 us)
Async XLA Ops:
  7.2 37.4 %all-gather.7.cloned.1.call-start = ((), (), s32[]{:S(2)}) async-start(), calls=%async_computation.11 | async-start | bytes 1351680 | tf_op jit(solution)/shard_map/all_gather | solution.py:1198
  10.6 69.9 %all-gather.9.cloned.1.call-start = ((), (), s32[]{:S(2)}) async-start(), calls=%async_computation.12 | async-start | bytes 1310720 | tf_op jit(solution)/shard_map/all_gather | solution.py:1198
  30.4 9.3 %collective-permute-start = (bf16[128,1024]{1,0:T(8,128)(2,1)S(1)}, bf16[128,1024]{1,0:T(8,128)(2,1)}, u32[]{:S(2)}, u32[]{:S(2)}) collective-permute-start(bf16[128,1024]{1,0:T(8,128)(2,1)S(1)} %bitcast.67), channel_id=1, source_target_pairs={{0,2},{1,3},{2,0},{3,1},{4,6},{5,7},{6,4},{7,5},{8,10},{9,11},{10,... | collective-permute-start | bytes 786440 | tf_op jit(solution)/shard_map/ppermute | solution.py:1039
  31.0 13.7 %collective-permute-start.1 = (bf16[128,1024]{1,0:T(8,128)(2,1)S(1)}, bf16[128,1024]{1,0:T(8,128)(2,1)}, u32[]{:S(2)}, u32[]{:S(2)}) collective-permute-start(bf16[128,1024]{1,0:T(8,128)(2,1)S(1)} %bitcast.68), channel_id=1, source_target_pairs={{0,4},{1,5},{2,6},{3,7},{4,0},{5,1},{6,2},{7,3},{8,12},{9,13},{10,... | collective-permute-start | bytes 786440 | tf_op jit(solution)/shard_map/ppermute | solution.py:1039
  31.5 13.1 %collective-permute-start.2 = (bf16[128,1024]{1,0:T(8,128)(2,1)S(1)}, bf16[128,1024]{1,0:T(8,128)(2,1)}, u32[]{:S(2)}, u32[]{:S(2)}) collective-permute-start(bf16[128,1024]{1,0:T(8,128)(2,1)S(1)} %bitcast.69), channel_id=1, source_target_pairs={{0,6},{1,7},{2,4},{3,5},{4,2},{5,3},{6,0},{7,1},{8,14},{9,15},{10,... | collective-permute-start | bytes 786440 | tf_op jit(solution)/shard_map/ppermute | solution.py:1039
  47.2 19.0 %all-to-all-start.1 = ((bf16[8,128,512]{2,1,0:T(8,128)(2,1)}), bf16[8,128,512]{2,1,0:T(8,128)(2,1)S(1)}, u32[]{:S(2)}, u32[]{:S(2)}) async-start(bf16[8,128,512]{2,1,0:T(8,128)(2,1)} %shard_map.230), calls=%async_computation.1 | async-start | bytes 2097152 | tf_op jit(solution)/shard_map/all_to_all | solution.py:1139
  50.9 122.1 %all-gather.11.cloned.1.call-start = ((), (), s32[]{:S(2)}) async-start(), calls=%async_computation.13 | async-start | bytes 5242880 | tf_op jit(solution)/shard_map/all_gather | solution.py:1198
  50.9 15.8 %collective-permute-start.6 = (bf16[128,1024]{1,0:T(8,128)(2,1)S(1)}, bf16[128,1024]{1,0:T(8,128)(2,1)}, u32[]{:S(2)}, u32[]{:S(2)}) collective-permute-start(bf16[128,1024]{1,0:T(8,128)(2,1)S(1)} %bitcast.70), channel_id=1, source_target_pairs={{0,1},{1,0},{2,3},{3,2},{4,5},{5,4},{6,7},{7,6},{8,9},{9,8},{10,11... | collective-permute-start | bytes 786440 | tf_op jit(solution)/shard_map/ppermute | solution.py:1039
  51.3 16.0 %collective-permute-start.7 = (bf16[128,1024]{1,0:T(8,128)(2,1)}, bf16[128,1024]{1,0:T(8,128)(2,1)}, u32[]{:S(2)}, u32[]{:S(2)}) collective-permute-start(bf16[128,1024]{1,0:T(8,128)(2,1)} %collective-permute-done.refs_1_), channel_id=1, source_target_pairs={{0,1},{1,0},{2,3},{3,2},{4,5},{5,4},{6,7},{7,6},{8,9},{9,8},{10,11... | collective-permute-start | bytes 786440 | tf_op jit(solution)/shard_map/ppermute | solution.py:1039
  51.5 18.2 %collective-permute-start.8 = (bf16[128,1024]{1,0:T(8,128)(2,1)}, bf16[128,1024]{1,0:T(8,128)(2,1)}, u32[]{:S(2)}, u32[]{:S(2)}) collective-permute-start(bf16[128,1024]{1,0:T(8,128)(2,1)} %collective-permute-done.1.refs_2_), channel_id=1, source_target_pairs={{0,1},{1,0},{2,3},{3,2},{4,5},{5,4},{6,7},{7,6},{8,9},{9,8},{10,11... | collective-permute-start | bytes 786440 | tf_op jit(solution)/shard_map/ppermute | solution.py:1039
  51.8 17.9 %collective-permute-start.9 = (bf16[128,1024]{1,0:T(8,128)(2,1)}, bf16[128,1024]{1,0:T(8,128)(2,1)}, u32[]{:S(2)}, u32[]{:S(2)}) collective-permute-start(bf16[128,1024]{1,0:T(8,128)(2,1)} %collective-permute-done.2.refs_3_), channel_id=1, source_target_pairs={{0,1},{1,0},{2,3},{3,2},{4,5},{5,4},{6,7},{7,6},{8,9},{9,8},{10,11... | collective-permute-start | bytes 786440 | tf_op jit(solution)/shard_map/ppermute | solution.py:1039
  66.2 9.7 %collective-permute-start.3 = (bf16[128,1024]{1,0:T(8,128)(2,1)S(1)}, bf16[128,1024]{1,0:T(8,128)(2,1)}, u32[]{:S(2)}, u32[]{:S(2)}) collective-permute-start(bf16[128,1024]{1,0:T(8,128)(2,1)S(1)} %bitcast.89), channel_id=1, source_target_pairs={{0,2},{1,3},{2,0},{3,1},{4,6},{5,7},{6,4},{7,5},{8,10},{9,11},{10,... | collective-permute-start | bytes 786440 | tf_op jit(solution)/shard_map/ppermute | solution.py:1039
  66.7 13.8 %collective-permute-start.4 = (bf16[128,1024]{1,0:T(8,128)(2,1)S(1)}, bf16[128,1024]{1,0:T(8,128)(2,1)}, u32[]{:S(2)}, u32[]{:S(2)}) collective-permute-start(bf16[128,1024]{1,0:T(8,128)(2,1)S(1)} %bitcast.90), channel_id=1, source_target_pairs={{0,4},{1,5},{2,6},{3,7},{4,0},{5,1},{6,2},{7,3},{8,12},{9,13},{10,... | collective-permute-start | bytes 786440 | tf_op jit(solution)/shard_map/ppermute | solution.py:1039
  67.4 13.2 %collective-permute-start.5 = (bf16[128,1024]{1,0:T(8,128)(2,1)S(1)}, bf16[128,1024]{1,0:T(8,128)(2,1)}, u32[]{:S(2)}, u32[]{:S(2)}) collective-permute-start(bf16[128,1024]{1,0:T(8,128)(2,1)S(1)} %bitcast.91), channel_id=1, source_target_pairs={{0,6},{1,7},{2,4},{3,5},{4,2},{5,3},{6,0},{7,1},{8,14},{9,15},{10,... | collective-permute-start | bytes 786440 | tf_op jit(solution)/shard_map/ppermute | solution.py:1039
  80.6 225.9 %reduce-scatter.4.cloned.1.call-start = ((), (), s32[]{:S(2)}) async-start(), calls=%async_computation.8 | async-start | bytes 5242880 | tf_op jit(solution)/shard_map/reduce_scatter | solution.py:1267
  83.1 18.9 %collective-permute-start.18 = (bf16[128,1024]{1,0:T(8,128)(2,1)S(1)}, bf16[128,1024]{1,0:T(8,128)(2,1)S(1)}, u32[]{:S(2)}, u32[]{:S(2)}) collective-permute-start(bf16[128,1024]{1,0:T(8,128)(2,1)S(1)} %bitcast.92), channel_id=1, source_target_pairs={{0,1},{1,0},{2,3},{3,2},{4,5},{5,4},{6,7},{7,6},{8,9},{9,8},{10,11... | collective-permute-start | bytes 786440 | tf_op jit(solution)/shard_map/ppermute | solution.py:1039
  83.6 18.7 %collective-permute-start.19 = (bf16[128,1024]{1,0:T(8,128)(2,1)}, bf16[128,1024]{1,0:T(8,128)(2,1)S(1)}, u32[]{:S(2)}, u32[]{:S(2)}) collective-permute-start(bf16[128,1024]{1,0:T(8,128)(2,1)} %collective-permute-done.3.refs_1_), channel_id=1, source_target_pairs={{0,1},{1,0},{2,3},{3,2},{4,5},{5,4},{6,7},{7,6},{8,9},{9,8},{10,11... | collective-permute-start | bytes 786440 | tf_op jit(solution)/shard_map/ppermute | solution.py:1039
  84.2 9.2 %collective-permute-start.11 = (bf16[128,1024]{1,0:T(8,128)(2,1)S(1)}, bf16[128,1024]{1,0:T(8,128)(2,1)S(1)}, u32[]{:S(2)}, u32[]{:S(2)}) collective-permute-start(bf16[128,1024]{1,0:T(8,128)(2,1)S(1)} %shard_map.233.refs_8_.weight), channel_id=1, source_target_pairs={{0,2},{1,3},{2,0},{3,1},{4,6},{5,7},{6,4},{7,5},{8,10},{9,11},{10,... | collective-permute-start | bytes 786440 | tf_op jit(solution)/shard_map/ppermute | solution.py:1039
  84.7 14.0 %collective-permute-start.12 = (bf16[128,1024]{1,0:T(8,128)(2,1)S(1)}, bf16[128,1024]{1,0:T(8,128)(2,1)S(1)}, u32[]{:S(2)}, u32[]{:S(2)}) collective-permute-start(bf16[128,1024]{1,0:T(8,128)(2,1)S(1)} %shard_map.233.refs_8_.weight), channel_id=1, source_target_pairs={{0,4},{1,5},{2,6},{3,7},{4,0},{5,1},{6,2},{7,3},{8,12},{9,13},{10,... | collective-permute-start | bytes 786440 | tf_op jit(solution)/shard_map/ppermute | solution.py:1039
  86.0 12.7 %collective-permute-start.13 = (bf16[128,1024]{1,0:T(8,128)(2,1)S(1)}, bf16[128,1024]{1,0:T(8,128)(2,1)S(1)}, u32[]{:S(2)}, u32[]{:S(2)}) collective-permute-start(bf16[128,1024]{1,0:T(8,128)(2,1)S(1)} %shard_map.233.refs_8_.weight), channel_id=1, source_target_pairs={{0,6},{1,7},{2,4},{3,5},{4,2},{5,3},{6,0},{7,1},{8,14},{9,15},{10,... | collective-permute-start | bytes 786440 | tf_op jit(solution)/shard_map/ppermute | solution.py:1039
  93.4 9.3 %collective-permute-start.20 = (bf16[128,1024]{1,0:T(8,128)(2,1)}, bf16[128,1024]{1,0:T(8,128)(2,1)S(1)}, u32[]{:S(2)}, u32[]{:S(2)}) collective-permute-start(bf16[128,1024]{1,0:T(8,128)(2,1)} %collective-permute-done.4.refs_2_), channel_id=1, source_target_pairs={{0,1},{1,0},{2,3},{3,2},{4,5},{5,4},{6,7},{7,6},{8,9},{9,8},{10,11... | collective-permute-start | bytes 786440 | tf_op jit(solution)/shard_map/ppermute | solution.py:1039
  98.7 5.5 %collective-permute-start.21 = (bf16[128,1024]{1,0:T(8,128)(2,1)}, bf16[128,1024]{1,0:T(8,128)(2,1)S(1)}, u32[]{:S(2)}, u32[]{:S(2)}) collective-permute-start(bf16[128,1024]{1,0:T(8,128)(2,1)} %collective-permute-done.5.refs_3_), channel_id=1, source_target_pairs={{0,1},{1,0},{2,3},{3,2},{4,5},{5,4},{6,7},{7,6},{8,9},{9,8},{10,11... | collective-permute-start | bytes 786440 | tf_op jit(solution)/shard_map/ppermute | solution.py:1039
  98.7 9.4 %collective-permute-start.14 = (bf16[1024,128]{1,0:T(8,128)(2,1)}, bf16[1024,128]{1,0:T(8,128)(2,1)S(1)}, u32[]{:S(2)}, u32[]{:S(2)}) collective-permute-start(bf16[1024,128]{1,0:T(8,128)(2,1)} %get-tuple-element.215.refs_0_), channel_id=1, source_target_pairs={{0,2},{1,3},{2,0},{3,1},{4,6},{5,7},{6,4},{7,5},{8,10},{9,11},{10,... | collective-permute-start | bytes 786440 | tf_op jit(solution)/shard_map/ppermute | solution.py:1039
  102.4 14.2 %collective-permute-start.15 = (bf16[1024,128]{1,0:T(8,128)(2,1)S(1)}, bf16[1024,128]{1,0:T(8,128)(2,1)S(1)}, u32[]{:S(2)}, u32[]{:S(2)}) collective-permute-start(bf16[1024,128]{1,0:T(8,128)(2,1)S(1)} %copy-done.69), channel_id=1, source_target_pairs={{0,4},{1,5},{2,6},{3,7},{4,0},{5,1},{6,2},{7,3},{8,12},{9,13},{10,... | collective-permute-start | bytes 786440 | tf_op jit(solution)/shard_map/ppermute | solution.py:1039
  102.7 13.8 %collective-permute-start.16 = (bf16[1024,128]{1,0:T(8,128)(2,1)S(1)}, bf16[1024,128]{1,0:T(8,128)(2,1)S(1)}, u32[]{:S(2)}, u32[]{:S(2)}) collective-permute-start(bf16[1024,128]{1,0:T(8,128)(2,1)S(1)} %copy-done.69), channel_id=1, source_target_pairs={{0,6},{1,7},{2,4},{3,5},{4,2},{5,3},{6,0},{7,1},{8,14},{9,15},{10,... | collective-permute-start | bytes 786440 | tf_op jit(solution)/shard_map/ppermute | solution.py:1039
  104.2 12.8 %collective-permute-start.29 = (bf16[128,1024]{1,0:T(8,128)(2,1)S(1)}, bf16[128,1024]{1,0:T(8,128)(2,1)S(1)}, u32[]{:S(2)}, u32[]{:S(2)}) collective-permute-start(bf16[128,1024]{1,0:T(8,128)(2,1)S(1)} %shard_map.233.refs_8_.weight), channel_id=1, source_target_pairs={{0,1},{1,0},{2,3},{3,2},{4,5},{5,4},{6,7},{7,6},{8,9},{9,8},{10,11... | collective-permute-start | bytes 786440 | tf_op jit(solution)/shard_map/ppermute | solution.py:1039
  104.9 12.3 %collective-permute-start.30 = (bf16[128,1024]{1,0:T(8,128)(2,1)S(1)}, bf16[128,1024]{1,0:T(8,128)(2,1)S(1)}, u32[]{:S(2)}, u32[]{:S(2)}) collective-permute-start(bf16[128,1024]{1,0:T(8,128)(2,1)S(1)} %collective-permute-done.11.refs_9_), channel_id=1, source_target_pairs={{0,1},{1,0},{2,3},{3,2},{4,5},{5,4},{6,7},{7,6},{8,9},{9,8},{10,11... | collective-permute-start | bytes 786440 | tf_op jit(solution)/shard_map/ppermute | solution.py:1039
  108.1 9.5 %collective-permute-start.31 = (bf16[128,1024]{1,0:T(8,128)(2,1)S(1)}, bf16[128,1024]{1,0:T(8,128)(2,1)S(1)}, u32[]{:S(2)}, u32[]{:S(2)}) collective-permute-start(bf16[128,1024]{1,0:T(8,128)(2,1)S(1)} %collective-permute-done.12.refs_10_), channel_id=1, source_target_pairs={{0,1},{1,0},{2,3},{3,2},{4,5},{5,4},{6,7},{7,6},{8,9},{9,8},{10,11... | collective-permute-start | bytes 786440 | tf_op jit(solution)/shard_map/ppermute | solution.py:1039
  117.2 5.5 %collective-permute-start.27 = (bf16[1024,128]{1,0:T(8,128)(2,1)S(1)}, bf16[1024,128]{1,0:T(8,128)(2,1)S(1)}, u32[]{:S(2)}, u32[]{:S(2)}) collective-permute-start(bf16[1024,128]{1,0:T(8,128)(2,1)S(1)} %collective-permute-done.15.refs_2_), channel_id=1, source_target_pairs={{0,1},{1,0},{2,3},{3,2},{4,5},{5,4},{6,7},{7,6},{8,9},{9,8},{10,11... | collective-permute-start | bytes 786440 | tf_op jit(solution)/shard_map/ppermute | solution.py:1039
  119.2 14.7 %collective-permute-start.22 = (bf16[128,1024]{1,0:T(8,128)(2,1)S(1)}, bf16[128,1024]{1,0:T(8,128)(2,1)S(1)}, u32[]{:S(2)}, u32[]{:S(2)}) collective-permute-start(bf16[128,1024]{1,0:T(8,128)(2,1)S(1)} %shard_map.236.refs_8_.weight), channel_id=1, source_target_pairs={{0,2},{1,3},{2,0},{3,1},{4,6},{5,7},{6,4},{7,5},{8,10},{9,11},{10,... | collective-permute-start | bytes 786440 | tf_op jit(solution)/shard_map/ppermute | solution.py:1039
  119.6 14.4 %collective-permute-start.23 = (bf16[128,1024]{1,0:T(8,128)(2,1)S(1)}, bf16[128,1024]{1,0:T(8,128)(2,1)S(1)}, u32[]{:S(2)}, u32[]{:S(2)}) collective-permute-start(bf16[128,1024]{1,0:T(8,128)(2,1)S(1)} %shard_map.236.refs_8_.weight), channel_id=1, source_target_pairs={{0,4},{1,5},{2,6},{3,7},{4,0},{5,1},{6,2},{7,3},{8,12},{9,13},{10,... | collective-permute-start | bytes 786440 | tf_op jit(solution)/shard_map/ppermute | solution.py:1039
  120.9 13.1 %collective-permute-start.24 = (bf16[128,1024]{1,0:T(8,128)(2,1)S(1)}, bf16[128,1024]{1,0:T(8,128)(2,1)S(1)}, u32[]{:S(2)}, u32[]{:S(2)}) collective-permute-start(bf16[128,1024]{1,0:T(8,128)(2,1)S(1)} %shard_map.236.refs_8_.weight), channel_id=1, source_target_pairs={{0,6},{1,7},{2,4},{3,5},{4,2},{5,3},{6,0},{7,1},{8,14},{9,15},{10,... | collective-permute-start | bytes 786440 | tf_op jit(solution)/shard_map/ppermute | solution.py:1039
  140.0 9.5 %collective-permute-start.33 = (bf16[1024,128]{1,0:T(8,128)(2,1)}, bf16[1024,128]{1,0:T(8,128)(2,1)S(1)}, u32[]{:S(2)}, u32[]{:S(2)}) collective-permute-start(bf16[1024,128]{1,0:T(8,128)(2,1)} %get-tuple-element.231.refs_0_), channel_id=1, source_target_pairs={{0,2},{1,3},{2,0},{3,1},{4,6},{5,7},{6,4},{7,5},{8,10},{9,11},{10,... | collective-permute-start | bytes 786440 | tf_op jit(solution)/shard_map/ppermute | solution.py:1039
  140.9 8.6 %collective-permute-start.34 = (bf16[1024,128]{1,0:T(8,128)(2,1)}, bf16[1024,128]{1,0:T(8,128)(2,1)S(1)}, u32[]{:S(2)}, u32[]{:S(2)}) collective-permute-start(bf16[1024,128]{1,0:T(8,128)(2,1)} %get-tuple-element.231.refs_0_), channel_id=1, source_target_pairs={{0,4},{1,5},{2,6},{3,7},{4,0},{5,1},{6,2},{7,3},{8,12},{9,13},{10,... | collective-permute-start | bytes 786440 | tf_op jit(solution)/shard_map/ppermute | solution.py:1039
  141.7 11.7 %collective-permute-start.35 = (bf16[1024,128]{1,0:T(8,128)(2,1)}, bf16[1024,128]{1,0:T(8,128)(2,1)S(1)}, u32[]{:S(2)}, u32[]{:S(2)}) collective-permute-start(bf16[1024,128]{1,0:T(8,128)(2,1)} %get-tuple-element.231.refs_0_), channel_id=1, source_target_pairs={{0,6},{1,7},{2,4},{3,5},{4,2},{5,3},{6,0},{7,1},{8,14},{9,15},{10,... | collective-permute-start | bytes 786440 | tf_op jit(solution)/shard_map/ppermute | solution.py:1039
  143.5 9.9 %collective-permute-start.39 = (bf16[1024,128]{1,0:T(8,128)(2,1)}, bf16[1024,128]{1,0:T(8,128)(2,1)S(1)}, u32[]{:S(2)}, u32[]{:S(2)}) collective-permute-start(bf16[1024,128]{1,0:T(8,128)(2,1)} %get-tuple-element.231.refs_0_), channel_id=1, source_target_pairs={{0,1},{1,0},{2,3},{3,2},{4,5},{5,4},{6,7},{7,6},{8,9},{9,8},{10,11... | collective-permute-start | bytes 786440 | tf_op jit(solution)/shard_map/ppermute | solution.py:1039
  143.5 10.4 %collective-permute-start.43 = (bf16[128,1024]{1,0:T(8,128)(2,1)S(1)}, bf16[128,1024]{1,0:T(8,128)(2,1)S(1)}, u32[]{:S(2)}, u32[]{:S(2)}) collective-permute-start(bf16[128,1024]{1,0:T(8,128)(2,1)S(1)} %shard_map.236.refs_8_.weight), channel_id=1, source_target_pairs={{0,1},{1,0},{2,3},{3,2},{4,5},{5,4},{6,7},{7,6},{8,9},{9,8},{10,11... | collective-permute-start | bytes 786440 | tf_op jit(solution)/shard_map/ppermute | solution.py:1039
  154.4 14.2 %collective-permute-start.36 = (bf16[128,1024]{1,0:T(8,128)(2,1)S(1)}, bf16[128,1024]{1,0:T(8,128)(2,1)S(1)}, u32[]{:S(2)}, u32[]{:S(2)}) collective-permute-start(bf16[128,1024]{1,0:T(8,128)(2,1)S(1)} %bitcast.60), channel_id=1, source_target_pairs={{0,2},{1,3},{2,0},{3,1},{4,6},{5,7},{6,4},{7,5},{8,10},{9,11},{10,... | collective-permute-start | bytes 786440 | tf_op jit(solution)/shard_map/ppermute | solution.py:1039
  156.6 13.7 %collective-permute-start.37 = (bf16[128,1024]{1,0:T(8,128)(2,1)S(1)}, bf16[128,1024]{1,0:T(8,128)(2,1)S(1)}, u32[]{:S(2)}, u32[]{:S(2)}) collective-permute-start(bf16[128,1024]{1,0:T(8,128)(2,1)S(1)} %bitcast.61), channel_id=1, source_target_pairs={{0,4},{1,5},{2,6},{3,7},{4,0},{5,1},{6,2},{7,3},{8,12},{9,13},{10,... | collective-permute-start | bytes 786440 | tf_op jit(solution)/shard_map/ppermute | solution.py:1039
  157.2 13.1 %collective-permute-start.38 = (bf16[128,1024]{1,0:T(8,128)(2,1)S(1)}, bf16[128,1024]{1,0:T(8,128)(2,1)S(1)}, u32[]{:S(2)}, u32[]{:S(2)}) collective-permute-start(bf16[128,1024]{1,0:T(8,128)(2,1)S(1)} %bitcast.62), channel_id=1, source_target_pairs={{0,6},{1,7},{2,4},{3,5},{4,2},{5,3},{6,0},{7,1},{8,14},{9,15},{10,... | collective-permute-start | bytes 786440 | tf_op jit(solution)/shard_map/ppermute | solution.py:1039
  187.8 11.7 %collective-permute-start.52 = (bf16[128,1024]{1,0:T(8,128)(2,1)S(1)}, bf16[128,1024]{1,0:T(8,128)(2,1)S(1)}, u32[]{:S(2)}, u32[]{:S(2)}) collective-permute-start(bf16[128,1024]{1,0:T(8,128)(2,1)S(1)} %get-tuple-element.251), channel_id=1, source_target_pairs={{0,2},{1,3},{2,0},{3,1},{4,6},{5,7},{6,4},{7,5},{8,10},{9,11},{10,... | collective-permute-start | bytes 786440 | tf_op jit(solution)/shard_map/ppermute | solution.py:1039
  188.7 13.7 %collective-permute-start.53 = (bf16[128,1024]{1,0:T(8,128)(2,1)S(1)}, bf16[128,1024]{1,0:T(8,128)(2,1)S(1)}, u32[]{:S(2)}, u32[]{:S(2)}) collective-permute-start(bf16[128,1024]{1,0:T(8,128)(2,1)S(1)} %get-tuple-element.252), channel_id=1, source_target_pairs={{0,4},{1,5},{2,6},{3,7},{4,0},{5,1},{6,2},{7,3},{8,12},{9,13},{10,... | collective-permute-start | bytes 786440 | tf_op jit(solution)/shard_map/ppermute | solution.py:1039
  189.6 12.8 %collective-permute-start.54 = (bf16[128,1024]{1,0:T(8,128)(2,1)S(1)}, bf16[128,1024]{1,0:T(8,128)(2,1)S(1)}, u32[]{:S(2)}, u32[]{:S(2)}) collective-permute-start(bf16[128,1024]{1,0:T(8,128)(2,1)S(1)} %get-tuple-element.253), channel_id=1, source_target_pairs={{0,6},{1,7},{2,4},{3,5},{4,2},{5,3},{6,0},{7,1},{8,14},{9,15},{10,... | collective-permute-start | bytes 786440 | tf_op jit(solution)/shard_map/ppermute | solution.py:1039
  202.4 120.7 %reduce-scatter.6.cloned.1.call-start = ((), (), s32[]{:S(2)}) async-start(), calls=%async_computation.9 | async-start | bytes 1310720 | tf_op jit(solution)/shard_map/reduce_scatter | solution.py:1307
  204.1 9.2 %collective-permute-start.55 = (bf16[128,1024]{1,0:T(8,128)(2,1)S(1)}, bf16[128,1024]{1,0:T(8,128)(2,1)S(1)}, u32[]{:S(2)}, u32[]{:S(2)}) collective-permute-start(bf16[128,1024]{1,0:T(8,128)(2,1)S(1)} %get-tuple-element.262.refs_1_), channel_id=1, source_target_pairs={{0,2},{1,3},{2,0},{3,1},{4,6},{5,7},{6,4},{7,5},{8,10},{9,11},{10,... | collective-permute-start | bytes 786440 | tf_op jit(solution)/shard_map/ppermute | solution.py:1039
  205.3 11.0 %collective-permute-start.56 = (bf16[128,1024]{1,0:T(8,128)(2,1)S(1)}, bf16[128,1024]{1,0:T(8,128)(2,1)S(1)}, u32[]{:S(2)}, u32[]{:S(2)}) collective-permute-start(bf16[128,1024]{1,0:T(8,128)(2,1)S(1)} %get-tuple-element.262.refs_1_), channel_id=1, source_target_pairs={{0,4},{1,5},{2,6},{3,7},{4,0},{5,1},{6,2},{7,3},{8,12},{9,13},{10,... | collective-permute-start | bytes 786440 | tf_op jit(solution)/shard_map/ppermute | solution.py:1039
  205.8 11.8 %collective-permute-start.57 = (bf16[128,1024]{1,0:T(8,128)(2,1)S(1)}, bf16[128,1024]{1,0:T(8,128)(2,1)S(1)}, u32[]{:S(2)}, u32[]{:S(2)}) collective-permute-start(bf16[128,1024]{1,0:T(8,128)(2,1)S(1)} %get-tuple-element.262.refs_1_), channel_id=1, source_target_pairs={{0,6},{1,7},{2,4},{3,5},{4,2},{5,3},{6,0},{7,1},{8,14},{9,15},{10,... | collective-permute-start | bytes 786440 | tf_op jit(solution)/shard_map/ppermute | solution.py:1039
  207.6 10.0 %collective-permute-start.58 = (bf16[128,1024]{1,0:T(8,128)(2,1)S(1)}, bf16[128,1024]{1,0:T(8,128)(2,1)S(1)}, u32[]{:S(2)}, u32[]{:S(2)}) collective-permute-start(bf16[128,1024]{1,0:T(8,128)(2,1)S(1)} %get-tuple-element.262.refs_1_), channel_id=1, source_target_pairs={{0,1},{1,0},{2,3},{3,2},{4,5},{5,4},{6,7},{7,6},{8,9},{9,8},{10,11... | collective-permute-start | bytes 786440 | tf_op jit(solution)/shard_map/ppermute | solution.py:1039
  237.7 12.6 %collective-permute-start.63 = (bf16[128,1024]{1,0:T(8,128)(2,1)S(1)}, bf16[128,1024]{1,0:T(8,128)(2,1)S(1)}, u32[]{:S(2)}, u32[]{:S(2)}) collective-permute-start(bf16[128,1024]{1,0:T(8,128)(2,1)S(1)} %get-tuple-element.266), channel_id=1, source_target_pairs={{0,2},{1,3},{2,0},{3,1},{4,6},{5,7},{6,4},{7,5},{8,10},{9,11},{10,... | collective-permute-start | bytes 786440 | tf_op jit(solution)/shard_map/ppermute | solution.py:1039
  238.7 13.3 %collective-permute-start.64 = (bf16[128,1024]{1,0:T(8,128)(2,1)S(1)}, bf16[128,1024]{1,0:T(8,128)(2,1)S(1)}, u32[]{:S(2)}, u32[]{:S(2)}) collective-permute-start(bf16[128,1024]{1,0:T(8,128)(2,1)S(1)} %get-tuple-element.267), channel_id=1, source_target_pairs={{0,4},{1,5},{2,6},{3,7},{4,0},{5,1},{6,2},{7,3},{8,12},{9,13},{10,... | collective-permute-start | bytes 786440 | tf_op jit(solution)/shard_map/ppermute | solution.py:1039
  240.8 12.3 %collective-permute-start.65 = (bf16[128,1024]{1,0:T(8,128)(2,1)S(1)}, bf16[128,1024]{1,0:T(8,128)(2,1)S(1)}, u32[]{:S(2)}, u32[]{:S(2)}) collective-permute-start(bf16[128,1024]{1,0:T(8,128)(2,1)S(1)} %get-tuple-element.268), channel_id=1, source_target_pairs={{0,6},{1,7},{2,4},{3,5},{4,2},{5,3},{6,0},{7,1},{8,14},{9,15},{10,... | collective-permute-start | bytes 786440 | tf_op jit(solution)/shard_map/ppermute | solution.py:1039
  254.6 6.9 %collective-permute-start.70 = (bf16[512,2048]{1,0:T(8,128)(2,1)}, bf16[512,2048]{1,0:T(8,128)(2,1)S(1)}, u32[]{:S(2)}, u32[]{:S(2)}) collective-permute-start(bf16[512,2048]{1,0:T(8,128)(2,1)} %get-tuple-element.288), channel_id=1, source_target_pairs={{0,1},{1,0},{2,3},{3,2},{4,5},{5,4},{6,7},{7,6},{8,9},{9,8},{10,11... | collective-permute-start | bytes 6291464 | tf_op jit(solution)/shard_map/ppermute | solution.py:1039
  255.1 11.4 %collective-permute-start.66 = (bf16[128,1024]{1,0:T(8,128)(2,1)S(1)}, bf16[128,1024]{1,0:T(8,128)(2,1)}, u32[]{:S(2)}, u32[]{:S(2)}) collective-permute-start(bf16[128,1024]{1,0:T(8,128)(2,1)S(1)} %get-tuple-element.303.refs_1_), channel_id=1, source_target_pairs={{0,2},{1,3},{2,0},{3,1},{4,6},{5,7},{6,4},{7,5},{8,10},{9,11},{10,... | collective-permute-start | bytes 786440 | tf_op jit(solution)/shard_map/ppermute | solution.py:1039
  256.3 12.4 %collective-permute-start.67 = (bf16[128,1024]{1,0:T(8,128)(2,1)S(1)}, bf16[128,1024]{1,0:T(8,128)(2,1)}, u32[]{:S(2)}, u32[]{:S(2)}) collective-permute-start(bf16[128,1024]{1,0:T(8,128)(2,1)S(1)} %get-tuple-element.303.refs_1_), channel_id=1, source_target_pairs={{0,4},{1,5},{2,6},{3,7},{4,0},{5,1},{6,2},{7,3},{8,12},{9,13},{10,... | collective-permute-start | bytes 786440 | tf_op jit(solution)/shard_map/ppermute | solution.py:1039
  257.5 12.5 %collective-permute-start.68 = (bf16[128,1024]{1,0:T(8,128)(2,1)S(1)}, bf16[128,1024]{1,0:T(8,128)(2,1)}, u32[]{:S(2)}, u32[]{:S(2)}) collective-permute-start(bf16[128,1024]{1,0:T(8,128)(2,1)S(1)} %get-tuple-element.303.refs_1_), channel_id=1, source_target_pairs={{0,6},{1,7},{2,4},{3,5},{4,2},{5,3},{6,0},{7,1},{8,14},{9,15},{10,... | collective-permute-start | bytes 786440 | tf_op jit(solution)/shard_map/ppermute | solution.py:1039
  274.3 32.1 %collective-permute-start.75 = (bf16[128,2048]{1,0:T(8,128)(2,1)}, bf16[128,2048]{1,0:T(8,128)(2,1)S(1)}, u32[]{:S(2)}, u32[]{:S(2)}) collective-permute-start(bf16[128,2048]{1,0:T(8,128)(2,1)} %copy-done.18), channel_id=1, source_target_pairs={{0,2},{1,3},{2,0},{3,1},{4,6},{5,7},{6,4},{7,5},{8,10},{9,11},{10,... | collective-permute-start | bytes 1572872 | tf_op jit(solution)/shard_map/ppermute | solution.py:1039
  275.3 31.2 %collective-permute-start.76 = (bf16[128,2048]{1,0:T(8,128)(2,1)}, bf16[128,2048]{1,0:T(8,128)(2,1)S(1)}, u32[]{:S(2)}, u32[]{:S(2)}) collective-permute-start(bf16[128,2048]{1,0:T(8,128)(2,1)} %copy-done.17), channel_id=1, source_target_pairs={{0,4},{1,5},{2,6},{3,7},{4,0},{5,1},{6,2},{7,3},{8,12},{9,13},{10,... | collective-permute-start | bytes 1572872 | tf_op jit(solution)/shard_map/ppermute | solution.py:1039
  276.7 29.8 %collective-permute-start.77 = (bf16[128,2048]{1,0:T(8,128)(2,1)}, bf16[128,2048]{1,0:T(8,128)(2,1)S(1)}, u32[]{:S(2)}, u32[]{:S(2)}) collective-permute-start(bf16[128,2048]{1,0:T(8,128)(2,1)} %copy-done.16), channel_id=1, source_target_pairs={{0,6},{1,7},{2,4},{3,5},{4,2},{5,3},{6,0},{7,1},{8,14},{9,15},{10,... | collective-permute-start | bytes 1572872 | tf_op jit(solution)/shard_map/ppermute | solution.py:1039
  292.0 58.1 %reduce-scatter.8.cloned.1.call-start = ((), (), s32[]{:S(2)}) async-start(), calls=%async_computation.10 | async-start | bytes 1310720 | tf_op jit(solution)/shard_map/reduce_scatter | solution.py:1357
  319.5 9.4 %collective-permute-start.79 = (bf16[128,1024]{1,0:T(8,128)(2,1)}, bf16[128,1024]{1,0:T(8,128)(2,1)S(1)}, u32[]{:S(2)}, u32[]{:S(2)}) collective-permute-start(bf16[128,1024]{1,0:T(8,128)(2,1)} %get-tuple-element.326), channel_id=1, source_target_pairs={{0,2},{1,3},{2,0},{3,1},{4,6},{5,7},{6,4},{7,5},{8,10},{9,11},{10,... | collective-permute-start | bytes 786440 | tf_op jit(solution)/shard_map/ppermute | solution.py:1039
  320.2 13.9 %collective-permute-start.80 = (bf16[128,1024]{1,0:T(8,128)(2,1)S(1)}, bf16[128,1024]{1,0:T(8,128)(2,1)S(1)}, u32[]{:S(2)}, u32[]{:S(2)}) collective-permute-start(bf16[128,1024]{1,0:T(8,128)(2,1)S(1)} %copy-done.31), channel_id=1, source_target_pairs={{0,4},{1,5},{2,6},{3,7},{4,0},{5,1},{6,2},{7,3},{8,12},{9,13},{10,... | collective-permute-start | bytes 786440 | tf_op jit(solution)/shard_map/ppermute | solution.py:1039
  320.8 13.3 %collective-permute-start.81 = (bf16[128,1024]{1,0:T(8,128)(2,1)S(1)}, bf16[128,1024]{1,0:T(8,128)(2,1)}, u32[]{:S(2)}, u32[]{:S(2)}) collective-permute-start(bf16[128,1024]{1,0:T(8,128)(2,1)S(1)} %get-tuple-element.328), channel_id=1, source_target_pairs={{0,6},{1,7},{2,4},{3,5},{4,2},{5,3},{6,0},{7,1},{8,14},{9,15},{10,... | collective-permute-start | bytes 786440 | tf_op jit(solution)/shard_map/ppermute | solution.py:1039
  336.1 15.6 %all-to-all-start.4 = ((bf16[8,32,1408]{2,1,0:T(8,128)(2,1)}), bf16[8,32,1408]{2,1,0:T(8,128)(2,1)S(1)}, u32[]{:S(2)}, u32[]{:S(2)}) async-start(bf16[8,32,1408]{2,1,0:T(8,128)(2,1)} %pad_maximum_fusion.1), calls=%async_computation.7 | async-start | bytes 1441792 | tf_op jit(solution)/shard_map/all_to_all | solution.py:1139
  351.7 10.2 %all-to-all-start.3 = ((bf16[8,32,384]{2,1,0:T(8,128)(2,1)}), bf16[8,32,384]{2,1,0:T(8,128)(2,1)S(1)}, u32[]{:S(2)}, u32[]{:S(2)}) async-start(bf16[8,32,384]{2,1,0:T(8,128)(2,1)} %bitcast.33), calls=%async_computation.6 | async-start | bytes 393216 | tf_op jit(solution)/shard_map/all_to_all | solution.py:1139
  (141 other events, 732.4 us)
Sparse Core Ops, SparseCore 0:
  10.7 31.1 all-gather.6
  44.8 27.8 all-gather.8
  80.7 80.7 all-gather.10
  202.5 76.7 reduce-scatter.3
  292.1 29.2 reduce-scatter.5
  324.1 25.8 reduce-scatter.7

commit v5 on v4

--- a/solution.py
+++ b/solution.py
@@ -1344,17 +1344,16 @@
         jnp.zeros((shares, INNER, hidden), WIDE), h_bias_grad.reshape(shares, 1, hidden), here, 1
     ).reshape(devices, hidden)
     tiny = jnp.concatenate([vector_part.reshape(devices, -1), bias_part], axis=1)
-    tiny = lax.all_to_all(tiny, ALL, 0, 0, tiled=True)
-    give, side_parts, tiny, mlp_home = lax.optimization_barrier(
-        (give, side_parts, tiny, mlp_home)
-    )
-    tiny = jnp.sum(after(tiny, give), axis=0)
+    give, side_parts, mlp_home = lax.optimization_barrier((give, side_parts, mlp_home))
     first_own, *first_parts = scatter_start(give, keep)
     first_parts = scatter_finish(first_parts)
     self_grad = column_part((after(h1, first_own), (dq, dk, dv)))
     self_rows = row_grads((self_rows[0], after(self_rows[1], first_own)), att, self_all)
     packed_grad = pack_grads(self_grad, self_rows)
     self_sum = lax.psum_scatter(packed_grad, OUTER, scatter_dimension=0, tiled=True)
+    tiny = lax.all_to_all(after(tiny, packed_grad), ALL, 0, 0, tiled=True)
+    first_parts, tiny = lax.optimization_barrier((first_parts, tiny))
+    tiny = jnp.sum(tiny, axis=0)
     target_grad, target_low, _ = norm_back(
         0, first_own, first_parts, target[0], middle_grad, params
     )

time: 376 us -> 372 us (0.989)
    unnamed x232 -> x230, local copies, waits for them, and re-layouts: 37.5 us -> 35.3 us
  transfers between devices with their start and end apart: 92 -> 92, of which waited for: 32 -> 33; matrix products, arithmetic and copies ran while one was open for 4% -> 5% of each run, Pallas kernels for 25% -> 25%
where the time goes in v5:
time: 372 us; the launch traced here: 367 us
  Pallas kernels  104 us (28%)
  waiting for transfers between devices  93.4 us (25%)
  starting transfers between devices  66.9 us (18%)
  local copies, waits for them, and re-layouts  48.2 us (13%)
  blocking collectives  31.8 us (9%)
  between operations  15.6 us (4%)
  other arithmetic  6.95 us (2%)
    ppermute x83, waiting for transfers between devices, hop(): return lax.ppermute(value, 'inner', route)  77.6 us
    ppermute x83, starting transfers between devices, hop(): return lax.ppermute(value, 'inner', route)  54.8 us
    unnamed x230, local copies, waits for them, and re-layouts  35.3 us
    pallas_call x2, Pallas kernels, attend_back(): pl.pallas_call(functools.partial(attend_back_kernel, causal, rows, pair /...  25.5 us
    all_to_all x1, blocking collectives, exchange(): return lax.all_to_all(value, 'inner', 0, 0)  16.8 us
    all_to_all x3, waiting for transfers between devices, exchange(): return lax.all_to_all(value, 'inner', 0, 0)  15.7 us
    all_to_all x1, blocking collectives, per_device(): tiny = lax.all_to_all(after(tiny, packed_grad), ALL, 0, 0, tiled=True)  14.9 us
    pallas_call x1, Pallas kernels, feed(): pl.pallas_call(feed_kernel, out_shape=(jax.ShapeDtypeStruct((span, hidden...  11.9 us
  transfers between devices with their start and end apart: 92, of which 33 were waited for; matrix products, arithmetic and copies ran while one was open for 5% of the time, Pallas kernels for 25%

profile of v5, /device:TPU:0, one launch (start us, length us, event | category | flops | bytes accessed | tf_op | source)
XLA Modules:
  0.0 367.0 jit_solution(14002165611556376982)
XLA Ops:
  8.9 1.7 fusion.1
  13.6 16.8 %all_to_all.32 = bf16[8,32,1408]{2,1,0:T(8,128)(2,1)S(1)} all-to-all(bf16[8,32,1408]{2,1,0:T(8,128)(2,1)S(1)} %shard_map.229), channel_id=1, replica_groups=mesh['ulys'=4,'blk'=8] {'blk'}, dimensions={0} | all-to-all | bytes 1441792 | tf_op jit(solution)/shard_map/all_to_all | solution.py:1139
  31.5 2.4 collective-permute-start.2
  34.7 5.1 %collective-permute-done.refs_1_ = bf16[128,1024]{1,0:T(8,128)(2,1)} collective-permute-done((bf16[128,1024]{1,0:T(8,128)(2,1)S(1)}, bf16[128,1024]{1,0:T(8,128)(2,1)}, u32[]{:S(2)}, u32[]{:S(2)}) %collective-permute-start) | collective-permute-done | bytes 262176 | tf_op jit(solution)/shard_map/ppermute | solution.py:1039
  39.7 4.9 %collective-permute-done.1.refs_2_ = bf16[128,1024]{1,0:T(8,128)(2,1)} collective-permute-done((bf16[128,1024]{1,0:T(8,128)(2,1)S(1)}, bf16[128,1024]{1,0:T(8,128)(2,1)}, u32[]{:S(2)}, u32[]{:S(2)}) %collective-permute-start.1) | collective-permute-done | bytes 262176 | tf_op jit(solution)/shard_map/ppermute | solution.py:1039
  47.2 3.7 %all-to-all-start.1 = ((bf16[8,128,512]{2,1,0:T(8,128)(2,1)}), bf16[8,128,512]{2,1,0:T(8,128)(2,1)S(1)}, u32[]{:S(2)}, u32[]{:S(2)}) async-start(bf16[8,128,512]{2,1,0:T(8,128)(2,1)} %shard_map.230), calls=%async_computation.1 | async-start | bytes 2097152 | tf_op jit(solution)/shard_map/all_to_all | solution.py:1139
  53.8 12.4 %all-to-all-done.1 = bf16[8,128,512]{2,1,0:T(8,128)(2,1)S(1)} async-done(((bf16[8,128,512]{2,1,0:T(8,128)(2,1)}), bf16[8,128,512]{2,1,0:T(8,128)(2,1)S(1)}, u32[]{:S(2)}, u32[]{:S(2)}) %all-to-all-start.1) | async-done | bytes 1048608 | tf_op jit(solution)/shard_map/all_to_all | solution.py:1139
  67.4 2.3 collective-permute-start.5
  69.7 6.2 %shard_map.231 = (bf16[1024,128]{1,0:T(8,128)(2,1)}, bf16[1024,128]{1,0:T(8,128)(2,1)}, bf16[1024,128]{1,0:T(8,128)(2,1)}, bf16[1024,1024]{1,0:T(8,128)(2,1)}, f...) custom-call(s32[2]{0:T(128)} %pad_add_fusion.1.table, ...), custom_call_target="tpu_custom_call" | custom-call | flops 4400000000 | bytes 14000000 | tf_op jit(solution)/shard_map/pallas_call | solution.py:415
  75.9 4.6 %collective-permute-done.4.refs_2_ = bf16[128,1024]{1,0:T(8,128)(2,1)} collective-permute-done((bf16[128,1024]{1,0:T(8,128)(2,1)S(1)}, bf16[128,1024]{1,0:T(8,128)(2,1)}, u32[]{:S(2)}, u32[]{:S(2)}) %collective-permute-start.4) | collective-permute-done | bytes 262176 | tf_op jit(solution)/shard_map/ppermute | solution.py:1039
  84.7 1.4 collective-permute-start.12
  86.0 1.8 collective-permute-start.13
  87.8 5.3 %shard_map.234 = (bf16[1024,128]{1,0:T(8,128)(2,1)}, f32[2,1024]{1,0:T(2,128)}) custom-call(s32[10]{0:T(128)} %concatenate.50.table, bf16[1024,128]{1,0:T(8,128)(2,1)} %get-tuple-element.195.q, bf16[1024,128]{1,0:T(8,128)(2,1)} %get-tuple-element.196.k, bf16[1024,128]{1,0:T(8,128)(2,1)} %get-tuple-element.197.v), custom_call_target="tpu_custom_call" | custom-call | flops 6600000000 | bytes 21000000 | tf_op jit(solution)/shard_map/pallas_call | solution.py:307
  93.4 5.3 %collective-permute-done.12.refs_10_ = bf16[128,1024]{1,0:T(8,128)(2,1)S(1)} collective-permute-done((bf16[128,1024]{1,0:T(8,128)(2,1)S(1)}, bf16[128,1024]{1,0:T(8,128)(2,1)S(1)}, u32[]{:S(2)}, u32[]{:S(2)}) %collective-permute-start.12) | collective-permute-done | bytes 262176 | tf_op jit(solution)/shard_map/ppermute | solution.py:1039
  98.7 1.7 collective-permute-start.14
  102.7 1.5 collective-permute-start.16
  104.9 3.1 collective-permute-done.14.refs_1_
  108.1 4.3 %shard_map.237 = (bf16[1024,1024]{1,0:T(8,128)(2,1)}, bf16[1024,128]{1,0:T(8,128)(2,1)}, bf16[1024,128]{1,0:T(8,128)(2,1)}, bf16[1024,384]{1,0:T(8,128)(2,1)}) custom-call(f32[16,128]{1,0:T(8,128)} %get-tuple-element.204.biases.refs_19_, bf16[1024,512]{1,0:T(8,128)(2,1)} %bitcast.81, bf16[128,1024]{1,0:T(8,128)(2,1)} %bitcast.88, ...), custom_call_target="tpu_custom_call" | custom-call | flops 3300000000 | bytes 10500000 | tf_op jit(solution)/shard_map/pallas_call | solution.py:739
  113.0 3.5 collective-permute-done.15.refs_2_
  120.9 1.8 collective-permute-start.24
  123.5 10.4 %shard_map.238 = (f32[128,1024]{1,0:T(8,128)}, bf16[1024,1024]{1,0:T(8,128)(2,1)}, bf16[1024,1024]{1,0:T(8,128)(2,1)}, bf16[1024,128]{1,0:T(8,128)(2,1)}) custom-call(bf16[1024,128]{1,0:T(8,128)(2,1)} %get-tuple-element.218.refs_0_, bf16[1024,128]{1,0:T(8,128)(2,1)} %copy-done.71, bf16[1024,128]{1,0:T(8,128)(2,1)} %copy-done.75, ...), custom_call_target="tpu_custom_call" | custom-call | flops 6600000000 | bytes 21000000 | tf_op jit(solution)/shard_map/pallas_call | solution.py:481
  134.0 6.0 %shard_map.239 = (bf16[1024,128]{1,0:T(8,128)(2,1)}, f32[2,1024]{1,0:T(2,128)}) custom-call(s32[10]{0:T(128)} %concatenate.47.table, bf16[1024,128]{1,0:T(8,128)(2,1)} %get-tuple-element.230.q, bf16[1024,128]{1,0:T(8,128)(2,1)} %get-tuple-element.231.k, bf16[1024,128]{1,0:T(8,128)(2,1)} %get-tuple-element.232.v), custom_call_target="tpu_custom_call" | custom-call | flops 6600000000 | bytes 21000000 | tf_op jit(solution)/shard_map/pallas_call | solution.py:307
  141.7 1.8 collective-permute-start.35
  144.0 5.4 %collective-permute-done.33.refs_1_ = bf16[1024,128]{1,0:T(8,128)(2,1)S(1)} collective-permute-done((bf16[1024,128]{1,0:T(8,128)(2,1)}, bf16[1024,128]{1,0:T(8,128)(2,1)S(1)}, u32[]{:S(2)}, u32[]{:S(2)}) %collective-permute-start.33) | collective-permute-done | bytes 262176 | tf_op jit(solution)/shard_map/ppermute | solution.py:1039
  150.1 3.4 collective-permute-done.35.refs_3_
  154.5 2.1 collective-permute-start.36
  157.2 1.4 collective-permute-start.38
  160.0 8.7 %shard_map.240 = (f32[128,1024]{1,0:T(8,128)}, bf16[1024,1024]{1,0:T(8,128)(2,1)}) custom-call(bf16[1024,128]{1,0:T(8,128)(2,1)} %get-tuple-element.234.refs_0_, bf16[1024,128]{1,0:T(8,128)(2,1)} %copy-done.82, bf16[1024,128]{1,0:T(8,128)(2,1)} %copy-done.83, bf16[1024,128]{1,0:T(8,128)(2,1)} %copy-done.84, bf16[1024,128]{1,0:T(8,128)(2,1)} %copy-done.85, ...), custom_call_target="tpu_custom_call" | custom-call | flops 5500000256 | bytes 17500000 | tf_op jit(solution)/shard_map/pallas_call | solution.py:506
  168.7 1.6 collective-permute-done.37.refs_2_
  173.0 11.9 %shard_map.241 = (bf16[1024,1024]{1,0:T(8,128)(2,1)S(1)}, bf16[1024,1024]{1,0:T(8,128)(2,1)S(1)}, bf16[512,1024]{1,0:T(8,128)(2,1)S(1)}, f32[512,1024]{1,0:T(8,1...) custom-call(bf16[1024,1024]{1,0:T(8,128)(2,1)} %get-tuple-element.259.h, f32[1,1024]{1,0:T(1,128)S(1)} %reshape.183.bias, ...), custom_call_target="tpu_custom_call" | custom-call | flops 14300000256 | bytes 45500000 | tf_op jit(solution)/shard_map/pallas_call | solution.py:572
  185.1 2.5 collective-permute-done.51.took
  189.6 1.8 collective-permute-start.54
  191.3 1.6 copy-done.52
  192.9 4.5 %shard_map.243 = bf16[1024,2048]{1,0:T(8,128)(2,1)S(1)} custom-call(bf16[1024,1024]{1,0:T(8,128)(2,1)S(1)} %get-tuple-element.278.act, bf16[1024,1024]{1,0:T(8,128)(2,1)S(1)} %get-tuple-element.258.slope, bf16[1024,1024]{1,0:T(8,128)(2,1)S(1)} %copy-done.51, bf16[1024,1024]{1,0:T(8,128)(2,1)S(1)} %copy-done.52), custom_call_target="tpu_custom_call" | custom-call | flops 6600000000 | bytes 21000000 | tf_op jit(solution)/shard_map/pallas_call | solution.py:661
  197.5 2.0 copy-done.4
  199.5 2.9 collective-permute-done.53.two
  205.9 1.7 collective-permute-start.57
  207.6 5.8 %collective-permute-done.55.refs_2_ = bf16[128,1024]{1,0:T(8,128)(2,1)S(1)} collective-permute-done((bf16[128,1024]{1,0:T(8,128)(2,1)S(1)}, bf16[128,1024]{1,0:T(8,128)(2,1)S(1)}, u32[]{:S(2)}, u32[]{:S(2)}) %collective-permute-start.55) | collective-permute-done | bytes 262176 | tf_op jit(solution)/shard_map/ppermute | solution.py:1039
  213.3 2.9 collective-permute-done.56.refs_3_
  217.8 1.4 collective-permute-done.61.refs_8_
  219.9 13.1 %shard_map.245 = (bf16[512,1024]{1,0:T(8,128)(2,1)}, f32[512,1024]{1,0:T(8,128)}, bf16[1024,128]{1,0:T(8,128)(2,1)}, bf16[1024,128]{1,0:T(8,128)(2,1)}, bf16[102...) custom-call(s32[10]{0:T(128)} %concatenate.47.table, ...), custom_call_target="tpu_custom_call" | custom-call | flops 11000000512 | bytes 35000000 | tf_op jit(solution)/shard_map/pallas_call | solution.py:339
  233.2 2.7 collective-permute-done.62.took
  236.0 1.6 copy-done.34
  238.7 2.1 collective-permute-start.64
  241.3 2.2 copy-done.8
  244.7 3.5 shard_map.248
  250.2 1.8 collective-permute-done.64.two
  258.6 1.7 shard_map.250
  260.3 2.2 copy-done.3
  264.4 4.2 %collective-permute-done.67.refs_3_ = bf16[128,1024]{1,0:T(8,128)(2,1)} collective-permute-done((bf16[128,1024]{1,0:T(8,128)(2,1)S(1)}, bf16[128,1024]{1,0:T(8,128)(2,1)}, u32[]{:S(2)}, u32[]{:S(2)}) %collective-permute-start.67) | collective-permute-done | bytes 262176 | tf_op jit(solution)/shard_map/ppermute | solution.py:1039
  268.6 1.4 collective-permute-done.68.refs_4_
  273.8 1.4 collective-permute-start.76
  276.7 12.4 %shard_map.252 = (bf16[512,1024]{1,0:T(8,128)(2,1)}, f32[512,1024]{1,0:T(8,128)}, f32[2,1024]{1,0:T(2,128)}, bf16[1024,128]{1,0:T(8,128)(2,1)}, bf16[1024,128]{1...) custom-call(s32[10]{0:T(128)} %concatenate.50.table, ...), custom_call_target="tpu_custom_call" | custom-call | flops 11000000512 | bytes 35000000 | tf_op jit(solution)/shard_map/pallas_call | solution.py:339
  289.1 8.9 %collective-permute-done.76.two = bf16[128,2048]{1,0:T(8,128)(2,1)S(1)} collective-permute-done((bf16[128,2048]{1,0:T(8,128)(2,1)}, bf16[128,2048]{1,0:T(8,128)(2,1)S(1)}, u32[]{:S(2)}, u32[]{:S(2)}) %collective-permute-start.76) | collective-permute-done | bytes 524320 | tf_op jit(solution)/shard_map/ppermute | solution.py:1039
  302.6 1.6 copy-done.33
  307.5 1.6 shard_map.255
  311.3 2.0 collective-permute-start.80
  314.0 14.9 %all_to_all.33 = f32[32,1,672]{2,1,0:T(1,128)S(1)} all-to-all(f32[32,1,672]{2,1,0:T(1,128)S(1)} %copy.57), channel_id=1, replica_groups=mesh['ulys'=4,'blk'=8] {'ulys','blk'}, dimensions={0} | all-to-all | bytes 172032 | tf_op jit(solution)/shard_map/all_to_all | solution.py:1354
  332.3 3.7 %all-to-all-start.4 = ((bf16[8,32,1408]{2,1,0:T(8,128)(2,1)}), bf16[8,32,1408]{2,1,0:T(8,128)(2,1)S(1)}, u32[]{:S(2)}, u32[]{:S(2)}) async-start(bf16[8,32,1408]{2,1,0:T(8,128)(2,1)} %pad_maximum_fusion.1), calls=%async_computation.7 | async-start | bytes 1441792 | tf_op jit(solution)/shard_map/all_to_all | solution.py:1139
  345.5 1.4 shard_map.257
  346.9 1.6 slice.83
  348.6 4.1 %all-to-all-start.3 = ((bf16[8,32,384]{2,1,0:T(8,128)(2,1)}), bf16[8,32,384]{2,1,0:T(8,128)(2,1)S(1)}, u32[]{:S(2)}, u32[]{:S(2)}) async-start(bf16[8,32,384]{2,1,0:T(8,128)(2,1)} %bitcast.33), calls=%async_computation.6 | async-start | bytes 393216 | tf_op jit(solution)/shard_map/all_to_all | solution.py:1139
  352.7 1.6 shard_map.259
  355.7 3.3 all-to-all-done.3.got
  (444 shorter events, 86.8 us)
Async XLA Ops:
  7.2 37.4 %all-gather.7.cloned.1.call-start = ((), (), s32[]{:S(2)}) async-start(), calls=%async_computation.11 | async-start | bytes 1351680 | tf_op jit(solution)/shard_map/all_gather | solution.py:1198
  10.6 69.9 %all-gather.9.cloned.1.call-start = ((), (), s32[]{:S(2)}) async-start(), calls=%async_computation.12 | async-start | bytes 1310720 | tf_op jit(solution)/shard_map/all_gather | solution.py:1198
  30.4 9.3 %collective-permute-start = (bf16[128,1024]{1,0:T(8,128)(2,1)S(1)}, bf16[128,1024]{1,0:T(8,128)(2,1)}, u32[]{:S(2)}, u32[]{:S(2)}) collective-permute-start(bf16[128,1024]{1,0:T(8,128)(2,1)S(1)} %bitcast.66), channel_id=1, source_target_pairs={{0,2},{1,3},{2,0},{3,1},{4,6},{5,7},{6,4},{7,5},{8,10},{9,11},{10,... | collective-permute-start | bytes 786440 | tf_op jit(solution)/shard_map/ppermute | solution.py:1039
  31.0 13.7 %collective-permute-start.1 = (bf16[128,1024]{1,0:T(8,128)(2,1)S(1)}, bf16[128,1024]{1,0:T(8,128)(2,1)}, u32[]{:S(2)}, u32[]{:S(2)}) collective-permute-start(bf16[128,1024]{1,0:T(8,128)(2,1)S(1)} %bitcast.67), channel_id=1, source_target_pairs={{0,4},{1,5},{2,6},{3,7},{4,0},{5,1},{6,2},{7,3},{8,12},{9,13},{10,... | collective-permute-start | bytes 786440 | tf_op jit(solution)/shard_map/ppermute | solution.py:1039
  31.5 13.1 %collective-permute-start.2 = (bf16[128,1024]{1,0:T(8,128)(2,1)S(1)}, bf16[128,1024]{1,0:T(8,128)(2,1)}, u32[]{:S(2)}, u32[]{:S(2)}) collective-permute-start(bf16[128,1024]{1,0:T(8,128)(2,1)S(1)} %bitcast.68), channel_id=1, source_target_pairs={{0,6},{1,7},{2,4},{3,5},{4,2},{5,3},{6,0},{7,1},{8,14},{9,15},{10,... | collective-permute-start | bytes 786440 | tf_op jit(solution)/shard_map/ppermute | solution.py:1039
  47.2 19.0 %all-to-all-start.1 = ((bf16[8,128,512]{2,1,0:T(8,128)(2,1)}), bf16[8,128,512]{2,1,0:T(8,128)(2,1)S(1)}, u32[]{:S(2)}, u32[]{:S(2)}) async-start(bf16[8,128,512]{2,1,0:T(8,128)(2,1)} %shard_map.230), calls=%async_computation.1 | async-start | bytes 2097152 | tf_op jit(solution)/shard_map/all_to_all | solution.py:1139
  50.9 122.1 %all-gather.11.cloned.1.call-start = ((), (), s32[]{:S(2)}) async-start(), calls=%async_computation.13 | async-start | bytes 5242880 | tf_op jit(solution)/shard_map/all_gather | solution.py:1198
  50.9 15.8 %collective-permute-start.6 = (bf16[128,1024]{1,0:T(8,128)(2,1)S(1)}, bf16[128,1024]{1,0:T(8,128)(2,1)}, u32[]{:S(2)}, u32[]{:S(2)}) collective-permute-start(bf16[128,1024]{1,0:T(8,128)(2,1)S(1)} %bitcast.69), channel_id=1, source_target_pairs={{0,1},{1,0},{2,3},{3,2},{4,5},{5,4},{6,7},{7,6},{8,9},{9,8},{10,11... | collective-permute-start | bytes 786440 | tf_op jit(solution)/shard_map/ppermute | solution.py:1039
  51.3 16.0 %collective-permute-start.7 = (bf16[128,1024]{1,0:T(8,128)(2,1)}, bf16[128,1024]{1,0:T(8,128)(2,1)}, u32[]{:S(2)}, u32[]{:S(2)}) collective-permute-start(bf16[128,1024]{1,0:T(8,128)(2,1)} %collective-permute-done.refs_1_), channel_id=1, source_target_pairs={{0,1},{1,0},{2,3},{3,2},{4,5},{5,4},{6,7},{7,6},{8,9},{9,8},{10,11... | collective-permute-start | bytes 786440 | tf_op jit(solution)/shard_map/ppermute | solution.py:1039
  51.5 18.2 %collective-permute-start.8 = (bf16[128,1024]{1,0:T(8,128)(2,1)}, bf16[128,1024]{1,0:T(8,128)(2,1)}, u32[]{:S(2)}, u32[]{:S(2)}) collective-permute-start(bf16[128,1024]{1,0:T(8,128)(2,1)} %collective-permute-done.1.refs_2_), channel_id=1, source_target_pairs={{0,1},{1,0},{2,3},{3,2},{4,5},{5,4},{6,7},{7,6},{8,9},{9,8},{10,11... | collective-permute-start | bytes 786440 | tf_op jit(solution)/shard_map/ppermute | solution.py:1039
  51.8 17.9 %collective-permute-start.9 = (bf16[128,1024]{1,0:T(8,128)(2,1)}, bf16[128,1024]{1,0:T(8,128)(2,1)}, u32[]{:S(2)}, u32[]{:S(2)}) collective-permute-start(bf16[128,1024]{1,0:T(8,128)(2,1)} %collective-permute-done.2.refs_3_), channel_id=1, source_target_pairs={{0,1},{1,0},{2,3},{3,2},{4,5},{5,4},{6,7},{7,6},{8,9},{9,8},{10,11... | collective-permute-start | bytes 786440 | tf_op jit(solution)/shard_map/ppermute | solution.py:1039
  66.2 9.7 %collective-permute-start.3 = (bf16[128,1024]{1,0:T(8,128)(2,1)S(1)}, bf16[128,1024]{1,0:T(8,128)(2,1)}, u32[]{:S(2)}, u32[]{:S(2)}) collective-permute-start(bf16[128,1024]{1,0:T(8,128)(2,1)S(1)} %bitcast.89), channel_id=1, source_target_pairs={{0,2},{1,3},{2,0},{3,1},{4,6},{5,7},{6,4},{7,5},{8,10},{9,11},{10,... | collective-permute-start | bytes 786440 | tf_op jit(solution)/shard_map/ppermute | solution.py:1039
  66.7 13.8 %collective-permute-start.4 = (bf16[128,1024]{1,0:T(8,128)(2,1)S(1)}, bf16[128,1024]{1,0:T(8,128)(2,1)}, u32[]{:S(2)}, u32[]{:S(2)}) collective-permute-start(bf16[128,1024]{1,0:T(8,128)(2,1)S(1)} %bitcast.90), channel_id=1, source_target_pairs={{0,4},{1,5},{2,6},{3,7},{4,0},{5,1},{6,2},{7,3},{8,12},{9,13},{10,... | collective-permute-start | bytes 786440 | tf_op jit(solution)/shard_map/ppermute | solution.py:1039
  67.4 13.2 %collective-permute-start.5 = (bf16[128,1024]{1,0:T(8,128)(2,1)S(1)}, bf16[128,1024]{1,0:T(8,128)(2,1)}, u32[]{:S(2)}, u32[]{:S(2)}) collective-permute-start(bf16[128,1024]{1,0:T(8,128)(2,1)S(1)} %bitcast.91), channel_id=1, source_target_pairs={{0,6},{1,7},{2,4},{3,5},{4,2},{5,3},{6,0},{7,1},{8,14},{9,15},{10,... | collective-permute-start | bytes 786440 | tf_op jit(solution)/shard_map/ppermute | solution.py:1039
  80.6 219.1 %reduce-scatter.4.cloned.1.call-start = ((), (), s32[]{:S(2)}) async-start(), calls=%async_computation.8 | async-start | bytes 5242880 | tf_op jit(solution)/shard_map/reduce_scatter | solution.py:1267
  83.1 18.9 %collective-permute-start.18 = (bf16[128,1024]{1,0:T(8,128)(2,1)S(1)}, bf16[128,1024]{1,0:T(8,128)(2,1)S(1)}, u32[]{:S(2)}, u32[]{:S(2)}) collective-permute-start(bf16[128,1024]{1,0:T(8,128)(2,1)S(1)} %bitcast.92), channel_id=1, source_target_pairs={{0,1},{1,0},{2,3},{3,2},{4,5},{5,4},{6,7},{7,6},{8,9},{9,8},{10,11... | collective-permute-start | bytes 786440 | tf_op jit(solution)/shard_map/ppermute | solution.py:1039
  83.6 18.7 %collective-permute-start.19 = (bf16[128,1024]{1,0:T(8,128)(2,1)}, bf16[128,1024]{1,0:T(8,128)(2,1)S(1)}, u32[]{:S(2)}, u32[]{:S(2)}) collective-permute-start(bf16[128,1024]{1,0:T(8,128)(2,1)} %collective-permute-done.3.refs_1_), channel_id=1, source_target_pairs={{0,1},{1,0},{2,3},{3,2},{4,5},{5,4},{6,7},{7,6},{8,9},{9,8},{10,11... | collective-permute-start | bytes 786440 | tf_op jit(solution)/shard_map/ppermute | solution.py:1039
  84.2 9.2 %collective-permute-start.11 = (bf16[128,1024]{1,0:T(8,128)(2,1)S(1)}, bf16[128,1024]{1,0:T(8,128)(2,1)S(1)}, u32[]{:S(2)}, u32[]{:S(2)}) collective-permute-start(bf16[128,1024]{1,0:T(8,128)(2,1)S(1)} %shard_map.233.refs_8_.weight), channel_id=1, source_target_pairs={{0,2},{1,3},{2,0},{3,1},{4,6},{5,7},{6,4},{7,5},{8,10},{9,11},{10,... | collective-permute-start | bytes 786440 | tf_op jit(solution)/shard_map/ppermute | solution.py:1039
  84.7 14.0 %collective-permute-start.12 = (bf16[128,1024]{1,0:T(8,128)(2,1)S(1)}, bf16[128,1024]{1,0:T(8,128)(2,1)S(1)}, u32[]{:S(2)}, u32[]{:S(2)}) collective-permute-start(bf16[128,1024]{1,0:T(8,128)(2,1)S(1)} %shard_map.233.refs_8_.weight), channel_id=1, source_target_pairs={{0,4},{1,5},{2,6},{3,7},{4,0},{5,1},{6,2},{7,3},{8,12},{9,13},{10,... | collective-permute-start | bytes 786440 | tf_op jit(solution)/shard_map/ppermute | solution.py:1039
  86.0 12.7 %collective-permute-start.13 = (bf16[128,1024]{1,0:T(8,128)(2,1)S(1)}, bf16[128,1024]{1,0:T(8,128)(2,1)S(1)}, u32[]{:S(2)}, u32[]{:S(2)}) collective-permute-start(bf16[128,1024]{1,0:T(8,128)(2,1)S(1)} %shard_map.233.refs_8_.weight), channel_id=1, source_target_pairs={{0,6},{1,7},{2,4},{3,5},{4,2},{5,3},{6,0},{7,1},{8,14},{9,15},{10,... | collective-permute-start | bytes 786440 | tf_op jit(solution)/shard_map/ppermute | solution.py:1039
  93.4 9.3 %collective-permute-start.20 = (bf16[128,1024]{1,0:T(8,128)(2,1)}, bf16[128,1024]{1,0:T(8,128)(2,1)S(1)}, u32[]{:S(2)}, u32[]{:S(2)}) collective-permute-start(bf16[128,1024]{1,0:T(8,128)(2,1)} %collective-permute-done.4.refs_2_), channel_id=1, source_target_pairs={{0,1},{1,0},{2,3},{3,2},{4,5},{5,4},{6,7},{7,6},{8,9},{9,8},{10,11... | collective-permute-start | bytes 786440 | tf_op jit(solution)/shard_map/ppermute | solution.py:1039
  98.7 5.5 %collective-permute-start.21 = (bf16[128,1024]{1,0:T(8,128)(2,1)}, bf16[128,1024]{1,0:T(8,128)(2,1)S(1)}, u32[]{:S(2)}, u32[]{:S(2)}) collective-permute-start(bf16[128,1024]{1,0:T(8,128)(2,1)} %collective-permute-done.5.refs_3_), channel_id=1, source_target_pairs={{0,1},{1,0},{2,3},{3,2},{4,5},{5,4},{6,7},{7,6},{8,9},{9,8},{10,11... | collective-permute-start | bytes 786440 | tf_op jit(solution)/shard_map/ppermute | solution.py:1039
  98.7 9.4 %collective-permute-start.14 = (bf16[1024,128]{1,0:T(8,128)(2,1)}, bf16[1024,128]{1,0:T(8,128)(2,1)S(1)}, u32[]{:S(2)}, u32[]{:S(2)}) collective-permute-start(bf16[1024,128]{1,0:T(8,128)(2,1)} %get-tuple-element.218.refs_0_), channel_id=1, source_target_pairs={{0,2},{1,3},{2,0},{3,1},{4,6},{5,7},{6,4},{7,5},{8,10},{9,11},{10,... | collective-permute-start | bytes 786440 | tf_op jit(solution)/shard_map/ppermute | solution.py:1039
  102.4 14.2 %collective-permute-start.15 = (bf16[1024,128]{1,0:T(8,128)(2,1)S(1)}, bf16[1024,128]{1,0:T(8,128)(2,1)S(1)}, u32[]{:S(2)}, u32[]{:S(2)}) collective-permute-start(bf16[1024,128]{1,0:T(8,128)(2,1)S(1)} %copy-done.67), channel_id=1, source_target_pairs={{0,4},{1,5},{2,6},{3,7},{4,0},{5,1},{6,2},{7,3},{8,12},{9,13},{10,... | collective-permute-start | bytes 786440 | tf_op jit(solution)/shard_map/ppermute | solution.py:1039
  102.7 13.8 %collective-permute-start.16 = (bf16[1024,128]{1,0:T(8,128)(2,1)S(1)}, bf16[1024,128]{1,0:T(8,128)(2,1)S(1)}, u32[]{:S(2)}, u32[]{:S(2)}) collective-permute-start(bf16[1024,128]{1,0:T(8,128)(2,1)S(1)} %copy-done.67), channel_id=1, source_target_pairs={{0,6},{1,7},{2,4},{3,5},{4,2},{5,3},{6,0},{7,1},{8,14},{9,15},{10,... | collective-permute-start | bytes 786440 | tf_op jit(solution)/shard_map/ppermute | solution.py:1039
  104.2 12.8 %collective-permute-start.29 = (bf16[128,1024]{1,0:T(8,128)(2,1)S(1)}, bf16[128,1024]{1,0:T(8,128)(2,1)S(1)}, u32[]{:S(2)}, u32[]{:S(2)}) collective-permute-start(bf16[128,1024]{1,0:T(8,128)(2,1)S(1)} %shard_map.233.refs_8_.weight), channel_id=1, source_target_pairs={{0,1},{1,0},{2,3},{3,2},{4,5},{5,4},{6,7},{7,6},{8,9},{9,8},{10,11... | collective-permute-start | bytes 786440 | tf_op jit(solution)/shard_map/ppermute | solution.py:1039
  104.9 12.3 %collective-permute-start.30 = (bf16[128,1024]{1,0:T(8,128)(2,1)S(1)}, bf16[128,1024]{1,0:T(8,128)(2,1)S(1)}, u32[]{:S(2)}, u32[]{:S(2)}) collective-permute-start(bf16[128,1024]{1,0:T(8,128)(2,1)S(1)} %collective-permute-done.11.refs_9_), channel_id=1, source_target_pairs={{0,1},{1,0},{2,3},{3,2},{4,5},{5,4},{6,7},{7,6},{8,9},{9,8},{10,11... | collective-permute-start | bytes 786440 | tf_op jit(solution)/shard_map/ppermute | solution.py:1039
  108.1 9.5 %collective-permute-start.31 = (bf16[128,1024]{1,0:T(8,128)(2,1)S(1)}, bf16[128,1024]{1,0:T(8,128)(2,1)S(1)}, u32[]{:S(2)}, u32[]{:S(2)}) collective-permute-start(bf16[128,1024]{1,0:T(8,128)(2,1)S(1)} %collective-permute-done.12.refs_10_), channel_id=1, source_target_pairs={{0,1},{1,0},{2,3},{3,2},{4,5},{5,4},{6,7},{7,6},{8,9},{9,8},{10,11... | collective-permute-start | bytes 786440 | tf_op jit(solution)/shard_map/ppermute | solution.py:1039
  117.2 5.5 %collective-permute-start.27 = (bf16[1024,128]{1,0:T(8,128)(2,1)S(1)}, bf16[1024,128]{1,0:T(8,128)(2,1)S(1)}, u32[]{:S(2)}, u32[]{:S(2)}) collective-permute-start(bf16[1024,128]{1,0:T(8,128)(2,1)S(1)} %collective-permute-done.15.refs_2_), channel_id=1, source_target_pairs={{0,1},{1,0},{2,3},{3,2},{4,5},{5,4},{6,7},{7,6},{8,9},{9,8},{10,11... | collective-permute-start | bytes 786440 | tf_op jit(solution)/shard_map/ppermute | solution.py:1039
  119.2 14.7 %collective-permute-start.22 = (bf16[128,1024]{1,0:T(8,128)(2,1)S(1)}, bf16[128,1024]{1,0:T(8,128)(2,1)S(1)}, u32[]{:S(2)}, u32[]{:S(2)}) collective-permute-start(bf16[128,1024]{1,0:T(8,128)(2,1)S(1)} %shard_map.236.refs_8_.weight), channel_id=1, source_target_pairs={{0,2},{1,3},{2,0},{3,1},{4,6},{5,7},{6,4},{7,5},{8,10},{9,11},{10,... | collective-permute-start | bytes 786440 | tf_op jit(solution)/shard_map/ppermute | solution.py:1039
  119.6 14.3 %collective-permute-start.23 = (bf16[128,1024]{1,0:T(8,128)(2,1)S(1)}, bf16[128,1024]{1,0:T(8,128)(2,1)S(1)}, u32[]{:S(2)}, u32[]{:S(2)}) collective-permute-start(bf16[128,1024]{1,0:T(8,128)(2,1)S(1)} %shard_map.236.refs_8_.weight), channel_id=1, source_target_pairs={{0,4},{1,5},{2,6},{3,7},{4,0},{5,1},{6,2},{7,3},{8,12},{9,13},{10,... | collective-permute-start | bytes 786440 | tf_op jit(solution)/shard_map/ppermute | solution.py:1039
  120.9 13.1 %collective-permute-start.24 = (bf16[128,1024]{1,0:T(8,128)(2,1)S(1)}, bf16[128,1024]{1,0:T(8,128)(2,1)S(1)}, u32[]{:S(2)}, u32[]{:S(2)}) collective-permute-start(bf16[128,1024]{1,0:T(8,128)(2,1)S(1)} %shard_map.236.refs_8_.weight), channel_id=1, source_target_pairs={{0,6},{1,7},{2,4},{3,5},{4,2},{5,3},{6,0},{7,1},{8,14},{9,15},{10,... | collective-permute-start | bytes 786440 | tf_op jit(solution)/shard_map/ppermute | solution.py:1039
  140.0 9.5 %collective-permute-start.33 = (bf16[1024,128]{1,0:T(8,128)(2,1)}, bf16[1024,128]{1,0:T(8,128)(2,1)S(1)}, u32[]{:S(2)}, u32[]{:S(2)}) collective-permute-start(bf16[1024,128]{1,0:T(8,128)(2,1)} %get-tuple-element.234.refs_0_), channel_id=1, source_target_pairs={{0,2},{1,3},{2,0},{3,1},{4,6},{5,7},{6,4},{7,5},{8,10},{9,11},{10,... | collective-permute-start | bytes 786440 | tf_op jit(solution)/shard_map/ppermute | solution.py:1039
  140.9 8.6 %collective-permute-start.34 = (bf16[1024,128]{1,0:T(8,128)(2,1)}, bf16[1024,128]{1,0:T(8,128)(2,1)S(1)}, u32[]{:S(2)}, u32[]{:S(2)}) collective-permute-start(bf16[1024,128]{1,0:T(8,128)(2,1)} %get-tuple-element.234.refs_0_), channel_id=1, source_target_pairs={{0,4},{1,5},{2,6},{3,7},{4,0},{5,1},{6,2},{7,3},{8,12},{9,13},{10,... | collective-permute-start | bytes 786440 | tf_op jit(solution)/shard_map/ppermute | solution.py:1039
  141.7 11.7 %collective-permute-start.35 = (bf16[1024,128]{1,0:T(8,128)(2,1)}, bf16[1024,128]{1,0:T(8,128)(2,1)S(1)}, u32[]{:S(2)}, u32[]{:S(2)}) collective-permute-start(bf16[1024,128]{1,0:T(8,128)(2,1)} %get-tuple-element.234.refs_0_), channel_id=1, source_target_pairs={{0,6},{1,7},{2,4},{3,5},{4,2},{5,3},{6,0},{7,1},{8,14},{9,15},{10,... | collective-permute-start | bytes 786440 | tf_op jit(solution)/shard_map/ppermute | solution.py:1039
  143.5 9.9 %collective-permute-start.39 = (bf16[1024,128]{1,0:T(8,128)(2,1)}, bf16[1024,128]{1,0:T(8,128)(2,1)S(1)}, u32[]{:S(2)}, u32[]{:S(2)}) collective-permute-start(bf16[1024,128]{1,0:T(8,128)(2,1)} %get-tuple-element.234.refs_0_), channel_id=1, source_target_pairs={{0,1},{1,0},{2,3},{3,2},{4,5},{5,4},{6,7},{7,6},{8,9},{9,8},{10,11... | collective-permute-start | bytes 786440 | tf_op jit(solution)/shard_map/ppermute | solution.py:1039
  143.5 10.4 %collective-permute-start.43 = (bf16[128,1024]{1,0:T(8,128)(2,1)S(1)}, bf16[128,1024]{1,0:T(8,128)(2,1)S(1)}, u32[]{:S(2)}, u32[]{:S(2)}) collective-permute-start(bf16[128,1024]{1,0:T(8,128)(2,1)S(1)} %shard_map.236.refs_8_.weight), channel_id=1, source_target_pairs={{0,1},{1,0},{2,3},{3,2},{4,5},{5,4},{6,7},{7,6},{8,9},{9,8},{10,11... | collective-permute-start | bytes 786440 | tf_op jit(solution)/shard_map/ppermute | solution.py:1039
  154.5 14.2 %collective-permute-start.36 = (bf16[128,1024]{1,0:T(8,128)(2,1)S(1)}, bf16[128,1024]{1,0:T(8,128)(2,1)S(1)}, u32[]{:S(2)}, u32[]{:S(2)}) collective-permute-start(bf16[128,1024]{1,0:T(8,128)(2,1)S(1)} %bitcast.59), channel_id=1, source_target_pairs={{0,2},{1,3},{2,0},{3,1},{4,6},{5,7},{6,4},{7,5},{8,10},{9,11},{10,... | collective-permute-start | bytes 786440 | tf_op jit(solution)/shard_map/ppermute | solution.py:1039
  156.6 13.7 %collective-permute-start.37 = (bf16[128,1024]{1,0:T(8,128)(2,1)S(1)}, bf16[128,1024]{1,0:T(8,128)(2,1)S(1)}, u32[]{:S(2)}, u32[]{:S(2)}) collective-permute-start(bf16[128,1024]{1,0:T(8,128)(2,1)S(1)} %bitcast.60), channel_id=1, source_target_pairs={{0,4},{1,5},{2,6},{3,7},{4,0},{5,1},{6,2},{7,3},{8,12},{9,13},{10,... | collective-permute-start | bytes 786440 | tf_op jit(solution)/shard_map/ppermute | solution.py:1039
  157.2 13.1 %collective-permute-start.38 = (bf16[128,1024]{1,0:T(8,128)(2,1)S(1)}, bf16[128,1024]{1,0:T(8,128)(2,1)S(1)}, u32[]{:S(2)}, u32[]{:S(2)}) collective-permute-start(bf16[128,1024]{1,0:T(8,128)(2,1)S(1)} %bitcast.61), channel_id=1, source_target_pairs={{0,6},{1,7},{2,4},{3,5},{4,2},{5,3},{6,0},{7,1},{8,14},{9,15},{10,... | collective-permute-start | bytes 786440 | tf_op jit(solution)/shard_map/ppermute | solution.py:1039
  187.8 11.7 %collective-permute-start.52 = (bf16[128,1024]{1,0:T(8,128)(2,1)S(1)}, bf16[128,1024]{1,0:T(8,128)(2,1)S(1)}, u32[]{:S(2)}, u32[]{:S(2)}) collective-permute-start(bf16[128,1024]{1,0:T(8,128)(2,1)S(1)} %get-tuple-element.254), channel_id=1, source_target_pairs={{0,2},{1,3},{2,0},{3,1},{4,6},{5,7},{6,4},{7,5},{8,10},{9,11},{10,... | collective-permute-start | bytes 786440 | tf_op jit(solution)/shard_map/ppermute | solution.py:1039
  188.7 13.7 %collective-permute-start.53 = (bf16[128,1024]{1,0:T(8,128)(2,1)S(1)}, bf16[128,1024]{1,0:T(8,128)(2,1)S(1)}, u32[]{:S(2)}, u32[]{:S(2)}) collective-permute-start(bf16[128,1024]{1,0:T(8,128)(2,1)S(1)} %get-tuple-element.255), channel_id=1, source_target_pairs={{0,4},{1,5},{2,6},{3,7},{4,0},{5,1},{6,2},{7,3},{8,12},{9,13},{10,... | collective-permute-start | bytes 786440 | tf_op jit(solution)/shard_map/ppermute | solution.py:1039
  189.6 12.8 %collective-permute-start.54 = (bf16[128,1024]{1,0:T(8,128)(2,1)S(1)}, bf16[128,1024]{1,0:T(8,128)(2,1)S(1)}, u32[]{:S(2)}, u32[]{:S(2)}) collective-permute-start(bf16[128,1024]{1,0:T(8,128)(2,1)S(1)} %get-tuple-element.256), channel_id=1, source_target_pairs={{0,6},{1,7},{2,4},{3,5},{4,2},{5,3},{6,0},{7,1},{8,14},{9,15},{10,... | collective-permute-start | bytes 786440 | tf_op jit(solution)/shard_map/ppermute | solution.py:1039
  202.4 128.0 %reduce-scatter.6.cloned.1.call-start = ((), (), s32[]{:S(2)}) async-start(), calls=%async_computation.9 | async-start | bytes 1310720 | tf_op jit(solution)/shard_map/reduce_scatter | solution.py:1307
  204.1 9.2 %collective-permute-start.55 = (bf16[128,1024]{1,0:T(8,128)(2,1)S(1)}, bf16[128,1024]{1,0:T(8,128)(2,1)S(1)}, u32[]{:S(2)}, u32[]{:S(2)}) collective-permute-start(bf16[128,1024]{1,0:T(8,128)(2,1)S(1)} %get-tuple-element.265.refs_1_), channel_id=1, source_target_pairs={{0,2},{1,3},{2,0},{3,1},{4,6},{5,7},{6,4},{7,5},{8,10},{9,11},{10,... | collective-permute-start | bytes 786440 | tf_op jit(solution)/shard_map/ppermute | solution.py:1039
  205.3 11.0 %collective-permute-start.56 = (bf16[128,1024]{1,0:T(8,128)(2,1)S(1)}, bf16[128,1024]{1,0:T(8,128)(2,1)S(1)}, u32[]{:S(2)}, u32[]{:S(2)}) collective-permute-start(bf16[128,1024]{1,0:T(8,128)(2,1)S(1)} %get-tuple-element.265.refs_1_), channel_id=1, source_target_pairs={{0,4},{1,5},{2,6},{3,7},{4,0},{5,1},{6,2},{7,3},{8,12},{9,13},{10,... | collective-permute-start | bytes 786440 | tf_op jit(solution)/shard_map/ppermute | solution.py:1039
  205.9 11.7 %collective-permute-start.57 = (bf16[128,1024]{1,0:T(8,128)(2,1)S(1)}, bf16[128,1024]{1,0:T(8,128)(2,1)S(1)}, u32[]{:S(2)}, u32[]{:S(2)}) collective-permute-start(bf16[128,1024]{1,0:T(8,128)(2,1)S(1)} %get-tuple-element.265.refs_1_), channel_id=1, source_target_pairs={{0,6},{1,7},{2,4},{3,5},{4,2},{5,3},{6,0},{7,1},{8,14},{9,15},{10,... | collective-permute-start | bytes 786440 | tf_op jit(solution)/shard_map/ppermute | solution.py:1039
  207.6 10.0 %collective-permute-start.58 = (bf16[128,1024]{1,0:T(8,128)(2,1)S(1)}, bf16[128,1024]{1,0:T(8,128)(2,1)S(1)}, u32[]{:S(2)}, u32[]{:S(2)}) collective-permute-start(bf16[128,1024]{1,0:T(8,128)(2,1)S(1)} %get-tuple-element.265.refs_1_), channel_id=1, source_target_pairs={{0,1},{1,0},{2,3},{3,2},{4,5},{5,4},{6,7},{7,6},{8,9},{9,8},{10,11... | collective-permute-start | bytes 786440 | tf_op jit(solution)/shard_map/ppermute | solution.py:1039
  237.7 12.4 %collective-permute-start.63 = (bf16[128,1024]{1,0:T(8,128)(2,1)S(1)}, bf16[128,1024]{1,0:T(8,128)(2,1)S(1)}, u32[]{:S(2)}, u32[]{:S(2)}) collective-permute-start(bf16[128,1024]{1,0:T(8,128)(2,1)S(1)} %get-tuple-element.269), channel_id=1, source_target_pairs={{0,2},{1,3},{2,0},{3,1},{4,6},{5,7},{6,4},{7,5},{8,10},{9,11},{10,... | collective-permute-start | bytes 786440 | tf_op jit(solution)/shard_map/ppermute | solution.py:1039
  238.7 13.3 %collective-permute-start.64 = (bf16[128,1024]{1,0:T(8,128)(2,1)S(1)}, bf16[128,1024]{1,0:T(8,128)(2,1)S(1)}, u32[]{:S(2)}, u32[]{:S(2)}) collective-permute-start(bf16[128,1024]{1,0:T(8,128)(2,1)S(1)} %get-tuple-element.270), channel_id=1, source_target_pairs={{0,4},{1,5},{2,6},{3,7},{4,0},{5,1},{6,2},{7,3},{8,12},{9,13},{10,... | collective-permute-start | bytes 786440 | tf_op jit(solution)/shard_map/ppermute | solution.py:1039
  240.8 12.3 %collective-permute-start.65 = (bf16[128,1024]{1,0:T(8,128)(2,1)S(1)}, bf16[128,1024]{1,0:T(8,128)(2,1)S(1)}, u32[]{:S(2)}, u32[]{:S(2)}) collective-permute-start(bf16[128,1024]{1,0:T(8,128)(2,1)S(1)} %get-tuple-element.271), channel_id=1, source_target_pairs={{0,6},{1,7},{2,4},{3,5},{4,2},{5,3},{6,0},{7,1},{8,14},{9,15},{10,... | collective-permute-start | bytes 786440 | tf_op jit(solution)/shard_map/ppermute | solution.py:1039
  254.6 5.7 %collective-permute-start.70 = (bf16[512,2048]{1,0:T(8,128)(2,1)}, bf16[512,2048]{1,0:T(8,128)(2,1)S(1)}, u32[]{:S(2)}, u32[]{:S(2)}) collective-permute-start(bf16[512,2048]{1,0:T(8,128)(2,1)} %get-tuple-element.291), channel_id=1, source_target_pairs={{0,1},{1,0},{2,3},{3,2},{4,5},{5,4},{6,7},{7,6},{8,9},{9,8},{10,11... | collective-permute-start | bytes 6291464 | tf_op jit(solution)/shard_map/ppermute | solution.py:1039
  255.1 9.3 %collective-permute-start.66 = (bf16[128,1024]{1,0:T(8,128)(2,1)S(1)}, bf16[128,1024]{1,0:T(8,128)(2,1)}, u32[]{:S(2)}, u32[]{:S(2)}) collective-permute-start(bf16[128,1024]{1,0:T(8,128)(2,1)S(1)} %get-tuple-element.306.refs_1_), channel_id=1, source_target_pairs={{0,2},{1,3},{2,0},{3,1},{4,6},{5,7},{6,4},{7,5},{8,10},{9,11},{10,... | collective-permute-start | bytes 786440 | tf_op jit(solution)/shard_map/ppermute | solution.py:1039
  256.2 12.4 %collective-permute-start.67 = (bf16[128,1024]{1,0:T(8,128)(2,1)S(1)}, bf16[128,1024]{1,0:T(8,128)(2,1)}, u32[]{:S(2)}, u32[]{:S(2)}) collective-permute-start(bf16[128,1024]{1,0:T(8,128)(2,1)S(1)} %get-tuple-element.306.refs_1_), channel_id=1, source_target_pairs={{0,4},{1,5},{2,6},{3,7},{4,0},{5,1},{6,2},{7,3},{8,12},{9,13},{10,... | collective-permute-start | bytes 786440 | tf_op jit(solution)/shard_map/ppermute | solution.py:1039
  257.4 12.5 %collective-permute-start.68 = (bf16[128,1024]{1,0:T(8,128)(2,1)S(1)}, bf16[128,1024]{1,0:T(8,128)(2,1)}, u32[]{:S(2)}, u32[]{:S(2)}) collective-permute-start(bf16[128,1024]{1,0:T(8,128)(2,1)S(1)} %get-tuple-element.306.refs_1_), channel_id=1, source_target_pairs={{0,6},{1,7},{2,4},{3,5},{4,2},{5,3},{6,0},{7,1},{8,14},{9,15},{10,... | collective-permute-start | bytes 786440 | tf_op jit(solution)/shard_map/ppermute | solution.py:1039
  272.9 16.2 %collective-permute-start.75 = (bf16[128,2048]{1,0:T(8,128)(2,1)}, bf16[128,2048]{1,0:T(8,128)(2,1)S(1)}, u32[]{:S(2)}, u32[]{:S(2)}) collective-permute-start(bf16[128,2048]{1,0:T(8,128)(2,1)} %get-tuple-element.315), channel_id=1, source_target_pairs={{0,2},{1,3},{2,0},{3,1},{4,6},{5,7},{6,4},{7,5},{8,10},{9,11},{10,... | collective-permute-start | bytes 1572872 | tf_op jit(solution)/shard_map/ppermute | solution.py:1039
  273.8 24.2 %collective-permute-start.76 = (bf16[128,2048]{1,0:T(8,128)(2,1)}, bf16[128,2048]{1,0:T(8,128)(2,1)S(1)}, u32[]{:S(2)}, u32[]{:S(2)}) collective-permute-start(bf16[128,2048]{1,0:T(8,128)(2,1)} %get-tuple-element.316), channel_id=1, source_target_pairs={{0,4},{1,5},{2,6},{3,7},{4,0},{5,1},{6,2},{7,3},{8,12},{9,13},{10,... | collective-permute-start | bytes 1572872 | tf_op jit(solution)/shard_map/ppermute | solution.py:1039
  275.2 23.7 %collective-permute-start.77 = (bf16[128,2048]{1,0:T(8,128)(2,1)}, bf16[128,2048]{1,0:T(8,128)(2,1)S(1)}, u32[]{:S(2)}, u32[]{:S(2)}) collective-permute-start(bf16[128,2048]{1,0:T(8,128)(2,1)} %get-tuple-element.317), channel_id=1, source_target_pairs={{0,6},{1,7},{2,4},{3,5},{4,2},{5,3},{6,0},{7,1},{8,14},{9,15},{10,... | collective-permute-start | bytes 1572872 | tf_op jit(solution)/shard_map/ppermute | solution.py:1039
  276.4 70.5 %reduce-scatter.8.cloned.1.call-start = ((), (), s32[]{:S(2)}) async-start(), calls=%async_computation.10 | async-start | bytes 1310720 | tf_op jit(solution)/shard_map/reduce_scatter | solution.py:1353
  310.1 18.8 %collective-permute-start.79 = (bf16[128,1024]{1,0:T(8,128)(2,1)S(1)}, bf16[128,1024]{1,0:T(8,128)(2,1)S(1)}, u32[]{:S(2)}, u32[]{:S(2)}) collective-permute-start(bf16[128,1024]{1,0:T(8,128)(2,1)S(1)} %copy-done.23), channel_id=1, source_target_pairs={{0,2},{1,3},{2,0},{3,1},{4,6},{5,7},{6,4},{7,5},{8,10},{9,11},{10,... | collective-permute-start | bytes 786440 | tf_op jit(solution)/shard_map/ppermute | solution.py:1039
  311.3 17.7 %collective-permute-start.80 = (bf16[128,1024]{1,0:T(8,128)(2,1)S(1)}, bf16[128,1024]{1,0:T(8,128)(2,1)S(1)}, u32[]{:S(2)}, u32[]{:S(2)}) collective-permute-start(bf16[128,1024]{1,0:T(8,128)(2,1)S(1)} %get-tuple-element.324), channel_id=1, source_target_pairs={{0,4},{1,5},{2,6},{3,7},{4,0},{5,1},{6,2},{7,3},{8,12},{9,13},{10,... | collective-permute-start | bytes 786440 | tf_op jit(solution)/shard_map/ppermute | solution.py:1039
  313.2 16.5 %collective-permute-start.81 = (bf16[128,1024]{1,0:T(8,128)(2,1)S(1)}, bf16[128,1024]{1,0:T(8,128)(2,1)S(1)}, u32[]{:S(2)}, u32[]{:S(2)}) collective-permute-start(bf16[128,1024]{1,0:T(8,128)(2,1)S(1)} %get-tuple-element.325), channel_id=1, source_target_pairs={{0,6},{1,7},{2,4},{3,5},{4,2},{5,3},{6,0},{7,1},{8,14},{9,15},{10,... | collective-permute-start | bytes 786440 | tf_op jit(solution)/shard_map/ppermute | solution.py:1039
  332.3 16.2 %all-to-all-start.4 = ((bf16[8,32,1408]{2,1,0:T(8,128)(2,1)}), bf16[8,32,1408]{2,1,0:T(8,128)(2,1)S(1)}, u32[]{:S(2)}, u32[]{:S(2)}) async-start(bf16[8,32,1408]{2,1,0:T(8,128)(2,1)} %pad_maximum_fusion.1), calls=%async_computation.7 | async-start | bytes 1441792 | tf_op jit(solution)/shard_map/all_to_all | solution.py:1139
  348.6 10.4 %all-to-all-start.3 = ((bf16[8,32,384]{2,1,0:T(8,128)(2,1)}), bf16[8,32,384]{2,1,0:T(8,128)(2,1)S(1)}, u32[]{:S(2)}, u32[]{:S(2)}) async-start(bf16[8,32,384]{2,1,0:T(8,128)(2,1)} %bitcast.33), calls=%async_computation.6 | async-start | bytes 393216 | tf_op jit(solution)/shard_map/all_to_all | solution.py:1139
  (140 other events, 708.4 us)
Sparse Core Ops, SparseCore 0:
  10.7 31.1 all-gather.6
  44.8 27.8 all-gather.8
  80.7 80.7 all-gather.10
  202.5 76.7 reduce-scatter.3
  281.6 27.6 reduce-scatter.5
  312.0 27.4 reduce-scatter.7

commit v6 on v5

--- a/solution.py
+++ b/solution.py
@@ -639,7 +639,7 @@
         out_shape=(out, out),
         in_specs=[VMEM] * 6,
         out_specs=(VMEM,) * 2,
-        compiler_params=room(16),
+        compiler_params=room(60),
         cost_estimate=cost(1),
     )(own, *parts, y, params)
 

time: 372 us -> 368 us (0.989)
  local copies, waits for them, and re-layouts: 48.2 us -> 40.7 us
    unnamed x230 -> x210, local copies, waits for them, and re-layouts: 35.3 us -> 28.6 us
  transfers between devices with their start and end apart: 92 -> 92, of which waited for: 33 -> 33; matrix products, arithmetic and copies ran while one was open for 5% -> 4% of each run, Pallas kernels for 25% -> 26%
where the time goes in v6:
time: 368 us; the launch traced here: 362 us
  Pallas kernels  106 us (29%)
  waiting for transfers between devices  96.4 us (26%)
  starting transfers between devices  65.9 us (18%)
  local copies, waits for them, and re-layouts  40.7 us (11%)
  blocking collectives  31 us (8%)
  between operations  15.6 us (4%)
  other arithmetic  6.96 us (2%)
    ppermute x83, waiting for transfers between devices, hop(): return lax.ppermute(value, 'inner', route)  78.2 us
    ppermute x83, starting transfers between devices, hop(): return lax.ppermute(value, 'inner', route)  54.7 us
    unnamed x210, local copies, waits for them, and re-layouts  28.6 us
    pallas_call x2, Pallas kernels, attend_back(): pl.pallas_call(functools.partial(attend_back_kernel, causal, rows, pair /...  25.5 us
    all_to_all x3, waiting for transfers between devices, exchange(): return lax.all_to_all(value, 'inner', 0, 0)  18.1 us
    all_to_all x1, blocking collectives, exchange(): return lax.all_to_all(value, 'inner', 0, 0)  16.8 us
    all_to_all x1, blocking collectives, per_device(): tiny = lax.all_to_all(after(tiny, packed_grad), ALL, 0, 0, tiled=True)  14.2 us
    pallas_call x1, Pallas kernels, feed(): pl.pallas_call(feed_kernel, out_shape=(jax.ShapeDtypeStruct((span, hidden...  11.9 us
  transfers between devices with their start and end apart: 92, of which 33 were waited for; matrix products, arithmetic and copies ran while one was open for 4% of the time, Pallas kernels for 26%

profile of v6, /device:TPU:0, one launch (start us, length us, event | category | flops | bytes accessed | tf_op | source)
XLA Modules:
  0.0 362.3 jit_solution(13921046201441579662)
XLA Ops:
  8.9 1.7 fusion.1
  13.6 16.8 %all_to_all.32 = bf16[8,32,1408]{2,1,0:T(8,128)(2,1)S(1)} all-to-all(bf16[8,32,1408]{2,1,0:T(8,128)(2,1)S(1)} %shard_map.229), channel_id=1, replica_groups=mesh['ulys'=4,'blk'=8] {'blk'}, dimensions={0} | all-to-all | bytes 1441792 | tf_op jit(solution)/shard_map/all_to_all | solution.py:1139
  31.5 2.4 collective-permute-start.2
  34.7 5.1 %collective-permute-done.refs_1_ = bf16[128,1024]{1,0:T(8,128)(2,1)} collective-permute-done((bf16[128,1024]{1,0:T(8,128)(2,1)S(1)}, bf16[128,1024]{1,0:T(8,128)(2,1)}, u32[]{:S(2)}, u32[]{:S(2)}) %collective-permute-start) | collective-permute-done | bytes 262176 | tf_op jit(solution)/shard_map/ppermute | solution.py:1039
  39.7 4.9 %collective-permute-done.1.refs_2_ = bf16[128,1024]{1,0:T(8,128)(2,1)} collective-permute-done((bf16[128,1024]{1,0:T(8,128)(2,1)S(1)}, bf16[128,1024]{1,0:T(8,128)(2,1)}, u32[]{:S(2)}, u32[]{:S(2)}) %collective-permute-start.1) | collective-permute-done | bytes 262176 | tf_op jit(solution)/shard_map/ppermute | solution.py:1039
  47.2 3.7 %all-to-all-start.1 = ((bf16[8,128,512]{2,1,0:T(8,128)(2,1)}), bf16[8,128,512]{2,1,0:T(8,128)(2,1)S(1)}, u32[]{:S(2)}, u32[]{:S(2)}) async-start(bf16[8,128,512]{2,1,0:T(8,128)(2,1)} %shard_map.230), calls=%async_computation.1 | async-start | bytes 2097152 | tf_op jit(solution)/shard_map/all_to_all | solution.py:1139
  53.7 12.4 %all-to-all-done.1 = bf16[8,128,512]{2,1,0:T(8,128)(2,1)S(1)} async-done(((bf16[8,128,512]{2,1,0:T(8,128)(2,1)}), bf16[8,128,512]{2,1,0:T(8,128)(2,1)S(1)}, u32[]{:S(2)}, u32[]{:S(2)}) %all-to-all-start.1) | async-done | bytes 1048608 | tf_op jit(solution)/shard_map/all_to_all | solution.py:1139
  67.4 2.3 collective-permute-start.5
  69.7 6.2 %shard_map.231 = (bf16[1024,128]{1,0:T(8,128)(2,1)}, bf16[1024,128]{1,0:T(8,128)(2,1)}, bf16[1024,128]{1,0:T(8,128)(2,1)}, bf16[1024,1024]{1,0:T(8,128)(2,1)}, f...) custom-call(s32[2]{0:T(128)} %pad_add_fusion.1.table, ...), custom_call_target="tpu_custom_call" | custom-call | flops 4400000000 | bytes 14000000 | tf_op jit(solution)/shard_map/pallas_call | solution.py:415
  75.9 4.6 %collective-permute-done.4.refs_2_ = bf16[128,1024]{1,0:T(8,128)(2,1)} collective-permute-done((bf16[128,1024]{1,0:T(8,128)(2,1)S(1)}, bf16[128,1024]{1,0:T(8,128)(2,1)}, u32[]{:S(2)}, u32[]{:S(2)}) %collective-permute-start.4) | collective-permute-done | bytes 262176 | tf_op jit(solution)/shard_map/ppermute | solution.py:1039
  84.6 1.4 collective-permute-start.12
  86.0 1.8 collective-permute-start.13
  87.7 5.3 %shard_map.234 = (bf16[1024,128]{1,0:T(8,128)(2,1)}, f32[2,1024]{1,0:T(2,128)}) custom-call(s32[10]{0:T(128)} %concatenate.50.table, bf16[1024,128]{1,0:T(8,128)(2,1)} %get-tuple-element.195.q, bf16[1024,128]{1,0:T(8,128)(2,1)} %get-tuple-element.196.k, bf16[1024,128]{1,0:T(8,128)(2,1)} %get-tuple-element.197.v), custom_call_target="tpu_custom_call" | custom-call | flops 6600000000 | bytes 21000000 | tf_op jit(solution)/shard_map/pallas_call | solution.py:307
  93.3 5.3 %collective-permute-done.12.refs_10_ = bf16[128,1024]{1,0:T(8,128)(2,1)S(1)} collective-permute-done((bf16[128,1024]{1,0:T(8,128)(2,1)S(1)}, bf16[128,1024]{1,0:T(8,128)(2,1)S(1)}, u32[]{:S(2)}, u32[]{:S(2)}) %collective-permute-start.12) | collective-permute-done | bytes 262176 | tf_op jit(solution)/shard_map/ppermute | solution.py:1039
  98.7 1.7 collective-permute-start.14
  102.7 1.5 collective-permute-start.16
  104.9 3.1 collective-permute-done.14.refs_1_
  108.1 4.3 %shard_map.237 = (bf16[1024,1024]{1,0:T(8,128)(2,1)}, bf16[1024,128]{1,0:T(8,128)(2,1)}, bf16[1024,128]{1,0:T(8,128)(2,1)}, bf16[1024,384]{1,0:T(8,128)(2,1)}) custom-call(f32[16,128]{1,0:T(8,128)} %get-tuple-element.204.biases.refs_19_, bf16[1024,512]{1,0:T(8,128)(2,1)} %bitcast.81, bf16[128,1024]{1,0:T(8,128)(2,1)} %bitcast.88, ...), custom_call_target="tpu_custom_call" | custom-call | flops 3300000000 | bytes 10500000 | tf_op jit(solution)/shard_map/pallas_call | solution.py:739
  113.0 3.5 collective-permute-done.15.refs_2_
  120.7 1.8 collective-permute-start.24
  123.4 10.4 %shard_map.238 = (f32[128,1024]{1,0:T(8,128)}, bf16[1024,1024]{1,0:T(8,128)(2,1)}, bf16[1024,1024]{1,0:T(8,128)(2,1)}, bf16[1024,128]{1,0:T(8,128)(2,1)}) custom-call(bf16[1024,128]{1,0:T(8,128)(2,1)} %get-tuple-element.218.refs_0_, bf16[1024,128]{1,0:T(8,128)(2,1)} %copy-done.61, bf16[1024,128]{1,0:T(8,128)(2,1)} %copy-done.65, ...), custom_call_target="tpu_custom_call" | custom-call | flops 6600000000 | bytes 21000000 | tf_op jit(solution)/shard_map/pallas_call | solution.py:481
  133.8 6.0 %shard_map.239 = (bf16[1024,128]{1,0:T(8,128)(2,1)}, f32[2,1024]{1,0:T(2,128)}) custom-call(s32[10]{0:T(128)} %concatenate.47.table, bf16[1024,128]{1,0:T(8,128)(2,1)} %get-tuple-element.230.q, bf16[1024,128]{1,0:T(8,128)(2,1)} %get-tuple-element.231.k, bf16[1024,128]{1,0:T(8,128)(2,1)} %get-tuple-element.232.v), custom_call_target="tpu_custom_call" | custom-call | flops 6600000000 | bytes 21000000 | tf_op jit(solution)/shard_map/pallas_call | solution.py:307
  141.5 1.8 collective-permute-start.35
  143.9 5.5 %collective-permute-done.33.refs_1_ = bf16[1024,128]{1,0:T(8,128)(2,1)S(1)} collective-permute-done((bf16[1024,128]{1,0:T(8,128)(2,1)}, bf16[1024,128]{1,0:T(8,128)(2,1)S(1)}, u32[]{:S(2)}, u32[]{:S(2)}) %collective-permute-start.33) | collective-permute-done | bytes 262176 | tf_op jit(solution)/shard_map/ppermute | solution.py:1039
  149.9 3.4 collective-permute-done.35.refs_3_
  154.3 2.2 collective-permute-start.36
  157.0 1.4 collective-permute-start.38
  159.8 8.6 %shard_map.240 = (f32[128,1024]{1,0:T(8,128)}, bf16[1024,1024]{1,0:T(8,128)(2,1)}) custom-call(bf16[1024,128]{1,0:T(8,128)(2,1)} %get-tuple-element.234.refs_0_, bf16[1024,128]{1,0:T(8,128)(2,1)} %copy-done.72, bf16[1024,128]{1,0:T(8,128)(2,1)} %copy-done.73, bf16[1024,128]{1,0:T(8,128)(2,1)} %copy-done.74, bf16[1024,128]{1,0:T(8,128)(2,1)} %copy-done.75, ...), custom_call_target="tpu_custom_call" | custom-call | flops 5500000256 | bytes 17500000 | tf_op jit(solution)/shard_map/pallas_call | solution.py:506
  168.5 1.7 collective-permute-done.37.refs_2_
  172.8 11.9 %shard_map.241 = (bf16[1024,1024]{1,0:T(8,128)(2,1)S(1)}, bf16[1024,1024]{1,0:T(8,128)(2,1)S(1)}, bf16[512,1024]{1,0:T(8,128)(2,1)S(1)}, f32[512,1024]{1,0:T(8,1...) custom-call(bf16[1024,1024]{1,0:T(8,128)(2,1)} %get-tuple-element.259.h, f32[1,1024]{1,0:T(1,128)S(1)} %reshape.183.bias, ...), custom_call_target="tpu_custom_call" | custom-call | flops 14300000256 | bytes 45500000 | tf_op jit(solution)/shard_map/pallas_call | solution.py:572
  184.9 2.5 collective-permute-done.51.took
  189.4 1.8 collective-permute-start.54
  191.2 1.6 copy-done.40
  192.8 4.5 %shard_map.243 = bf16[1024,2048]{1,0:T(8,128)(2,1)S(1)} custom-call(bf16[1024,1024]{1,0:T(8,128)(2,1)S(1)} %get-tuple-element.278.act, bf16[1024,1024]{1,0:T(8,128)(2,1)S(1)} %get-tuple-element.258.slope, bf16[1024,1024]{1,0:T(8,128)(2,1)S(1)} %copy-done.39, bf16[1024,1024]{1,0:T(8,128)(2,1)S(1)} %copy-done.40), custom_call_target="tpu_custom_call" | custom-call | flops 6600000000 | bytes 21000000 | tf_op jit(solution)/shard_map/pallas_call | solution.py:661
  197.3 2.0 copy-done.4
  199.4 2.8 collective-permute-done.53.two
  205.7 1.7 collective-permute-start.57
  207.5 5.8 %collective-permute-done.55.refs_2_ = bf16[128,1024]{1,0:T(8,128)(2,1)S(1)} collective-permute-done((bf16[128,1024]{1,0:T(8,128)(2,1)S(1)}, bf16[128,1024]{1,0:T(8,128)(2,1)S(1)}, u32[]{:S(2)}, u32[]{:S(2)}) %collective-permute-start.55) | collective-permute-done | bytes 262176 | tf_op jit(solution)/shard_map/ppermute | solution.py:1039
  213.2 2.9 collective-permute-done.56.refs_3_
  219.8 13.1 %shard_map.245 = (bf16[512,1024]{1,0:T(8,128)(2,1)}, f32[512,1024]{1,0:T(8,128)}, bf16[1024,128]{1,0:T(8,128)(2,1)}, bf16[1024,128]{1,0:T(8,128)(2,1)}, bf16[102...) custom-call(s32[10]{0:T(128)} %concatenate.47.table, ...), custom_call_target="tpu_custom_call" | custom-call | flops 11000000512 | bytes 35000000 | tf_op jit(solution)/shard_map/pallas_call | solution.py:339
  233.1 2.7 collective-permute-done.62.took
  235.8 1.6 copy-done.23
  238.5 2.1 collective-permute-start.64
  241.2 2.2 copy-done.8
  244.5 3.5 shard_map.248
  250.1 1.8 collective-permute-done.64.two
  258.4 1.7 shard_map.250
  260.1 2.2 copy-done.3
  264.4 4.1 %collective-permute-done.67.refs_3_ = bf16[128,1024]{1,0:T(8,128)(2,1)} collective-permute-done((bf16[128,1024]{1,0:T(8,128)(2,1)S(1)}, bf16[128,1024]{1,0:T(8,128)(2,1)}, u32[]{:S(2)}, u32[]{:S(2)}) %collective-permute-start.67) | collective-permute-done | bytes 262176 | tf_op jit(solution)/shard_map/ppermute | solution.py:1039
  268.4 1.4 collective-permute-done.68.refs_4_
  273.6 1.4 collective-permute-start.76
  276.6 12.4 %shard_map.252 = (bf16[512,1024]{1,0:T(8,128)(2,1)}, f32[512,1024]{1,0:T(8,128)}, f32[2,1024]{1,0:T(2,128)}, bf16[1024,128]{1,0:T(8,128)(2,1)}, bf16[1024,128]{1...) custom-call(s32[10]{0:T(128)} %concatenate.50.table, ...), custom_call_target="tpu_custom_call" | custom-call | flops 11000000512 | bytes 35000000 | tf_op jit(solution)/shard_map/pallas_call | solution.py:339
  289.0 8.5 %collective-permute-done.76.two = bf16[128,2048]{1,0:T(8,128)(2,1)S(1)} collective-permute-done((bf16[128,2048]{1,0:T(8,128)(2,1)S(1)}, bf16[128,2048]{1,0:T(8,128)(2,1)S(1)}, u32[]{:S(2)}, u32[]{:S(2)}) %collective-permute-start.76) | collective-permute-done | bytes 524320 | tf_op jit(solution)/shard_map/ppermute | solution.py:1039
  302.4 1.6 copy-done.22
  307.2 1.6 shard_map.255
  313.2 14.2 %all_to_all.33 = f32[32,1,672]{2,1,0:T(1,128)S(1)} all-to-all(f32[32,1,672]{2,1,0:T(1,128)S(1)} %copy.57), channel_id=1, replica_groups=mesh['ulys'=4,'blk'=8] {'ulys','blk'}, dimensions={0} | all-to-all | bytes 172032 | tf_op jit(solution)/shard_map/all_to_all | solution.py:1354
  329.3 3.5 all-to-all-start.4
  334.2 2.8 shard_map.256
  339.2 1.4 shard_map.257
  340.6 1.6 slice.83
  342.2 2.5 all-to-all-done.4.got
  344.7 3.4 all-to-all-start.3
  348.1 1.6 shard_map.259
  351.1 3.2 all-to-all-done.3.got
  (424 shorter events, 82.3 us)
Async XLA Ops:
  7.2 37.4 %all-gather.7.cloned.1.call-start = ((), (), s32[]{:S(2)}) async-start(), calls=%async_computation.11 | async-start | bytes 1351680 | tf_op jit(solution)/shard_map/all_gather | solution.py:1198
  10.6 69.9 %all-gather.9.cloned.1.call-start = ((), (), s32[]{:S(2)}) async-start(), calls=%async_computation.12 | async-start | bytes 1310720 | tf_op jit(solution)/shard_map/all_gather | solution.py:1198
  30.4 9.3 %collective-permute-start = (bf16[128,1024]{1,0:T(8,128)(2,1)S(1)}, bf16[128,1024]{1,0:T(8,128)(2,1)}, u32[]{:S(2)}, u32[]{:S(2)}) collective-permute-start(bf16[128,1024]{1,0:T(8,128)(2,1)S(1)} %bitcast.66), channel_id=1, source_target_pairs={{0,2},{1,3},{2,0},{3,1},{4,6},{5,7},{6,4},{7,5},{8,10},{9,11},{10,... | collective-permute-start | bytes 786440 | tf_op jit(solution)/shard_map/ppermute | solution.py:1039
  31.0 13.7 %collective-permute-start.1 = (bf16[128,1024]{1,0:T(8,128)(2,1)S(1)}, bf16[128,1024]{1,0:T(8,128)(2,1)}, u32[]{:S(2)}, u32[]{:S(2)}) collective-permute-start(bf16[128,1024]{1,0:T(8,128)(2,1)S(1)} %bitcast.67), channel_id=1, source_target_pairs={{0,4},{1,5},{2,6},{3,7},{4,0},{5,1},{6,2},{7,3},{8,12},{9,13},{10,... | collective-permute-start | bytes 786440 | tf_op jit(solution)/shard_map/ppermute | solution.py:1039
  31.5 13.1 %collective-permute-start.2 = (bf16[128,1024]{1,0:T(8,128)(2,1)S(1)}, bf16[128,1024]{1,0:T(8,128)(2,1)}, u32[]{:S(2)}, u32[]{:S(2)}) collective-permute-start(bf16[128,1024]{1,0:T(8,128)(2,1)S(1)} %bitcast.68), channel_id=1, source_target_pairs={{0,6},{1,7},{2,4},{3,5},{4,2},{5,3},{6,0},{7,1},{8,14},{9,15},{10,... | collective-permute-start | bytes 786440 | tf_op jit(solution)/shard_map/ppermute | solution.py:1039
  47.2 19.0 %all-to-all-start.1 = ((bf16[8,128,512]{2,1,0:T(8,128)(2,1)}), bf16[8,128,512]{2,1,0:T(8,128)(2,1)S(1)}, u32[]{:S(2)}, u32[]{:S(2)}) async-start(bf16[8,128,512]{2,1,0:T(8,128)(2,1)} %shard_map.230), calls=%async_computation.1 | async-start | bytes 2097152 | tf_op jit(solution)/shard_map/all_to_all | solution.py:1139
  50.9 121.9 %all-gather.11.cloned.1.call-start = ((), (), s32[]{:S(2)}) async-start(), calls=%async_computation.13 | async-start | bytes 5242880 | tf_op jit(solution)/shard_map/all_gather | solution.py:1198
  50.9 15.8 %collective-permute-start.6 = (bf16[128,1024]{1,0:T(8,128)(2,1)S(1)}, bf16[128,1024]{1,0:T(8,128)(2,1)}, u32[]{:S(2)}, u32[]{:S(2)}) collective-permute-start(bf16[128,1024]{1,0:T(8,128)(2,1)S(1)} %bitcast.69), channel_id=1, source_target_pairs={{0,1},{1,0},{2,3},{3,2},{4,5},{5,4},{6,7},{7,6},{8,9},{9,8},{10,11... | collective-permute-start | bytes 786440 | tf_op jit(solution)/shard_map/ppermute | solution.py:1039
  51.3 16.0 %collective-permute-start.7 = (bf16[128,1024]{1,0:T(8,128)(2,1)}, bf16[128,1024]{1,0:T(8,128)(2,1)}, u32[]{:S(2)}, u32[]{:S(2)}) collective-permute-start(bf16[128,1024]{1,0:T(8,128)(2,1)} %collective-permute-done.refs_1_), channel_id=1, source_target_pairs={{0,1},{1,0},{2,3},{3,2},{4,5},{5,4},{6,7},{7,6},{8,9},{9,8},{10,11... | collective-permute-start | bytes 786440 | tf_op jit(solution)/shard_map/ppermute | solution.py:1039
  51.5 18.2 %collective-permute-start.8 = (bf16[128,1024]{1,0:T(8,128)(2,1)}, bf16[128,1024]{1,0:T(8,128)(2,1)}, u32[]{:S(2)}, u32[]{:S(2)}) collective-permute-start(bf16[128,1024]{1,0:T(8,128)(2,1)} %collective-permute-done.1.refs_2_), channel_id=1, source_target_pairs={{0,1},{1,0},{2,3},{3,2},{4,5},{5,4},{6,7},{7,6},{8,9},{9,8},{10,11... | collective-permute-start | bytes 786440 | tf_op jit(solution)/shard_map/ppermute | solution.py:1039
  51.8 17.9 %collective-permute-start.9 = (bf16[128,1024]{1,0:T(8,128)(2,1)}, bf16[128,1024]{1,0:T(8,128)(2,1)}, u32[]{:S(2)}, u32[]{:S(2)}) collective-permute-start(bf16[128,1024]{1,0:T(8,128)(2,1)} %collective-permute-done.2.refs_3_), channel_id=1, source_target_pairs={{0,1},{1,0},{2,3},{3,2},{4,5},{5,4},{6,7},{7,6},{8,9},{9,8},{10,11... | collective-permute-start | bytes 786440 | tf_op jit(solution)/shard_map/ppermute | solution.py:1039
  66.2 9.7 %collective-permute-start.3 = (bf16[128,1024]{1,0:T(8,128)(2,1)S(1)}, bf16[128,1024]{1,0:T(8,128)(2,1)}, u32[]{:S(2)}, u32[]{:S(2)}) collective-permute-start(bf16[128,1024]{1,0:T(8,128)(2,1)S(1)} %bitcast.89), channel_id=1, source_target_pairs={{0,2},{1,3},{2,0},{3,1},{4,6},{5,7},{6,4},{7,5},{8,10},{9,11},{10,... | collective-permute-start | bytes 786440 | tf_op jit(solution)/shard_map/ppermute | solution.py:1039
  66.7 13.8 %collective-permute-start.4 = (bf16[128,1024]{1,0:T(8,128)(2,1)S(1)}, bf16[128,1024]{1,0:T(8,128)(2,1)}, u32[]{:S(2)}, u32[]{:S(2)}) collective-permute-start(bf16[128,1024]{1,0:T(8,128)(2,1)S(1)} %bitcast.90), channel_id=1, source_target_pairs={{0,4},{1,5},{2,6},{3,7},{4,0},{5,1},{6,2},{7,3},{8,12},{9,13},{10,... | collective-permute-start | bytes 786440 | tf_op jit(solution)/shard_map/ppermute | solution.py:1039
  67.4 13.2 %collective-permute-start.5 = (bf16[128,1024]{1,0:T(8,128)(2,1)S(1)}, bf16[128,1024]{1,0:T(8,128)(2,1)}, u32[]{:S(2)}, u32[]{:S(2)}) collective-permute-start(bf16[128,1024]{1,0:T(8,128)(2,1)S(1)} %bitcast.91), channel_id=1, source_target_pairs={{0,6},{1,7},{2,4},{3,5},{4,2},{5,3},{6,0},{7,1},{8,14},{9,15},{10,... | collective-permute-start | bytes 786440 | tf_op jit(solution)/shard_map/ppermute | solution.py:1039
  80.6 218.2 %reduce-scatter.4.cloned.1.call-start = ((), (), s32[]{:S(2)}) async-start(), calls=%async_computation.8 | async-start | bytes 5242880 | tf_op jit(solution)/shard_map/reduce_scatter | solution.py:1267
  83.1 18.9 %collective-permute-start.18 = (bf16[128,1024]{1,0:T(8,128)(2,1)S(1)}, bf16[128,1024]{1,0:T(8,128)(2,1)S(1)}, u32[]{:S(2)}, u32[]{:S(2)}) collective-permute-start(bf16[128,1024]{1,0:T(8,128)(2,1)S(1)} %bitcast.92), channel_id=1, source_target_pairs={{0,1},{1,0},{2,3},{3,2},{4,5},{5,4},{6,7},{7,6},{8,9},{9,8},{10,11... | collective-permute-start | bytes 786440 | tf_op jit(solution)/shard_map/ppermute | solution.py:1039
  83.6 18.7 %collective-permute-start.19 = (bf16[128,1024]{1,0:T(8,128)(2,1)}, bf16[128,1024]{1,0:T(8,128)(2,1)S(1)}, u32[]{:S(2)}, u32[]{:S(2)}) collective-permute-start(bf16[128,1024]{1,0:T(8,128)(2,1)} %collective-permute-done.3.refs_1_), channel_id=1, source_target_pairs={{0,1},{1,0},{2,3},{3,2},{4,5},{5,4},{6,7},{7,6},{8,9},{9,8},{10,11... | collective-permute-start | bytes 786440 | tf_op jit(solution)/shard_map/ppermute | solution.py:1039
  84.2 9.2 %collective-permute-start.11 = (bf16[128,1024]{1,0:T(8,128)(2,1)S(1)}, bf16[128,1024]{1,0:T(8,128)(2,1)S(1)}, u32[]{:S(2)}, u32[]{:S(2)}) collective-permute-start(bf16[128,1024]{1,0:T(8,128)(2,1)S(1)} %shard_map.233.refs_8_.weight), channel_id=1, source_target_pairs={{0,2},{1,3},{2,0},{3,1},{4,6},{5,7},{6,4},{7,5},{8,10},{9,11},{10,... | collective-permute-start | bytes 786440 | tf_op jit(solution)/shard_map/ppermute | solution.py:1039
  84.6 14.0 %collective-permute-start.12 = (bf16[128,1024]{1,0:T(8,128)(2,1)S(1)}, bf16[128,1024]{1,0:T(8,128)(2,1)S(1)}, u32[]{:S(2)}, u32[]{:S(2)}) collective-permute-start(bf16[128,1024]{1,0:T(8,128)(2,1)S(1)} %shard_map.233.refs_8_.weight), channel_id=1, source_target_pairs={{0,4},{1,5},{2,6},{3,7},{4,0},{5,1},{6,2},{7,3},{8,12},{9,13},{10,... | collective-permute-start | bytes 786440 | tf_op jit(solution)/shard_map/ppermute | solution.py:1039
  86.0 12.7 %collective-permute-start.13 = (bf16[128,1024]{1,0:T(8,128)(2,1)S(1)}, bf16[128,1024]{1,0:T(8,128)(2,1)S(1)}, u32[]{:S(2)}, u32[]{:S(2)}) collective-permute-start(bf16[128,1024]{1,0:T(8,128)(2,1)S(1)} %shard_map.233.refs_8_.weight), channel_id=1, source_target_pairs={{0,6},{1,7},{2,4},{3,5},{4,2},{5,3},{6,0},{7,1},{8,14},{9,15},{10,... | collective-permute-start | bytes 786440 | tf_op jit(solution)/shard_map/ppermute | solution.py:1039
  93.3 9.3 %collective-permute-start.20 = (bf16[128,1024]{1,0:T(8,128)(2,1)}, bf16[128,1024]{1,0:T(8,128)(2,1)S(1)}, u32[]{:S(2)}, u32[]{:S(2)}) collective-permute-start(bf16[128,1024]{1,0:T(8,128)(2,1)} %collective-permute-done.4.refs_2_), channel_id=1, source_target_pairs={{0,1},{1,0},{2,3},{3,2},{4,5},{5,4},{6,7},{7,6},{8,9},{9,8},{10,11... | collective-permute-start | bytes 786440 | tf_op jit(solution)/shard_map/ppermute | solution.py:1039
  98.6 5.5 %collective-permute-start.21 = (bf16[128,1024]{1,0:T(8,128)(2,1)}, bf16[128,1024]{1,0:T(8,128)(2,1)S(1)}, u32[]{:S(2)}, u32[]{:S(2)}) collective-permute-start(bf16[128,1024]{1,0:T(8,128)(2,1)} %collective-permute-done.5.refs_3_), channel_id=1, source_target_pairs={{0,1},{1,0},{2,3},{3,2},{4,5},{5,4},{6,7},{7,6},{8,9},{9,8},{10,11... | collective-permute-start | bytes 786440 | tf_op jit(solution)/shard_map/ppermute | solution.py:1039
  98.7 9.4 %collective-permute-start.14 = (bf16[1024,128]{1,0:T(8,128)(2,1)}, bf16[1024,128]{1,0:T(8,128)(2,1)S(1)}, u32[]{:S(2)}, u32[]{:S(2)}) collective-permute-start(bf16[1024,128]{1,0:T(8,128)(2,1)} %get-tuple-element.218.refs_0_), channel_id=1, source_target_pairs={{0,2},{1,3},{2,0},{3,1},{4,6},{5,7},{6,4},{7,5},{8,10},{9,11},{10,... | collective-permute-start | bytes 786440 | tf_op jit(solution)/shard_map/ppermute | solution.py:1039
  102.3 14.2 %collective-permute-start.15 = (bf16[1024,128]{1,0:T(8,128)(2,1)S(1)}, bf16[1024,128]{1,0:T(8,128)(2,1)S(1)}, u32[]{:S(2)}, u32[]{:S(2)}) collective-permute-start(bf16[1024,128]{1,0:T(8,128)(2,1)S(1)} %copy-done.57), channel_id=1, source_target_pairs={{0,4},{1,5},{2,6},{3,7},{4,0},{5,1},{6,2},{7,3},{8,12},{9,13},{10,... | collective-permute-start | bytes 786440 | tf_op jit(solution)/shard_map/ppermute | solution.py:1039
  102.7 13.8 %collective-permute-start.16 = (bf16[1024,128]{1,0:T(8,128)(2,1)S(1)}, bf16[1024,128]{1,0:T(8,128)(2,1)S(1)}, u32[]{:S(2)}, u32[]{:S(2)}) collective-permute-start(bf16[1024,128]{1,0:T(8,128)(2,1)S(1)} %copy-done.57), channel_id=1, source_target_pairs={{0,6},{1,7},{2,4},{3,5},{4,2},{5,3},{6,0},{7,1},{8,14},{9,15},{10,... | collective-permute-start | bytes 786440 | tf_op jit(solution)/shard_map/ppermute | solution.py:1039
  104.2 12.8 %collective-permute-start.29 = (bf16[128,1024]{1,0:T(8,128)(2,1)S(1)}, bf16[128,1024]{1,0:T(8,128)(2,1)S(1)}, u32[]{:S(2)}, u32[]{:S(2)}) collective-permute-start(bf16[128,1024]{1,0:T(8,128)(2,1)S(1)} %shard_map.233.refs_8_.weight), channel_id=1, source_target_pairs={{0,1},{1,0},{2,3},{3,2},{4,5},{5,4},{6,7},{7,6},{8,9},{9,8},{10,11... | collective-permute-start | bytes 786440 | tf_op jit(solution)/shard_map/ppermute | solution.py:1039
  104.9 12.3 %collective-permute-start.30 = (bf16[128,1024]{1,0:T(8,128)(2,1)S(1)}, bf16[128,1024]{1,0:T(8,128)(2,1)S(1)}, u32[]{:S(2)}, u32[]{:S(2)}) collective-permute-start(bf16[128,1024]{1,0:T(8,128)(2,1)S(1)} %collective-permute-done.11.refs_9_), channel_id=1, source_target_pairs={{0,1},{1,0},{2,3},{3,2},{4,5},{5,4},{6,7},{7,6},{8,9},{9,8},{10,11... | collective-permute-start | bytes 786440 | tf_op jit(solution)/shard_map/ppermute | solution.py:1039
  108.0 9.5 %collective-permute-start.31 = (bf16[128,1024]{1,0:T(8,128)(2,1)S(1)}, bf16[128,1024]{1,0:T(8,128)(2,1)S(1)}, u32[]{:S(2)}, u32[]{:S(2)}) collective-permute-start(bf16[128,1024]{1,0:T(8,128)(2,1)S(1)} %collective-permute-done.12.refs_10_), channel_id=1, source_target_pairs={{0,1},{1,0},{2,3},{3,2},{4,5},{5,4},{6,7},{7,6},{8,9},{9,8},{10,11... | collective-permute-start | bytes 786440 | tf_op jit(solution)/shard_map/ppermute | solution.py:1039
  117.2 5.4 %collective-permute-start.27 = (bf16[1024,128]{1,0:T(8,128)(2,1)S(1)}, bf16[1024,128]{1,0:T(8,128)(2,1)S(1)}, u32[]{:S(2)}, u32[]{:S(2)}) collective-permute-start(bf16[1024,128]{1,0:T(8,128)(2,1)S(1)} %collective-permute-done.15.refs_2_), channel_id=1, source_target_pairs={{0,1},{1,0},{2,3},{3,2},{4,5},{5,4},{6,7},{7,6},{8,9},{9,8},{10,11... | collective-permute-start | bytes 786440 | tf_op jit(solution)/shard_map/ppermute | solution.py:1039
  119.1 14.7 %collective-permute-start.22 = (bf16[128,1024]{1,0:T(8,128)(2,1)S(1)}, bf16[128,1024]{1,0:T(8,128)(2,1)S(1)}, u32[]{:S(2)}, u32[]{:S(2)}) collective-permute-start(bf16[128,1024]{1,0:T(8,128)(2,1)S(1)} %shard_map.236.refs_8_.weight), channel_id=1, source_target_pairs={{0,2},{1,3},{2,0},{3,1},{4,6},{5,7},{6,4},{7,5},{8,10},{9,11},{10,... | collective-permute-start | bytes 786440 | tf_op jit(solution)/shard_map/ppermute | solution.py:1039
  119.4 14.3 %collective-permute-start.23 = (bf16[128,1024]{1,0:T(8,128)(2,1)S(1)}, bf16[128,1024]{1,0:T(8,128)(2,1)S(1)}, u32[]{:S(2)}, u32[]{:S(2)}) collective-permute-start(bf16[128,1024]{1,0:T(8,128)(2,1)S(1)} %shard_map.236.refs_8_.weight), channel_id=1, source_target_pairs={{0,4},{1,5},{2,6},{3,7},{4,0},{5,1},{6,2},{7,3},{8,12},{9,13},{10,... | collective-permute-start | bytes 786440 | tf_op jit(solution)/shard_map/ppermute | solution.py:1039
  120.7 13.1 %collective-permute-start.24 = (bf16[128,1024]{1,0:T(8,128)(2,1)S(1)}, bf16[128,1024]{1,0:T(8,128)(2,1)S(1)}, u32[]{:S(2)}, u32[]{:S(2)}) collective-permute-start(bf16[128,1024]{1,0:T(8,128)(2,1)S(1)} %shard_map.236.refs_8_.weight), channel_id=1, source_target_pairs={{0,6},{1,7},{2,4},{3,5},{4,2},{5,3},{6,0},{7,1},{8,14},{9,15},{10,... | collective-permute-start | bytes 786440 | tf_op jit(solution)/shard_map/ppermute | solution.py:1039
  139.9 9.5 %collective-permute-start.33 = (bf16[1024,128]{1,0:T(8,128)(2,1)}, bf16[1024,128]{1,0:T(8,128)(2,1)S(1)}, u32[]{:S(2)}, u32[]{:S(2)}) collective-permute-start(bf16[1024,128]{1,0:T(8,128)(2,1)} %get-tuple-element.234.refs_0_), channel_id=1, source_target_pairs={{0,2},{1,3},{2,0},{3,1},{4,6},{5,7},{6,4},{7,5},{8,10},{9,11},{10,... | collective-permute-start | bytes 786440 | tf_op jit(solution)/shard_map/ppermute | solution.py:1039
  140.7 8.6 %collective-permute-start.34 = (bf16[1024,128]{1,0:T(8,128)(2,1)}, bf16[1024,128]{1,0:T(8,128)(2,1)S(1)}, u32[]{:S(2)}, u32[]{:S(2)}) collective-permute-start(bf16[1024,128]{1,0:T(8,128)(2,1)} %get-tuple-element.234.refs_0_), channel_id=1, source_target_pairs={{0,4},{1,5},{2,6},{3,7},{4,0},{5,1},{6,2},{7,3},{8,12},{9,13},{10,... | collective-permute-start | bytes 786440 | tf_op jit(solution)/shard_map/ppermute | solution.py:1039
  141.5 11.7 %collective-permute-start.35 = (bf16[1024,128]{1,0:T(8,128)(2,1)}, bf16[1024,128]{1,0:T(8,128)(2,1)S(1)}, u32[]{:S(2)}, u32[]{:S(2)}) collective-permute-start(bf16[1024,128]{1,0:T(8,128)(2,1)} %get-tuple-element.234.refs_0_), channel_id=1, source_target_pairs={{0,6},{1,7},{2,4},{3,5},{4,2},{5,3},{6,0},{7,1},{8,14},{9,15},{10,... | collective-permute-start | bytes 786440 | tf_op jit(solution)/shard_map/ppermute | solution.py:1039
  143.3 9.9 %collective-permute-start.39 = (bf16[1024,128]{1,0:T(8,128)(2,1)}, bf16[1024,128]{1,0:T(8,128)(2,1)S(1)}, u32[]{:S(2)}, u32[]{:S(2)}) collective-permute-start(bf16[1024,128]{1,0:T(8,128)(2,1)} %get-tuple-element.234.refs_0_), channel_id=1, source_target_pairs={{0,1},{1,0},{2,3},{3,2},{4,5},{5,4},{6,7},{7,6},{8,9},{9,8},{10,11... | collective-permute-start | bytes 786440 | tf_op jit(solution)/shard_map/ppermute | solution.py:1039
  143.3 10.4 %collective-permute-start.43 = (bf16[128,1024]{1,0:T(8,128)(2,1)S(1)}, bf16[128,1024]{1,0:T(8,128)(2,1)S(1)}, u32[]{:S(2)}, u32[]{:S(2)}) collective-permute-start(bf16[128,1024]{1,0:T(8,128)(2,1)S(1)} %shard_map.236.refs_8_.weight), channel_id=1, source_target_pairs={{0,1},{1,0},{2,3},{3,2},{4,5},{5,4},{6,7},{7,6},{8,9},{9,8},{10,11... | collective-permute-start | bytes 786440 | tf_op jit(solution)/shard_map/ppermute | solution.py:1039
  154.3 14.2 %collective-permute-start.36 = (bf16[128,1024]{1,0:T(8,128)(2,1)S(1)}, bf16[128,1024]{1,0:T(8,128)(2,1)S(1)}, u32[]{:S(2)}, u32[]{:S(2)}) collective-permute-start(bf16[128,1024]{1,0:T(8,128)(2,1)S(1)} %bitcast.59), channel_id=1, source_target_pairs={{0,2},{1,3},{2,0},{3,1},{4,6},{5,7},{6,4},{7,5},{8,10},{9,11},{10,... | collective-permute-start | bytes 786440 | tf_op jit(solution)/shard_map/ppermute | solution.py:1039
  156.5 13.7 %collective-permute-start.37 = (bf16[128,1024]{1,0:T(8,128)(2,1)S(1)}, bf16[128,1024]{1,0:T(8,128)(2,1)S(1)}, u32[]{:S(2)}, u32[]{:S(2)}) collective-permute-start(bf16[128,1024]{1,0:T(8,128)(2,1)S(1)} %bitcast.60), channel_id=1, source_target_pairs={{0,4},{1,5},{2,6},{3,7},{4,0},{5,1},{6,2},{7,3},{8,12},{9,13},{10,... | collective-permute-start | bytes 786440 | tf_op jit(solution)/shard_map/ppermute | solution.py:1039
  157.0 13.1 %collective-permute-start.38 = (bf16[128,1024]{1,0:T(8,128)(2,1)S(1)}, bf16[128,1024]{1,0:T(8,128)(2,1)S(1)}, u32[]{:S(2)}, u32[]{:S(2)}) collective-permute-start(bf16[128,1024]{1,0:T(8,128)(2,1)S(1)} %bitcast.61), channel_id=1, source_target_pairs={{0,6},{1,7},{2,4},{3,5},{4,2},{5,3},{6,0},{7,1},{8,14},{9,15},{10,... | collective-permute-start | bytes 786440 | tf_op jit(solution)/shard_map/ppermute | solution.py:1039
  187.6 11.8 %collective-permute-start.52 = (bf16[128,1024]{1,0:T(8,128)(2,1)S(1)}, bf16[128,1024]{1,0:T(8,128)(2,1)S(1)}, u32[]{:S(2)}, u32[]{:S(2)}) collective-permute-start(bf16[128,1024]{1,0:T(8,128)(2,1)S(1)} %get-tuple-element.254), channel_id=1, source_target_pairs={{0,2},{1,3},{2,0},{3,1},{4,6},{5,7},{6,4},{7,5},{8,10},{9,11},{10,... | collective-permute-start | bytes 786440 | tf_op jit(solution)/shard_map/ppermute | solution.py:1039
  188.5 13.7 %collective-permute-start.53 = (bf16[128,1024]{1,0:T(8,128)(2,1)S(1)}, bf16[128,1024]{1,0:T(8,128)(2,1)S(1)}, u32[]{:S(2)}, u32[]{:S(2)}) collective-permute-start(bf16[128,1024]{1,0:T(8,128)(2,1)S(1)} %get-tuple-element.255), channel_id=1, source_target_pairs={{0,4},{1,5},{2,6},{3,7},{4,0},{5,1},{6,2},{7,3},{8,12},{9,13},{10,... | collective-permute-start | bytes 786440 | tf_op jit(solution)/shard_map/ppermute | solution.py:1039
  189.4 12.8 %collective-permute-start.54 = (bf16[128,1024]{1,0:T(8,128)(2,1)S(1)}, bf16[128,1024]{1,0:T(8,128)(2,1)S(1)}, u32[]{:S(2)}, u32[]{:S(2)}) collective-permute-start(bf16[128,1024]{1,0:T(8,128)(2,1)S(1)} %get-tuple-element.256), channel_id=1, source_target_pairs={{0,6},{1,7},{2,4},{3,5},{4,2},{5,3},{6,0},{7,1},{8,14},{9,15},{10,... | collective-permute-start | bytes 786440 | tf_op jit(solution)/shard_map/ppermute | solution.py:1039
  202.2 125.2 %reduce-scatter.6.cloned.1.call-start = ((), (), s32[]{:S(2)}) async-start(), calls=%async_computation.9 | async-start | bytes 1310720 | tf_op jit(solution)/shard_map/reduce_scatter | solution.py:1307
  204.0 9.2 %collective-permute-start.55 = (bf16[128,1024]{1,0:T(8,128)(2,1)S(1)}, bf16[128,1024]{1,0:T(8,128)(2,1)S(1)}, u32[]{:S(2)}, u32[]{:S(2)}) collective-permute-start(bf16[128,1024]{1,0:T(8,128)(2,1)S(1)} %get-tuple-element.265.refs_1_), channel_id=1, source_target_pairs={{0,2},{1,3},{2,0},{3,1},{4,6},{5,7},{6,4},{7,5},{8,10},{9,11},{10,... | collective-permute-start | bytes 786440 | tf_op jit(solution)/shard_map/ppermute | solution.py:1039
  205.2 11.0 %collective-permute-start.56 = (bf16[128,1024]{1,0:T(8,128)(2,1)S(1)}, bf16[128,1024]{1,0:T(8,128)(2,1)S(1)}, u32[]{:S(2)}, u32[]{:S(2)}) collective-permute-start(bf16[128,1024]{1,0:T(8,128)(2,1)S(1)} %get-tuple-element.265.refs_1_), channel_id=1, source_target_pairs={{0,4},{1,5},{2,6},{3,7},{4,0},{5,1},{6,2},{7,3},{8,12},{9,13},{10,... | collective-permute-start | bytes 786440 | tf_op jit(solution)/shard_map/ppermute | solution.py:1039
  205.7 11.7 %collective-permute-start.57 = (bf16[128,1024]{1,0:T(8,128)(2,1)S(1)}, bf16[128,1024]{1,0:T(8,128)(2,1)S(1)}, u32[]{:S(2)}, u32[]{:S(2)}) collective-permute-start(bf16[128,1024]{1,0:T(8,128)(2,1)S(1)} %get-tuple-element.265.refs_1_), channel_id=1, source_target_pairs={{0,6},{1,7},{2,4},{3,5},{4,2},{5,3},{6,0},{7,1},{8,14},{9,15},{10,... | collective-permute-start | bytes 786440 | tf_op jit(solution)/shard_map/ppermute | solution.py:1039
  207.5 10.0 %collective-permute-start.58 = (bf16[128,1024]{1,0:T(8,128)(2,1)S(1)}, bf16[128,1024]{1,0:T(8,128)(2,1)S(1)}, u32[]{:S(2)}, u32[]{:S(2)}) collective-permute-start(bf16[128,1024]{1,0:T(8,128)(2,1)S(1)} %get-tuple-element.265.refs_1_), channel_id=1, source_target_pairs={{0,1},{1,0},{2,3},{3,2},{4,5},{5,4},{6,7},{7,6},{8,9},{9,8},{10,11... | collective-permute-start | bytes 786440 | tf_op jit(solution)/shard_map/ppermute | solution.py:1039
  237.6 12.5 %collective-permute-start.63 = (bf16[128,1024]{1,0:T(8,128)(2,1)S(1)}, bf16[128,1024]{1,0:T(8,128)(2,1)S(1)}, u32[]{:S(2)}, u32[]{:S(2)}) collective-permute-start(bf16[128,1024]{1,0:T(8,128)(2,1)S(1)} %get-tuple-element.269), channel_id=1, source_target_pairs={{0,2},{1,3},{2,0},{3,1},{4,6},{5,7},{6,4},{7,5},{8,10},{9,11},{10,... | collective-permute-start | bytes 786440 | tf_op jit(solution)/shard_map/ppermute | solution.py:1039
  238.5 13.3 %collective-permute-start.64 = (bf16[128,1024]{1,0:T(8,128)(2,1)S(1)}, bf16[128,1024]{1,0:T(8,128)(2,1)S(1)}, u32[]{:S(2)}, u32[]{:S(2)}) collective-permute-start(bf16[128,1024]{1,0:T(8,128)(2,1)S(1)} %get-tuple-element.270), channel_id=1, source_target_pairs={{0,4},{1,5},{2,6},{3,7},{4,0},{5,1},{6,2},{7,3},{8,12},{9,13},{10,... | collective-permute-start | bytes 786440 | tf_op jit(solution)/shard_map/ppermute | solution.py:1039
  240.7 12.3 %collective-permute-start.65 = (bf16[128,1024]{1,0:T(8,128)(2,1)S(1)}, bf16[128,1024]{1,0:T(8,128)(2,1)S(1)}, u32[]{:S(2)}, u32[]{:S(2)}) collective-permute-start(bf16[128,1024]{1,0:T(8,128)(2,1)S(1)} %get-tuple-element.271), channel_id=1, source_target_pairs={{0,6},{1,7},{2,4},{3,5},{4,2},{5,3},{6,0},{7,1},{8,14},{9,15},{10,... | collective-permute-start | bytes 786440 | tf_op jit(solution)/shard_map/ppermute | solution.py:1039
  254.4 5.7 %collective-permute-start.70 = (bf16[512,2048]{1,0:T(8,128)(2,1)}, bf16[512,2048]{1,0:T(8,128)(2,1)S(1)}, u32[]{:S(2)}, u32[]{:S(2)}) collective-permute-start(bf16[512,2048]{1,0:T(8,128)(2,1)} %get-tuple-element.291), channel_id=1, source_target_pairs={{0,1},{1,0},{2,3},{3,2},{4,5},{5,4},{6,7},{7,6},{8,9},{9,8},{10,11... | collective-permute-start | bytes 6291464 | tf_op jit(solution)/shard_map/ppermute | solution.py:1039
  254.9 9.4 %collective-permute-start.66 = (bf16[128,1024]{1,0:T(8,128)(2,1)S(1)}, bf16[128,1024]{1,0:T(8,128)(2,1)}, u32[]{:S(2)}, u32[]{:S(2)}) collective-permute-start(bf16[128,1024]{1,0:T(8,128)(2,1)S(1)} %get-tuple-element.306.refs_1_), channel_id=1, source_target_pairs={{0,2},{1,3},{2,0},{3,1},{4,6},{5,7},{6,4},{7,5},{8,10},{9,11},{10,... | collective-permute-start | bytes 786440 | tf_op jit(solution)/shard_map/ppermute | solution.py:1039
  256.1 12.4 %collective-permute-start.67 = (bf16[128,1024]{1,0:T(8,128)(2,1)S(1)}, bf16[128,1024]{1,0:T(8,128)(2,1)}, u32[]{:S(2)}, u32[]{:S(2)}) collective-permute-start(bf16[128,1024]{1,0:T(8,128)(2,1)S(1)} %get-tuple-element.306.refs_1_), channel_id=1, source_target_pairs={{0,4},{1,5},{2,6},{3,7},{4,0},{5,1},{6,2},{7,3},{8,12},{9,13},{10,... | collective-permute-start | bytes 786440 | tf_op jit(solution)/shard_map/ppermute | solution.py:1039
  257.3 12.5 %collective-permute-start.68 = (bf16[128,1024]{1,0:T(8,128)(2,1)S(1)}, bf16[128,1024]{1,0:T(8,128)(2,1)}, u32[]{:S(2)}, u32[]{:S(2)}) collective-permute-start(bf16[128,1024]{1,0:T(8,128)(2,1)S(1)} %get-tuple-element.306.refs_1_), channel_id=1, source_target_pairs={{0,6},{1,7},{2,4},{3,5},{4,2},{5,3},{6,0},{7,1},{8,14},{9,15},{10,... | collective-permute-start | bytes 786440 | tf_op jit(solution)/shard_map/ppermute | solution.py:1039
  272.7 16.3 %collective-permute-start.75 = (bf16[128,2048]{1,0:T(8,128)(2,1)}, bf16[128,2048]{1,0:T(8,128)(2,1)S(1)}, u32[]{:S(2)}, u32[]{:S(2)}) collective-permute-start(bf16[128,2048]{1,0:T(8,128)(2,1)} %get-tuple-element.315), channel_id=1, source_target_pairs={{0,2},{1,3},{2,0},{3,1},{4,6},{5,7},{6,4},{7,5},{8,10},{9,11},{10,... | collective-permute-start | bytes 1572872 | tf_op jit(solution)/shard_map/ppermute | solution.py:1039
  273.6 23.9 %collective-permute-start.76 = (bf16[128,2048]{1,0:T(8,128)(2,1)S(1)}, bf16[128,2048]{1,0:T(8,128)(2,1)S(1)}, u32[]{:S(2)}, u32[]{:S(2)}) collective-permute-start(bf16[128,2048]{1,0:T(8,128)(2,1)S(1)} %get-tuple-element.316), channel_id=1, source_target_pairs={{0,4},{1,5},{2,6},{3,7},{4,0},{5,1},{6,2},{7,3},{8,12},{9,13},{10,... | collective-permute-start | bytes 1572872 | tf_op jit(solution)/shard_map/ppermute | solution.py:1039
  275.0 23.7 %collective-permute-start.77 = (bf16[128,2048]{1,0:T(8,128)(2,1)S(1)}, bf16[128,2048]{1,0:T(8,128)(2,1)S(1)}, u32[]{:S(2)}, u32[]{:S(2)}) collective-permute-start(bf16[128,2048]{1,0:T(8,128)(2,1)S(1)} %get-tuple-element.317), channel_id=1, source_target_pairs={{0,6},{1,7},{2,4},{3,5},{4,2},{5,3},{6,0},{7,1},{8,14},{9,15},{10,... | collective-permute-start | bytes 1572872 | tf_op jit(solution)/shard_map/ppermute | solution.py:1039
  276.3 64.3 %reduce-scatter.8.cloned.1.call-start = ((), (), s32[]{:S(2)}) async-start(), calls=%async_computation.10 | async-start | bytes 1310720 | tf_op jit(solution)/shard_map/reduce_scatter | solution.py:1353
  309.4 17.9 %collective-permute-start.79 = (bf16[128,1024]{1,0:T(8,128)(2,1)S(1)}, bf16[128,1024]{1,0:T(8,128)(2,1)S(1)}, u32[]{:S(2)}, u32[]{:S(2)}) collective-permute-start(bf16[128,1024]{1,0:T(8,128)(2,1)S(1)} %get-tuple-element.323), channel_id=1, source_target_pairs={{0,2},{1,3},{2,0},{3,1},{4,6},{5,7},{6,4},{7,5},{8,10},{9,11},{10,... | collective-permute-start | bytes 786440 | tf_op jit(solution)/shard_map/ppermute | solution.py:1039
  310.6 16.7 %collective-permute-start.80 = (bf16[128,1024]{1,0:T(8,128)(2,1)S(1)}, bf16[128,1024]{1,0:T(8,128)(2,1)S(1)}, u32[]{:S(2)}, u32[]{:S(2)}) collective-permute-start(bf16[128,1024]{1,0:T(8,128)(2,1)S(1)} %get-tuple-element.324), channel_id=1, source_target_pairs={{0,4},{1,5},{2,6},{3,7},{4,0},{5,1},{6,2},{7,3},{8,12},{9,13},{10,... | collective-permute-start | bytes 786440 | tf_op jit(solution)/shard_map/ppermute | solution.py:1039
  311.8 15.6 %collective-permute-start.81 = (bf16[128,1024]{1,0:T(8,128)(2,1)S(1)}, bf16[128,1024]{1,0:T(8,128)(2,1)S(1)}, u32[]{:S(2)}, u32[]{:S(2)}) collective-permute-start(bf16[128,1024]{1,0:T(8,128)(2,1)S(1)} %get-tuple-element.325), channel_id=1, source_target_pairs={{0,6},{1,7},{2,4},{3,5},{4,2},{5,3},{6,0},{7,1},{8,14},{9,15},{10,... | collective-permute-start | bytes 786440 | tf_op jit(solution)/shard_map/ppermute | solution.py:1039
  329.3 15.4 %all-to-all-start.4 = ((bf16[8,32,1408]{2,1,0:T(8,128)(2,1)}), bf16[8,32,1408]{2,1,0:T(8,128)(2,1)S(1)}, u32[]{:S(2)}, u32[]{:S(2)}) async-start(bf16[8,32,1408]{2,1,0:T(8,128)(2,1)} %pad_maximum_fusion.1), calls=%async_computation.7 | async-start | bytes 1441792 | tf_op jit(solution)/shard_map/all_to_all | solution.py:1139
  344.7 9.6 %all-to-all-start.3 = ((bf16[8,32,384]{2,1,0:T(8,128)(2,1)}), bf16[8,32,384]{2,1,0:T(8,128)(2,1)S(1)}, u32[]{:S(2)}, u32[]{:S(2)}) async-start(bf16[8,32,384]{2,1,0:T(8,128)(2,1)} %bitcast.33), calls=%async_computation.6 | async-start | bytes 393216 | tf_op jit(solution)/shard_map/all_to_all | solution.py:1139
  (130 other events, 699.3 us)
Sparse Core Ops, SparseCore 0:
  10.7 31.1 all-gather.6
  44.8 27.8 all-gather.8
  80.7 80.7 all-gather.10
  202.4 76.7 reduce-scatter.3
  281.4 27.6 reduce-scatter.5
  311.8 27.3 reduce-scatter.7
